TPU v7x, 32 devices: a whole 2x2x4 slice. The times are simulated.
32 devices in a mesh: expert: 2 (over y), context: 4 (over x, core), dp: 4 (over z).
Axes of the slice: x: 2, y: 2, z: 4, core: 2. Of those that a mesh axis runs over, the one named last changes fastest.
Arguments:
- inputs: bfloat16 [8, 3072, 1536], P(('expert', 'dp'), 'context'), may hold values from -6 to 6
- cotangent: bfloat16 [8, 3072, 1536], P(('expert', 'dp'), 'context'), may hold values from -6 to 6
- routes: int32 [8, 3072, 4], P(('expert', 'dp'), 'context'), may hold values from 0 to 31, all different within a row; in each aligned block of 768 rows (0 to 767, 768 to 1535, ..., all dimensions but the last counted through in order) at most 103 rows name the same one
- attn_q: float32 [1536, 1536], P('dp'), may hold values from -0.15625 to 0.15625
- attn_k: float32 [1536, 256], P('dp'), may hold values from -0.15625 to 0.15625
- attn_v: float32 [1536, 256], P('dp'), may hold values from -0.15625 to 0.15625
- attn_o: float32 [1536, 1536], P('dp'), may hold values from -0.625 to 0.625
- norm_attn: float32 [1536], P('dp'), may hold values from 0.5 to 1.5
- norm_moe: float32 [1536], P('dp'), may hold values from 0.5 to 1.5
- router: float32 [1536, 32], P('dp'), may hold values from -0.109375 to 0.109375
- expert_gate: float32 [1536, 32, 768], P('dp', 'expert'), may hold values from -0.15625 to 0.15625
- expert_up: float32 [1536, 32, 768], P('dp', 'expert'), may hold values from -0.15625 to 0.15625
- expert_down: float32 [768, 32, 1536], P('dp', 'expert'), may hold values from -0.4375 to 0.4375
Outputs:
- output: bfloat16 [8, 3072, 1536], P(('expert', 'dp'), 'context')
- grad_inputs: bfloat16 [8, 3072, 1536], P(('expert', 'dp'), 'context')
- grad_attn_q: float32 [1536, 1536], P('dp')
- grad_attn_k: float32 [1536, 256], P('dp')
- grad_attn_v: float32 [1536, 256], P('dp')
- grad_attn_o: float32 [1536, 1536], P('dp')
- grad_norm_attn: float32 [1536], P('dp')
- grad_norm_moe: float32 [1536], P('dp')
- grad_router: float32 [1536, 32], P('dp')
- grad_expert_gate: float32 [1536, 32, 768], P('dp', 'expert')
- grad_expert_up: float32 [1536, 32, 768], P('dp', 'expert')
- grad_expert_down: float32 [768, 32, 1536], P('dp', 'expert')
Inputs may be any that keep to these rules, and one draw needn't show every extreme that they name: `routes`: each row names 4 different experts. In the 768 rows of one block no expert is named more than 103 times, a bound that some block reaches.
All inputs are finite; a program needn't handle non-finite values.
Results may differ from a plain program's by a relative error of at most 0.02.
Values may be sent and summed in bfloat16 or wider, within the bound.
A program may use at most 576 MiB of HBM per device.

v0:
```python
import math

import jax
import jax.numpy as jnp
from jax import lax
from jax.sharding import PartitionSpec as P

D = 1536
HEADS = 12
KVH = 2
HD = 128
EXPERTS = 32
TOP = 4
PBLK = 256
CONT = 512
CAP = 103


epsilon = 1e-06
rope_base = 1000000.0
masked_score = -1e30


def rms_scale(values, gain):
    return values * lax.rsqrt(jnp.mean(values * values, axis=-1, keepdims=True) + epsilon) * gain


def angle_table(positions):
    steps_half = jnp.arange(HD // 2, dtype=jnp.float32)
    inverse = jnp.exp(steps_half * (-2.0 * math.log(rope_base) / HD))
    return positions.astype(jnp.float32)[..., None] * inverse


def rotary(values, angles, direction):
    halfway = values.shape[-1] // 2
    cosine = jnp.cos(angles)[..., None, :]
    sine_part = direction * jnp.sin(angles)[..., None, :]
    leading = values[..., :halfway]
    trailing = values[..., halfway:]
    return jnp.concatenate(
        [leading * cosine - trailing * sine_part, trailing * cosine + leading * sine_part], axis=-1
    )


def visible(query_pos, key_pos, prompt_len):
    query_cont = jnp.arange(query_pos.shape[0]) >= PBLK
    key_prompt = jnp.arange(key_pos.shape[0]) < prompt_len
    return (key_pos[None, :] <= query_pos[:, None]) & (key_prompt[None, :] | query_cont[:, None])


def gating(logit_rows, route_rows):
    picker = (route_rows[:, :, None] == jnp.arange(EXPERTS, dtype=jnp.int32)[None, None, :]).astype(
        logit_rows.dtype
    )
    chosen = jnp.sum(picker * logit_rows[:, None, :], axis=-1)
    return jax.nn.softmax(chosen, axis=-1)


def gated(gate_pre, up_pre):
    return jax.nn.silu(gate_pre) * up_pre


def expert_slots(flat_experts):
    picker = (flat_experts[:, None] == jnp.arange(EXPERTS, dtype=jnp.int32)[None, :]).astype(
        jnp.int32
    )
    earlier = jnp.cumsum(picker, axis=0) - picker
    return jnp.sum(earlier * picker, axis=1)


def local(
    inputs,
    cotangent,
    routes,
    attn_q,
    attn_k,
    attn_v,
    attn_o,
    norm_attn,
    norm_moe,
    router,
    expert_gate,
    expert_up,
    expert_down,
):
    low_type = jnp.bfloat16
    full_type = jnp.float32
    w_query, w_key, w_value, w_out, gain_first, gain_second, w_router, w_gate, w_up, w_down = (
        lax.all_gather(attn_q.astype(low_type), "dp", axis=0, tiled=True),
        lax.all_gather(attn_k.astype(low_type), "dp", axis=0, tiled=True),
        lax.all_gather(attn_v.astype(low_type), "dp", axis=0, tiled=True),
        lax.all_gather(attn_o.astype(low_type), "dp", axis=0, tiled=True),
        lax.all_gather(norm_attn.astype(low_type), "dp", axis=0, tiled=True),
        lax.all_gather(norm_moe.astype(low_type), "dp", axis=0, tiled=True),
        lax.all_gather(router.astype(low_type), "dp", axis=0, tiled=True),
        lax.all_gather(expert_gate.astype(low_type), "dp", axis=0, tiled=True),
        lax.all_gather(expert_up.astype(low_type), "dp", axis=0, tiled=True),
        lax.all_gather(expert_down.astype(low_type), "dp", axis=0, tiled=True),
    )
    n_context = lax.axis_size("context")
    n_expert = lax.axis_size("expert")
    block_index = lax.axis_index("context")
    prompt_len = PBLK * n_context
    tokens = inputs.shape[1]
    local_experts = w_gate.shape[1]
    group_width = HEADS // KVH
    score_scale = 1.0 / math.sqrt(HD)
    gain_one = gain_first.astype(full_type)
    gain_two = gain_second.astype(full_type)
    x_rows = inputs[0].astype(full_type)
    positions = jnp.concatenate(
        [
            block_index * PBLK + jnp.arange(PBLK, dtype=jnp.int32),
            prompt_len + jnp.arange(CONT, dtype=jnp.int32),
        ]
    )
    angles = angle_table(positions)
    normed_one = rms_scale(x_rows, gain_one).astype(low_type)
    q_proj = jnp.dot(normed_one, w_query, preferred_element_type=full_type)
    k_proj = jnp.dot(normed_one, w_key, preferred_element_type=full_type)
    v_proj = jnp.dot(normed_one, w_value, preferred_element_type=full_type)
    queries = (rotary(q_proj.reshape(tokens, HEADS, HD), angles, 1.0) * score_scale).astype(
        low_type
    )
    queries = queries.reshape(tokens, KVH, group_width, HD)
    keys_own = rotary(k_proj.reshape(tokens, KVH, HD), angles, 1.0).astype(low_type)
    values_own = v_proj.astype(low_type).reshape(tokens, KVH, HD)
    prompt_keys, prompt_values = (
        lax.all_gather(keys_own[:PBLK], "context", axis=0, tiled=True),
        lax.all_gather(values_own[:PBLK], "context", axis=0, tiled=True),
    )
    all_keys = jnp.concatenate([prompt_keys, keys_own[PBLK:]], axis=0)
    all_values = jnp.concatenate([prompt_values, values_own[PBLK:]], axis=0)
    key_pos = jnp.concatenate(
        [jnp.arange(prompt_len, dtype=jnp.int32), prompt_len + jnp.arange(CONT, dtype=jnp.int32)]
    )
    allowed = visible(positions, key_pos, prompt_len)
    head_outs = []
    log_totals = []
    for kv_head in range(KVH):
        scores = jnp.einsum(
            "tgn,kn->gtk",
            queries[:, kv_head],
            all_keys[:, kv_head],
            preferred_element_type=full_type,
        )
        scores = jnp.where(allowed[None], scores, masked_score)
        top_score = jnp.max(scores, axis=-1, keepdims=True)
        unnormed = jnp.exp(scores - top_score)
        totals = jnp.sum(unnormed, axis=-1, keepdims=True)
        attn_probs = (unnormed / totals).astype(low_type)
        head_outs.append(
            jnp.einsum(
                "gtk,kn->tgn", attn_probs, all_values[:, kv_head], preferred_element_type=full_type
            )
        )
        log_totals.append(top_score + jnp.log(totals))
    attended_low = jnp.stack(head_outs, axis=1).reshape(tokens, D).astype(low_type)
    mid_rows = x_rows + jnp.dot(attended_low, w_out, preferred_element_type=full_type)
    normed_two = rms_scale(mid_rows, gain_two).astype(low_type)
    logits = jnp.dot(normed_two, w_router, preferred_element_type=full_type)
    route_rows = routes[0]
    gate_weights = gating(logits, route_rows)
    flat_experts = route_rows.reshape(-1)
    slot_rank = expert_slots(flat_experts)
    destination = (
        flat_experts % local_experts * n_expert + flat_experts // local_experts
    ) * CAP + slot_rank
    capacity_rows = local_experts * n_expert * CAP
    assignments = tokens * TOP
    source = (
        jnp.full((capacity_rows,), assignments, dtype=jnp.int32)
        .at[destination]
        .set(jnp.arange(assignments, dtype=jnp.int32))
    )
    filled = source < assignments
    source_row = jnp.minimum(source, assignments - 1)
    send_rows = jnp.where(filled[:, None], normed_two[source_row // TOP], jnp.zeros((), low_type))
    received = lax.all_to_all(
        send_rows.reshape(local_experts, n_expert, CAP, D),
        "expert",
        split_axis=1,
        concat_axis=1,
        tiled=True,
    )
    received = received.reshape(local_experts, n_expert * CAP, D)
    gate_pre = jnp.einsum("lrd,dlf->lrf", received, w_gate, preferred_element_type=full_type)
    up_pre = jnp.einsum("lrd,dlf->lrf", received, w_up, preferred_element_type=full_type)
    activation = gated(gate_pre, up_pre).astype(low_type)
    expert_rows = jnp.einsum(
        "lrf,fld->lrd", activation, w_down, preferred_element_type=full_type
    ).astype(low_type)
    returned = lax.all_to_all(
        expert_rows.reshape(local_experts, n_expert, CAP, D),
        "expert",
        split_axis=1,
        concat_axis=1,
        tiled=True,
    )
    returned = returned.reshape(capacity_rows, D)
    picked = returned[destination].reshape(tokens, TOP, D)
    moe_out = jnp.sum(gate_weights[:, :, None] * picked.astype(full_type), axis=1)
    result = (mid_rows + moe_out).astype(low_type)
    grad_out = cotangent[0].astype(full_type)
    slot_grads = (
        (gate_weights[:, :, None] * grad_out[:, None, :]).reshape(assignments, D).astype(low_type)
    )
    send_grads = jnp.where(filled[:, None], slot_grads[source_row], jnp.zeros((), low_type))
    grad_rows = lax.all_to_all(
        send_grads.reshape(local_experts, n_expert, CAP, D),
        "expert",
        split_axis=1,
        concat_axis=1,
        tiled=True,
    )
    grad_rows = grad_rows.reshape(local_experts, n_expert * CAP, D)
    grad_gates = jnp.sum(picked.astype(full_type) * grad_out[:, None, :], axis=-1)
    grad_wdown = jnp.einsum("lrf,lrd->fld", activation, grad_rows, preferred_element_type=full_type)
    grad_act = jnp.einsum("lrd,fld->lrf", grad_rows, w_down, preferred_element_type=full_type)
    primal_gate, gated_back = jax.vjp(gated, gate_pre, up_pre)
    grad_gpre, grad_upre = gated_back(grad_act)
    grad_gpre = grad_gpre.astype(low_type)
    grad_upre = grad_upre.astype(low_type)
    grad_wgate = jnp.einsum("lrd,lrf->dlf", received, grad_gpre, preferred_element_type=full_type)
    grad_wup = jnp.einsum("lrd,lrf->dlf", received, grad_upre, preferred_element_type=full_type)
    grad_recv = jnp.einsum("lrf,dlf->lrd", grad_gpre, w_gate, preferred_element_type=full_type)
    grad_recv = (
        grad_recv + jnp.einsum("lrf,dlf->lrd", grad_upre, w_up, preferred_element_type=full_type)
    ).astype(low_type)
    back_rows = lax.all_to_all(
        grad_recv.reshape(local_experts, n_expert, CAP, D),
        "expert",
        split_axis=1,
        concat_axis=1,
        tiled=True,
    )
    back_rows = back_rows.reshape(capacity_rows, D)
    grad_normed_two = jnp.sum(
        back_rows[destination].reshape(tokens, TOP, D).astype(full_type), axis=1
    )

    def gate_of(logit_rows):
        return gating(logit_rows, route_rows)

    primal_gates, gate_back = jax.vjp(gate_of, logits)
    grad_logits = gate_back(grad_gates)[0].astype(low_type)
    grad_wrouter = jnp.einsum(
        "td,te->de", normed_two, grad_logits, preferred_element_type=full_type
    )
    grad_normed_two = grad_normed_two + jnp.einsum(
        "te,de->td", grad_logits, w_router, preferred_element_type=full_type
    )
    primal_two, norm_back_two = jax.vjp(rms_scale, mid_rows, gain_two)
    grad_mid_norm, grad_gain_two = norm_back_two(grad_normed_two)
    grad_mid = grad_out + grad_mid_norm
    grad_attn = grad_mid.astype(low_type)
    grad_wout = jnp.einsum("td,te->de", attended_low, grad_attn, preferred_element_type=full_type)
    grad_attended = jnp.einsum(
        "te,de->td", grad_attn, w_out, preferred_element_type=full_type
    ).astype(low_type)
    grad_attended = grad_attended.reshape(tokens, KVH, group_width, HD)
    query_grads = []
    key_grads = []
    value_grads = []
    for kv_head in range(KVH):
        scores = jnp.einsum(
            "tgn,kn->gtk",
            queries[:, kv_head],
            all_keys[:, kv_head],
            preferred_element_type=full_type,
        )
        scores = jnp.where(allowed[None], scores, masked_score)
        exact_probs = jnp.exp(scores - log_totals[kv_head])
        grad_probs = jnp.einsum(
            "tgn,kn->gtk",
            grad_attended[:, kv_head],
            all_values[:, kv_head],
            preferred_element_type=full_type,
        )
        row_dots = jnp.sum(exact_probs * grad_probs, axis=-1, keepdims=True)
        grad_scores = (exact_probs * (grad_probs - row_dots)).astype(low_type)
        query_grads.append(
            jnp.einsum(
                "gtk,kn->tgn", grad_scores, all_keys[:, kv_head], preferred_element_type=full_type
            )
        )
        key_grads.append(
            jnp.einsum(
                "gtk,tgn->kn", grad_scores, queries[:, kv_head], preferred_element_type=full_type
            )
        )
        value_grads.append(
            jnp.einsum(
                "gtk,tgn->kn",
                exact_probs.astype(low_type),
                grad_attended[:, kv_head],
                preferred_element_type=full_type,
            )
        )
    grad_queries = jnp.stack(query_grads, axis=1).reshape(tokens, HEADS, HD)
    grad_keys = jnp.stack(key_grads, axis=1)
    grad_values = jnp.stack(value_grads, axis=1)
    prompt_key_grad, prompt_value_grad = (
        lax.psum_scatter(
            grad_keys[:prompt_len].astype(jnp.bfloat16), "context", scatter_dimension=0, tiled=True
        ).astype(jnp.float32),
        lax.psum_scatter(
            grad_values[:prompt_len].astype(jnp.bfloat16),
            "context",
            scatter_dimension=0,
            tiled=True,
        ).astype(jnp.float32),
    )
    own_key_grad = jnp.concatenate([prompt_key_grad, grad_keys[prompt_len:]], axis=0)
    own_value_grad = jnp.concatenate([prompt_value_grad, grad_values[prompt_len:]], axis=0)
    grad_qproj = (
        rotary(grad_queries * score_scale, angles, -1.0).reshape(tokens, D).astype(low_type)
    )
    grad_kproj = rotary(own_key_grad, angles, -1.0).reshape(tokens, KVH * HD).astype(low_type)
    grad_vproj = own_value_grad.reshape(tokens, KVH * HD).astype(low_type)
    grad_wquery = jnp.einsum("td,te->de", normed_one, grad_qproj, preferred_element_type=full_type)
    grad_wkey = jnp.einsum("td,te->de", normed_one, grad_kproj, preferred_element_type=full_type)
    grad_wvalue = jnp.einsum("td,te->de", normed_one, grad_vproj, preferred_element_type=full_type)
    grad_normed_one = jnp.einsum("te,de->td", grad_qproj, w_query, preferred_element_type=full_type)
    grad_normed_one = grad_normed_one + jnp.einsum(
        "te,de->td", grad_kproj, w_key, preferred_element_type=full_type
    )
    grad_normed_one = grad_normed_one + jnp.einsum(
        "te,de->td", grad_vproj, w_value, preferred_element_type=full_type
    )
    primal_one, norm_back_one = jax.vjp(rms_scale, x_rows, gain_one)
    grad_x_norm, grad_gain_one = norm_back_one(grad_normed_one)
    grad_inputs = (grad_mid + grad_x_norm).astype(low_type)
    shares = (
        lax.psum_scatter(
            grad_wquery.astype(jnp.bfloat16), "dp", scatter_dimension=0, tiled=True
        ).astype(jnp.float32),
        lax.psum_scatter(
            grad_wkey.astype(jnp.bfloat16), "dp", scatter_dimension=0, tiled=True
        ).astype(jnp.float32),
        lax.psum_scatter(
            grad_wvalue.astype(jnp.bfloat16), "dp", scatter_dimension=0, tiled=True
        ).astype(jnp.float32),
        lax.psum_scatter(
            grad_wout.astype(jnp.bfloat16), "dp", scatter_dimension=0, tiled=True
        ).astype(jnp.float32),
        lax.psum_scatter(
            grad_gain_one.astype(jnp.bfloat16), "dp", scatter_dimension=0, tiled=True
        ).astype(jnp.float32),
        lax.psum_scatter(
            grad_gain_two.astype(jnp.bfloat16), "dp", scatter_dimension=0, tiled=True
        ).astype(jnp.float32),
        lax.psum_scatter(
            grad_wrouter.astype(jnp.bfloat16), "dp", scatter_dimension=0, tiled=True
        ).astype(jnp.float32),
        lax.psum_scatter(
            grad_wgate.astype(jnp.bfloat16), "dp", scatter_dimension=0, tiled=True
        ).astype(jnp.float32),
        lax.psum_scatter(
            grad_wup.astype(jnp.bfloat16), "dp", scatter_dimension=0, tiled=True
        ).astype(jnp.float32),
        lax.psum_scatter(
            grad_wdown.astype(jnp.bfloat16), "dp", scatter_dimension=0, tiled=True
        ).astype(jnp.float32),
    )
    dense_sum = lax.psum(
        (shares[0], shares[1], shares[2], shares[3], shares[4], shares[5], shares[6]),
        ("expert", "context"),
    )
    expert_sum = (
        lax.psum(shares[7].astype(jnp.bfloat16), "context").astype(jnp.float32),
        lax.psum(shares[8].astype(jnp.bfloat16), "context").astype(jnp.float32),
        lax.psum(shares[9].astype(jnp.bfloat16), "context").astype(jnp.float32),
    )
    totals_all = tuple(dense_sum) + tuple(expert_sum)
    return (
        result[None],
        grad_inputs[None],
        totals_all[0],
        totals_all[1],
        totals_all[2],
        totals_all[3],
        totals_all[4],
        totals_all[5],
        totals_all[6],
        totals_all[7],
        totals_all[8],
        totals_all[9],
    )


def solution(mesh):
    in_specs = (
        P(("expert", "dp"), "context", None),
        P(("expert", "dp"), "context", None),
        P(("expert", "dp"), "context", None),
        P("dp", None),
        P("dp", None),
        P("dp", None),
        P("dp", None),
        P("dp"),
        P("dp"),
        P("dp", None),
        P("dp", "expert", None),
        P("dp", "expert", None),
        P("dp", "expert", None),
    )
    out_specs = (
        P(("expert", "dp"), "context", None),
        P(("expert", "dp"), "context", None),
        P("dp", None),
        P("dp", None),
        P("dp", None),
        P("dp", None),
        P("dp"),
        P("dp"),
        P("dp", None),
        P("dp", "expert", None),
        P("dp", "expert", None),
        P("dp", "expert", None),
    )
    return jax.shard_map(local, mesh=mesh, in_specs=in_specs, out_specs=out_specs, check_vma=False)
```

profile of v0, /device:TPU:0, one launch (start us, length us, event | category | flops | bytes accessed | tf_op | source)
XLA Modules:
  0.0 5572.8 jit_solution(16549202093964645796)
XLA Ops:
  11.5 15.1 copy.307
  26.7 14.8 copy.308
  41.5 19.3 copy.306
  63.6 15.3 all-gather
  79.7 29.9 all_gather.37
  149.0 28.9 all_gather.39
  192.0 22.0 mul.486
  214.0 14.1 all_gather.44
  292.9 23.8 fusion.6
  379.6 25.8 gather_fusion.2
  435.8 14.9 broadcast_select_fusion
  450.7 13.6 copy.217
  485.5 98.3 %all-to-all-done = bf16[16,2,103,1536]{3,0,2,1:T(8,128)(2,1)} async-done(((bf16[16,2,103,1536]{3,0,2,1:T(8,128)(2,1)}), bf16[16,2,103,1536]{3,0,2,1:T(8,128)(2,1)}, u32[]{:S(2)}, u32[]{:S(2)}) %all-to-all-start) | async-done | bytes 10125344 | tf_op jit(solution)/shard_map/all_to_all | solution.py:179
  591.9 257.8 %all-gather.14.cloned.1.call-done = bf16[1536,16,768]{2,0,1:T(8,128)(2,1)} async-done(((bf16[384,16,768]{2,0,1:T(8,128)(2,1)}), bf16[1536,16,768]{2,0,1:T(8,128)(2,1)}) %all-gather.14.cloned.1.call-update) | async-done | bytes 37748752 | tf_op jit(solution)/shard_map/all_gather | solution.py:97
  849.7 32.6 fusion.29
  882.3 598.8 %all-gather.12.cloned.1.call-done = bf16[1536,16,768]{2,0,1:T(8,128)(2,1)} async-done(((bf16[384,16,768]{2,0,1:T(8,128)(2,1)}), bf16[1536,16,768]{2,0,1:T(8,128)(2,1)}) %all-gather.12.cloned.1.call-update) | async-done | bytes 37748752 | tf_op jit(solution)/shard_map/all_gather | solution.py:96
  1481.1 32.8 fusion.31
  1513.9 598.6 %all-gather.16.cloned.1.call-done = bf16[768,16,1536]{2,0,1:T(8,128)(2,1)} async-done(((bf16[192,16,1536]{2,0,1:T(8,128)(2,1)}), bf16[768,16,1536]{2,0,1:T(8,128)(2,1)}) %all-gather.16.cloned.1.call-update) | async-done | bytes 37748752 | tf_op jit(solution)/shard_map/all_gather | solution.py:98
  2112.4 31.6 multiply_convert_fusion.1
  2144.1 24.6 fusion.131
  2168.7 26.3 add_convert_fusion
  2215.9 21.2 convolution_convert_fusion.2
  2250.7 76.5 %all-to-all-done.3 = bf16[16,2,103,1536]{3,0,2,1:T(8,128)(2,1)} async-done(((bf16[16,2,103,1536]{3,0,2,1:T(8,128)(2,1)}), bf16[16,2,103,1536]{3,0,2,1:T(8,128)(2,1)}, u32[]{:S(2)}, u32[]{:S(2)}) %all-to-all-start.3) | async-done | bytes 10125344 | tf_op jit(solution)/shard_map/all_to_all | solution.py:230
  2358.4 86.8 %all-to-all-done.1 = bf16[16,2,103,1536]{3,0,2,1:T(8,128)(2,1)} async-done(((bf16[16,2,103,1536]{3,0,2,1:T(8,128)(2,1)}), bf16[16,2,103,1536]{3,0,2,1:T(8,128)(2,1)}, u32[]{:S(2)}, u32[]{:S(2)}) %all-to-all-start.1) | async-done | bytes 10125344 | tf_op jit(solution)/shard_map/all_to_all | solution.py:193
  2467.8 24.5 gather_fusion.3
  2492.3 24.4 gather_fusion.1
  2516.7 18.2 reshape.609
  2534.9 24.3 multiply_reduce_fusion
  2559.4 17.8 reshape.611
  2577.2 17.9 reduce_sum.176
  2656.0 40.7 fusion.3
  2696.7 46.8 fusion.5
  2764.8 22.0 convolution_convert_fusion
  2786.8 47.1 copy.285
  2834.0 21.8 convolution_convert_fusion.1
  2855.8 44.2 copy.283
  2900.0 20.8 convert_bitcast_fusion
  2920.8 48.4 copy.251
  3032.8 418.6 %reduce-scatter.35.cloned.1.call-done = bf16[384,12288]{1,0:T(8,128)(2,1)} async-done(((bf16[1536,12288]{1,0:T(8,128)(2,1)}), bf16[384,12288]{1,0:T(8,128)(2,1)}) %reduce-scatter.35.cloned.1.call-update) | async-done | bytes 9437200
  3464.1 610.2 %reduce-scatter.33.cloned.1.call-done = bf16[384,12288]{1,0:T(8,128)(2,1)} async-done(((bf16[1536,12288]{1,0:T(8,128)(2,1)}), bf16[384,12288]{1,0:T(8,128)(2,1)}) %reduce-scatter.33.cloned.1.call-update) | async-done | bytes 9437200
  4086.9 609.9 %reduce-scatter.29.cloned.1.call-done = bf16[192,16,1536]{2,1,0:T(8,128)(2,1)} async-done(((bf16[768,16,1536]{2,1,0:T(8,128)(2,1)}), bf16[192,16,1536]{2,1,0:T(8,128)(2,1)}) %reduce-scatter.29.cloned.1.call-update) | async-done | bytes 9437200 | tf_op jit(solution)/shard_map/reduce_scatter | solution.py:362
  4744.9 25.6 reduce-scatter.23.cloned.1.call-done
  4770.6 86.7 %reduce-scatter.27.cloned.1.call-done = bf16[384,1536]{1,0:T(8,128)(2,1)} async-done(((bf16[1536,1536]{1,0:T(8,128)(2,1)}), bf16[384,1536]{1,0:T(8,128)(2,1)}) %reduce-scatter.27.cloned.1.call-update) | async-done | bytes 1179664 | tf_op jit(solution)/shard_map/reduce_scatter | solution.py:344
  4857.2 88.0 %reduce-scatter.21.cloned.1.call-done = bf16[384,1536]{1,0:T(8,128)(2,1)} async-done(((bf16[1536,1536]{1,0:T(8,128)(2,1)}), bf16[384,1536]{1,0:T(8,128)(2,1)}) %reduce-scatter.21.cloned.1.call-update) | async-done | bytes 1179664 | tf_op jit(solution)/shard_map/reduce_scatter | solution.py:335
  4945.2 217.6 %all-reduce.9 = (f32[384,1536]{1,0:T(8,128)}, f32[384,256]{1,0:T(8,128)}, f32[384,256]{1,0:T(8,128)}, f32[384,1536]{1,0:T(8,128)}, f32[384]{0:T(512)}, /*index=5*/f32[384]{0:T(512)}, f32[384,32]{0,1:T(8,128)}) all-reduce(bf16[384,1536]{1,0:T(8,128)(2,1)} %reduce-scatter.21.clo, ...), channel_id=1, replica_groups=mesh['expert'=2,'context'=4,'dp'=4] {'expert','context'}, use_global_device_ids=true, to_apply=%region_25.26 | all-reduce | flops 1389312 | bytes 8337408 | tf_op jit(solution)/shard_map/psum | solution.py:366
  5162.8 361.7 %all-reduce.8.cloned.1.call-done = (bf16[384,16,768]{0,2,1:T(8,128)(2,1)}, bf16[384,16,768]{0,2,1:T(8,128)(2,1)}, bf16[192,16,1536]{2,1,0:T(8,128)(2,1)}) async-done(((bf16[384,16,768]{0,2,1:T(8,128)(2,1)}, bf16[384,16,768]{0,2,1:T(8,128)(2,1)}, bf16[192,16,1536]{2,1,0:T(8,128)(2,1)}), (bf16[384,16,768]{0,2,1:T(8,128)(2,1)}, bf16[384,16,768]{0,2,1:T(8,128)(2,1)}, ...) | async-done | bytes 28311568 | tf_op jit(solution)/shard_map/psum | solution.py:371
  5524.6 14.1 copy.252
  5538.7 14.1 copy.253
  (362 shorter events, 567.8 us)
Async XLA Ops:
  7.2 243.1 %all-gather.8.cloned.1.call-start = ((), (), s32[]{:S(2)}) async-start(), calls=%async_computation.14 | async-start | bytes 5898240 | tf_op jit(solution)/shard_map/all_gather | solution.py:89
  10.2 346.8 %all-gather.10.cloned.1.call-start = ((), (), s32[]{:S(2)}) async-start(), calls=%async_computation.15 | async-start | bytes 5898240 | tf_op jit(solution)/shard_map/all_gather | solution.py:92
  11.4 838.2 %all-gather.14.cloned.1.call-start = ((), (), s32[]{:S(2)}) async-start(), calls=%async_computation.17 | async-start | bytes 47185920 | tf_op jit(solution)/shard_map/all_gather | solution.py:97
  26.7 1454.4 %all-gather.12.cloned.1.call-start = ((), (), s32[]{:S(2)}) async-start(), calls=%async_computation.16 | async-start | bytes 47185920 | tf_op jit(solution)/shard_map/all_gather | solution.py:96
  41.5 2070.9 %all-gather.16.cloned.1.call-start = ((), (), s32[]{:S(2)}) async-start(), calls=%async_computation.18 | async-start | bytes 47185920 | tf_op jit(solution)/shard_map/all_gather | solution.py:98
  60.9 18.1 copy-start.47
  60.9 18.2 copy-start.8
  79.0 178.4 %copy-start.63 = (f32[1536]{0:T(1024)}, f32[1536]{0:T(1024)S(1)}, u32[]{:S(2)}) copy-start(f32[1536]{0:T(1024)S(1)} %reshape.658) | copy-start | bytes 18436
  79.1 33.2 copy-start.83
  79.1 45.7 copy-start.71
  79.1 45.7 copy-start.48
  79.6 54.4 copy-start.74
  79.6 177.7 %copy-start.76 = (f32[768]{0:T(1024)}, f32[768]{0:T(1024)S(1)}, u32[]{:S(2)}) copy-start(f32[768]{0:T(1024)S(1)} %fusion.112) | copy-start | bytes 9220
  136.5 45.0 copy-start.72
  177.9 14.0 copy-start.16
  250.3 92.1 %copy-start.2 = (pred[768,1536]{0,1:T(8,128)(4,1)}, pred[768,1536]{0,1:T(8,128)(4,1)S(1)}, u32[]{:S(2)}) copy-start(pred[768,1536]{0,1:T(8,128)(4,1)S(1)} %or_and_fusion) | copy-start | bytes 3538948
  292.9 49.5 copy-start.42
  316.7 25.6 copy-start.58
  329.1 13.2 copy-start.60
  365.0 49.7 copy-start
  464.3 119.5 %all-to-all-start = ((bf16[16,2,103,1536]{3,0,2,1:T(8,128)(2,1)}), bf16[16,2,103,1536]{3,0,2,1:T(8,128)(2,1)}, u32[]{:S(2)}, u32[]{:S(2)}) async-start(bf16[16,2,103,1536]{3,0,2,1:T(8,128)(2,1)} %copy.217), calls=%async_computation | async-start | bytes 20250624 | tf_op jit(solution)/shard_map/all_to_all | solution.py:179
  583.9 930.0 %all-to-all-start.2 = ((bf16[16,2,103,1536]{3,0,2,1:T(8,128)(2,1)}), bf16[16,2,103,1536]{3,0,2,1:T(8,128)(2,1)}, u32[]{:S(2)}, u32[]{:S(2)}) async-start(bf16[16,2,103,1536]{3,0,2,1:T(8,128)(2,1)} %copy.226), calls=%async_computation.2 | async-start | bytes 20250624 | tf_op jit(solution)/shard_map/all_to_all | solution.py:209
  2208.4 118.7 %all-to-all-start.3 = ((bf16[16,2,103,1536]{3,0,2,1:T(8,128)(2,1)}), bf16[16,2,103,1536]{3,0,2,1:T(8,128)(2,1)}, u32[]{:S(2)}, u32[]{:S(2)}) async-start(bf16[16,2,103,1536]{3,0,2,1:T(8,128)(2,1)} %bitcast.308), calls=%async_computation.3 | async-start | bytes 20250624 | tf_op jit(solution)/shard_map/all_to_all | solution.py:230
  2327.2 118.0 %all-to-all-start.1 = ((bf16[16,2,103,1536]{3,0,2,1:T(8,128)(2,1)}), bf16[16,2,103,1536]{3,0,2,1:T(8,128)(2,1)}, u32[]{:S(2)}, u32[]{:S(2)}) async-start(bf16[16,2,103,1536]{3,0,2,1:T(8,128)(2,1)} %bitcast.307), calls=%async_computation.1 | async-start | bytes 20250624 | tf_op jit(solution)/shard_map/all_to_all | solution.py:193
  2334.9 640.8 %reduce-scatter.19.cloned.1.call-start = ((), (), s32[]{:S(2)}) async-start(), calls=%async_computation.20 | async-start | bytes 655360 | tf_op jit(solution)/shard_map/reduce_scatter | solution.py:307
  2516.7 18.2 copy-start.23
  2534.8 24.4 copy-start.45
  2534.8 24.4 copy-start.57
  2534.9 24.5 copy-start.55
  2559.4 35.7 copy-start.46
  2577.2 17.9 copy-start.41
  2577.2 17.9 copy-start.52
  2577.2 17.9 copy-start.70
  2655.9 324.3 %reduce-scatter.17.cloned.1.call-start = ((), (), s32[]{:S(2)}) async-start(), calls=%async_computation.19 | async-start | bytes 655360 | tf_op jit(solution)/shard_map/reduce_scatter | solution.py:304
  2696.7 46.8 copy-start.7
  2764.8 686.7 %reduce-scatter.35.cloned.1.call-start = ((), (), s32[]{:S(2)}) async-start(), calls=%async_computation.28 | async-start | bytes 47185920
  2833.9 1240.3 %reduce-scatter.33.cloned.1.call-start = ((), (), s32[]{:S(2)}) async-start(), calls=%async_computation.27 | async-start | bytes 47185920
  2900.0 1796.8 %reduce-scatter.29.cloned.1.call-start = ((), (), s32[]{:S(2)}) async-start(), calls=%async_computation.25 | async-start | bytes 47185920 | tf_op jit(solution)/shard_map/reduce_scatter | solution.py:362
  2969.3 1751.6 %reduce-scatter.31.cloned.1.call-start = ((), (), s32[]{:S(2)}) async-start(), calls=%async_computation.26 | async-start | bytes 491520
  2975.6 1769.3 %reduce-scatter.25.cloned.1.call-start = ((), (), s32[]{:S(2)}) async-start(), calls=%async_computation.23 | async-start | bytes 983040 | tf_op jit(solution)/shard_map/reduce_scatter | solution.py:341
  2980.0 1790.6 %reduce-scatter.23.cloned.1.call-start = ((), (), s32[]{:S(2)}) async-start(), calls=%async_computation.22 | async-start | bytes 983040 | tf_op jit(solution)/shard_map/reduce_scatter | solution.py:338
  2984.7 1872.5 %reduce-scatter.27.cloned.1.call-start = ((), (), s32[]{:S(2)}) async-start(), calls=%async_computation.24 | async-start | bytes 5898240 | tf_op jit(solution)/shard_map/reduce_scatter | solution.py:344
  2994.0 1951.2 %reduce-scatter.21.cloned.1.call-start = ((), (), s32[]{:S(2)}) async-start(), calls=%async_computation.21 | async-start | bytes 5898240 | tf_op jit(solution)/shard_map/reduce_scatter | solution.py:335
  3032.6 2492.0 %all-reduce.8.cloned.1.call-start = ((), (), s32[]{:S(2)}) async-start(), calls=%async_computation.29 | async-start | bytes 56623104 | tf_op jit(solution)/shard_map/psum | solution.py:371
  4698.7 24.9 copy-start.17
  4698.7 24.9 copy-start.27
  4725.4 13.4 copy-start.75
  4738.8 206.4 %copy-start.62 = (bf16[384,32]{0,1:T(8,128)(2,1)S(1)}, bf16[384,32]{0,1:T(8,128)(2,1)}, u32[]{:S(2)}) copy-start(bf16[384,32]{0,1:T(8,128)(2,1)} %copy.278) | copy-start | bytes 73732
  (61 other events, 338.1 us)
Sparse Core Ops, SparseCore 0:
  10.3 104.6 all-gather.7
  117.2 101.0 all-gather.9
  219.8 629.8 all-gather.13
  851.1 629.8 all-gather.11
  1482.5 629.8 all-gather.15
  2656.1 19.5 reduce-scatter.18
  2764.9 19.6 reduce-scatter.16
  2834.0 617.3 reduce-scatter.34
  3453.9 620.2 reduce-scatter.32
  4076.5 620.2 reduce-scatter.28
  4699.2 21.6 reduce-scatter.30
  4723.0 21.8 reduce-scatter.24
  4747.8 22.7 reduce-scatter.22
  4772.7 84.4 reduce-scatter.26
  4859.4 85.7 reduce-scatter.20
  4948.5 576.0 all-reduce.7
where the time goes:
time: 5590 us; the launch traced here: 5570 us
  waiting for transfers between devices  3930 us (70%)
  local copies, waits for them, and re-layouts  577 us (10%)
  matrix products  477 us (9%)
  blocking collectives  342 us (6%)
  other arithmetic  197 us (4%)
    unnamed x19, waiting for transfers between devices  1040 us
    reduce_scatter x1, waiting for transfers between devices, local(): lax.psum_scatter(grad_wdown.astype(jnp.bfloat16), 'dp', scatter_dimension...  610 us
    all_gather x1, waiting for transfers between devices, local(): lax.all_gather(expert_gate.astype(low_type), 'dp', axis=0, tiled=True)  599 us
    all_gather x1, waiting for transfers between devices, local(): lax.all_gather(expert_down.astype(low_type), 'dp', axis=0, tiled=True)  599 us
    psum x1, waiting for transfers between devices, local(): lax.psum(shares[7].astype(jnp.bfloat16), 'context').astype(jnp.float32)  362 us
    all_gather x1, waiting for transfers between devices, local(): lax.all_gather(expert_up.astype(low_type), 'dp', axis=0, tiled=True)  258 us
    psum x1, blocking collectives, local(): lax.psum((shares[0], shares[1], shares[2], shares[3], shares[4], shares[5...  218 us
    unnamed x193, local copies, waits for them, and re-layouts  214 us
  transfers between devices with their start and end apart: 20, of which 15 were waited for; matrix products, arithmetic and copies ran while one was open for 16% of the time, Pallas kernels for 0%

commit v1 on v0

--- a/solution.py
+++ b/solution.py
@@ -1,8 +1,11 @@
+import functools
 import math
 
 import jax
 import jax.numpy as jnp
 from jax import lax
+from jax.experimental import pallas as pl
+from jax.experimental.pallas import tpu as pltpu
 from jax.sharding import PartitionSpec as P
 
 D = 1536
@@ -389,6 +392,647 @@
     )
 
 
+BF = jnp.bfloat16
+F32 = jnp.float32
+SLOTS = 104
+PLANE = ("expert", "context")
+VMEM_BYTES = 60 * 1024 * 1024
+
+
+def mxu(lhs, rhs, contract=((1,), (0,))):
+    return lax.dot_general(lhs, rhs, (contract, ((), ())), preferred_element_type=F32)
+
+
+def grant(bytes_wanted=VMEM_BYTES):
+    return pltpu.CompilerParams(vmem_limit_bytes=bytes_wanted)
+
+
+def turn(values, cosine, sine):
+    return values * cosine + pltpu.roll(values, HD // 2, 1) * sine
+
+
+def project_kernel(x_ref, gain_ref, w_ref, cos_ref, sin_ref, out_ref, normed_ref):
+    step = pl.program_id(0)
+
+    @pl.when(step == 0)
+    def _():
+        rows = x_ref[...].astype(F32)
+        scale = lax.rsqrt(jnp.mean(rows * rows, axis=-1, keepdims=True) + epsilon)
+        normed_ref[...] = (rows * scale * gain_ref[...]).astype(BF)
+
+    product = mxu(normed_ref[...], w_ref[...])
+    is_query = step < HEADS // 2
+    is_value = step == HEADS // 2 + KVH // 2
+    cosine = jnp.where(is_value, 1.0, cos_ref[...])
+    sine = jnp.where(is_value, 0.0, sin_ref[...])
+    factor = jnp.where(is_query, 1.0 / math.sqrt(HD), 1.0)
+    for half in range(2):
+        part = product[:, half * HD : (half + 1) * HD]
+        out_ref[:, half * HD : (half + 1) * HD] = (turn(part, cosine, sine) * factor).astype(BF)
+
+
+def project(x_low, gain, w_qkv, cosine, sine):
+    tokens, width = x_low.shape[0], w_qkv.shape[1]
+    whole = lambda j: (0, 0)
+    return pl.pallas_call(
+        project_kernel,
+        grid=(width // (2 * HD),),
+        in_specs=[
+            pl.BlockSpec((tokens, D), whole),
+            pl.BlockSpec((1, D), whole),
+            pl.BlockSpec((D, 2 * HD), lambda j: (0, j)),
+            pl.BlockSpec((tokens, HD), whole),
+            pl.BlockSpec((tokens, HD), whole),
+        ],
+        out_specs=[
+            pl.BlockSpec((tokens, 2 * HD), lambda j: (0, j)),
+            pl.BlockSpec((tokens, D), whole),
+        ],
+        out_shape=[
+            jax.ShapeDtypeStruct((tokens, width), BF),
+            jax.ShapeDtypeStruct((tokens, D), BF),
+        ],
+        compiler_params=grant(),
+        name="project",
+    )(x_low, gain, w_qkv, cosine, sine)
+
+
+def row_blocks(prompt_len):
+    blocks = [(0, prompt_len)]
+    for start in range(0, CONT, PBLK):
+        blocks.append((PBLK + start, prompt_len + start + PBLK))
+    return blocks
+
+
+def masked_scores(scores, first_row, prompt_len, block_index):
+    row = lax.broadcasted_iota(jnp.int32, scores.shape, 0)
+    column = lax.broadcasted_iota(jnp.int32, scores.shape, 1)
+    if first_row == 0:
+        limit = row + block_index * PBLK
+    else:
+        limit = row + (prompt_len + first_row - PBLK)
+    return jnp.where(column <= limit, scores, masked_score)
+
+
+def attend_kernel(prompt_len, block_ref, q_ref, k_ref, v_ref, out_ref, log_ref):
+    for first_row, keys in row_blocks(prompt_len):
+        rows = slice(first_row, first_row + PBLK)
+        scores = mxu(q_ref[rows, :], k_ref[:keys, :], ((1,), (1,)))
+        scores = masked_scores(scores, first_row, prompt_len, block_ref[0])
+        top = jnp.max(scores, axis=-1, keepdims=True)
+        unnormed = jnp.exp(scores - top)
+        total = jnp.sum(unnormed, axis=-1, keepdims=True)
+        mixed = mxu(unnormed.astype(BF), v_ref[:keys, :]) / total
+        out_ref[rows, :] = mixed.astype(BF)
+        log_ref[0, rows, :] = top + jnp.log(total)
+
+
+def attend(block_index, qkv, keys_values, prompt_len):
+    tokens, key_rows = qkv.shape[0], keys_values.shape[0]
+    width = HEADS // KVH
+    return pl.pallas_call(
+        functools.partial(attend_kernel, prompt_len),
+        grid=(HEADS,),
+        in_specs=[
+            pl.BlockSpec(memory_space=pltpu.SMEM),
+            pl.BlockSpec((tokens, HD), lambda h: (0, h)),
+            pl.BlockSpec((key_rows, HD), lambda h: (0, h // width)),
+            pl.BlockSpec((key_rows, HD), lambda h: (0, KVH + h // width)),
+        ],
+        out_specs=[
+            pl.BlockSpec((tokens, HD), lambda h: (0, h)),
+            pl.BlockSpec((1, tokens, 1), lambda h: (h, 0, 0)),
+        ],
+        out_shape=[
+            jax.ShapeDtypeStruct((tokens, D), BF),
+            jax.ShapeDtypeStruct((HEADS, tokens, 1), F32),
+        ],
+        compiler_params=grant(),
+        name="attend",
+    )(block_index, qkv, keys_values, keys_values)
+
+
+def attend_back_kernel(
+    prompt_len, block_ref, q_ref, k_ref, v_ref, do_ref, log_ref, cos_ref, sin_ref, dq_ref, dk_ref, dv_ref
+):
+    @pl.when(pl.program_id(1) == 0)
+    def _():
+        dk_ref[...] = jnp.zeros_like(dk_ref)
+        dv_ref[...] = jnp.zeros_like(dv_ref)
+
+    for first_row, keys in row_blocks(prompt_len):
+        rows = slice(first_row, first_row + PBLK)
+        queries, grads = q_ref[rows, :], do_ref[rows, :]
+        scores = mxu(queries, k_ref[:keys, :], ((1,), (1,)))
+        scores = masked_scores(scores, first_row, prompt_len, block_ref[0])
+        probs = jnp.exp(scores - log_ref[0, rows, :])
+        grad_probs = mxu(grads, v_ref[:keys, :], ((1,), (1,)))
+        dots = jnp.sum(probs * grad_probs, axis=-1, keepdims=True)
+        grad_scores = (probs * (grad_probs - dots)).astype(BF)
+        grad_query = mxu(grad_scores, k_ref[:keys, :])
+        grad_query = turn(grad_query, cos_ref[rows, :], -sin_ref[rows, :]) * (1.0 / math.sqrt(HD))
+        dq_ref[rows, :] = grad_query.astype(BF)
+        dk_ref[:keys, :] += mxu(grad_scores, queries, ((0,), (0,)))
+        dv_ref[:keys, :] += mxu(probs.astype(BF), grads, ((0,), (0,)))
+
+
+def attend_back(block_index, qkv, keys_values, grad_heads, logs, cosine, sine, prompt_len):
+    tokens, key_rows = qkv.shape[0], keys_values.shape[0]
+    width = HEADS // KVH
+    head = lambda i, g: (0, i * width + g)
+    whole = lambda i, g: (0, 0)
+    return pl.pallas_call(
+        functools.partial(attend_back_kernel, prompt_len),
+        grid=(KVH, width),
+        in_specs=[
+            pl.BlockSpec(memory_space=pltpu.SMEM),
+            pl.BlockSpec((tokens, HD), head),
+            pl.BlockSpec((key_rows, HD), lambda i, g: (0, i)),
+            pl.BlockSpec((key_rows, HD), lambda i, g: (0, KVH + i)),
+            pl.BlockSpec((tokens, HD), head),
+            pl.BlockSpec((1, tokens, 1), lambda i, g: (i * width + g, 0, 0)),
+            pl.BlockSpec((tokens, HD), whole),
+            pl.BlockSpec((tokens, HD), whole),
+        ],
+        out_specs=[
+            pl.BlockSpec((tokens, HD), head),
+            pl.BlockSpec((key_rows, HD), lambda i, g: (0, i)),
+            pl.BlockSpec((key_rows, HD), lambda i, g: (0, i)),
+        ],
+        out_shape=[
+            jax.ShapeDtypeStruct((tokens, D), BF),
+            jax.ShapeDtypeStruct((key_rows, KVH * HD), F32),
+            jax.ShapeDtypeStruct((key_rows, KVH * HD), F32),
+        ],
+        compiler_params=grant(),
+        name="attend_back",
+    )(block_index, qkv, keys_values, keys_values, grad_heads, logs, cosine, sine)
+
+
+def segment_matrix(parts, transposed):
+    shape = (parts * SLOTS, parts) if transposed else (parts, parts * SLOTS)
+    long = lax.broadcasted_iota(jnp.int32, shape, 0 if transposed else 1)
+    short = lax.broadcasted_iota(jnp.int32, shape, 1 if transposed else 0)
+    inside = (long >= short * SLOTS) & (long < (short + 1) * SLOTS)
+    return jnp.where(inside, 1.0, 0.0).astype(BF)
+
+
+def slot_matrix(ranks, parts, transposed):
+    if transposed:
+        spread = mxu(segment_matrix(parts, True), ranks)
+        slot = lax.broadcasted_iota(jnp.int32, (parts * SLOTS, 1), 0)
+    else:
+        spread = mxu(ranks, segment_matrix(parts, False))
+        slot = lax.broadcasted_iota(jnp.int32, (1, parts * SLOTS), 1)
+    for part in range(parts - 1, 0, -1):
+        slot = jnp.where(slot >= part * SLOTS, slot - SLOTS, slot)
+    return jnp.where(spread == slot.astype(F32), 1.0, 0.0).astype(BF)
+
+
+def spread_kernel(parts, rank0_ref, rank1_ref, rows_ref, out0_ref, out1_ref):
+    for rank_ref, out_ref in ((rank0_ref, out0_ref), (rank1_ref, out1_ref)):
+        chooser = slot_matrix(rank_ref[0], parts, True)
+        out_ref[...] = mxu(chooser, rows_ref[...]).astype(BF)
+
+
+def spread_rows(rank0, rank1, rows):
+    dests, tokens = rank0.shape
+    steps = 2
+    parts = dests // steps
+    rank0 = rank0.reshape(steps, parts, tokens)
+    rank1 = rank1.reshape(steps, parts, tokens)
+    ranks = pl.BlockSpec((1, parts, tokens), lambda j: (j, 0, 0))
+    block = pl.BlockSpec((parts * SLOTS, D), lambda j: (j, 0))
+    shape = jax.ShapeDtypeStruct((dests * SLOTS, D), BF)
+    return pl.pallas_call(
+        functools.partial(spread_kernel, parts),
+        grid=(steps,),
+        in_specs=[ranks, ranks, pl.BlockSpec((tokens, D), lambda j: (0, 0))],
+        out_specs=[block, block],
+        out_shape=[shape, shape],
+        compiler_params=grant(),
+        name="spread_rows",
+    )(rank0, rank1, rows)
+
+
+def collect_kernel(parts, rank0_ref, rank1_ref, rows0_ref, rows1_ref, out_ref):
+    total = mxu(slot_matrix(rank0_ref[...], parts, False), rows0_ref[...])
+    total = total + mxu(slot_matrix(rank1_ref[...], parts, False), rows1_ref[...])
+    out_ref[...] = total.astype(out_ref.dtype)
+
+
+def collect_rows(rank0, rank1, rows0, rows1, kind):
+    tokens, dests = rank0.shape
+    step = PBLK
+    ranks = pl.BlockSpec((step, dests), lambda j: (j, 0))
+    slots = pl.BlockSpec((dests * SLOTS, D), lambda j: (0, 0))
+    return pl.pallas_call(
+        functools.partial(collect_kernel, dests),
+        grid=(tokens // step,),
+        in_specs=[ranks, ranks, slots, slots],
+        out_specs=pl.BlockSpec((step, D), lambda j: (j, 0)),
+        out_shape=jax.ShapeDtypeStruct((tokens, D), kind),
+        compiler_params=grant(),
+        name="collect_rows",
+    )(rank0, rank1, rows0, rows1)
+
+
+def expert_kernel(n_dp, half_steps, *refs):
+    (z_ref, xo_ref, xp_ref, go_ref, gp_ref, so_ref, sp_ref) = refs[:7]
+    pieces = refs[7 : 7 + 3 * n_dp]
+    outs = refs[7 + 3 * n_dp :]
+    (yo_ref, yp_ref, bo_ref, bp_ref, do_ref, dp_ref, xc_ref, a_ref, dg_ref, du_ref, de_ref) = outs[:11]
+    weights = outs[11:]
+    wg_ref, wu_ref, wd_ref = weights
+    step = pl.program_id(0)
+    own = step < half_steps
+
+    @pl.when(step == 0)
+    def _():
+        for which in range(3):
+            for flip in range(n_dp):
+                piece = pieces[which * n_dp + flip]
+                size = piece.shape[1]
+                start = pl.multiple_of((z_ref[0] ^ flip) * size, 64)
+                weights[which][pl.ds(start, size), :] = piece[0]
+
+    rows = jnp.where(own, xo_ref[...], xp_ref[...])
+    cot = jnp.where(own, go_ref[...], gp_ref[...])
+    share = jnp.where(own, so_ref[...], sp_ref[...])
+    xc_ref[...] = rows
+    gate_pre = mxu(rows, wg_ref[...])
+    up_pre = mxu(rows, wu_ref[...])
+    sigma = 1.0 / (1.0 + jnp.exp(-gate_pre))
+    silu = gate_pre * sigma
+    act = (silu * up_pre).astype(BF)
+    a_ref[...] = act
+    cot_full = cot.astype(F32)
+    weighted = (cot_full * share).astype(BF)
+    de_ref[...] = weighted
+    result = mxu(act, wd_ref[...])
+    dots = jnp.sum(result.astype(BF).astype(F32) * cot_full, axis=-1, keepdims=True)
+    scaled = (result * share).astype(BF)
+    grad_act = mxu(weighted, wd_ref[...], ((1,), (1,)))
+    grad_gate = (grad_act * up_pre * sigma * (1.0 + gate_pre * (1.0 - sigma))).astype(BF)
+    grad_up = (grad_act * silu).astype(BF)
+    dg_ref[...] = grad_gate
+    du_ref[...] = grad_up
+    back = mxu(grad_gate, wg_ref[...], ((1,), (1,))) + mxu(grad_up, wu_ref[...], ((1,), (1,)))
+    back = back.astype(BF)
+
+    @pl.when(own)
+    def _():
+        yo_ref[...] = scaled
+        bo_ref[...] = back
+        do_ref[...] = dots
+
+    @pl.when(jnp.logical_not(own))
+    def _():
+        yp_ref[...] = scaled
+        bp_ref[...] = back
+        dp_ref[...] = dots
+
+
+def run_expert(which, z_index, x_own, x_par, g_own, g_par, s_own, s_par, gate_pieces, up_pieces, down_pieces):
+    half_rows = x_own.shape[0]
+    step_rows = half_rows // 2
+    half_steps = 2
+    n_dp = len(gate_pieces)
+    full_hidden = gate_pieces[0].shape[2]
+    own_map = lambda j: (jnp.minimum(j, half_steps - 1), 0)
+    par_map = lambda j: (jnp.maximum(j - half_steps, 0), 0)
+    all_map = lambda j: (j, 0)
+    piece_map = lambda j: (which, 0, 0)
+
+    def pair(width):
+        return [pl.BlockSpec((step_rows, width), own_map), pl.BlockSpec((step_rows, width), par_map)]
+
+    def piece_specs(pieces):
+        return [
+            pl.BlockSpec((1,) + p.shape[1:], piece_map, pipeline_mode=pl.Buffered(1)) for p in pieces
+        ]
+
+    wide = pl.BlockSpec((step_rows, D), all_map)
+    narrow = pl.BlockSpec((step_rows, full_hidden), all_map)
+    half_shape = jax.ShapeDtypeStruct((half_rows, D), BF)
+    dot_shape = jax.ShapeDtypeStruct((half_rows, 1), F32)
+    wide_shape = jax.ShapeDtypeStruct((2 * half_rows, D), BF)
+    narrow_shape = jax.ShapeDtypeStruct((2 * half_rows, full_hidden), BF)
+    return pl.pallas_call(
+        functools.partial(expert_kernel, n_dp, half_steps),
+        grid=(2 * half_steps,),
+        in_specs=[pl.BlockSpec(memory_space=pltpu.SMEM)]
+        + pair(D)
+        + pair(D)
+        + pair(1)
+        + piece_specs(gate_pieces)
+        + piece_specs(up_pieces)
+        + piece_specs(down_pieces),
+        out_specs=pair(D) + pair(D) + pair(1) + [wide, narrow, narrow, narrow, wide],
+        out_shape=[half_shape] * 4
+        + [dot_shape] * 2
+        + [wide_shape, narrow_shape, narrow_shape, narrow_shape, wide_shape],
+        scratch_shapes=[
+            pltpu.VMEM((D, full_hidden), BF),
+            pltpu.VMEM((D, full_hidden), BF),
+            pltpu.VMEM((full_hidden, D), BF),
+        ],
+        compiler_params=grant(62 * 1024 * 1024),
+        name="experts",
+    )(z_index, x_own, x_par, g_own, g_par, s_own, s_par, *gate_pieces, *up_pieces, *down_pieces)
+
+
+def flip_permute(value, axis, size, flip):
+    return lax.ppermute(value, axis, [(i, i ^ flip) for i in range(size)])
+
+
+def plane_exchange(rows):
+    plane = lax.axis_size("expert") * lax.axis_size("context")
+    parted = rows.reshape(plane, rows.shape[0] // plane, *rows.shape[1:])
+    moved = lax.all_to_all(parted, PLANE, split_axis=0, concat_axis=0, tiled=True)
+    return moved.reshape(rows.shape)
+
+
+def gather_dense(shard):
+    n_context, n_expert = lax.axis_size("context"), lax.axis_size("expert")
+    plane = n_context * n_expert
+    here = lax.axis_index("expert") * n_context + lax.axis_index("context")
+    rows = shard.shape[0] // plane
+    part = lax.dynamic_slice_in_dim(shard, here * rows, rows, 0)
+    part = lax.all_gather(part, "dp", axis=0, tiled=False)
+    whole = lax.all_gather(part, PLANE, axis=1, tiled=False)
+    return whole.reshape(-1, shard.shape[1])
+
+
+def scatter_dense(share):
+    n_context, n_expert, n_dp = lax.axis_size("context"), lax.axis_size("expert"), lax.axis_size("dp")
+    plane = n_context * n_expert
+    width = share.shape[1]
+    rows = share.shape[0] // (plane * n_dp)
+    parts = share.astype(BF).reshape(n_dp, plane, rows, width)
+    parts = lax.psum_scatter(parts, PLANE, scatter_dimension=1, tiled=True)
+    parts = lax.psum_scatter(parts.reshape(n_dp, rows, width), "dp", scatter_dimension=0, tiled=True)
+    whole = lax.all_gather(parts.reshape(rows, width), PLANE, axis=0, tiled=True)
+    return whole.astype(F32)
+
+
+def local_paired(
+    inputs,
+    cotangent,
+    routes,
+    attn_q,
+    attn_k,
+    attn_v,
+    attn_o,
+    norm_attn,
+    norm_moe,
+    router,
+    expert_gate,
+    expert_up,
+    expert_down,
+):
+    n_context, n_expert, n_dp = lax.axis_size("context"), lax.axis_size("expert"), lax.axis_size("dp")
+    plane = n_context * n_expert
+    tokens = inputs.shape[1]
+    block_index = lax.axis_index("context")
+    z_index = lax.axis_index("dp")
+    parity = z_index % 2
+    prompt_len = PBLK * n_context
+    x_low = inputs[0]
+    cot_low = cotangent[0]
+    route_rows = routes[0]
+
+    small = jnp.concatenate(
+        [router, norm_attn[:, None], norm_moe[:, None]], axis=1
+    ).astype(BF)
+    small = jnp.pad(small, ((0, 0), (0, 128 - small.shape[1])))
+    shard_in = jnp.concatenate([attn_q.astype(BF), attn_k.astype(BF), attn_v.astype(BF), small], axis=1)
+    whole_in = gather_dense(shard_in)
+    w_out = gather_dense(attn_o.astype(BF))
+    qkv_width = D + 2 * KVH * HD
+    w_qkv = whole_in[:, :qkv_width]
+    w_router = whole_in[:, qkv_width : qkv_width + EXPERTS]
+    gain_one = whole_in[:, qkv_width + EXPERTS].astype(F32)
+    gain_two = whole_in[:, qkv_width + EXPERTS + 1].astype(F32)
+
+    per_device = expert_gate.shape[1] // n_context
+
+    def weight_pieces(weight):
+        mine = lax.dynamic_slice_in_dim(weight, block_index * per_device, per_device, 1)
+        mine = mine.astype(BF).transpose(1, 0, 2)
+        mine = mine.reshape(2, per_device // 2, mine.shape[1], mine.shape[2])
+        same = lax.dynamic_index_in_dim(mine, parity, 0, keepdims=False)
+        other = lax.dynamic_index_in_dim(mine, 1 - parity, 0, keepdims=False)
+        return [same] + [
+            flip_permute(other if flip % 2 else same, "dp", n_dp, flip) for flip in range(1, n_dp)
+        ]
+
+    gate_pieces, up_pieces, down_pieces = (
+        weight_pieces(expert_gate),
+        weight_pieces(expert_up),
+        weight_pieces(expert_down),
+    )
+
+    partner_routes = flip_permute(route_rows, "dp", n_dp, 1)
+
+    def ranks_of(rows):
+        named = jnp.sum(
+            (rows[:, :, None] == jnp.arange(EXPERTS, dtype=jnp.int32)[None, None, :]).astype(F32), axis=1
+        )
+        order = jnp.arange(tokens, dtype=jnp.int32)
+        before = (order[None, :] < order[:, None]).astype(BF)
+        count = mxu(before, named.astype(BF))
+        return named > 0, jnp.where(named > 0, count, -1.0)
+
+    named, own_ranks = ranks_of(route_rows)
+    partner_ranks = ranks_of(partner_routes)[1]
+
+    def mine_of(table):
+        parted = table.reshape(tokens, plane, 2, 2)
+        return lax.dynamic_index_in_dim(parted, parity, 2, keepdims=False)
+
+    own_sel = mine_of(own_ranks)
+    partner_sel = mine_of(partner_ranks)
+    own_pair = [own_sel[:, :, i].astype(BF) for i in range(2)]
+    partner_pair = [partner_sel[:, :, i].astype(BF) for i in range(2)]
+
+    def dispatch(rows, ranks):
+        slots = spread_rows(ranks[0].T, ranks[1].T, rows)
+        return [plane_exchange(s) for s in slots]
+
+    partner_cot = flip_permute(cot_low, "dp", n_dp, 1)
+    cot_own = dispatch(cot_low, own_pair)
+    cot_partner = dispatch(partner_cot, partner_pair)
+
+    positions = jnp.concatenate(
+        [
+            block_index * PBLK + jnp.arange(PBLK, dtype=jnp.int32),
+            prompt_len + jnp.arange(CONT, dtype=jnp.int32),
+        ]
+    )
+    angles = angle_table(positions)
+    cos_half, sin_half = jnp.cos(angles), jnp.sin(angles)
+    cosine = jnp.concatenate([cos_half, cos_half], axis=1)
+    sine = jnp.concatenate([-sin_half, sin_half], axis=1)
+    block_word = block_index.astype(jnp.int32).reshape(1)
+    z_word = z_index.astype(jnp.int32).reshape(1)
+    qkv, normed_one = project(x_low, gain_one[None, :], w_qkv, cosine, sine)
+    keys_own = qkv[:, D:]
+    prompt_kv = lax.all_gather(keys_own[:PBLK], "context", axis=0, tiled=True)
+    keys_values = jnp.concatenate([prompt_kv, keys_own[PBLK:]], axis=0)
+    attended, logs = attend(block_word, qkv, keys_values, prompt_len)
+    x_rows = x_low.astype(F32)
+    mid_rows = x_rows + mxu(attended, w_out)
+    normed_two = rms_scale(mid_rows, gain_two).astype(BF)
+
+    partner_normed = flip_permute(normed_two, "dp", n_dp, 1)
+    rows_own = dispatch(normed_two, own_pair)
+    rows_partner = dispatch(partner_normed, partner_pair)
+    logits = mxu(normed_two, w_router)
+    top_logit = jnp.max(jnp.where(named, logits, masked_score), axis=1, keepdims=True)
+    raised = jnp.where(named, jnp.exp(jnp.where(named, logits - top_logit, 0.0)), 0.0)
+    gates = raised / jnp.sum(raised, axis=1, keepdims=True)
+
+    slot_ids = jnp.arange(SLOTS, dtype=F32)
+    hits = own_ranks.T[:, None, :] == slot_ids[None, :, None]
+    slot_gates = jnp.sum(jnp.where(hits, gates.T[:, None, :], 0.0), axis=-1)
+    slot_gates = slot_gates.reshape(plane, 2, 2, SLOTS)
+    own_gates = lax.dynamic_index_in_dim(slot_gates, parity, 1, keepdims=False)
+    other_gates = lax.dynamic_index_in_dim(slot_gates, 1 - parity, 1, keepdims=False)
+    partner_gates = flip_permute(other_gates, "dp", n_dp, 1)
+    both_gates = jnp.stack([own_gates, partner_gates], axis=1)
+    both_gates = lax.all_to_all(both_gates, PLANE, split_axis=0, concat_axis=0, tiled=True)
+
+    shares = []
+    returned = []
+    for i in range(2):
+        column = lambda side: both_gates[:, side, i].reshape(plane * SLOTS, 1)
+        returned.append(
+            run_expert(
+                i,
+                z_word,
+                rows_own[i],
+                rows_partner[i],
+                cot_own[i],
+                cot_partner[i],
+                column(0),
+                column(1),
+                gate_pieces,
+                up_pieces,
+                down_pieces,
+            )
+        )
+
+    back_partner = [plane_exchange(r[3]) for r in returned]
+    back_own = [plane_exchange(r[2]) for r in returned]
+    dots = jnp.stack(
+        [
+            jnp.stack([r[4].reshape(plane, SLOTS), r[5].reshape(plane, SLOTS)], axis=1) for r in returned
+        ],
+        axis=2,
+    )
+    dots = lax.all_to_all(dots, PLANE, split_axis=0, concat_axis=0, tiled=True)
+    other_dots = flip_permute(dots[:, 1], "dp", n_dp, 1)
+    all_dots = jnp.where(
+        parity == 0,
+        jnp.stack([dots[:, 0], other_dots], axis=1),
+        jnp.stack([other_dots, dots[:, 0]], axis=1),
+    ).reshape(EXPERTS, SLOTS)
+    grad_gates = jnp.sum(
+        jnp.where(own_ranks[:, :, None] == slot_ids[None, None, :], all_dots[None], 0.0), axis=-1
+    )
+    for_partner = collect_rows(partner_pair[0], partner_pair[1], back_partner[0], back_partner[1], BF)
+    from_partner = flip_permute(for_partner, "dp", n_dp, 1)
+    grad_normed_two = collect_rows(own_pair[0], own_pair[1], back_own[0], back_own[1], F32)
+    grad_normed_two = grad_normed_two + from_partner.astype(F32)
+    grad_logits = gates * (grad_gates - jnp.sum(gates * grad_gates, axis=1, keepdims=True))
+    grad_logits = grad_logits.astype(BF)
+    grad_wrouter = mxu(normed_two, grad_logits, ((0,), (0,)))
+    grad_normed_two = grad_normed_two + mxu(grad_logits, w_router, ((1,), (1,)))
+    grad_out = cot_low.astype(F32)
+    norm_back_two = jax.vjp(rms_scale, mid_rows, gain_two)[1]
+    grad_mid_norm, grad_gain_two = norm_back_two(grad_normed_two)
+    grad_mid = grad_out + grad_mid_norm
+    grad_attn = grad_mid.astype(BF)
+    grad_attended = mxu(grad_attn, w_out, ((1,), (1,))).astype(BF)
+    grad_wout = mxu(attended, grad_attn, ((0,), (0,)))
+
+    def weight_shares(index_lhs, index_rhs):
+        made = [mxu(r[index_lhs], r[index_rhs], ((0,), (0,))).astype(BF) for r in returned]
+        made = jnp.stack(made, axis=0)
+        made = made.reshape(2, n_dp, made.shape[1] // n_dp, made.shape[2])
+
+        def quarter(flip):
+            return lax.dynamic_index_in_dim(made, z_index ^ flip, 1, keepdims=False)
+
+        got = [quarter(0)] + [
+            flip_permute(quarter(flip), "dp", n_dp, flip) for flip in range(1, n_dp)
+        ]
+        same = sum(got[flip].astype(F32) for flip in range(0, n_dp, 2)).astype(BF)
+        other = sum(got[flip].astype(F32) for flip in range(1, n_dp, 2)).astype(BF)
+        four = jnp.where(
+            parity == 0, jnp.concatenate([same, other], axis=0), jnp.concatenate([other, same], axis=0)
+        )
+        everything = lax.all_gather(four, "context", axis=0, tiled=True)
+        return everything.transpose(1, 0, 2).astype(F32)
+
+    grad_wdown = weight_shares(7, 10)
+    grad_wgate = weight_shares(6, 8)
+    grad_wup = weight_shares(6, 9)
+
+    grad_qproj, grad_keys, grad_values = attend_back(
+        block_word, qkv, keys_values, grad_attended, logs, cosine, sine, prompt_len
+    )
+    grad_kv = jnp.concatenate([grad_keys, grad_values], axis=1)
+    prompt_share = lax.psum_scatter(
+        grad_kv[:prompt_len].astype(BF), "context", scatter_dimension=0, tiled=True
+    ).astype(F32)
+    grad_kv = jnp.concatenate([prompt_share, grad_kv[prompt_len:]], axis=0)
+    grad_kproj = rotary(grad_kv[:, : KVH * HD].reshape(tokens, KVH, HD), angles, -1.0)
+    grad_kv = jnp.concatenate([grad_kproj.reshape(tokens, KVH * HD), grad_kv[:, KVH * HD :]], axis=1)
+    grad_qkv = jnp.concatenate([grad_qproj, grad_kv.astype(BF)], axis=1)
+    grad_wqkv = mxu(normed_one, grad_qkv, ((0,), (0,)))
+    grad_normed_one = mxu(grad_qkv, w_qkv, ((1,), (1,)))
+    norm_back_one = jax.vjp(rms_scale, x_rows, gain_one)[1]
+    grad_x_norm, grad_gain_one = norm_back_one(grad_normed_one)
+    grad_inputs = (grad_mid + grad_x_norm).astype(BF)
+
+    out_partner = [plane_exchange(r[1]) for r in returned]
+    out_own = [plane_exchange(r[0]) for r in returned]
+    out_for_partner = collect_rows(partner_pair[0], partner_pair[1], out_partner[0], out_partner[1], BF)
+    out_from_partner = flip_permute(out_for_partner, "dp", n_dp, 1)
+    moe_out = collect_rows(own_pair[0], own_pair[1], out_own[0], out_own[1], F32)
+    result = (mid_rows + moe_out + out_from_partner.astype(F32)).astype(BF)
+
+    grad_small = jnp.concatenate(
+        [grad_wrouter, grad_gain_one[:, None], grad_gain_two[:, None]], axis=1
+    )
+    grad_small = jnp.pad(grad_small, ((0, 0), (0, 128 - grad_small.shape[1])))
+    total_out = scatter_dense(grad_wout)
+    total_in = scatter_dense(jnp.concatenate([grad_wqkv, grad_small], axis=1))
+    return (
+        result[None],
+        grad_inputs[None],
+        total_in[:, :D],
+        total_in[:, D : D + KVH * HD],
+        total_in[:, D + KVH * HD : qkv_width],
+        total_out,
+        total_in[:, qkv_width + EXPERTS],
+        total_in[:, qkv_width + EXPERTS + 1],
+        total_in[:, qkv_width : qkv_width + EXPERTS],
+        grad_wgate,
+        grad_wup,
+        grad_wdown,
+    )
+
+
+def paired_plan(mesh):
+    n_expert, n_context, n_dp = mesh.shape["expert"], mesh.shape["context"], mesh.shape["dp"]
+    owners = 2 * n_expert * n_context
+    small_axes = all(size & (size - 1) == 0 for size in (n_expert, n_context, n_dp))
+    return small_axes and n_dp % 2 == 0 and EXPERTS == 2 * owners
+
+
 def solution(mesh):
     in_specs = (
         P(("expert", "dp"), "context", None),
@@ -419,4 +1063,5 @@
         P("dp", "expert", None),
         P("dp", "expert", None),
     )
-    return jax.shard_map(local, mesh=mesh, in_specs=in_specs, out_specs=out_specs, check_vma=False)
+    chosen = local_paired if paired_plan(mesh) else local
+    return jax.shard_map(chosen, mesh=mesh, in_specs=in_specs, out_specs=out_specs, check_vma=False)

time: 5590 us -> 1880 us (0.34)
  waiting for transfers between devices: 3930 us -> 788 us
  local copies, waits for them, and re-layouts: 577 us -> 140 us
  matrix products: 477 us -> 96.7 us
  Pallas kernels: 0 us -> 236 us
  starting transfers between devices: 32 us -> 185 us
  other arithmetic: 197 us -> 101 us
    all_gather x5 -> x8, waiting for transfers between devices: 1460 us -> 46.1 us  [the longest x2 42.4 us: gather_dense(): whole = lax.all_gather(part, PLANE, axis=1, tiled=False)]
    unnamed x19 -> x13, waiting for transfers between devices: 1040 us -> 0.22 us
    reduce_scatter x7 -> x5, waiting for transfers between devices: 811 us -> 103 us  [the longest x2 83.9 us: scatter_dense(): parts = lax.psum_scatter(parts, PLANE, scatter_dimension=1, tiled=True)]
    ppermute x0 -> x25, waiting for transfers between devices: none -> 530 us  [flip_permute(): return lax.ppermute(value, axis, [(i, i ^ flip) for i in range(size)])]
    dot_general x36 -> x16, matrix products: 477 us -> 96.7 us  [mxu(): lax.dot_general(lhs, rhs, (contract, ((), ())), preferred_element_type=F32)]
    psum x1 -> x0, waiting for transfers between devices: 362 us -> none  [local(): lax.psum(shares[7].astype(jnp.bfloat16), 'context').astype(jnp.float32)]
    all_to_all x0 -> x8, blocking collectives: none -> 255 us  [the longest x7 247 us: plane_exchange(): lax.all_to_all(parted, PLANE, split_axis=0, concat_axis=0, tiled=True)]
    pallas_call x0 -> x13, Pallas kernels: none -> 236 us  [the longest x2 80.5 us: run_expert(): pl.pallas_call(functools.partial(expert_kernel, n_dp, half_steps), grid=(...]
  transfers between devices with their start and end apart: 20 -> 48, of which waited for: 15 -> 26; matrix products, arithmetic and copies ran while one was open for 16% -> 16% of each run, Pallas kernels for 0% -> 7%
where the time goes in v1:
time: 1880 us; the launch traced here: 1860 us
  waiting for transfers between devices  788 us (42%)
  blocking collectives  294 us (16%)
  Pallas kernels  236 us (13%)
  starting transfers between devices  185 us (10%)
  local copies, waits for them, and re-layouts  140 us (7%)
  other arithmetic  101 us (5%)
  matrix products  96.7 us (5%)
    ppermute x25, waiting for transfers between devices, flip_permute(): return lax.ppermute(value, axis, [(i, i ^ flip) for i in range(size)])  530 us
    all_to_all x7, blocking collectives, plane_exchange(): lax.all_to_all(parted, PLANE, split_axis=0, concat_axis=0, tiled=True)  247 us
    ppermute x25, starting transfers between devices, flip_permute(): return lax.ppermute(value, axis, [(i, i ^ flip) for i in range(size)])  141 us
    all_to_all x9, waiting for transfers between devices, plane_exchange(): lax.all_to_all(parted, PLANE, split_axis=0, concat_axis=0, tiled=True)  109 us
    dot_general x16, matrix products, mxu(): lax.dot_general(lhs, rhs, (contract, ((), ())), preferred_element_type=F32)  96.7 us
    unnamed x94, local copies, waits for them, and re-layouts  84.1 us
    reduce_scatter x2, waiting for transfers between devices, scatter_dense(): parts = lax.psum_scatter(parts, PLANE, scatter_dimension=1, tiled=True)  83.9 us
    pallas_call x2, Pallas kernels, run_expert(): pl.pallas_call(functools.partial(expert_kernel, n_dp, half_steps), grid=(...  80.5 us
  transfers between devices with their start and end apart: 48, of which 26 were waited for; matrix products, arithmetic and copies ran while one was open for 16% of the time, Pallas kernels for 7%

profile of v1, /device:TPU:0, one launch (start us, length us, event | category | flops | bytes accessed | tf_op | source)
XLA Modules:
  0.0 1856.4 jit_solution(14233610136279086871)
XLA Ops:
  13.5 22.3 %all-gather = bf16[192,2176]{1,0:T(8,128)(2,1)} all-gather(bf16[48,2176]{1,0:T(8,128)(2,1)S(1)} %fusion.57), channel_id=2, replica_groups=mesh['expert'=2,'context'=4,'dp'=4] {'dp'}, dimensions={0}, use_global_device_ids=true | all-gather | bytes 1044480 | tf_op jit(solution)/shard_map/all_gather | solution.py:762
  40.2 42.4 %all-gather.23.cloned.1.call-done = bf16[4,384,2176]{2,1,0:T(8,128)(2,1)} async-done(((bf16[4,48,2176]{2,1,0:T(8,128)(2,1)}), bf16[4,384,2176]{2,1,0:T(8,128)(2,1)}) %all-gather.23.cloned.1.call-update) | async-done | bytes 6684688 | tf_op jit(solution)/shard_map/all_gather | solution.py:763
  91.6 12.3 project.1
  106.6 17.1 all-gather.2
  125.9 50.0 %collective-permute-done = s32[768,4]{0,1:T(4,128)S(1)} collective-permute-done((s32[768,4]{0,1:T(4,128)S(1)}, s32[768,4]{0,1:T(4,128)S(1)}, u32[]{:S(2)}, u32[]{:S(2)}) %collective-permute-start) | collective-permute-done | bytes 12320 | tf_op jit(solution)/shard_map/ppermute | solution.py:746
  195.1 26.1 %attend.1 = (bf16[768,1536]{1,0:T(8,128)(2,1)}, f32[12,768,1]{2,1,0:T(8,128)}) custom-call(s32[1]{0:T(128)} %bitcast.1.block_ref, bf16[768,2048]{1,0:T(8,128)(2,1)} %get-tuple-element.49.q_ref, bf16[1536,512]{1,0:T(8,128)(2,1)} %pad_maximum_fusion.2.k_ref.v_ref, bf16[1536,512]{1,0:T(8,128)(2,1)} %pad_maximum_fusion.2.k_ref.v_ref), custom_call_target="tpu_custom_call" | custom-call | tf_op jit(solution)/shard_map/attend/pallas_call | solution.py:493
  245.3 21.0 %all-to-all-done.3 = bf16[8,104,1536]{2,1,0:T(8,128)(2,1)} async-done(((bf16[8,104,1536]{2,1,0:T(8,128)(2,1)}), bf16[8,104,1536]{2,1,0:T(8,128)(2,1)}, u32[]{:S(2)}, u32[]{:S(2)}) %all-to-all-start.3) | async-done | bytes 2555936 | tf_op jit(solution)/shard_map/all_to_all | solution.py:752
  279.7 35.9 %all_to_all.90 = bf16[8,104,1536]{2,1,0:T(8,128)(2,1)} all-to-all(bf16[8,104,1536]{2,1,0:T(8,128)(2,1)} %bitcast.272), channel_id=1, replica_groups=mesh['expert'=2,'context'=4,'dp'=4] {'expert','context'}, dimensions={0} | all-to-all | bytes 5111808 | tf_op jit(solution)/shard_map/all_to_all | solution.py:752
  327.1 23.8 %all-to-all-done.2 = bf16[8,104,1536]{2,1,0:T(8,128)(2,1)S(1)} async-done(((bf16[8,104,1536]{2,1,0:T(8,128)(2,1)}), bf16[8,104,1536]{2,1,0:T(8,128)(2,1)S(1)}, u32[]{:S(2)}, u32[]{:S(2)}) %all-to-all-start.2) | async-done | bytes 2555936 | tf_op jit(solution)/shard_map/all_to_all | solution.py:752
  357.6 30.9 %all-to-all-done.6 = bf16[8,104,1536]{2,1,0:T(8,128)(2,1)} async-done(((bf16[8,104,1536]{2,1,0:T(8,128)(2,1)}), bf16[8,104,1536]{2,1,0:T(8,128)(2,1)}, u32[]{:S(2)}, u32[]{:S(2)}) %all-to-all-start.6) | async-done | bytes 2555936 | tf_op jit(solution)/shard_map/all_to_all | solution.py:752
  392.9 17.7 collective-permute-done.1.rows_ref
  439.7 10.6 fusion.7
  471.6 21.6 %collective-permute-done.10.refs_16_ = bf16[2,192,1536]{2,1,0:T(8,128)(2,1)} collective-permute-done((bf16[2,192,1536]{2,1,0:T(8,128)(2,1)}, bf16[2,192,1536]{2,1,0:T(8,128)(2,1)}, u32[]{:S(2)}, u32[]{:S(2)}) %collective-permute-start.10) | collective-permute-done | bytes 1179680 | tf_op jit(solution)/shard_map/ppermute | solution.py:746
  493.1 72.5 %collective-permute-done.11.refs_17_ = bf16[2,192,1536]{2,1,0:T(8,128)(2,1)} collective-permute-done((bf16[2,192,1536]{2,1,0:T(8,128)(2,1)S(1)}, bf16[2,192,1536]{2,1,0:T(8,128)(2,1)}, u32[]{:S(2)}, u32[]{:S(2)}) %collective-permute-start.11) | collective-permute-done | bytes 1179680 | tf_op jit(solution)/shard_map/ppermute | solution.py:746
  565.6 51.7 %collective-permute-start.8 = (bf16[2,384,768]{2,1,0:T(8,128)(2,1)}, bf16[2,384,768]{2,1,0:T(8,128)(2,1)}, u32[]{:S(2)}, u32[]{:S(2)}) collective-permute-start(bf16[2,384,768]{2,1,0:T(8,128)(2,1)} %get-tuple-element.176.refs_11_), channel_id=1, source_target_pairs={{0,2},{1,3},{2,0},{3,1},{4,6},{5,7},{6,4},{7,5},{8,10},{9,11},{10,... | collective-permute-start | bytes 3538952 | tf_op jit(solution)/shard_map/ppermute | solution.py:746
  621.2 96.0 %collective-permute-done.5.refs_9_ = bf16[2,384,768]{2,1,0:T(8,128)(2,1)S(1)} collective-permute-done((bf16[2,384,768]{2,1,0:T(8,128)(2,1)S(1)}, bf16[2,384,768]{2,1,0:T(8,128)(2,1)S(1)}, u32[]{:S(2)}, u32[]{:S(2)}) %collective-permute-start.5) | collective-permute-done | bytes 1179680 | tf_op jit(solution)/shard_map/ppermute | solution.py:746
  717.2 24.8 %collective-permute-done.8.refs_13_ = bf16[2,384,768]{2,1,0:T(8,128)(2,1)} collective-permute-done((bf16[2,384,768]{2,1,0:T(8,128)(2,1)}, bf16[2,384,768]{2,1,0:T(8,128)(2,1)}, u32[]{:S(2)}, u32[]{:S(2)}) %collective-permute-start.8) | collective-permute-done | bytes 1179680 | tf_op jit(solution)/shard_map/ppermute | solution.py:746
  742.0 40.2 %experts.2 = (bf16[832,1536]{1,0:T(8,128)(2,1)}, bf16[832,1536]{1,0:T(8,128)(2,1)}, bf16[832,1536]{1,0:T(8,128)(2,1)}, bf16[832,1536]{1,0:T(8,128)(2,1)}, f32[83...) custom-call(s32[1]{0:T(128)} %bitcast.10.refs_0_, ...), custom_call_target="tpu_custom_call" | custom-call | tf_op jit(solution)/shard_map/experts/pallas_call | solution.py:721
  784.8 40.4 %experts.3 = (bf16[832,1536]{1,0:T(8,128)(2,1)}, bf16[832,1536]{1,0:T(8,128)(2,1)}, bf16[832,1536]{1,0:T(8,128)(2,1)}, bf16[832,1536]{1,0:T(8,128)(2,1)}, f32[83...) custom-call(s32[1]{0:T(128)} %bitcast.10.refs_0_, ...), custom_call_target="tpu_custom_call" | custom-call | tf_op jit(solution)/shard_map/experts/pallas_call | solution.py:721
  836.3 36.2 %all_to_all.92 = bf16[8,104,1536]{2,1,0:T(8,128)(2,1)} all-to-all(bf16[8,104,1536]{2,1,0:T(8,128)(2,1)} %bitcast.263), channel_id=1, replica_groups=mesh['expert'=2,'context'=4,'dp'=4] {'expert','context'}, dimensions={0} | all-to-all | bytes 5111808 | tf_op jit(solution)/shard_map/all_to_all | solution.py:752
  872.4 35.0 %all_to_all.93 = bf16[8,104,1536]{2,1,0:T(8,128)(2,1)} all-to-all(bf16[8,104,1536]{2,1,0:T(8,128)(2,1)S(1)} %bitcast.262), channel_id=1, replica_groups=mesh['expert'=2,'context'=4,'dp'=4] {'expert','context'}, dimensions={0} | all-to-all | bytes 5111808 | tf_op jit(solution)/shard_map/all_to_all | solution.py:752
  907.4 34.9 %all_to_all.94 = bf16[8,104,1536]{2,1,0:T(8,128)(2,1)} all-to-all(bf16[8,104,1536]{2,1,0:T(8,128)(2,1)S(1)} %bitcast.261), channel_id=1, replica_groups=mesh['expert'=2,'context'=4,'dp'=4] {'expert','context'}, dimensions={0} | all-to-all | bytes 5111808 | tf_op jit(solution)/shard_map/all_to_all | solution.py:752
  942.3 35.0 %all_to_all.95 = bf16[8,104,1536]{2,1,0:T(8,128)(2,1)} all-to-all(bf16[8,104,1536]{2,1,0:T(8,128)(2,1)S(1)} %bitcast.260), channel_id=1, replica_groups=mesh['expert'=2,'context'=4,'dp'=4] {'expert','context'}, dimensions={0} | all-to-all | bytes 5111808 | tf_op jit(solution)/shard_map/all_to_all | solution.py:752
  977.3 34.9 %all_to_all.96 = bf16[8,104,1536]{2,1,0:T(8,128)(2,1)} all-to-all(bf16[8,104,1536]{2,1,0:T(8,128)(2,1)S(1)} %bitcast.266), channel_id=1, replica_groups=mesh['expert'=2,'context'=4,'dp'=4] {'expert','context'}, dimensions={0} | all-to-all | bytes 5111808 | tf_op jit(solution)/shard_map/all_to_all | solution.py:752
  1012.3 34.7 %all_to_all.97 = bf16[8,104,1536]{2,1,0:T(8,128)(2,1)} all-to-all(bf16[8,104,1536]{2,1,0:T(8,128)(2,1)S(1)} %bitcast.265), channel_id=1, replica_groups=mesh['expert'=2,'context'=4,'dp'=4] {'expert','context'}, dimensions={0} | all-to-all | bytes 5111808 | tf_op jit(solution)/shard_map/all_to_all | solution.py:752
  1060.1 22.0 %all-to-all-done.10 = bf16[8,104,1536]{2,1,0:T(8,128)(2,1)S(1)} async-done(((bf16[8,104,1536]{2,1,0:T(8,128)(2,1)}), bf16[8,104,1536]{2,1,0:T(8,128)(2,1)S(1)}, u32[]{:S(2)}, u32[]{:S(2)}) %all-to-all-start.10) | async-done | bytes 2555936 | tf_op jit(solution)/shard_map/all_to_all | solution.py:752
  1088.0 9.7 collect_rows.5
  1099.9 64.7 %collective-permute-done.15 = f32[8,2,104]{2,1,0:T(2,128)S(1)} collective-permute-done((f32[8,2,104]{2,1,0:T(2,128)S(1)}, f32[8,2,104]{2,1,0:T(2,128)S(1)}, u32[]{:S(2)}, u32[]{:S(2)}) %collective-permute-start.15) | collective-permute-done | bytes 6688 | tf_op jit(solution)/shard_map/ppermute | solution.py:746
  1167.1 9.8 collect_rows.4
  1177.0 9.9 collect_rows.6
  1203.5 47.5 %attend_back.1 = (bf16[768,1536]{1,0:T(8,128)(2,1)}, f32[1536,256]{1,0:T(8,128)}, f32[1536,256]{1,0:T(8,128)}) custom-call(s32[1]{0:T(128)} %bitcast.1.block_ref, bf16[768,2048]{1,0:T(8,128)(2,1)} %get-tuple-element.49.q_ref, bf16[1536,512]{1,0:T(8,128)(2,1)} %pad_maximum_fusion.2.k_ref.v_ref, bf16[1536,512]{1,0:T(8,128)(2,1)} %pad_maximum_fusion.2.k_ref.v_ref, ...), custom_call_target="tpu_custom_call" | custom-call | tf_op jit(solution)/shard_map/attend_back/pallas_call | solution.py:544
  1269.3 11.5 reduce-scatter.6.cloned.1.call-done
  1286.4 11.0 fusion.6
  1297.8 41.2 %reduce-scatter.12.cloned.1.call-done = bf16[4,1,48,1536]{3,2,0,1:T(8,128)(2,1)} async-done(((bf16[4,8,48,1536]{3,2,0,1:T(8,128)(2,1)}), bf16[4,1,48,1536]{3,2,0,1:T(8,128)(2,1)}) %reduce-scatter.12.cloned.1.call-update) | async-done | bytes 589840 | tf_op jit(solution)/shard_map/reduce_scatter | solution.py:773
  1386.6 42.7 %reduce-scatter.8.cloned.1.call-done = bf16[4,1,48,2176]{3,2,0,1:T(8,128)(2,1)} async-done(((bf16[4,8,48,2176]{3,2,0,1:T(8,128)(2,1)}), bf16[4,1,48,2176]{3,2,0,1:T(8,128)(2,1)}) %reduce-scatter.8.cloned.1.call-update) | async-done | bytes 835600 | tf_op jit(solution)/shard_map/reduce_scatter | solution.py:773
  1437.8 20.9 %collective-permute-done.20 = bf16[2,384,768]{2,1,0:T(8,128)(2,1)} collective-permute-done((bf16[2,384,768]{2,1,0:T(8,128)(2,1)}, bf16[2,384,768]{2,1,0:T(8,128)(2,1)}, u32[]{:S(2)}, u32[]{:S(2)}) %collective-permute-start.20) | collective-permute-done | bytes 1179680 | tf_op jit(solution)/shard_map/ppermute | solution.py:746
  1478.0 40.8 %collective-permute-start.16 = (bf16[2,384,768]{2,1,0:T(8,128)(2,1)S(1)}, bf16[2,384,768]{2,1,0:T(8,128)(2,1)S(1)}, u32[]{:S(2)}, u32[]{:S(2)}) collective-permute-start(bf16[2,384,768]{2,1,0:T(8,128)(2,1)S(1)} %get-tuple-element.166), channel_id=1, source_target_pairs={{0,2},{1,3},{2,0},{3,1},{4,6},{5,7},{6,4},{7,5},{8,10},{9,11},{10,... | collective-permute-start | bytes 3538952 | tf_op jit(solution)/shard_map/ppermute | solution.py:746
  1520.4 50.8 %collective-permute-done.16 = bf16[2,384,768]{2,1,0:T(8,128)(2,1)S(1)} collective-permute-done((bf16[2,384,768]{2,1,0:T(8,128)(2,1)S(1)}, bf16[2,384,768]{2,1,0:T(8,128)(2,1)S(1)}, u32[]{:S(2)}, u32[]{:S(2)}) %collective-permute-start.16) | collective-permute-done | bytes 1179680 | tf_op jit(solution)/shard_map/ppermute | solution.py:746
  1571.5 25.4 %collective-permute-done.18 = bf16[2,384,768]{2,1,0:T(8,128)(2,1)S(1)} collective-permute-done((bf16[2,384,768]{2,1,0:T(8,128)(2,1)S(1)}, bf16[2,384,768]{2,1,0:T(8,128)(2,1)S(1)}, u32[]{:S(2)}, u32[]{:S(2)}) %collective-permute-start.18) | collective-permute-done | bytes 1179680 | tf_op jit(solution)/shard_map/ppermute | solution.py:746
  1614.4 25.4 %collective-permute-start.22 = (bf16[2,192,1536]{2,1,0:T(8,128)(2,1)S(1)}, bf16[2,192,1536]{2,1,0:T(8,128)(2,1)S(1)}, u32[]{:S(2)}, u32[]{:S(2)}) collective-permute-start(bf16[2,192,1536]{2,1,0:T(8,128)(2,1)S(1)} %get-tuple-element.160), channel_id=1, source_target_pairs={{0,2},{1,3},{2,0},{3,1},{4,6},{5,7},{6,4},{7,5},{8,10},{9,11},{10,... | collective-permute-start | bytes 3538952 | tf_op jit(solution)/shard_map/ppermute | solution.py:746
  1642.1 50.3 %collective-permute-done.22 = bf16[2,192,1536]{2,1,0:T(8,128)(2,1)S(1)} collective-permute-done((bf16[2,192,1536]{2,1,0:T(8,128)(2,1)S(1)}, bf16[2,192,1536]{2,1,0:T(8,128)(2,1)S(1)}, u32[]{:S(2)}, u32[]{:S(2)}) %collective-permute-start.22) | collective-permute-done | bytes 1179680 | tf_op jit(solution)/shard_map/ppermute | solution.py:746
  1692.8 25.5 %collective-permute-done.24 = bf16[2,192,1536]{2,1,0:T(8,128)(2,1)S(1)} collective-permute-done((bf16[2,192,1536]{2,1,0:T(8,128)(2,1)S(1)}, bf16[2,192,1536]{2,1,0:T(8,128)(2,1)S(1)}, u32[]{:S(2)}, u32[]{:S(2)}) %collective-permute-start.24) | collective-permute-done | bytes 1179680 | tf_op jit(solution)/shard_map/ppermute | solution.py:746
  1729.0 12.6 convert_bitcast_fusion.1
  1741.6 24.3 %copy.194 = f32[384,16,768]{2,1,0:T(8,128)} copy(f32[384,16,768]{2,0,1:T(8,128)} %convert_bitcast_fusion.1) | data formatting | bytes 37748736
  1765.9 12.7 convert_bitcast_fusion.2
  1778.6 24.6 %copy.193 = f32[384,16,768]{2,1,0:T(8,128)} copy(f32[384,16,768]{2,0,1:T(8,128)} %convert_bitcast_fusion.2) | data formatting | bytes 37748736
  1806.8 12.8 convert_bitcast_fusion
  1819.6 24.1 %copy.195 = f32[192,16,1536]{2,1,0:T(8,128)} copy(f32[192,16,1536]{2,0,1:T(8,128)} %convert_bitcast_fusion) | data formatting | bytes 37748736
  (316 shorter events, 353.1 us)
Async XLA Ops:
  7.2 75.5 %all-gather.23.cloned.1.call-start = ((), (), s32[]{:S(2)}) async-start(), calls=%async_computation.32 | async-start | bytes 7520256 | tf_op jit(solution)/shard_map/all_gather | solution.py:763
  35.7 156.9 %all-gather.15.cloned.1.call-start = ((), (), s32[]{:S(2)}) async-start(), calls=%async_computation.23 | async-start | bytes 1310720 | tf_op jit(solution)/shard_map/all_gather | solution.py:881
  105.6 115.6 %all-gather.25.cloned.1.call-start = ((), (), s32[]{:S(2)}) async-start(), calls=%async_computation.33 | async-start | bytes 5308416 | tf_op jit(solution)/shard_map/all_gather | solution.py:763
  123.8 55.1 %collective-permute-start.2 = (bf16[768,1536]{1,0:T(8,128)(2,1)S(1)}, bf16[768,1536]{1,0:T(8,128)(2,1)}, u32[]{:S(2)}, u32[]{:S(2)}) collective-permute-start(bf16[768,1536]{1,0:T(8,128)(2,1)S(1)} %bitcast.248), channel_id=1, source_target_pairs={{0,1},{1,0},{2,3},{3,2},{4,5},{5,4},{6,7},{7,6},{8,9},{9,8},{10,11... | collective-permute-start | bytes 7077896 | tf_op jit(solution)/shard_map/ppermute | solution.py:746
  125.7 50.1 %collective-permute-start = (s32[768,4]{0,1:T(4,128)S(1)}, s32[768,4]{0,1:T(4,128)S(1)}, u32[]{:S(2)}, u32[]{:S(2)}) collective-permute-start(s32[768,4]{0,1:T(4,128)S(1)} %bitcast.285), channel_id=1, source_target_pairs={{0,1},{1,0},{2,3},{3,2},{4,5},{5,4},{6,7},{7,6},{8,9},{9,8},{10,11... | collective-permute-start | bytes 36872 | tf_op jit(solution)/shard_map/ppermute | solution.py:746
  186.6 43.7 %all-to-all-start.9 = ((bf16[8,104,1536]{2,1,0:T(8,128)(2,1)}), bf16[8,104,1536]{2,1,0:T(8,128)(2,1)}, u32[]{:S(2)}, u32[]{:S(2)}) async-start(bf16[8,104,1536]{2,1,0:T(8,128)(2,1)} %bitcast.268), calls=%async_computation.9 | async-start | bytes 5111808 | tf_op jit(solution)/shard_map/all_to_all | solution.py:752
  230.2 36.0 %all-to-all-start.3 = ((bf16[8,104,1536]{2,1,0:T(8,128)(2,1)}), bf16[8,104,1536]{2,1,0:T(8,128)(2,1)}, u32[]{:S(2)}, u32[]{:S(2)}) async-start(bf16[8,104,1536]{2,1,0:T(8,128)(2,1)} %bitcast.259), calls=%async_computation.3 | async-start | bytes 5111808 | tf_op jit(solution)/shard_map/all_to_all | solution.py:752
  240.9 3.7 collective-permute-start.3
  266.3 13.4 all-to-all-start.4
  315.6 35.3 %all-to-all-start.2 = ((bf16[8,104,1536]{2,1,0:T(8,128)(2,1)}), bf16[8,104,1536]{2,1,0:T(8,128)(2,1)S(1)}, u32[]{:S(2)}, u32[]{:S(2)}) async-start(bf16[8,104,1536]{2,1,0:T(8,128)(2,1)} %bitcast.270), calls=%async_computation.2 | async-start | bytes 5111808 | tf_op jit(solution)/shard_map/all_to_all | solution.py:752
  352.4 36.1 %all-to-all-start.6 = ((bf16[8,104,1536]{2,1,0:T(8,128)(2,1)}), bf16[8,104,1536]{2,1,0:T(8,128)(2,1)}, u32[]{:S(2)}, u32[]{:S(2)}) async-start(bf16[8,104,1536]{2,1,0:T(8,128)(2,1)} %bitcast.271), calls=%async_computation.6 | async-start | bytes 5111808 | tf_op jit(solution)/shard_map/all_to_all | solution.py:752
  356.9 53.6 %collective-permute-start.1 = (bf16[768,1536]{1,0:T(8,128)(2,1)S(1)}, bf16[768,1536]{1,0:T(8,128)(2,1)}, u32[]{:S(2)}, u32[]{:S(2)}) collective-permute-start(bf16[768,1536]{1,0:T(8,128)(2,1)S(1)} %copy-done.1), channel_id=1, source_target_pairs={{0,1},{1,0},{2,3},{3,2},{4,5},{5,4},{6,7},{7,6},{8,9},{9,8},{10,11... | collective-permute-start | bytes 7077896 | tf_op jit(solution)/shard_map/ppermute | solution.py:746
  388.5 36.0 %all-to-all-start = ((bf16[8,104,1536]{2,1,0:T(8,128)(2,1)}), bf16[8,104,1536]{2,1,0:T(8,128)(2,1)}, u32[]{:S(2)}, u32[]{:S(2)}) async-start(bf16[8,104,1536]{2,1,0:T(8,128)(2,1)} %bitcast.269), calls=%async_computation | async-start | bytes 5111808 | tf_op jit(solution)/shard_map/all_to_all | solution.py:752
  424.5 36.0 %all-to-all-start.1 = ((bf16[8,104,1536]{2,1,0:T(8,128)(2,1)}), bf16[8,104,1536]{2,1,0:T(8,128)(2,1)}, u32[]{:S(2)}, u32[]{:S(2)}) async-start(bf16[8,104,1536]{2,1,0:T(8,128)(2,1)} %bitcast.267), calls=%async_computation.1 | async-start | bytes 5111808 | tf_op jit(solution)/shard_map/all_to_all | solution.py:752
  435.3 34.2 %collective-permute-start.12 = (bf16[2,192,1536]{2,1,0:T(8,128)(2,1)}, bf16[2,192,1536]{2,1,0:T(8,128)(2,1)}, u32[]{:S(2)}, u32[]{:S(2)}) collective-permute-start(bf16[2,192,1536]{2,1,0:T(8,128)(2,1)} %get-tuple-element.173), channel_id=1, source_target_pairs={{0,3},{1,2},{2,1},{3,0},{4,7},{5,6},{6,5},{7,4},{8,11},{9,10},{10,... | collective-permute-start | bytes 3538952 | tf_op jit(solution)/shard_map/ppermute | solution.py:746
  437.5 55.6 %collective-permute-start.10 = (bf16[2,192,1536]{2,1,0:T(8,128)(2,1)}, bf16[2,192,1536]{2,1,0:T(8,128)(2,1)}, u32[]{:S(2)}, u32[]{:S(2)}) collective-permute-start(bf16[2,192,1536]{2,1,0:T(8,128)(2,1)} %get-tuple-element.173), channel_id=1, source_target_pairs={{0,1},{1,0},{2,3},{3,2},{4,5},{5,4},{6,7},{7,6},{8,9},{9,8},{10,11... | collective-permute-start | bytes 3538952 | tf_op jit(solution)/shard_map/ppermute | solution.py:746
  437.5 128.1 %collective-permute-start.11 = (bf16[2,192,1536]{2,1,0:T(8,128)(2,1)S(1)}, bf16[2,192,1536]{2,1,0:T(8,128)(2,1)}, u32[]{:S(2)}, u32[]{:S(2)}) collective-permute-start(bf16[2,192,1536]{2,1,0:T(8,128)(2,1)S(1)} %get-tuple-element.174.refs_15_), channel_id=1, source_target_pairs={{0,2},{1,3},{2,0},{3,1},{4,6},{5,7},{6,4},{7,5},{8,10},{9,11},{10,... | collective-permute-start | bytes 3538952 | tf_op jit(solution)/shard_map/ppermute | solution.py:746
  453.5 112.1 %collective-permute-start.6 = (bf16[2,384,768]{2,1,0:T(8,128)(2,1)}, bf16[2,384,768]{2,1,0:T(8,128)(2,1)}, u32[]{:S(2)}, u32[]{:S(2)}) collective-permute-start(bf16[2,384,768]{2,1,0:T(8,128)(2,1)} %get-tuple-element.177), channel_id=1, source_target_pairs={{0,3},{1,2},{2,1},{3,0},{4,7},{5,6},{6,5},{7,4},{8,11},{9,10},{10,... | collective-permute-start | bytes 3538952 | tf_op jit(solution)/shard_map/ppermute | solution.py:746
  460.4 324.4 %all-to-all-start.7 = ((bf16[8,104,1536]{2,1,0:T(8,128)(2,1)}), bf16[8,104,1536]{2,1,0:T(8,128)(2,1)}, u32[]{:S(2)}, u32[]{:S(2)}) async-start(bf16[8,104,1536]{2,1,0:T(8,128)(2,1)} %bitcast.257), calls=%async_computation.7 | async-start | bytes 5111808 | tf_op jit(solution)/shard_map/all_to_all | solution.py:752
  465.2 155.9 %collective-permute-start.4 = (bf16[2,384,768]{2,1,0:T(8,128)(2,1)}, bf16[2,384,768]{2,1,0:T(8,128)(2,1)}, u32[]{:S(2)}, u32[]{:S(2)}) collective-permute-start(bf16[2,384,768]{2,1,0:T(8,128)(2,1)} %get-tuple-element.177), channel_id=1, source_target_pairs={{0,1},{1,0},{2,3},{3,2},{4,5},{5,4},{6,7},{7,6},{8,9},{9,8},{10,11... | collective-permute-start | bytes 3538952 | tf_op jit(solution)/shard_map/ppermute | solution.py:746
  469.5 247.7 %collective-permute-start.9 = (bf16[2,384,768]{2,1,0:T(8,128)(2,1)}, bf16[2,384,768]{2,1,0:T(8,128)(2,1)}, u32[]{:S(2)}, u32[]{:S(2)}) collective-permute-start(bf16[2,384,768]{2,1,0:T(8,128)(2,1)} %get-tuple-element.175), channel_id=1, source_target_pairs={{0,3},{1,2},{2,1},{3,0},{4,7},{5,6},{6,5},{7,4},{8,11},{9,10},{10,... | collective-permute-start | bytes 3538952 | tf_op jit(solution)/shard_map/ppermute | solution.py:746
  493.1 224.1 %collective-permute-start.7 = (bf16[2,384,768]{2,1,0:T(8,128)(2,1)}, bf16[2,384,768]{2,1,0:T(8,128)(2,1)}, u32[]{:S(2)}, u32[]{:S(2)}) collective-permute-start(bf16[2,384,768]{2,1,0:T(8,128)(2,1)} %get-tuple-element.175), channel_id=1, source_target_pairs={{0,1},{1,0},{2,3},{3,2},{4,5},{5,4},{6,7},{7,6},{8,9},{9,8},{10,11... | collective-permute-start | bytes 3538952 | tf_op jit(solution)/shard_map/ppermute | solution.py:746
  565.6 151.6 %collective-permute-start.5 = (bf16[2,384,768]{2,1,0:T(8,128)(2,1)S(1)}, bf16[2,384,768]{2,1,0:T(8,128)(2,1)S(1)}, u32[]{:S(2)}, u32[]{:S(2)}) collective-permute-start(bf16[2,384,768]{2,1,0:T(8,128)(2,1)S(1)} %get-tuple-element.178.refs_7_), channel_id=1, source_target_pairs={{0,2},{1,3},{2,0},{3,1},{4,6},{5,7},{6,4},{7,5},{8,10},{9,11},{10,... | collective-permute-start | bytes 3538952 | tf_op jit(solution)/shard_map/ppermute | solution.py:746
  565.6 176.4 %collective-permute-start.8 = (bf16[2,384,768]{2,1,0:T(8,128)(2,1)}, bf16[2,384,768]{2,1,0:T(8,128)(2,1)}, u32[]{:S(2)}, u32[]{:S(2)}) collective-permute-start(bf16[2,384,768]{2,1,0:T(8,128)(2,1)} %get-tuple-element.176.refs_11_), channel_id=1, source_target_pairs={{0,2},{1,3},{2,0},{3,1},{4,6},{5,7},{6,4},{7,5},{8,10},{9,11},{10,... | collective-permute-start | bytes 3538952 | tf_op jit(solution)/shard_map/ppermute | solution.py:746
  1047.0 35.1 %all-to-all-start.10 = ((bf16[8,104,1536]{2,1,0:T(8,128)(2,1)}), bf16[8,104,1536]{2,1,0:T(8,128)(2,1)S(1)}, u32[]{:S(2)}, u32[]{:S(2)}) async-start(bf16[8,104,1536]{2,1,0:T(8,128)(2,1)} %bitcast.264), calls=%async_computation.10 | async-start | bytes 5111808 | tf_op jit(solution)/shard_map/all_to_all | solution.py:752
  1060.1 126.7 %collective-permute-start.14 = (bf16[768,1536]{1,0:T(8,128)(2,1)}, bf16[768,1536]{1,0:T(8,128)(2,1)}, u32[]{:S(2)}, u32[]{:S(2)}) collective-permute-start(bf16[768,1536]{1,0:T(8,128)(2,1)} %collect_rows.7), channel_id=1, source_target_pairs={{0,1},{1,0},{2,3},{3,2},{4,5},{5,4},{6,7},{7,6},{8,9},{9,8},{10,11... | collective-permute-start | bytes 7077896 | tf_op jit(solution)/shard_map/ppermute | solution.py:746
  1083.6 93.4 %all-to-all-start.14 = ((bf16[8,104,1536]{2,1,0:T(8,128)(2,1)}), bf16[8,104,1536]{2,1,0:T(8,128)(2,1)}, u32[]{:S(2)}, u32[]{:S(2)}) async-start(bf16[8,104,1536]{2,1,0:T(8,128)(2,1)} %bitcast.258), calls=%async_computation.14 | async-start | bytes 5111808 | tf_op jit(solution)/shard_map/all_to_all | solution.py:752
  1088.0 192.8 %reduce-scatter.6.cloned.1.call-start = ((), (), s32[]{:S(2)}) async-start(), calls=%async_computation.24 | async-start | bytes 1310720 | tf_op jit(solution)/shard_map/reduce_scatter | solution.py:987
  1097.8 95.0 %collective-permute-start.13 = (bf16[768,1536]{1,0:T(8,128)(2,1)}, bf16[768,1536]{1,0:T(8,128)(2,1)S(1)}, u32[]{:S(2)}, u32[]{:S(2)}) collective-permute-start(bf16[768,1536]{1,0:T(8,128)(2,1)} %collect_rows.5), channel_id=1, source_target_pairs={{0,1},{1,0},{2,3},{3,2},{4,5},{5,4},{6,7},{7,6},{8,9},{9,8},{10,11... | collective-permute-start | bytes 7077896 | tf_op jit(solution)/shard_map/ppermute | solution.py:746
  1097.8 66.8 %collective-permute-start.15 = (f32[8,2,104]{2,1,0:T(2,128)S(1)}, f32[8,2,104]{2,1,0:T(2,128)S(1)}, u32[]{:S(2)}, u32[]{:S(2)}) collective-permute-start(f32[8,2,104]{2,1,0:T(2,128)S(1)} %bitcast.288), channel_id=1, source_target_pairs={{0,1},{1,0},{2,3},{3,2},{4,5},{5,4},{6,7},{7,6},{8,9},{9,8},{10,11... | collective-permute-start | bytes 19976 | tf_op jit(solution)/shard_map/ppermute | solution.py:746
  1255.9 83.1 %reduce-scatter.12.cloned.1.call-start = ((), (), s32[]{:S(2)}) async-start(), calls=%async_computation.27 | async-start | bytes 5308416 | tf_op jit(solution)/shard_map/reduce_scatter | solution.py:773
  1265.0 98.2 %reduce-scatter.14.cloned.1.call-start = ((), (), s32[]{:S(2)}) async-start(), calls=%async_computation.28 | async-start | bytes 737280 | tf_op jit(solution)/shard_map/reduce_scatter | solution.py:774
  1339.0 90.2 %reduce-scatter.8.cloned.1.call-start = ((), (), s32[]{:S(2)}) async-start(), calls=%async_computation.25 | async-start | bytes 7520256 | tf_op jit(solution)/shard_map/reduce_scatter | solution.py:773
  1355.4 370.6 %all-gather.29.cloned.1.call-start = ((), (), s32[]{:S(2)}) async-start(), calls=%async_computation.35 | async-start | bytes 1327104 | tf_op jit(solution)/shard_map/all_gather | solution.py:775
  1363.2 365.8 %reduce-scatter.10.cloned.1.call-start = ((), (), s32[]{:S(2)}) async-start(), calls=%async_computation.26 | async-start | bytes 1044480 | tf_op jit(solution)/shard_map/reduce_scatter | solution.py:774
  1382.2 53.7 %collective-permute-start.19 = (bf16[2,384,768]{2,1,0:T(8,128)(2,1)}, bf16[2,384,768]{2,1,0:T(8,128)(2,1)}, u32[]{:S(2)}, u32[]{:S(2)}) collective-permute-start(bf16[2,384,768]{2,1,0:T(8,128)(2,1)} %get-tuple-element.163), channel_id=1, source_target_pairs={{0,2},{1,3},{2,0},{3,1},{4,6},{5,7},{6,4},{7,5},{8,10},{9,11},{10,... | collective-permute-start | bytes 3538952 | tf_op jit(solution)/shard_map/ppermute | solution.py:746
  1382.5 76.1 %collective-permute-start.20 = (bf16[2,384,768]{2,1,0:T(8,128)(2,1)}, bf16[2,384,768]{2,1,0:T(8,128)(2,1)}, u32[]{:S(2)}, u32[]{:S(2)}) collective-permute-start(bf16[2,384,768]{2,1,0:T(8,128)(2,1)} %get-tuple-element.164), channel_id=1, source_target_pairs={{0,1},{1,0},{2,3},{3,2},{4,5},{5,4},{6,7},{7,6},{8,9},{9,8},{10,11... | collective-permute-start | bytes 3538952 | tf_op jit(solution)/shard_map/ppermute | solution.py:746
  1383.4 75.3 %collective-permute-start.21 = (bf16[2,384,768]{2,1,0:T(8,128)(2,1)S(1)}, bf16[2,384,768]{2,1,0:T(8,128)(2,1)}, u32[]{:S(2)}, u32[]{:S(2)}) collective-permute-start(bf16[2,384,768]{2,1,0:T(8,128)(2,1)S(1)} %get-tuple-element.165), channel_id=1, source_target_pairs={{0,3},{1,2},{2,1},{3,0},{4,7},{5,6},{6,5},{7,4},{8,11},{9,10},{10,... | collective-permute-start | bytes 3538952 | tf_op jit(solution)/shard_map/ppermute | solution.py:746
  1429.3 299.7 %all-gather.19.cloned.1.call-start = ((), (), s32[]{:S(2)}) async-start(), calls=%async_computation.30 | async-start | bytes 11796480 | tf_op jit(solution)/shard_map/all_gather | solution.py:976
  1462.2 303.7 %all-gather.17.cloned.1.call-start = ((), (), s32[]{:S(2)}) async-start(), calls=%async_computation.29 | async-start | bytes 11796480 | tf_op jit(solution)/shard_map/all_gather | solution.py:976
  1478.0 93.1 %collective-permute-start.16 = (bf16[2,384,768]{2,1,0:T(8,128)(2,1)S(1)}, bf16[2,384,768]{2,1,0:T(8,128)(2,1)S(1)}, u32[]{:S(2)}, u32[]{:S(2)}) collective-permute-start(bf16[2,384,768]{2,1,0:T(8,128)(2,1)S(1)} %get-tuple-element.166), channel_id=1, source_target_pairs={{0,2},{1,3},{2,0},{3,1},{4,6},{5,7},{6,4},{7,5},{8,10},{9,11},{10,... | collective-permute-start | bytes 3538952 | tf_op jit(solution)/shard_map/ppermute | solution.py:746
  1518.8 52.7 %collective-permute-start.17 = (bf16[2,384,768]{2,1,0:T(8,128)(2,1)S(1)}, bf16[2,384,768]{2,1,0:T(8,128)(2,1)S(1)}, u32[]{:S(2)}, u32[]{:S(2)}) collective-permute-start(bf16[2,384,768]{2,1,0:T(8,128)(2,1)S(1)} %get-tuple-element.167), channel_id=1, source_target_pairs={{0,1},{1,0},{2,3},{3,2},{4,5},{5,4},{6,7},{7,6},{8,9},{9,8},{10,11... | collective-permute-start | bytes 3538952 | tf_op jit(solution)/shard_map/ppermute | solution.py:746
  1518.8 78.1 %collective-permute-start.18 = (bf16[2,384,768]{2,1,0:T(8,128)(2,1)S(1)}, bf16[2,384,768]{2,1,0:T(8,128)(2,1)S(1)}, u32[]{:S(2)}, u32[]{:S(2)}) collective-permute-start(bf16[2,384,768]{2,1,0:T(8,128)(2,1)S(1)} %get-tuple-element.168), channel_id=1, source_target_pairs={{0,3},{1,2},{2,1},{3,0},{4,7},{5,6},{6,5},{7,4},{8,11},{9,10},{10,... | collective-permute-start | bytes 3538952 | tf_op jit(solution)/shard_map/ppermute | solution.py:746
  1598.9 207.9 %all-gather.21.cloned.1.call-start = ((), (), s32[]{:S(2)}) async-start(), calls=%async_computation.31 | async-start | bytes 11796480 | tf_op jit(solution)/shard_map/all_gather | solution.py:976
  1614.4 78.0 %collective-permute-start.22 = (bf16[2,192,1536]{2,1,0:T(8,128)(2,1)S(1)}, bf16[2,192,1536]{2,1,0:T(8,128)(2,1)S(1)}, u32[]{:S(2)}, u32[]{:S(2)}) collective-permute-start(bf16[2,192,1536]{2,1,0:T(8,128)(2,1)S(1)} %get-tuple-element.160), channel_id=1, source_target_pairs={{0,2},{1,3},{2,0},{3,1},{4,6},{5,7},{6,4},{7,5},{8,10},{9,11},{10,... | collective-permute-start | bytes 3538952 | tf_op jit(solution)/shard_map/ppermute | solution.py:746
  1639.8 52.9 %collective-permute-start.23 = (bf16[2,192,1536]{2,1,0:T(8,128)(2,1)S(1)}, bf16[2,192,1536]{2,1,0:T(8,128)(2,1)S(1)}, u32[]{:S(2)}, u32[]{:S(2)}) collective-permute-start(bf16[2,192,1536]{2,1,0:T(8,128)(2,1)S(1)} %get-tuple-element.161), channel_id=1, source_target_pairs={{0,1},{1,0},{2,3},{3,2},{4,5},{5,4},{6,7},{7,6},{8,9},{9,8},{10,11... | collective-permute-start | bytes 3538952 | tf_op jit(solution)/shard_map/ppermute | solution.py:746
  1639.9 78.4 %collective-permute-start.24 = (bf16[2,192,1536]{2,1,0:T(8,128)(2,1)S(1)}, bf16[2,192,1536]{2,1,0:T(8,128)(2,1)S(1)}, u32[]{:S(2)}, u32[]{:S(2)}) collective-permute-start(bf16[2,192,1536]{2,1,0:T(8,128)(2,1)S(1)} %get-tuple-element.162), channel_id=1, source_target_pairs={{0,3},{1,2},{2,1},{3,0},{4,7},{5,6},{6,5},{7,4},{8,11},{9,10},{10,... | collective-permute-start | bytes 3538952 | tf_op jit(solution)/shard_map/ppermute | solution.py:746
  1720.2 123.5 %all-gather.27.cloned.1.call-start = ((), (), s32[]{:S(2)}) async-start(), calls=%async_computation.34 | async-start | bytes 1880064 | tf_op jit(solution)/shard_map/all_gather | solution.py:775
  (42 other events, 801.4 us)
Sparse Core Ops, SparseCore 0:
  35.9 46.7 all-gather.22
  105.7 16.7 all-gather.14
  124.3 39.1 all-gather.24
  1256.0 24.7 reduce-scatter.5
  1285.1 53.8 reduce-scatter.11
  1341.1 21.9 reduce-scatter.13
  1367.2 62.0 reduce-scatter.7
  1431.2 24.0 all-gather.28
  1457.5 28.3 reduce-scatter.9
  1488.0 76.2 all-gather.18
  1599.0 86.3 all-gather.16
  1720.4 86.3 all-gather.20
  1808.8 26.0 all-gather.26

commit v2 on v1

--- a/solution.py
+++ b/solution.py
@@ -394,7 +394,8 @@
 
 BF = jnp.bfloat16
 F32 = jnp.float32
-SLOTS = 104
+SLOTS = 112
+MESH_ID = pl.DeviceIdType.MESH
 PLANE = ("expert", "context")
 VMEM_BYTES = 60 * 1024 * 1024
 
@@ -742,6 +743,471 @@
     )(z_index, x_own, x_par, g_own, g_par, s_own, s_par, *gate_pieces, *up_pieces, *down_pieces)
 
 
+def plane_peer(index):
+    n_context = lax.axis_size("context")
+    return {"expert": index // n_context, "context": index % n_context}
+
+
+def plane_here():
+    return lax.axis_index("expert") * lax.axis_size("context") + lax.axis_index("context")
+
+
+def greet(peers):
+    barrier = pltpu.get_barrier_semaphore()
+    for peer in peers:
+        pl.semaphore_signal(barrier, inc=1, device_id=peer, device_id_type=MESH_ID)
+    pl.semaphore_wait(barrier, len(peers))
+
+
+def plane_and_partner(plane):
+    here = plane_here()
+    return [plane_peer(here ^ flip) for flip in range(1, plane)] + [{"dp": lax.axis_index("dp") ^ 1}]
+
+
+def remote(source, target, send, receive, peer):
+    return pltpu.make_async_remote_copy(
+        src_ref=source,
+        dst_ref=target,
+        send_sem=send,
+        recv_sem=receive,
+        device_id=peer,
+        device_id_type=MESH_ID,
+    )
+
+
+def gather_kernel(
+    n_dp, in_ref, out_part_ref, whole_ref, out_ref, local_sems, z_send, o_send, o_recv, sends, recvs
+):
+    here = plane_here()
+    z_index = lax.axis_index("dp")
+    z_peer = lambda flip: {"dp": z_index ^ flip}
+    greet([z_peer(flip) for flip in range(1, n_dp)] + [plane_peer(here ^ flip) for flip in (1, 2, 4)])
+    keep = [
+        pltpu.make_async_copy(in_ref, whole_ref.at[z_index, here], local_sems.at[0]),
+        pltpu.make_async_copy(out_part_ref, out_ref.at[z_index], local_sems.at[1]),
+    ]
+    for copy in keep:
+        copy.start()
+    started = []
+    for flip in range(1, n_dp):
+        started.append(
+            remote(in_ref, whole_ref.at[z_index, here], z_send.at[flip], recvs.at[z_index, here], z_peer(flip))
+        )
+        started[-1].start()
+    for flip in range(1, n_dp):
+        started.append(
+            remote(out_part_ref, out_ref.at[z_index], o_send.at[flip], o_recv.at[z_index], z_peer(flip))
+        )
+        started[-1].start()
+
+    def pass_on(lane, flip, z_from, place, source=None):
+        block = whole_ref.at[z_from, place]
+        move = remote(
+            block if source is None else source,
+            block,
+            sends.at[lane, z_from, place],
+            recvs.at[z_from, place],
+            plane_peer(here ^ flip),
+        )
+        move.start()
+        started.append(move)
+
+    def landed(z_from, place):
+        block = whole_ref.at[z_from, place]
+        remote(block, block, z_send.at[0], recvs.at[z_from, place], z_peer(1)).wait_recv()
+
+    froms = [z_index ^ flip for flip in range(n_dp)]
+    for n, z_from in enumerate(froms):
+        if n > 0:
+            landed(z_from, here)
+        source = in_ref if n == 0 else None
+        pass_on(0, 2, z_from, here, source)
+        pass_on(1, 4, z_from, here, source)
+        pass_on(2, 1, z_from, here, source)
+    for n, z_from in enumerate(froms):
+        landed(z_from, here ^ 2)
+        if n % 2 == 1:
+            pass_on(1, 4, z_from, here ^ 2)
+        pass_on(2, 1, z_from, here ^ 2)
+        landed(z_from, here ^ 4)
+        if n % 2 == 0:
+            pass_on(0, 2, z_from, here ^ 4)
+        pass_on(2, 1, z_from, here ^ 4)
+    for z_from in froms:
+        landed(z_from, here ^ 6)
+        pass_on(2, 1, z_from, here ^ 6)
+    for place in (1, 3, 5, 7):
+        for z_from in froms:
+            landed(z_from, here ^ place)
+    for flip in range(1, n_dp):
+        z_from = z_index ^ flip
+        remote(out_part_ref, out_ref.at[z_from], o_send.at[0], o_recv.at[z_from], z_peer(1)).wait_recv()
+    for move in started:
+        move.wait_send()
+    for copy in keep:
+        copy.wait()
+
+
+def gather_parts(part_in, part_out, n_dp, plane):
+    anywhere = pl.BlockSpec(memory_space=pl.ANY)
+    return pl.pallas_call(
+        functools.partial(gather_kernel, n_dp),
+        in_specs=[anywhere] * 2,
+        out_specs=[anywhere] * 2,
+        out_shape=[
+            jax.ShapeDtypeStruct((n_dp, plane) + part_in.shape, BF),
+            jax.ShapeDtypeStruct((n_dp,) + part_out.shape, BF),
+        ],
+        scratch_shapes=[
+            pltpu.SemaphoreType.DMA((2,)),
+            pltpu.SemaphoreType.DMA((n_dp,)),
+            pltpu.SemaphoreType.DMA((n_dp,)),
+            pltpu.SemaphoreType.DMA((n_dp,)),
+            pltpu.SemaphoreType.DMA((3, n_dp, plane)),
+            pltpu.SemaphoreType.DMA((n_dp, plane)),
+        ],
+        compiler_params=pltpu.CompilerParams(collective_id=3, has_side_effects=True),
+        name="gather_parts",
+    )(part_in, part_out)
+
+
+RIDING = ((0, 2), (1, 1), (1, 2), (1, 3), (2, 1), (2, 2), (2, 3))
+
+
+def dispatch_kernel(
+    plane,
+    n_dp,
+    normed_ref,
+    cot_ref,
+    cot_partner_ref,
+    own_rank_ref,
+    partner_rank_ref,
+    *refs,
+):
+    riders = len(RIDING)
+    sources, refs = refs[:riders], refs[riders:]
+    outs, targets, refs = refs[:8], refs[8 : 8 + riders], refs[8 + riders :]
+    stage, normed_partner, pair_sems, local_sems, send_sems, recv_sems, ride_send, ride_recv = refs
+    z_index = lax.axis_index("dp")
+    here = plane_here()
+    partner = {"dp": lax.axis_index("dp") ^ 1}
+    greet(plane_and_partner(plane) + [{"dp": z_index ^ flip} for flip in range(2, n_dp)])
+    pair = remote(normed_ref, normed_partner, pair_sems.at[0], pair_sems.at[1], partner)
+    pair.start()
+    rides = [
+        remote(source, target, ride_send.at[n], ride_recv.at[n], {"dp": z_index ^ flip})
+        for n, (source, target, (_, flip)) in enumerate(zip(sources, targets, RIDING))
+    ]
+    for ride in rides:
+        ride.start()
+    plans = (
+        (0, normed_ref, own_rank_ref),
+        (2, cot_ref, own_rank_ref),
+        (6, cot_partner_ref, partner_rank_ref),
+        (4, normed_partner, partner_rank_ref),
+    )
+    for base, rows_ref, rank_ref in plans:
+        if base == 4:
+            pair.wait()
+        for expert in range(2):
+            slot = base + expert
+            chooser = slot_matrix(rank_ref[expert], plane, True)
+            stage[slot] = mxu(chooser, rows_ref[...]).astype(BF).reshape(plane, SLOTS, D)
+            pltpu.make_async_copy(stage.at[slot, here], outs[slot].at[here], local_sems.at[slot]).start()
+
+            def begin(flip, carry):
+                peer = here ^ flip
+                remote(
+                    stage.at[slot, peer],
+                    outs[slot].at[here],
+                    send_sems.at[slot, peer],
+                    recv_sems.at[slot, here],
+                    plane_peer(peer),
+                ).start()
+                return carry
+
+            lax.fori_loop(1, plane, begin, 0)
+    for slot in range(8):
+        pltpu.make_async_copy(stage.at[slot, here], outs[slot].at[here], local_sems.at[slot]).wait()
+
+        def finish(flip, carry):
+            peer = here ^ flip
+            done = remote(
+                stage.at[slot, peer],
+                outs[slot].at[peer],
+                send_sems.at[slot, peer],
+                recv_sems.at[slot, peer],
+                plane_peer(peer),
+            )
+            done.wait_send()
+            done.wait_recv()
+            return carry
+
+        lax.fori_loop(1, plane, finish, 0)
+    for ride in rides:
+        ride.wait()
+
+
+def dispatch_rows(normed, cot, cot_partner, own_ranks, partner_ranks, riders, n_dp):
+    plane, tokens = own_ranks.shape[1:]
+    vmem = pl.BlockSpec(memory_space=pltpu.VMEM)
+    anywhere = pl.BlockSpec(memory_space=pl.ANY)
+    return pl.pallas_call(
+        functools.partial(dispatch_kernel, plane, n_dp),
+        in_specs=[vmem] * 5 + [anywhere] * len(riders),
+        out_specs=[anywhere] * (8 + len(riders)),
+        out_shape=[jax.ShapeDtypeStruct((plane, SLOTS, D), BF)] * 8
+        + [jax.ShapeDtypeStruct(rider.shape, rider.dtype) for rider in riders],
+        scratch_shapes=[
+            pltpu.VMEM((8, plane, SLOTS, D), BF),
+            pltpu.VMEM((tokens, D), BF),
+            pltpu.SemaphoreType.DMA((2,)),
+            pltpu.SemaphoreType.DMA((8,)),
+            pltpu.SemaphoreType.DMA((8, plane)),
+            pltpu.SemaphoreType.DMA((8, plane)),
+            pltpu.SemaphoreType.DMA((len(riders),)),
+            pltpu.SemaphoreType.DMA((len(riders),)),
+        ],
+        compiler_params=pltpu.CompilerParams(
+            vmem_limit_bytes=VMEM_BYTES, collective_id=1, has_side_effects=True
+        ),
+        cost_estimate=pl.CostEstimate(flops=2 * 10**10, bytes_accessed=7 * 10**8, transcendentals=0),
+        name="dispatch_rows",
+    )(normed, cot, cot_partner, own_ranks, partner_ranks, *riders)
+
+
+HOMING = ((0, 2), (0, 3), (1, 2), (0, 1))
+
+
+def return_kernel(plane, n_dp, own_rank_ref, partner_rank_ref, *refs):
+    back = refs[:4]
+    operands = (refs[4:9], refs[9:14])
+    total_ref, gate_ref, up_ref, down_ref = refs[14:18]
+    homes = refs[18 : 18 + len(HOMING)]
+    (
+        held,
+        to_partner,
+        of_partner,
+        rows_buf,
+        weighted_buf,
+        act_buf,
+        grad_gate_buf,
+        grad_up_buf,
+        stage,
+        load_sems,
+        store_sems,
+        pair_sems,
+        local_sems,
+        send_sems,
+        recv_sems,
+        home_send,
+        home_recv,
+    ) = refs[18 + len(HOMING) :]
+    here = plane_here()
+    z_index = lax.axis_index("dp")
+    greet(plane_and_partner(plane) + [{"dp": z_index ^ flip} for flip in range(2, n_dp)])
+    share_refs = (gate_ref, up_ref, down_ref)
+    homing = [
+        remote(
+            share_refs[which].at[flip],
+            home,
+            home_send.at[n],
+            home_recv.at[n],
+            {"dp": z_index ^ flip},
+        )
+        for n, (home, (which, flip)) in enumerate(zip(homes, HOMING))
+    ]
+
+    order = [(side, expert) for side in (1, 0) for expert in range(2)]
+    for side, expert in order:
+        slot = 2 * side + expert
+        source = back[2 * expert + side]
+        pltpu.make_async_copy(source.at[here], held.at[slot, here], local_sems.at[slot]).start()
+
+        def begin(flip, carry):
+            peer = here ^ flip
+            remote(
+                source.at[peer],
+                held.at[slot, here],
+                send_sems.at[slot, peer],
+                recv_sems.at[slot, here],
+                plane_peer(peer),
+            ).start()
+            return carry
+
+        lax.fori_loop(1, plane, begin, 0)
+
+    def send_home(which):
+        for move, (matrix, _) in zip(homing, HOMING):
+            if matrix == which:
+                move.start()
+
+    buffers = (rows_buf, weighted_buf, act_buf, grad_gate_buf, grad_up_buf)
+    quarter = D // n_dp
+    for expert in range(2):
+        loads = [
+            pltpu.make_async_copy(source, buffer, load_sems.at[n])
+            for n, (source, buffer) in enumerate(zip(operands[expert], buffers))
+        ]
+        for load in loads:
+            load.start()
+        for load in loads:
+            load.wait()
+
+        def of_rows(q, carry):
+            columns = pl.ds(pl.multiple_of(q * quarter, 128), quarter)
+            place = z_index ^ q
+            for n, (grad_buf, out_ref) in enumerate(((grad_gate_buf, gate_ref), (grad_up_buf, up_ref))):
+                made = mxu(rows_buf[:, columns], grad_buf[...], ((0,), (0,)))
+                stage[n] = made.astype(BF)
+                pltpu.make_async_copy(stage.at[n], out_ref.at[place, expert], store_sems.at[n]).start()
+            for n, out_ref in enumerate((gate_ref, up_ref)):
+                pltpu.make_async_copy(stage.at[n], out_ref.at[place, expert], store_sems.at[n]).wait()
+            return carry
+
+        lax.fori_loop(0, n_dp, of_rows, 0)
+        if expert == 1:
+            send_home(0)
+            send_home(1)
+
+        width = act_buf.shape[1]
+        rows = width // n_dp
+        for q in range(0, n_dp, 2):
+            made = mxu(act_buf[:, q * rows : (q + 2) * rows], weighted_buf[...], ((0,), (0,))).astype(BF)
+            stores = []
+            for half in range(2):
+                part = made[half * rows : (half + 1) * rows]
+                stage[half, :rows] = part[:, :width]
+                stage[half, rows:] = part[:, width:]
+                place = z_index ^ (q + half)
+                stores.append(
+                    pltpu.make_async_copy(stage.at[half], down_ref.at[place, expert], store_sems.at[half])
+                )
+                stores[-1].start()
+            for store in stores:
+                store.wait()
+    send_home(2)
+
+    def arrive(side):
+        for expert in range(2):
+            slot = 2 * side + expert
+            source = back[2 * expert + side]
+            pltpu.make_async_copy(source.at[here], held.at[slot, here], local_sems.at[slot]).wait()
+
+            def finish(flip, carry):
+                peer = here ^ flip
+                done = remote(
+                    source.at[peer],
+                    held.at[slot, peer],
+                    send_sems.at[slot, peer],
+                    recv_sems.at[slot, peer],
+                    plane_peer(peer),
+                )
+                done.wait_send()
+                done.wait_recv()
+                return carry
+
+            lax.fori_loop(1, plane, finish, 0)
+
+    def collect(rank_ref, side, target, kind):
+        def block(n, carry):
+            rows = pl.ds(pl.multiple_of(n * PBLK, PBLK), PBLK)
+            made = jnp.zeros((PBLK, D), F32)
+            for expert in range(2):
+                chooser = slot_matrix(rank_ref[expert, rows, :], plane, False)
+                made = made + mxu(chooser, held[2 * side + expert].reshape(plane * SLOTS, D))
+            target[rows, :] = made.astype(kind)
+            return carry
+
+        lax.fori_loop(0, total_ref.shape[0] // PBLK, block, 0)
+
+    arrive(1)
+    collect(partner_rank_ref, 1, to_partner, BF)
+    pair = remote(to_partner, of_partner, pair_sems.at[0], pair_sems.at[1], {"dp": z_index ^ 1})
+    pair.start()
+    arrive(0)
+    collect(own_rank_ref, 0, total_ref, F32)
+    pair.wait()
+    total_ref[...] += of_partner[...].astype(F32)
+    for move in homing:
+        move.wait()
+
+
+def return_rows(own_ranks, partner_ranks, back, operands, n_dp):
+    tokens, plane = own_ranks.shape[1:]
+    slot_rows, hidden = operands[0][2].shape
+    quarter = D // n_dp
+    vmem = pl.BlockSpec(memory_space=pltpu.VMEM)
+    anywhere = pl.BlockSpec(memory_space=pl.ANY)
+    shares = jax.ShapeDtypeStruct((n_dp, 2, quarter, hidden), BF)
+    return pl.pallas_call(
+        functools.partial(return_kernel, plane, n_dp),
+        in_specs=[vmem, vmem] + [anywhere] * 14,
+        out_specs=[vmem] + [anywhere] * (3 + len(HOMING)),
+        out_shape=[jax.ShapeDtypeStruct((tokens, D), F32), shares, shares, shares]
+        + [jax.ShapeDtypeStruct(shares.shape[1:], BF)] * len(HOMING),
+        scratch_shapes=[
+            pltpu.VMEM((4, plane, SLOTS, D), BF),
+            pltpu.VMEM((tokens, D), BF),
+            pltpu.VMEM((tokens, D), BF),
+            pltpu.VMEM((slot_rows, D), BF),
+            pltpu.VMEM((slot_rows, D), BF),
+            pltpu.VMEM((slot_rows, hidden), BF),
+            pltpu.VMEM((slot_rows, hidden), BF),
+            pltpu.VMEM((slot_rows, hidden), BF),
+            pltpu.VMEM((2, quarter, hidden), BF),
+            pltpu.SemaphoreType.DMA((5,)),
+            pltpu.SemaphoreType.DMA((2,)),
+            pltpu.SemaphoreType.DMA((2,)),
+            pltpu.SemaphoreType.DMA((4,)),
+            pltpu.SemaphoreType.DMA((4, plane)),
+            pltpu.SemaphoreType.DMA((4, plane)),
+            pltpu.SemaphoreType.DMA((len(HOMING),)),
+            pltpu.SemaphoreType.DMA((len(HOMING),)),
+        ],
+        compiler_params=pltpu.CompilerParams(
+            vmem_limit_bytes=VMEM_BYTES, collective_id=2, has_side_effects=True
+        ),
+        cost_estimate=pl.CostEstimate(flops=3 * 10**10, bytes_accessed=4 * 10**8, transcendentals=0),
+        name="return_rows",
+    )(own_ranks, partner_ranks, *back, *operands[0], *operands[1])
+
+
+def finish_kernel(in_ref, out_ref):
+    out_ref[...] = jnp.swapaxes(in_ref[...].astype(F32), 0, 1)
+
+
+def finish_down_kernel(in_ref, out_ref):
+    half = out_ref.shape[2] // 2
+    for side in range(2):
+        out_ref[:, :, side * half : (side + 1) * half] = jnp.swapaxes(in_ref[:, side].astype(F32), 0, 1)
+
+
+def finish_weight(parts, down):
+    experts, rows, width = parts.shape
+    step = 32
+    if down:
+        rows = rows // 2
+        parts = parts.reshape(experts, 2, rows, width)
+        spec = pl.BlockSpec((experts, 2, step, width), lambda j: (0, 0, j, 0))
+        width = 2 * width
+    else:
+        spec = pl.BlockSpec((experts, step, width), lambda j: (0, j, 0))
+    return pl.pallas_call(
+        finish_down_kernel if down else finish_kernel,
+        grid=(rows // step,),
+        in_specs=[spec],
+        out_specs=pl.BlockSpec((step, experts, width), lambda j: (j, 0, 0)),
+        out_shape=jax.ShapeDtypeStruct((rows, experts, width), F32),
+        compiler_params=grant(),
+        name="finish_weight",
+    )(parts)
+
+
+def tie(*values):
+    return lax.optimization_barrier(values)
+
+
 def flip_permute(value, axis, size, flip):
     return lax.ppermute(value, axis, [(i, i ^ flip) for i in range(size)])
 
@@ -807,8 +1273,12 @@
     ).astype(BF)
     small = jnp.pad(small, ((0, 0), (0, 128 - small.shape[1])))
     shard_in = jnp.concatenate([attn_q.astype(BF), attn_k.astype(BF), attn_v.astype(BF), small], axis=1)
-    whole_in = gather_dense(shard_in)
-    w_out = gather_dense(attn_o.astype(BF))
+    here = lax.axis_index("expert") * n_context + block_index
+    part_rows = attn_q.shape[0] // plane
+    part_of = lambda shard: lax.dynamic_slice_in_dim(shard, here * part_rows, part_rows, 0)
+    whole_in, out_parts = gather_parts(part_of(shard_in), part_of(attn_o).astype(BF), n_dp, plane)
+    whole_in = whole_in.reshape(-1, shard_in.shape[1])
+    w_out = lax.all_gather(out_parts, PLANE, axis=1, tiled=False).reshape(-1, D)
     qkv_width = D + 2 * KVH * HD
     w_qkv = whole_in[:, :qkv_width]
     w_router = whole_in[:, qkv_width : qkv_width + EXPERTS]
@@ -823,15 +1293,12 @@
         mine = mine.reshape(2, per_device // 2, mine.shape[1], mine.shape[2])
         same = lax.dynamic_index_in_dim(mine, parity, 0, keepdims=False)
         other = lax.dynamic_index_in_dim(mine, 1 - parity, 0, keepdims=False)
-        return [same] + [
-            flip_permute(other if flip % 2 else same, "dp", n_dp, flip) for flip in range(1, n_dp)
-        ]
-
-    gate_pieces, up_pieces, down_pieces = (
-        weight_pieces(expert_gate),
-        weight_pieces(expert_up),
-        weight_pieces(expert_down),
-    )
+        return same, other
+
+    weight_halves = [weight_pieces(weight) for weight in (expert_gate, expert_up, expert_down)]
+    pieces = [[halves[0]] + [None] * (n_dp - 1) for halves in weight_halves]
+    for flip in (1, 3):
+        pieces[0][flip] = flip_permute(weight_halves[0][flip % 2], "dp", n_dp, flip)
 
     partner_routes = flip_permute(route_rows, "dp", n_dp, 1)
 
@@ -856,13 +1323,9 @@
     own_pair = [own_sel[:, :, i].astype(BF) for i in range(2)]
     partner_pair = [partner_sel[:, :, i].astype(BF) for i in range(2)]
 
-    def dispatch(rows, ranks):
-        slots = spread_rows(ranks[0].T, ranks[1].T, rows)
-        return [plane_exchange(s) for s in slots]
-
+    own_ranks_t = jnp.stack(own_pair, axis=0).transpose(0, 2, 1)
+    partner_ranks_t = jnp.stack(partner_pair, axis=0).transpose(0, 2, 1)
     partner_cot = flip_permute(cot_low, "dp", n_dp, 1)
-    cot_own = dispatch(cot_low, own_pair)
-    cot_partner = dispatch(partner_cot, partner_pair)
 
     positions = jnp.concatenate(
         [
@@ -885,9 +1348,18 @@
     mid_rows = x_rows + mxu(attended, w_out)
     normed_two = rms_scale(mid_rows, gain_two).astype(BF)
 
-    partner_normed = flip_permute(normed_two, "dp", n_dp, 1)
-    rows_own = dispatch(normed_two, own_pair)
-    rows_partner = dispatch(partner_normed, partner_pair)
+    normed_two, partner_cot, pieces[0][1], pieces[0][3] = tie(
+        normed_two, partner_cot, pieces[0][1], pieces[0][3]
+    )
+    riders = [weight_halves[which][flip % 2] for which, flip in RIDING]
+    moved = dispatch_rows(
+        normed_two, cot_low, partner_cot, own_ranks_t, partner_ranks_t, riders, n_dp
+    )
+    for (which, flip), piece in zip(RIDING, moved[8:]):
+        pieces[which][flip] = piece
+    moved = moved[:8]
+    moved = [m.reshape(plane * SLOTS, D) for m in moved]
+    rows_own, cot_own, rows_partner, cot_partner = moved[0:2], moved[2:4], moved[4:6], moved[6:8]
     logits = mxu(normed_two, w_router)
     top_logit = jnp.max(jnp.where(named, logits, masked_score), axis=1, keepdims=True)
     raised = jnp.where(named, jnp.exp(jnp.where(named, logits - top_logit, 0.0)), 0.0)
@@ -917,14 +1389,21 @@
                 cot_partner[i],
                 column(0),
                 column(1),
-                gate_pieces,
-                up_pieces,
-                down_pieces,
+                *pieces,
             )
         )
 
-    back_partner = [plane_exchange(r[3]) for r in returned]
-    back_own = [plane_exchange(r[2]) for r in returned]
+    parted = lambda rows: rows.reshape(plane, SLOTS, D)
+    grad_normed_two, gate_share, up_share, down_share, *homes = return_rows(
+        jnp.stack(own_pair, axis=0),
+        jnp.stack(partner_pair, axis=0),
+        [parted(rows) for r in returned for rows in (r[2], r[3])],
+        [(r[6], r[10], r[7], r[8], r[9]) for r in returned],
+        n_dp,
+    )
+    grad_normed_two, *rows_out = tie(
+        grad_normed_two, *[rows for r in returned for rows in (r[0], r[1])]
+    )
     dots = jnp.stack(
         [
             jnp.stack([r[4].reshape(plane, SLOTS), r[5].reshape(plane, SLOTS)], axis=1) for r in returned
@@ -941,10 +1420,6 @@
     grad_gates = jnp.sum(
         jnp.where(own_ranks[:, :, None] == slot_ids[None, None, :], all_dots[None], 0.0), axis=-1
     )
-    for_partner = collect_rows(partner_pair[0], partner_pair[1], back_partner[0], back_partner[1], BF)
-    from_partner = flip_permute(for_partner, "dp", n_dp, 1)
-    grad_normed_two = collect_rows(own_pair[0], own_pair[1], back_own[0], back_own[1], F32)
-    grad_normed_two = grad_normed_two + from_partner.astype(F32)
     grad_logits = gates * (grad_gates - jnp.sum(gates * grad_gates, axis=1, keepdims=True))
     grad_logits = grad_logits.astype(BF)
     grad_wrouter = mxu(normed_two, grad_logits, ((0,), (0,)))
@@ -957,32 +1432,28 @@
     grad_attended = mxu(grad_attn, w_out, ((1,), (1,))).astype(BF)
     grad_wout = mxu(attended, grad_attn, ((0,), (0,)))
 
-    def weight_shares(index_lhs, index_rhs):
-        made = [mxu(r[index_lhs], r[index_rhs], ((0,), (0,))).astype(BF) for r in returned]
-        made = jnp.stack(made, axis=0)
-        made = made.reshape(2, n_dp, made.shape[1] // n_dp, made.shape[2])
-
-        def quarter(flip):
-            return lax.dynamic_index_in_dim(made, z_index ^ flip, 1, keepdims=False)
-
-        got = [quarter(0)] + [
-            flip_permute(quarter(flip), "dp", n_dp, flip) for flip in range(1, n_dp)
-        ]
+    home_of = dict(zip(HOMING, homes))
+
+    def move_share(which, share):
+        got = [share[0]] + [None] * (n_dp - 1)
+        for flip in range(1, n_dp):
+            got[flip] = home_of.get((which, flip))
+            if got[flip] is None:
+                got[flip] = flip_permute(share[flip], "dp", n_dp, flip)
         same = sum(got[flip].astype(F32) for flip in range(0, n_dp, 2)).astype(BF)
         other = sum(got[flip].astype(F32) for flip in range(1, n_dp, 2)).astype(BF)
-        four = jnp.where(
+        return jnp.where(
             parity == 0, jnp.concatenate([same, other], axis=0), jnp.concatenate([other, same], axis=0)
         )
-        everything = lax.all_gather(four, "context", axis=0, tiled=True)
-        return everything.transpose(1, 0, 2).astype(F32)
-
-    grad_wdown = weight_shares(7, 10)
-    grad_wgate = weight_shares(6, 8)
-    grad_wup = weight_shares(6, 9)
+
+    gate_four = move_share(0, gate_share)
+    up_four = move_share(1, up_share)
+    down_four = move_share(2, down_share)
 
     grad_qproj, grad_keys, grad_values = attend_back(
         block_word, qkv, keys_values, grad_attended, logs, cosine, sine, prompt_len
     )
+    grad_qproj, grad_keys, grad_values, gate_four = tie(grad_qproj, grad_keys, grad_values, gate_four)
     grad_kv = jnp.concatenate([grad_keys, grad_values], axis=1)
     prompt_share = lax.psum_scatter(
         grad_kv[:prompt_len].astype(BF), "context", scatter_dimension=0, tiled=True
@@ -993,12 +1464,13 @@
     grad_qkv = jnp.concatenate([grad_qproj, grad_kv.astype(BF)], axis=1)
     grad_wqkv = mxu(normed_one, grad_qkv, ((0,), (0,)))
     grad_normed_one = mxu(grad_qkv, w_qkv, ((1,), (1,)))
+    grad_wqkv, grad_normed_one, up_four = tie(grad_wqkv, grad_normed_one, up_four)
     norm_back_one = jax.vjp(rms_scale, x_rows, gain_one)[1]
     grad_x_norm, grad_gain_one = norm_back_one(grad_normed_one)
     grad_inputs = (grad_mid + grad_x_norm).astype(BF)
 
-    out_partner = [plane_exchange(r[1]) for r in returned]
-    out_own = [plane_exchange(r[0]) for r in returned]
+    out_partner = [plane_exchange(rows) for rows in rows_out[1::2]]
+    out_own = [plane_exchange(rows) for rows in rows_out[0::2]]
     out_for_partner = collect_rows(partner_pair[0], partner_pair[1], out_partner[0], out_partner[1], BF)
     out_from_partner = flip_permute(out_for_partner, "dp", n_dp, 1)
     moe_out = collect_rows(own_pair[0], own_pair[1], out_own[0], out_own[1], F32)
@@ -1020,9 +1492,9 @@
         total_in[:, qkv_width + EXPERTS],
         total_in[:, qkv_width + EXPERTS + 1],
         total_in[:, qkv_width : qkv_width + EXPERTS],
-        grad_wgate,
-        grad_wup,
-        grad_wdown,
+        finish_weight(lax.all_gather(gate_four, "context", axis=0, tiled=True), False),
+        finish_weight(lax.all_gather(up_four, "context", axis=0, tiled=True), False),
+        finish_weight(lax.all_gather(down_four, "context", axis=0, tiled=True), True),
     )
 
 

time: 1880 us -> 1580 us (0.84)
  Pallas kernels: 236 us -> 745 us
  waiting for transfers between devices: 788 us -> 508 us
  blocking collectives: 294 us -> 73.9 us
  starting transfers between devices: 185 us -> 31.7 us
  local copies, waits for them, and re-layouts: 140 us -> 81 us
  matrix products: 96.7 us -> 44 us
  other arithmetic: 101 us -> 74.2 us
    pallas_call x4 -> x6, Pallas kernels: 30.9 us -> 554 us  [the longest x1 249 us: dispatch_rows(): pl.pallas_call(functools.partial(dispatch_kernel, plane, n_dp), in_specs=...]
    ppermute x25 -> x12, waiting for transfers between devices: 530 us -> 203 us  [flip_permute(): return lax.ppermute(value, axis, [(i, i ^ flip) for i in range(size)])]
    all_to_all x7 -> x2, blocking collectives: 247 us -> 73.9 us  [plane_exchange(): lax.all_to_all(parted, PLANE, split_axis=0, concat_axis=0, tiled=True)]
    all_gather x5 -> x4, waiting for transfers between devices: 46.1 us -> 182 us  [the longest x1 76.4 us: local_paired(): lax.all_gather(down_four, 'context', axis=0, tiled=True)]
    ppermute x25 -> x12, starting transfers between devices: 141 us -> 16.3 us  [flip_permute(): return lax.ppermute(value, axis, [(i, i ^ flip) for i in range(size)])]
    all_to_all x9 -> x2, waiting for transfers between devices: 109 us -> 19.6 us  [plane_exchange(): lax.all_to_all(parted, PLANE, split_axis=0, concat_axis=0, tiled=True)]
    unnamed x94 -> x80, local copies, waits for them, and re-layouts: 84.1 us -> 15 us
    dot_general x16 -> x10, matrix products: 96.7 us -> 44 us  [mxu(): lax.dot_general(lhs, rhs, (contract, ((), ())), preferred_element_type=F32)]
  transfers between devices with their start and end apart: 48 -> 28, of which waited for: 26 -> 13; matrix products, arithmetic and copies ran while one was open for 16% -> 8% of each run, Pallas kernels for 7% -> 35%
where the time goes in v2:
time: 1580 us; the launch traced here: 1570 us
  Pallas kernels  745 us (47%)
  waiting for transfers between devices  508 us (32%)
  local copies, waits for them, and re-layouts  81 us (5%)
  other arithmetic  74.2 us (5%)
  blocking collectives  73.9 us (5%)
  matrix products  44 us (3%)
  starting transfers between devices  31.7 us (2%)
    pallas_call x1, Pallas kernels, dispatch_rows(): pl.pallas_call(functools.partial(dispatch_kernel, plane, n_dp), in_specs=...  249 us
    pallas_call x1, Pallas kernels, return_rows(): pl.pallas_call(functools.partial(return_kernel, plane, n_dp), in_specs=[v...  221 us
    ppermute x12, waiting for transfers between devices, flip_permute(): return lax.ppermute(value, axis, [(i, i ^ flip) for i in range(size)])  203 us
    pallas_call x2, Pallas kernels, run_expert(): pl.pallas_call(functools.partial(expert_kernel, n_dp, half_steps), grid=(...  86.2 us
    all_gather x1, waiting for transfers between devices, local_paired(): lax.all_gather(down_four, 'context', axis=0, tiled=True)  76.4 us
    all_to_all x2, blocking collectives, plane_exchange(): lax.all_to_all(parted, PLANE, split_axis=0, concat_axis=0, tiled=True)  73.9 us
    reduce_scatter x2, waiting for transfers between devices, scatter_dense(): parts = lax.psum_scatter(parts, PLANE, scatter_dimension=1, tiled=True)  62.9 us
    all_gather x1, waiting for transfers between devices, local_paired(): lax.all_gather(gate_four, 'context', axis=0, tiled=True)  53.4 us
  transfers between devices with their start and end apart: 28, of which 13 were waited for; matrix products, arithmetic and copies ran while one was open for 8% of the time, Pallas kernels for 35%

profile of v2, /device:TPU:0, one launch (start us, length us, event | category | flops | bytes accessed | tf_op | source)
XLA Modules:
  0.0 1573.1 jit_solution(13940006280288435525)
XLA Ops:
  15.8 43.2 %gather_parts.1 = (bf16[4,8,48,2176]{3,2,1,0:T(8,128)(2,1)}, bf16[4,48,1536]{2,1,0:T(8,128)(2,1)}) custom-call(bf16[48,2176]{1,0:T(8,128)(2,1)} %fusion.31.in_ref, bf16[48,1536]{1,0:T(8,128)(2,1)} %dynamic-slice_convert_fusion.3.out_part_ref), custom_call_target="tpu_custom_call" | custom-call | tf_op jit(solution)/shard_map/gather_parts/pallas_call | solution.py:853
  60.8 6.6 slice.151.w_ref
  72.3 12.1 project.1
  87.0 10.6 fusion.7
  101.6 4.1 collective-permute-start.2
  107.8 4.9 fusion.9
  120.1 37.0 %collective-permute-done = s32[768,4]{0,1:T(4,128)S(1)} collective-permute-done((s32[768,4]{0,1:T(4,128)S(1)}, s32[768,4]{0,1:T(4,128)S(1)}, u32[]{:S(2)}, u32[]{:S(2)}) %collective-permute-start) | collective-permute-done | bytes 12320 | tf_op jit(solution)/shard_map/ppermute | solution.py:1212
  162.7 26.2 %attend.1 = (bf16[768,1536]{1,0:T(8,128)(2,1)}, f32[12,768,1]{2,1,0:T(8,128)}) custom-call(s32[1]{0:T(128)} %bitcast.1.block_ref, bf16[768,2048]{1,0:T(8,128)(2,1)} %get-tuple-element.83.q_ref, bf16[1536,512]{1,0:T(8,128)(2,1)} %pad_maximum_fusion.2.k_ref.v_ref, bf16[1536,512]{1,0:T(8,128)(2,1)} %pad_maximum_fusion.2.k_ref.v_ref), custom_call_target="tpu_custom_call" | custom-call | tf_op jit(solution)/shard_map/attend/pallas_call | solution.py:494
  188.9 6.7 multiply_reduce_fusion.2
  197.9 9.8 collective-permute-done.1.cot_partner_ref
  223.9 3.3 all-to-all-start
  227.2 248.7 %dispatch_rows.1 = (bf16[8,112,1536]{2,1,0:T(8,128)(2,1)}, bf16[8,112,1536]{2,1,0:T(8,128)(2,1)}, bf16[8,112,1536]{2,1,0:T(8,128)(2,1)}, bf16[8,112,1536]{2,1,0:...) custom-call(bf16[768,1536]{1,0:T(8,128)(2,1)} %copy-done.3, ...), custom_call_target="tpu_custom_call" | custom-call | flops 20000000000 | bytes 700000000 | tf_op jit(solution)/shard_map/dispatch_rows/pallas_call | solution.py:955
  479.9 43.2 %experts.2 = (bf16[896,1536]{1,0:T(8,128)(2,1)}, bf16[896,1536]{1,0:T(8,128)(2,1)}, bf16[896,1536]{1,0:T(8,128)(2,1)}, bf16[896,1536]{1,0:T(8,128)(2,1)}, f32[89...) custom-call(s32[1]{0:T(128)} %bitcast.13.refs_0_, ...), custom_call_target="tpu_custom_call" | custom-call | tf_op jit(solution)/shard_map/experts/pallas_call | solution.py:722
  525.7 43.0 %experts.3 = (bf16[896,1536]{1,0:T(8,128)(2,1)}, bf16[896,1536]{1,0:T(8,128)(2,1)}, bf16[896,1536]{1,0:T(8,128)(2,1)}, bf16[896,1536]{1,0:T(8,128)(2,1)}, f32[89...) custom-call(s32[1]{0:T(128)} %bitcast.13.refs_0_, ...), custom_call_target="tpu_custom_call" | custom-call | tf_op jit(solution)/shard_map/experts/pallas_call | solution.py:722
  572.0 3.6 all-to-all-start.5
  575.6 220.7 %return_rows.1 = (f32[768,1536]{1,0:T(8,128)}, bf16[4,2,384,768]{3,2,1,0:T(8,128)(2,1)}, bf16[4,2,384,768]{3,2,1,0:T(8,128)(2,1)}, bf16[4,2,384,768]{3,2,1,0:T(8...) custom-call(bf16[2,768,8]{2,1,0:T(8,128)(2,1)} %get-tuple-element.25, ...), custom_call_target="tpu_custom_call" | custom-call | flops 30000001024 | bytes 400000000 | tf_op jit(solution)/shard_map/return_rows/pallas_call | solution.py:1143
  796.4 37.1 %all_to_all.30 = bf16[8,112,1536]{2,1,0:T(8,128)(2,1)} all-to-all(bf16[8,112,1536]{2,1,0:T(8,128)(2,1)S(1)} %bitcast.169), channel_id=1, replica_groups=mesh['expert'=2,'context'=4,'dp'=4] {'expert','context'}, dimensions={0} | all-to-all | bytes 5505024 | tf_op jit(solution)/shard_map/all_to_all | solution.py:1218
  833.5 36.8 %all_to_all.31 = bf16[8,112,1536]{2,1,0:T(8,128)(2,1)} all-to-all(bf16[8,112,1536]{2,1,0:T(8,128)(2,1)S(1)} %bitcast.171), channel_id=1, replica_groups=mesh['expert'=2,'context'=4,'dp'=4] {'expert','context'}, dimensions={0} | all-to-all | bytes 5505024 | tf_op jit(solution)/shard_map/all_to_all | solution.py:1218
  870.2 3.6 all-to-all-start.2
  873.9 2.9 fusion.14
  876.8 9.6 collect_rows.3
  887.9 19.6 %all-to-all-done.2 = bf16[8,112,1536]{2,1,0:T(8,128)(2,1)S(1)} async-done(((bf16[8,112,1536]{2,1,0:T(8,128)(2,1)}), bf16[8,112,1536]{2,1,0:T(8,128)(2,1)S(1)}, u32[]{:S(2)}, u32[]{:S(2)}) %all-to-all-start.2) | async-done | bytes 2752544 | tf_op jit(solution)/shard_map/all_to_all | solution.py:1218
  909.0 4.4 all-to-all-start.1
  919.1 21.3 %collective-permute-done.6 = f32[8,2,112]{2,1,0:T(2,128)S(1)} collective-permute-done((f32[8,2,112]{2,1,0:T(2,128)S(1)}, f32[8,2,112]{2,1,0:T(2,128)S(1)}, u32[]{:S(2)}, u32[]{:S(2)}) %collective-permute-start.6) | collective-permute-done | bytes 7200 | tf_op jit(solution)/shard_map/ppermute | solution.py:1212
  943.2 6.2 multiply_reduce_fusion
  949.4 10.0 collect_rows.2
  959.4 8.9 fusion
  968.3 5.2 convolution_convert_fusion.1.do_ref
  973.5 47.1 %attend_back.1 = (bf16[768,1536]{1,0:T(8,128)(2,1)}, f32[1536,256]{1,0:T(8,128)}, f32[1536,256]{1,0:T(8,128)}) custom-call(s32[1]{0:T(128)} %bitcast.1.block_ref, bf16[768,2048]{1,0:T(8,128)(2,1)} %get-tuple-element.83.q_ref, bf16[1536,512]{1,0:T(8,128)(2,1)} %pad_maximum_fusion.2.k_ref.v_ref, bf16[1536,512]{1,0:T(8,128)(2,1)} %pad_maximum_fusion.2.k_ref.v_ref, ...), custom_call_target="tpu_custom_call" | custom-call | tf_op jit(solution)/shard_map/attend_back/pallas_call | solution.py:545
  1026.3 6.6 convolution_convert_fusion
  1043.8 21.6 %collective-permute-done.7 = bf16[2,384,768]{2,1,0:T(8,128)(2,1)S(1)} collective-permute-done((bf16[2,384,768]{2,1,0:T(8,128)(2,1)S(1)}, bf16[2,384,768]{2,1,0:T(8,128)(2,1)S(1)}, u32[]{:S(2)}, u32[]{:S(2)}) %collective-permute-start.7) | collective-permute-done | bytes 1179680 | tf_op jit(solution)/shard_map/ppermute | solution.py:1212
  1065.4 26.2 %collective-permute-done.8 = bf16[2,384,768]{2,1,0:T(8,128)(2,1)S(1)} collective-permute-done((bf16[2,384,768]{2,1,0:T(8,128)(2,1)S(1)}, bf16[2,384,768]{2,1,0:T(8,128)(2,1)S(1)}, u32[]{:S(2)}, u32[]{:S(2)}) %collective-permute-start.8) | collective-permute-done | bytes 1179680 | tf_op jit(solution)/shard_map/ppermute | solution.py:1212
  1104.5 8.1 fusion.17
  1112.6 7.5 fusion.18
  1122.0 3.5 pad_maximum_fusion
  1125.5 3.5 copy.152
  1129.6 62.8 %reduce-scatter.8.cloned.1.call-done = bf16[4,1,48,2176]{3,2,0,1:T(8,128)(2,1)} async-done(((bf16[4,8,48,2176]{3,2,0,1:T(8,128)(2,1)}), bf16[4,1,48,2176]{3,2,0,1:T(8,128)(2,1)}) %reduce-scatter.8.cloned.1.call-update) | async-done | bytes 835600 | tf_op jit(solution)/shard_map/reduce_scatter | solution.py:1239
  1192.5 24.1 %reduce-scatter.14.cloned.1.call-done = bf16[1,48,1536]{2,1,0:T(8,128)(2,1)} async-done(((bf16[4,48,1536]{2,1,0:T(8,128)(2,1)}), bf16[1,48,1536]{2,1,0:T(8,128)(2,1)}) %reduce-scatter.14.cloned.1.call-update) | async-done | bytes 147472 | tf_op jit(solution)/shard_map/reduce_scatter | solution.py:1240
  1222.5 86.8 %collective-permute-done.9 = bf16[2,384,768]{2,1,0:T(8,128)(2,1)S(1)} collective-permute-done((bf16[2,384,768]{2,1,0:T(8,128)(2,1)S(1)}, bf16[2,384,768]{2,1,0:T(8,128)(2,1)S(1)}, u32[]{:S(2)}, u32[]{:S(2)}) %collective-permute-start.9) | collective-permute-done | bytes 1179680 | tf_op jit(solution)/shard_map/ppermute | solution.py:1212
  1314.9 5.5 fusion.11
  1320.4 3.0 bitcast_convert_fusion.1
  1323.4 76.4 %all-gather.17.cloned.1.call-done = bf16[16,384,768]{2,1,0:T(8,128)(2,1)} async-done(((bf16[4,384,768]{2,1,0:T(8,128)(2,1)}), bf16[16,384,768]{2,1,0:T(8,128)(2,1)}) %all-gather.17.cloned.1.call-update) | async-done | bytes 9437200 | tf_op jit(solution)/shard_map/all_gather | solution.py:1497
  1399.7 12.4 finish_weight.5
  1412.1 53.4 %all-gather.13.cloned.1.call-done.in_ref = bf16[16,384,768]{2,1,0:T(8,128)(2,1)} async-done(((bf16[4,384,768]{2,1,0:T(8,128)(2,1)}), bf16[16,384,768]{2,1,0:T(8,128)(2,1)}) %all-gather.13.cloned.1.call-update) | async-done | bytes 9437200 | tf_op jit(solution)/shard_map/all_gather | solution.py:1495
  1465.5 14.6 finish_weight.3
  1480.1 51.9 %all-gather.15.cloned.1.call-done.in_ref = bf16[16,384,768]{2,1,0:T(8,128)(2,1)} async-done(((bf16[4,384,768]{2,1,0:T(8,128)(2,1)}), bf16[16,384,768]{2,1,0:T(8,128)(2,1)}) %all-gather.15.cloned.1.call-update) | async-done | bytes 9437200 | tf_op jit(solution)/shard_map/all_gather | solution.py:1496
  1532.0 14.3 finish_weight.4
  1546.3 13.8 all-gather.21.cloned.1.call-done
  (240 shorter events, 125.3 us)
Async XLA Ops:
  7.2 153.0 %all-gather.11.cloned.1.call-start = ((), (), s32[]{:S(2)}) async-start(), calls=%async_computation.11 | async-start | bytes 1310720 | tf_op jit(solution)/shard_map/all_gather | solution.py:1344
  60.8 6.6 copy-start.24
  86.2 102.7 %all-gather.19.cloned.1.call-start = ((), (), s32[]{:S(2)}) async-start(), calls=%async_computation.20 | async-start | bytes 5308416 | tf_op jit(solution)/shard_map/all_gather | solution.py:1281
  99.6 6.2 copy-start.31
  101.1 96.7 %collective-permute-start.3 = (bf16[2,384,768]{2,1,0:T(8,128)(2,1)}, bf16[2,384,768]{2,1,0:T(8,128)(2,1)S(1)}, u32[]{:S(2)}, u32[]{:S(2)}) collective-permute-start(bf16[2,384,768]{2,1,0:T(8,128)(2,1)} %get-tuple-element.240), channel_id=1, source_target_pairs={{0,3},{1,2},{2,1},{3,0},{4,7},{5,6},{6,5},{7,4},{8,11},{9,10},{10,... | collective-permute-start | bytes 3538952 | tf_op jit(solution)/shard_map/ppermute | solution.py:1212
  101.6 96.2 %collective-permute-start.2 = (bf16[2,384,768]{2,1,0:T(8,128)(2,1)}, bf16[2,384,768]{2,1,0:T(8,128)(2,1)}, u32[]{:S(2)}, u32[]{:S(2)}) collective-permute-start(bf16[2,384,768]{2,1,0:T(8,128)(2,1)} %get-tuple-element.240), channel_id=1, source_target_pairs={{0,1},{1,0},{2,3},{3,2},{4,5},{5,4},{6,7},{7,6},{8,9},{9,8},{10,11... | collective-permute-start | bytes 3538952 | tf_op jit(solution)/shard_map/ppermute | solution.py:1212
  105.7 51.3 %collective-permute-start = (s32[768,4]{0,1:T(4,128)S(1)}, s32[768,4]{0,1:T(4,128)S(1)}, u32[]{:S(2)}, u32[]{:S(2)}) collective-permute-start(s32[768,4]{0,1:T(4,128)S(1)} %bitcast.191), channel_id=1, source_target_pairs={{0,1},{1,0},{2,3},{3,2},{4,5},{5,4},{6,7},{7,6},{8,9},{9,8},{10,11... | collective-permute-start | bytes 36872 | tf_op jit(solution)/shard_map/ppermute | solution.py:1212
  105.8 101.9 %collective-permute-start.1 = (bf16[768,1536]{1,0:T(8,128)(2,1)}, bf16[768,1536]{1,0:T(8,128)(2,1)}, u32[]{:S(2)}, u32[]{:S(2)}) collective-permute-start(bf16[768,1536]{1,0:T(8,128)(2,1)} %bitcast.14.cot_ref), channel_id=1, source_target_pairs={{0,1},{1,0},{2,3},{3,2},{4,5},{5,4},{6,7},{7,6},{8,9},{9,8},{10,11... | collective-permute-start | bytes 7077896 | tf_op jit(solution)/shard_map/ppermute | solution.py:1212
  162.7 26.2 %copy-start.1 = (bf16[1,768,1536]{2,1,0:T(8,128)(2,1)S(1)}, bf16[1,768,1536]{2,1,0:T(8,128)(2,1)}, u32[]{:S(2)}) copy-start(bf16[1,768,1536]{2,1,0:T(8,128)(2,1)} %param.13) | copy-start | bytes 7077892
  196.2 11.4 copy-start.22
  197.8 23.1 %copy-start.3 = (bf16[768,1536]{1,0:T(8,128)(2,1)}, bf16[768,1536]{1,0:T(8,128)(2,1)S(1)}, u32[]{:S(2)}) copy-start(bf16[768,1536]{1,0:T(8,128)(2,1)S(1)} %multiply_convert_fusion.normed_ref) | copy-start | bytes 7077892
  197.9 12.3 copy-start.26
  197.9 23.1 %copy-start.9 = (bf16[2,384,768]{2,1,0:T(8,128)(2,1)}, bf16[2,384,768]{2,1,0:T(8,128)(2,1)S(1)}, u32[]{:S(2)}) copy-start(bf16[2,384,768]{2,1,0:T(8,128)(2,1)S(1)} %collective-permute-done.3.refs_10_) | copy-start | bytes 3538948
  217.4 5.2 collective-permute-start.4
  223.9 252.1 %all-to-all-start = ((f32[8,2,2,112]{3,2,1,0:T(2,128)}), f32[8,2,2,112]{3,2,1,0:T(2,128)S(1)}, u32[]{:S(2)}, u32[]{:S(2)}) async-start(f32[8,2,2,112]{3,2,1,0:T(2,128)} %pad_maximum_fusion.13), calls=%async_computation | async-start | bytes 32768 | tf_op jit(solution)/shard_map/all_to_all | solution.py:1376
  572.0 224.3 %all-to-all-start.5 = ((f32[8,2,2,112]{3,1,2,0:T(2,128)}), f32[8,2,2,112]{3,1,2,0:T(2,128)S(1)}, u32[]{:S(2)}, u32[]{:S(2)}) async-start(f32[8,2,2,112]{3,1,2,0:T(2,128)} %copy.148), calls=%async_computation.5 | async-start | bytes 32768 | tf_op jit(solution)/shard_map/all_to_all | solution.py:1413
  575.6 220.8 %copy-start.15 = (bf16[896,1536]{1,0:T(8,128)(2,1)S(1)}, bf16[896,1536]{1,0:T(8,128)(2,1)}, u32[]{:S(2)}) copy-start(bf16[896,1536]{1,0:T(8,128)(2,1)} %get-tuple-element.126) | copy-start | bytes 8257540
  796.3 37.1 %copy-start.16 = (bf16[896,1536]{1,0:T(8,128)(2,1)S(1)}, bf16[896,1536]{1,0:T(8,128)(2,1)}, u32[]{:S(2)}) copy-start(bf16[896,1536]{1,0:T(8,128)(2,1)} %get-tuple-element.127) | copy-start | bytes 8257540
  870.2 37.2 %all-to-all-start.2 = ((bf16[8,112,1536]{2,1,0:T(8,128)(2,1)}), bf16[8,112,1536]{2,1,0:T(8,128)(2,1)S(1)}, u32[]{:S(2)}, u32[]{:S(2)}) async-start(bf16[8,112,1536]{2,1,0:T(8,128)(2,1)} %bitcast.170), calls=%async_computation.2 | async-start | bytes 5505024 | tf_op jit(solution)/shard_map/all_to_all | solution.py:1218
  886.5 72.9 %collective-permute-start.5 = (bf16[768,1536]{1,0:T(8,128)(2,1)}, bf16[768,1536]{1,0:T(8,128)(2,1)}, u32[]{:S(2)}, u32[]{:S(2)}) collective-permute-start(bf16[768,1536]{1,0:T(8,128)(2,1)} %collect_rows.3), channel_id=1, source_target_pairs={{0,1},{1,0},{2,3},{3,2},{4,5},{5,4},{6,7},{7,6},{8,9},{9,8},{10,11... | collective-permute-start | bytes 7077896 | tf_op jit(solution)/shard_map/ppermute | solution.py:1212
  909.0 40.4 %all-to-all-start.1 = ((bf16[8,112,1536]{2,1,0:T(8,128)(2,1)}), bf16[8,112,1536]{2,1,0:T(8,128)(2,1)}, u32[]{:S(2)}, u32[]{:S(2)}) async-start(bf16[8,112,1536]{2,1,0:T(8,128)(2,1)} %bitcast.168), calls=%async_computation.1 | async-start | bytes 5505024 | tf_op jit(solution)/shard_map/all_to_all | solution.py:1218
  913.5 181.4 %reduce-scatter.6.cloned.1.call-start = ((), (), s32[]{:S(2)}) async-start(), calls=%async_computation.12 | async-start | bytes 1310720 | tf_op jit(solution)/shard_map/reduce_scatter | solution.py:1458
  915.5 24.9 %copy-start.21 = (f32[768,32]{0,1:T(8,128)S(1)}, f32[768,32]{0,1:T(8,128)}, u32[]{:S(2)}) copy-start(f32[768,32]{0,1:T(8,128)} %get-tuple-element.256) | copy-start | bytes 294916
  915.6 27.5 %copy-start.18 = (f32[768,32]{0,1:T(8,128)S(1)}, f32[768,32]{0,1:T(8,128)}, u32[]{:S(2)}) copy-start(f32[768,32]{0,1:T(8,128)} %copy-done.17) | copy-start | bytes 294916
  915.6 27.5 %copy-start.23 = (pred[768,32]{0,1:T(32,128)(4,1)S(1)}, pred[768,32]{0,1:T(32,128)(4,1)}, u32[]{:S(2)}) copy-start(pred[768,32]{0,1:T(32,128)(4,1)} %get-tuple-element.225) | copy-start | bytes 73732
  915.6 27.6 %copy-start.28 = (f32[768]{0:T(1024)S(1)}, f32[768]{0:T(1024)}, u32[]{:S(2)}) copy-start(f32[768]{0:T(1024)} %copy-done.27) | copy-start | bytes 9220
  915.6 24.8 %collective-permute-start.6 = (f32[8,2,112]{2,1,0:T(2,128)S(1)}, f32[8,2,112]{2,1,0:T(2,128)S(1)}, u32[]{:S(2)}, u32[]{:S(2)}) collective-permute-start(f32[8,2,112]{2,1,0:T(2,128)S(1)} %bitcast.193), channel_id=1, source_target_pairs={{0,1},{1,0},{2,3},{3,2},{4,5},{5,4},{6,7},{7,6},{8,9},{9,8},{10,11... | collective-permute-start | bytes 21512 | tf_op jit(solution)/shard_map/ppermute | solution.py:1212
  943.1 6.2 copy-start.30
  949.4 18.9 %slice-start = ((s8[4718592]{0:T(1024)(128)(4,1)}), s8[524288]{0:T(1024)(128)(4,1)S(1)}, s32[]{:S(2)}) async-start(s8[4718592]{0:T(1024)(128)(4,1)} %bitcast.196), calls=%async_computation.23 | async-start | bytes 1048576
  959.4 8.9 slice-start.1
  968.3 5.2 copy-start.6
  1025.4 103.6 %reduce-scatter.12.cloned.1.call-start = ((), (), s32[]{:S(2)}) async-start(), calls=%async_computation.15 | async-start | bytes 5308416 | tf_op jit(solution)/shard_map/reduce_scatter | solution.py:1239
  1035.4 157.0 %reduce-scatter.8.cloned.1.call-start = ((), (), s32[]{:S(2)}) async-start(), calls=%async_computation.13 | async-start | bytes 7520256 | tf_op jit(solution)/shard_map/reduce_scatter | solution.py:1239
  1037.4 27.9 %collective-permute-start.7 = (bf16[2,384,768]{2,1,0:T(8,128)(2,1)S(1)}, bf16[2,384,768]{2,1,0:T(8,128)(2,1)S(1)}, u32[]{:S(2)}, u32[]{:S(2)}) collective-permute-start(bf16[2,384,768]{2,1,0:T(8,128)(2,1)S(1)} %get-tuple-element.229), channel_id=1, source_target_pairs={{0,1},{1,0},{2,3},{3,2},{4,5},{5,4},{6,7},{7,6},{8,9},{9,8},{10,11... | collective-permute-start | bytes 3538952 | tf_op jit(solution)/shard_map/ppermute | solution.py:1212
  1039.0 52.6 %collective-permute-start.8 = (bf16[2,384,768]{2,1,0:T(8,128)(2,1)S(1)}, bf16[2,384,768]{2,1,0:T(8,128)(2,1)S(1)}, u32[]{:S(2)}, u32[]{:S(2)}) collective-permute-start(bf16[2,384,768]{2,1,0:T(8,128)(2,1)S(1)} %get-tuple-element.230), channel_id=1, source_target_pairs={{0,3},{1,2},{2,1},{3,0},{4,7},{5,6},{6,5},{7,4},{8,11},{9,10},{10,... | collective-permute-start | bytes 3538952 | tf_op jit(solution)/shard_map/ppermute | solution.py:1212
  1104.5 8.2 copy-start.32
  1112.6 7.5 copy-start.5
  1112.6 7.5 copy-start.25
  1129.0 87.6 %reduce-scatter.14.cloned.1.call-start = ((), (), s32[]{:S(2)}) async-start(), calls=%async_computation.16 | async-start | bytes 737280 | tf_op jit(solution)/shard_map/reduce_scatter | solution.py:1240
  1129.6 184.8 %reduce-scatter.10.cloned.1.call-start = ((), (), s32[]{:S(2)}) async-start(), calls=%async_computation.14 | async-start | bytes 1044480 | tf_op jit(solution)/shard_map/reduce_scatter | solution.py:1240
  1192.5 127.9 %all-gather.23.cloned.1.call-start = ((), (), s32[]{:S(2)}) async-start(), calls=%async_computation.22 | async-start | bytes 1327104 | tf_op jit(solution)/shard_map/all_gather | solution.py:1241
  1216.6 183.1 %all-gather.17.cloned.1.call-start = ((), (), s32[]{:S(2)}) async-start(), calls=%async_computation.19 | async-start | bytes 11796480 | tf_op jit(solution)/shard_map/all_gather | solution.py:1497
  1218.9 90.3 %collective-permute-start.9 = (bf16[2,384,768]{2,1,0:T(8,128)(2,1)S(1)}, bf16[2,384,768]{2,1,0:T(8,128)(2,1)S(1)}, u32[]{:S(2)}, u32[]{:S(2)}) collective-permute-start(bf16[2,384,768]{2,1,0:T(8,128)(2,1)S(1)} %get-tuple-element.226), channel_id=1, source_target_pairs={{0,2},{1,3},{2,0},{3,1},{4,6},{5,7},{6,4},{7,5},{8,10},{9,11},{10,... | collective-permute-start | bytes 3538952 | tf_op jit(solution)/shard_map/ppermute | solution.py:1212
  1219.7 91.3 %collective-permute-start.11 = (bf16[2,384,768]{2,1,0:T(8,128)(2,1)S(1)}, bf16[2,384,768]{2,1,0:T(8,128)(2,1)S(1)}, u32[]{:S(2)}, u32[]{:S(2)}) collective-permute-start(bf16[2,384,768]{2,1,0:T(8,128)(2,1)S(1)} %get-tuple-element.227), channel_id=1, source_target_pairs={{0,3},{1,2},{2,1},{3,0},{4,7},{5,6},{6,5},{7,4},{8,11},{9,10},{10,... | collective-permute-start | bytes 3538952 | tf_op jit(solution)/shard_map/ppermute | solution.py:1212
  1220.1 91.0 %collective-permute-start.10 = (bf16[2,384,768]{2,1,0:T(8,128)(2,1)S(1)}, bf16[2,384,768]{2,1,0:T(8,128)(2,1)S(1)}, u32[]{:S(2)}, u32[]{:S(2)}) collective-permute-start(bf16[2,384,768]{2,1,0:T(8,128)(2,1)S(1)} %get-tuple-element.228), channel_id=1, source_target_pairs={{0,1},{1,0},{2,3},{3,2},{4,5},{5,4},{6,7},{7,6},{8,9},{9,8},{10,11... | collective-permute-start | bytes 3538952 | tf_op jit(solution)/shard_map/ppermute | solution.py:1212
  1313.0 152.5 %all-gather.13.cloned.1.call-start = ((), (), s32[]{:S(2)}) async-start(), calls=%async_computation.17 | async-start | bytes 11796480 | tf_op jit(solution)/shard_map/all_gather | solution.py:1495
  1313.6 218.4 %all-gather.15.cloned.1.call-start = ((), (), s32[]{:S(2)}) async-start(), calls=%async_computation.18 | async-start | bytes 11796480 | tf_op jit(solution)/shard_map/all_gather | solution.py:1496
  1314.3 245.7 %all-gather.21.cloned.1.call-start = ((), (), s32[]{:S(2)}) async-start(), calls=%async_computation.21 | async-start | bytes 1880064 | tf_op jit(solution)/shard_map/all_gather | solution.py:1241
  (17 other events, 36.4 us)
Sparse Core Ops, SparseCore 0:
  86.3 16.5 all-gather.10
  104.8 38.9 all-gather.18
  1025.5 25.4 reduce-scatter.5
  1054.7 53.9 reduce-scatter.11
  1129.1 63.3 reduce-scatter.7
  1194.6 21.9 reduce-scatter.13
  1218.9 71.7 reduce-scatter.9
  1292.8 24.0 all-gather.22
  1319.0 80.6 all-gather.16
  1401.2 64.2 all-gather.12
  1467.7 64.2 all-gather.14
  1533.9 26.0 all-gather.20

commit v3 on v1

--- a/solution.py
+++ b/solution.py
@@ -394,7 +394,8 @@
 
 BF = jnp.bfloat16
 F32 = jnp.float32
-SLOTS = 104
+SLOTS = 112
+MESH_ID = pl.DeviceIdType.MESH
 PLANE = ("expert", "context")
 VMEM_BYTES = 60 * 1024 * 1024
 
@@ -431,8 +432,8 @@
         out_ref[:, half * HD : (half + 1) * HD] = (turn(part, cosine, sine) * factor).astype(BF)
 
 
-def project(x_low, gain, w_qkv, cosine, sine):
-    tokens, width = x_low.shape[0], w_qkv.shape[1]
+def project(x_low, gain, w_in, width, cosine, sine):
+    tokens = x_low.shape[0]
     whole = lambda j: (0, 0)
     return pl.pallas_call(
         project_kernel,
@@ -454,7 +455,7 @@
         ],
         compiler_params=grant(),
         name="project",
-    )(x_low, gain, w_qkv, cosine, sine)
+    )(x_low, gain, w_in, cosine, sine)
 
 
 def row_blocks(prompt_len):
@@ -484,7 +485,9 @@
         total = jnp.sum(unnormed, axis=-1, keepdims=True)
         mixed = mxu(unnormed.astype(BF), v_ref[:keys, :]) / total
         out_ref[rows, :] = mixed.astype(BF)
-        log_ref[0, rows, :] = top + jnp.log(total)
+        lane = lax.broadcasted_iota(jnp.int32, (PBLK, log_ref.shape[1]), 1)
+        kept = jnp.where(pl.program_id(0) == 0, 0.0, log_ref[rows, :])
+        log_ref[rows, :] = jnp.where(lane == pl.program_id(0), top + jnp.log(total), kept)
 
 
 def attend(block_index, qkv, keys_values, prompt_len):
@@ -501,72 +504,15 @@
         ],
         out_specs=[
             pl.BlockSpec((tokens, HD), lambda h: (0, h)),
-            pl.BlockSpec((1, tokens, 1), lambda h: (h, 0, 0)),
+            pl.BlockSpec((tokens, 128), lambda h: (0, 0)),
         ],
         out_shape=[
             jax.ShapeDtypeStruct((tokens, D), BF),
-            jax.ShapeDtypeStruct((HEADS, tokens, 1), F32),
+            jax.ShapeDtypeStruct((tokens, 128), F32),
         ],
         compiler_params=grant(),
         name="attend",
     )(block_index, qkv, keys_values, keys_values)
-
-
-def attend_back_kernel(
-    prompt_len, block_ref, q_ref, k_ref, v_ref, do_ref, log_ref, cos_ref, sin_ref, dq_ref, dk_ref, dv_ref
-):
-    @pl.when(pl.program_id(1) == 0)
-    def _():
-        dk_ref[...] = jnp.zeros_like(dk_ref)
-        dv_ref[...] = jnp.zeros_like(dv_ref)
-
-    for first_row, keys in row_blocks(prompt_len):
-        rows = slice(first_row, first_row + PBLK)
-        queries, grads = q_ref[rows, :], do_ref[rows, :]
-        scores = mxu(queries, k_ref[:keys, :], ((1,), (1,)))
-        scores = masked_scores(scores, first_row, prompt_len, block_ref[0])
-        probs = jnp.exp(scores - log_ref[0, rows, :])
-        grad_probs = mxu(grads, v_ref[:keys, :], ((1,), (1,)))
-        dots = jnp.sum(probs * grad_probs, axis=-1, keepdims=True)
-        grad_scores = (probs * (grad_probs - dots)).astype(BF)
-        grad_query = mxu(grad_scores, k_ref[:keys, :])
-        grad_query = turn(grad_query, cos_ref[rows, :], -sin_ref[rows, :]) * (1.0 / math.sqrt(HD))
-        dq_ref[rows, :] = grad_query.astype(BF)
-        dk_ref[:keys, :] += mxu(grad_scores, queries, ((0,), (0,)))
-        dv_ref[:keys, :] += mxu(probs.astype(BF), grads, ((0,), (0,)))
-
-
-def attend_back(block_index, qkv, keys_values, grad_heads, logs, cosine, sine, prompt_len):
-    tokens, key_rows = qkv.shape[0], keys_values.shape[0]
-    width = HEADS // KVH
-    head = lambda i, g: (0, i * width + g)
-    whole = lambda i, g: (0, 0)
-    return pl.pallas_call(
-        functools.partial(attend_back_kernel, prompt_len),
-        grid=(KVH, width),
-        in_specs=[
-            pl.BlockSpec(memory_space=pltpu.SMEM),
-            pl.BlockSpec((tokens, HD), head),
-            pl.BlockSpec((key_rows, HD), lambda i, g: (0, i)),
-            pl.BlockSpec((key_rows, HD), lambda i, g: (0, KVH + i)),
-            pl.BlockSpec((tokens, HD), head),
-            pl.BlockSpec((1, tokens, 1), lambda i, g: (i * width + g, 0, 0)),
-            pl.BlockSpec((tokens, HD), whole),
-            pl.BlockSpec((tokens, HD), whole),
-        ],
-        out_specs=[
-            pl.BlockSpec((tokens, HD), head),
-            pl.BlockSpec((key_rows, HD), lambda i, g: (0, i)),
-            pl.BlockSpec((key_rows, HD), lambda i, g: (0, i)),
-        ],
-        out_shape=[
-            jax.ShapeDtypeStruct((tokens, D), BF),
-            jax.ShapeDtypeStruct((key_rows, KVH * HD), F32),
-            jax.ShapeDtypeStruct((key_rows, KVH * HD), F32),
-        ],
-        compiler_params=grant(),
-        name="attend_back",
-    )(block_index, qkv, keys_values, keys_values, grad_heads, logs, cosine, sine)
 
 
 def segment_matrix(parts, transposed):
@@ -587,32 +533,6 @@
     for part in range(parts - 1, 0, -1):
         slot = jnp.where(slot >= part * SLOTS, slot - SLOTS, slot)
     return jnp.where(spread == slot.astype(F32), 1.0, 0.0).astype(BF)
-
-
-def spread_kernel(parts, rank0_ref, rank1_ref, rows_ref, out0_ref, out1_ref):
-    for rank_ref, out_ref in ((rank0_ref, out0_ref), (rank1_ref, out1_ref)):
-        chooser = slot_matrix(rank_ref[0], parts, True)
-        out_ref[...] = mxu(chooser, rows_ref[...]).astype(BF)
-
-
-def spread_rows(rank0, rank1, rows):
-    dests, tokens = rank0.shape
-    steps = 2
-    parts = dests // steps
-    rank0 = rank0.reshape(steps, parts, tokens)
-    rank1 = rank1.reshape(steps, parts, tokens)
-    ranks = pl.BlockSpec((1, parts, tokens), lambda j: (j, 0, 0))
-    block = pl.BlockSpec((parts * SLOTS, D), lambda j: (j, 0))
-    shape = jax.ShapeDtypeStruct((dests * SLOTS, D), BF)
-    return pl.pallas_call(
-        functools.partial(spread_kernel, parts),
-        grid=(steps,),
-        in_specs=[ranks, ranks, pl.BlockSpec((tokens, D), lambda j: (0, 0))],
-        out_specs=[block, block],
-        out_shape=[shape, shape],
-        compiler_params=grant(),
-        name="spread_rows",
-    )(rank0, rank1, rows)
 
 
 def collect_kernel(parts, rank0_ref, rank1_ref, rows0_ref, rows1_ref, out_ref):
@@ -637,46 +557,138 @@
     )(rank0, rank1, rows0, rows1)
 
 
-def expert_kernel(n_dp, half_steps, *refs):
-    (z_ref, xo_ref, xp_ref, go_ref, gp_ref, so_ref, sp_ref) = refs[:7]
-    pieces = refs[7 : 7 + 3 * n_dp]
-    outs = refs[7 + 3 * n_dp :]
-    (yo_ref, yp_ref, bo_ref, bp_ref, do_ref, dp_ref, xc_ref, a_ref, dg_ref, du_ref, de_ref) = outs[:11]
-    weights = outs[11:]
-    wg_ref, wu_ref, wd_ref = weights
+def plane_exchange(slot, source, target, local_sems, send_sems, recv_sems):
+    here = plane_here()
+    plane = source.shape[0]
+
+    def begin():
+        pltpu.make_async_copy(source.at[here], target.at[here], local_sems.at[slot]).start()
+
+        def one(flip, carry):
+            peer = here ^ flip
+            remote(
+                source.at[peer],
+                target.at[here],
+                send_sems.at[slot, peer],
+                recv_sems.at[slot, here],
+                plane_peer(peer),
+            ).start()
+            return carry
+
+        lax.fori_loop(1, plane, one, 0)
+
+    def finish():
+        pltpu.make_async_copy(source.at[here], target.at[here], local_sems.at[slot]).wait()
+
+        def one(flip, carry):
+            peer = here ^ flip
+            done = remote(
+                source.at[peer],
+                target.at[peer],
+                send_sems.at[slot, peer],
+                recv_sems.at[slot, peer],
+                plane_peer(peer),
+            )
+            done.wait_send()
+            done.wait_recv()
+            return carry
+
+        lax.fori_loop(1, plane, one, 0)
+
+    return begin, finish
+
+
+ALL_FLIPS = (2, 3, 1)
+RIDE_DISPATCH = ((0, 3, 0),) + tuple((m, f, 0) for m in (1, 2) for f in ALL_FLIPS)
+RIDE_FIRST = ((0, 3, 1),) + tuple((m, f, 1) for m in (1, 2) for f in ALL_FLIPS)
+HOME_SECOND = tuple((m, f, 0) for m in (0, 1) for f in ALL_FLIPS) + ((2, 2, 0),)
+HOME_RETURN = ((2, 3, 0), (0, 2, 1), (0, 3, 1), (1, 2, 1), (2, 1, 0), (0, 1, 1))
+HOME_BACKWARD = ((1, 3, 1), (2, 2, 1), (2, 3, 1), (1, 1, 1), (2, 1, 1))
+
+
+def pick(array, index):
+    return array if index is None else array.at[index]
+
+
+def picked_shape(array, index):
+    return array.shape if index is None else array.shape[1:]
+
+
+def dp_moves(sources, targets, riders, sends, recvs):
+    z_index = lax.axis_index("dp")
+    return [
+        remote(pick(source, index), target, sends.at[n], recvs.at[n], {"dp": z_index ^ flip})
+        for n, (source, target, (index, flip)) in enumerate(zip(sources, targets, riders))
+    ]
+
+
+def dp_peers(n_dp):
+    return [{"dp": lax.axis_index("dp") ^ flip} for flip in range(1, n_dp)]
+
+
+def expert_kernel(plane, n_dp, half_steps, picks, riders, *refs):
+    (xo_ref, xp_ref, go_ref, gp_ref, so_ref, sp_ref), refs = refs[:6], refs[6:]
+    pieces, refs = refs[: 3 * n_dp], refs[3 * n_dp :]
+    carried, refs = refs[:4], refs[4:]
+    sources, refs = refs[: len(riders)], refs[len(riders) :]
+    (yo_ref, yp_ref, bo_ref, bp_ref, do_ref, dp_ref, gate_ref, up_ref, down_ref), refs = refs[:9], refs[9:]
+    landed, refs = refs[:4], refs[4:]
+    targets, refs = refs[: len(riders)], refs[len(riders) :]
+    (wg_ref, wu_ref, wd_ref, x_all, de_all, a_all, dg_all, du_all, stage), sems = refs[:9], refs[9:]
+    weight_sems, store_sems, local_sems, send_sems, recv_sems, ride_send, ride_recv = sems
+    weights = (wg_ref, wu_ref, wd_ref)
+    z_index = lax.axis_index("dp")
     step = pl.program_id(0)
     own = step < half_steps
+    rows_of_step = xo_ref.shape[0]
+    exchanges = [
+        plane_exchange(n, source, target, local_sems, send_sems, recv_sems)
+        for n, (source, target) in enumerate(zip(carried, landed))
+    ]
+    moves = dp_moves(sources, targets, riders, ride_send, ride_recv)
 
     @pl.when(step == 0)
     def _():
-        for which in range(3):
-            for flip in range(n_dp):
-                piece = pieces[which * n_dp + flip]
-                size = piece.shape[1]
-                start = pl.multiple_of((z_ref[0] ^ flip) * size, 64)
-                weights[which][pl.ds(start, size), :] = piece[0]
+        here = plane_here()
+        greet([plane_peer(here ^ flip) for flip in range(1, plane)] + dp_peers(n_dp))
+        loads = []
+        for n, piece in enumerate(pieces):
+            source = pick(piece, picks[n])
+            size = source.shape[0]
+            start = pl.multiple_of((z_index ^ (n % n_dp)) * size, 64)
+            loads.append(
+                pltpu.make_async_copy(source, weights[n // n_dp].at[pl.ds(start, size)], weight_sems.at[n])
+            )
+            loads[-1].start()
+        for begin, _ in exchanges:
+            begin()
+        for move in moves:
+            move.start()
+        for load in loads:
+            load.wait()
 
     rows = jnp.where(own, xo_ref[...], xp_ref[...])
     cot = jnp.where(own, go_ref[...], gp_ref[...])
     share = jnp.where(own, so_ref[...], sp_ref[...])
-    xc_ref[...] = rows
+    place = pl.ds(pl.multiple_of(step * rows_of_step, 32), rows_of_step)
+    x_all[place, :] = rows
     gate_pre = mxu(rows, wg_ref[...])
     up_pre = mxu(rows, wu_ref[...])
     sigma = 1.0 / (1.0 + jnp.exp(-gate_pre))
     silu = gate_pre * sigma
     act = (silu * up_pre).astype(BF)
-    a_ref[...] = act
+    a_all[place, :] = act
     cot_full = cot.astype(F32)
     weighted = (cot_full * share).astype(BF)
-    de_ref[...] = weighted
+    de_all[place, :] = weighted
     result = mxu(act, wd_ref[...])
     dots = jnp.sum(result.astype(BF).astype(F32) * cot_full, axis=-1, keepdims=True)
     scaled = (result * share).astype(BF)
     grad_act = mxu(weighted, wd_ref[...], ((1,), (1,)))
     grad_gate = (grad_act * up_pre * sigma * (1.0 + gate_pre * (1.0 - sigma))).astype(BF)
     grad_up = (grad_act * silu).astype(BF)
-    dg_ref[...] = grad_gate
-    du_ref[...] = grad_up
+    dg_all[place, :] = grad_gate
+    du_all[place, :] = grad_up
     back = mxu(grad_gate, wg_ref[...], ((1,), (1,))) + mxu(grad_up, wu_ref[...], ((1,), (1,)))
     back = back.astype(BF)
 
@@ -692,88 +704,963 @@
         bp_ref[...] = back
         dp_ref[...] = dots
 
-
-def run_expert(which, z_index, x_own, x_par, g_own, g_par, s_own, s_par, gate_pieces, up_pieces, down_pieces):
-    half_rows = x_own.shape[0]
-    step_rows = half_rows // 2
-    half_steps = 2
-    n_dp = len(gate_pieces)
-    full_hidden = gate_pieces[0].shape[2]
+    @pl.when(step == 2 * half_steps - 1)
+    def _():
+        quarter = D // n_dp
+        hidden = a_all.shape[1]
+
+        def of_rows(q, carry):
+            columns = pl.ds(pl.multiple_of(q * quarter, 128), quarter)
+            stores = []
+            for n, (grads, out_ref) in enumerate(((dg_all, gate_ref), (du_all, up_ref))):
+                stage[n] = mxu(x_all[:, columns], grads[...], ((0,), (0,))).astype(BF)
+                stores.append(pltpu.make_async_copy(stage.at[n], out_ref.at[z_index ^ q], store_sems.at[n]))
+                stores[-1].start()
+            for store in stores:
+                store.wait()
+            return carry
+
+        lax.fori_loop(0, n_dp, of_rows, 0)
+        size = hidden // n_dp
+        for q in range(0, n_dp, 2):
+            made = mxu(a_all[:, q * size : (q + 2) * size], de_all[...], ((0,), (0,))).astype(BF)
+            stores = []
+            for half in range(2):
+                part = made[half * size : (half + 1) * size]
+                stage[half, :size] = part[:, :hidden]
+                stage[half, size:] = part[:, hidden:]
+                stores.append(
+                    pltpu.make_async_copy(
+                        stage.at[half], down_ref.at[z_index ^ (q + half)], store_sems.at[half]
+                    )
+                )
+                stores[-1].start()
+            for store in stores:
+                store.wait()
+        for _, finish in exchanges:
+            finish()
+        for move in moves:
+            move.wait()
+
+
+def run_expert(name, number, rows, cots, gates, pieces, carried, riders):
+    half_rows = rows[0].shape[0]
+    half_steps = 4
+    step_rows = half_rows // half_steps
+    plane = carried[0].shape[0]
+    n_dp = lax.axis_size("dp")
+    hidden = picked_shape(*pieces[0])[1]
     own_map = lambda j: (jnp.minimum(j, half_steps - 1), 0)
     par_map = lambda j: (jnp.maximum(j - half_steps, 0), 0)
-    all_map = lambda j: (j, 0)
-    piece_map = lambda j: (which, 0, 0)
+    anywhere = pl.BlockSpec(memory_space=pl.ANY)
 
     def pair(width):
         return [pl.BlockSpec((step_rows, width), own_map), pl.BlockSpec((step_rows, width), par_map)]
 
-    def piece_specs(pieces):
-        return [
-            pl.BlockSpec((1,) + p.shape[1:], piece_map, pipeline_mode=pl.Buffered(1)) for p in pieces
+    shape = jax.ShapeDtypeStruct
+    share = shape((n_dp, D // n_dp, hidden), BF)
+    dma = pltpu.SemaphoreType.DMA
+    all_rows = 2 * half_rows
+    results = pl.pallas_call(
+        functools.partial(
+            expert_kernel,
+            plane,
+            n_dp,
+            half_steps,
+            [index for _, index in pieces],
+            [(index, flip) for _, index, flip in riders],
+        ),
+        grid=(2 * half_steps,),
+        in_specs=pair(D) + pair(D) + pair(1) + [anywhere] * (len(pieces) + 4 + len(riders)),
+        out_specs=pair(D) + pair(D) + pair(1) + [anywhere] * (7 + len(riders)),
+        out_shape=[shape((half_rows, D), BF)] * 4
+        + [shape((half_rows, 1), F32)] * 2
+        + [share] * 3
+        + [shape(array.shape, BF) for array in carried]
+        + [shape(picked_shape(array, index), BF) for array, index, _ in riders],
+        scratch_shapes=[
+            pltpu.VMEM((D, hidden), BF),
+            pltpu.VMEM((D, hidden), BF),
+            pltpu.VMEM((hidden, D), BF),
+            pltpu.VMEM((all_rows, D), BF),
+            pltpu.VMEM((all_rows, D), BF),
+            pltpu.VMEM((all_rows, hidden), BF),
+            pltpu.VMEM((all_rows, hidden), BF),
+            pltpu.VMEM((all_rows, hidden), BF),
+            pltpu.VMEM((2, D // n_dp, hidden), BF),
+            dma((len(pieces),)),
+            dma((2,)),
+            dma((4,)),
+            dma((4, plane)),
+            dma((4, plane)),
+            dma((len(riders),)),
+            dma((len(riders),)),
+        ],
+        compiler_params=pltpu.CompilerParams(
+            vmem_limit_bytes=56 * 1024 * 1024, collective_id=number, has_side_effects=True
+        ),
+        name=name,
+    )(*rows, *cots, *gates, *[a for a, _ in pieces], *carried, *[a for a, _, _ in riders])
+    return results[:4], results[4:6], results[6:9], results[9:13], results[13:]
+
+
+def plane_peer(index):
+    n_context = lax.axis_size("context")
+    return {"expert": index // n_context, "context": index % n_context}
+
+
+def plane_here():
+    return lax.axis_index("expert") * lax.axis_size("context") + lax.axis_index("context")
+
+
+def greet(peers):
+    barrier = pltpu.get_barrier_semaphore()
+    for peer in peers:
+        pl.semaphore_signal(barrier, inc=1, device_id=peer, device_id_type=MESH_ID)
+    pl.semaphore_wait(barrier, len(peers))
+
+
+def plane_and_partner(plane):
+    here = plane_here()
+    return [plane_peer(here ^ flip) for flip in range(1, plane)] + [{"dp": lax.axis_index("dp") ^ 1}]
+
+
+def remote(source, target, send, receive, peer):
+    return pltpu.make_async_remote_copy(
+        src_ref=source,
+        dst_ref=target,
+        send_sem=send,
+        recv_sem=receive,
+        device_id=peer,
+        device_id_type=MESH_ID,
+    )
+
+
+def gather_kernel(
+    n_dp,
+    in_ref,
+    out_part_ref,
+    routes_ref,
+    whole_ref,
+    out_ref,
+    partner_routes_ref,
+    local_sems,
+    z_send,
+    o_send,
+    o_recv,
+    sends,
+    recvs,
+    route_sems,
+):
+    here = plane_here()
+    z_index = lax.axis_index("dp")
+    z_peer = lambda flip: {"dp": z_index ^ flip}
+    greet([z_peer(flip) for flip in range(1, n_dp)] + [plane_peer(here ^ flip) for flip in (1, 2, 4)])
+    keep = [
+        pltpu.make_async_copy(in_ref, whole_ref.at[z_index, here], local_sems.at[0]),
+        pltpu.make_async_copy(out_part_ref, out_ref.at[z_index], local_sems.at[1]),
+    ]
+    for copy in keep:
+        copy.start()
+    routing = remote(routes_ref, partner_routes_ref, route_sems.at[0], route_sems.at[1], z_peer(1))
+    routing.start()
+    started = []
+    for flip in range(1, n_dp):
+        started.append(
+            remote(in_ref, whole_ref.at[z_index, here], z_send.at[flip], recvs.at[z_index, here], z_peer(flip))
+        )
+        started[-1].start()
+    for flip in range(1, n_dp):
+        started.append(
+            remote(out_part_ref, out_ref.at[z_index], o_send.at[flip], o_recv.at[z_index], z_peer(flip))
+        )
+        started[-1].start()
+
+    def pass_on(lane, flip, z_from, place, source=None):
+        block = whole_ref.at[z_from, place]
+        move = remote(
+            block if source is None else source,
+            block,
+            sends.at[lane, z_from, place],
+            recvs.at[z_from, place],
+            plane_peer(here ^ flip),
+        )
+        move.start()
+        started.append(move)
+
+    def landed(z_from, place):
+        block = whole_ref.at[z_from, place]
+        remote(block, block, z_send.at[0], recvs.at[z_from, place], z_peer(1)).wait_recv()
+
+    froms = [z_index ^ flip for flip in range(n_dp)]
+    for n, z_from in enumerate(froms):
+        if n > 0:
+            landed(z_from, here)
+        source = in_ref if n == 0 else None
+        pass_on(0, 2, z_from, here, source)
+        pass_on(1, 4, z_from, here, source)
+        pass_on(2, 1, z_from, here, source)
+    for n, z_from in enumerate(froms):
+        landed(z_from, here ^ 2)
+        if n % 2 == 1:
+            pass_on(1, 4, z_from, here ^ 2)
+        pass_on(2, 1, z_from, here ^ 2)
+        landed(z_from, here ^ 4)
+        if n % 2 == 0:
+            pass_on(0, 2, z_from, here ^ 4)
+        pass_on(2, 1, z_from, here ^ 4)
+    for z_from in froms:
+        landed(z_from, here ^ 6)
+        pass_on(2, 1, z_from, here ^ 6)
+    for place in (1, 3, 5, 7):
+        for z_from in froms:
+            landed(z_from, here ^ place)
+    for flip in range(1, n_dp):
+        z_from = z_index ^ flip
+        remote(out_part_ref, out_ref.at[z_from], o_send.at[0], o_recv.at[z_from], z_peer(1)).wait_recv()
+    for move in started:
+        move.wait_send()
+    for copy in keep:
+        copy.wait()
+    routing.wait()
+
+
+def gather_parts(part_in, part_out, routes, n_dp, plane):
+    anywhere = pl.BlockSpec(memory_space=pl.ANY)
+    return pl.pallas_call(
+        functools.partial(gather_kernel, n_dp),
+        in_specs=[anywhere] * 3,
+        out_specs=[anywhere] * 3,
+        out_shape=[
+            jax.ShapeDtypeStruct((n_dp, plane) + part_in.shape, BF),
+            jax.ShapeDtypeStruct((n_dp,) + part_out.shape, BF),
+            jax.ShapeDtypeStruct(routes.shape, routes.dtype),
+        ],
+        scratch_shapes=[
+            pltpu.SemaphoreType.DMA((2,)),
+            pltpu.SemaphoreType.DMA((n_dp,)),
+            pltpu.SemaphoreType.DMA((n_dp,)),
+            pltpu.SemaphoreType.DMA((n_dp,)),
+            pltpu.SemaphoreType.DMA((3, n_dp, plane)),
+            pltpu.SemaphoreType.DMA((n_dp, plane)),
+            pltpu.SemaphoreType.DMA((2,)),
+        ],
+        compiler_params=pltpu.CompilerParams(collective_id=3, has_side_effects=True),
+        name="gather_parts",
+    )(part_in, part_out, routes)
+
+
+def dispatch_kernel(plane, n_dp, riders, *refs):
+    (normed_ref, cot_ref, cot_partner_ref, own_rank_ref, partner_rank_ref), refs = refs[:5], refs[5:]
+    sources, refs = refs[: len(riders)], refs[len(riders) :]
+    landed, staged, targets = refs[:4], refs[4:8], refs[8 : 8 + len(riders)]
+    refs = refs[8 + len(riders) :]
+    stage, normed_partner, pair_sems, stage_sems, local_sems, send_sems, recv_sems, ride_send, ride_recv = refs
+    here = plane_here()
+    greet([plane_peer(here ^ flip) for flip in range(1, plane)] + dp_peers(n_dp))
+    pair = remote(
+        normed_ref, normed_partner, pair_sems.at[0], pair_sems.at[1], {"dp": lax.axis_index("dp") ^ 1}
+    )
+    pair.start()
+    moves = dp_moves(sources, targets, riders, ride_send, ride_recv)
+    for move in moves:
+        move.start()
+    plans = (
+        (0, normed_ref, own_rank_ref),
+        (1, cot_ref, own_rank_ref),
+        (2, cot_partner_ref, partner_rank_ref),
+        (3, normed_partner, partner_rank_ref),
+    )
+    exchanges = [
+        plane_exchange(n, stage.at[n], landed[n], local_sems, send_sems, recv_sems) for n in range(4)
+    ]
+    copies = [pltpu.make_async_copy(stage.at[4 + n], staged[n], stage_sems.at[n]) for n in range(4)]
+    for expert in range(2):
+        for n, rows_ref, rank_ref in plans:
+            if expert == 0 and n == 3:
+                pair.wait()
+            chooser = slot_matrix(rank_ref[expert], plane, True)
+            stage[4 * expert + n] = mxu(chooser, rows_ref[...]).astype(BF).reshape(plane, SLOTS, D)
+            if expert == 0:
+                exchanges[n][0]()
+            else:
+                copies[n].start()
+    for copy in copies:
+        copy.wait()
+    for _, finish in exchanges:
+        finish()
+    for move in moves:
+        move.wait()
+
+
+def dispatch_rows(normed, cot, cot_partner, own_ranks, partner_ranks, riders, n_dp):
+    plane, tokens = own_ranks.shape[1:]
+    vmem = pl.BlockSpec(memory_space=pltpu.VMEM)
+    anywhere = pl.BlockSpec(memory_space=pl.ANY)
+    shape = jax.ShapeDtypeStruct
+    dma = pltpu.SemaphoreType.DMA
+    results = pl.pallas_call(
+        functools.partial(dispatch_kernel, plane, n_dp, [(index, flip) for _, index, flip in riders]),
+        in_specs=[vmem] * 5 + [anywhere] * len(riders),
+        out_specs=[anywhere] * (8 + len(riders)),
+        out_shape=[shape((plane, SLOTS, D), BF)] * 8
+        + [shape(picked_shape(array, index), BF) for array, index, _ in riders],
+        scratch_shapes=[
+            pltpu.VMEM((8, plane, SLOTS, D), BF),
+            pltpu.VMEM((tokens, D), BF),
+            dma((2,)),
+            dma((4,)),
+            dma((4,)),
+            dma((4, plane)),
+            dma((4, plane)),
+            dma((len(riders),)),
+            dma((len(riders),)),
+        ],
+        compiler_params=pltpu.CompilerParams(
+            vmem_limit_bytes=VMEM_BYTES, collective_id=1, has_side_effects=True
+        ),
+        cost_estimate=pl.CostEstimate(flops=2 * 10**10, bytes_accessed=4 * 10**8, transcendentals=0),
+        name="dispatch_rows",
+    )(normed, cot, cot_partner, own_ranks, partner_ranks, *[array for array, _, _ in riders])
+    return results[:4], results[4:8], results[8:]
+
+
+def return_kernel(plane, n_dp, riders, own_rank_ref, partner_rank_ref, dots_ref, *refs):
+    early, back, results = refs[0:2], refs[2:4], refs[4:6]
+    sources, refs = refs[6 : 6 + len(riders)], refs[6 + len(riders) :]
+    total_ref, dots_here_ref, dots_other_ref = refs[:3]
+    results_back, targets = refs[3:5], refs[5 : 5 + len(riders)]
+    (
+        held,
+        to_partner,
+        of_partner,
+        load_sems,
+        pair_sems,
+        local_sems,
+        send_sems,
+        recv_sems,
+        ride_send,
+        ride_recv,
+        dot_sems,
+        dot_send,
+        dot_recv,
+    ) = refs[5 + len(riders) :]
+    here = plane_here()
+    partner = {"dp": lax.axis_index("dp") ^ 1}
+    greet([plane_peer(here ^ flip) for flip in range(1, plane)] + dp_peers(n_dp))
+    own_dots = pltpu.make_async_copy(dots_ref.at[here], dots_here_ref.at[here], dot_sems.at[0])
+    own_dots.start()
+    dot_moves = [
+        remote(
+            dots_ref.at[here ^ flip],
+            dots_here_ref.at[here],
+            dot_send.at[flip],
+            dot_recv.at[flip],
+            plane_peer(here ^ flip),
+        )
+        for flip in range(1, plane)
+    ]
+    for move in dot_moves:
+        move.start()
+    loads, exchanges = {}, {}
+    for side in (1, 0):
+        loads[side] = pltpu.make_async_copy(early[side], held.at[2 * side], load_sems.at[side])
+        loads[side].start()
+        exchanges[side] = plane_exchange(
+            side, back[side], held.at[2 * side + 1], local_sems, send_sems, recv_sems
+        )
+        exchanges[side][0]()
+    later = [
+        plane_exchange(2 + side, results[side], results_back[side], local_sems, send_sems, recv_sems)
+        for side in range(2)
+    ]
+    for begin, _ in later:
+        begin()
+    moves = dp_moves(sources, targets, riders, ride_send, ride_recv)
+    own_dots.wait()
+    for move in dot_moves:
+        move.wait()
+    dots_pair = remote(dots_here_ref, dots_other_ref, dot_sems.at[1], dot_sems.at[2], partner)
+    dots_pair.start()
+
+    def collect(rank_ref, side, target, kind):
+        loads[side].wait()
+        exchanges[side][1]()
+
+        def block(n, carry):
+            rows = pl.ds(pl.multiple_of(n * PBLK, PBLK), PBLK)
+            made = jnp.zeros((PBLK, D), F32)
+            for expert in range(2):
+                chooser = slot_matrix(rank_ref[expert, rows, :], plane, False)
+                made = made + mxu(chooser, held[2 * side + expert].reshape(plane * SLOTS, D))
+            target[rows, :] = made.astype(kind)
+            return carry
+
+        lax.fori_loop(0, total_ref.shape[0] // PBLK, block, 0)
+
+    for move in moves[: len(moves) // 2]:
+        move.start()
+    collect(partner_rank_ref, 1, to_partner, BF)
+    pair = remote(to_partner, of_partner, pair_sems.at[0], pair_sems.at[1], partner)
+    pair.start()
+    for move in moves[len(moves) // 2 :]:
+        move.start()
+    collect(own_rank_ref, 0, total_ref, F32)
+    pair.wait()
+    total_ref[...] += of_partner[...].astype(F32)
+    dots_pair.wait()
+    for _, finish in later:
+        finish()
+    for move in moves:
+        move.wait()
+
+
+def return_rows(own_ranks, partner_ranks, dots, early, back, results, riders, n_dp):
+    tokens, plane = own_ranks.shape[1:]
+    vmem = pl.BlockSpec(memory_space=pltpu.VMEM)
+    anywhere = pl.BlockSpec(memory_space=pl.ANY)
+    shape = jax.ShapeDtypeStruct
+    dma = pltpu.SemaphoreType.DMA
+    outcome = pl.pallas_call(
+        functools.partial(return_kernel, plane, n_dp, [(index, flip) for _, index, flip in riders]),
+        in_specs=[vmem, vmem, vmem] + [anywhere] * (6 + len(riders)),
+        out_specs=[vmem, vmem, vmem] + [anywhere] * (2 + len(riders)),
+        out_shape=[shape((tokens, D), F32)]
+        + [shape(dots.shape, F32)] * 2
+        + [shape(rows.shape, BF) for rows in results]
+        + [shape(picked_shape(array, index), BF) for array, index, _ in riders],
+        scratch_shapes=[
+            pltpu.VMEM((4, plane, SLOTS, D), BF),
+            pltpu.VMEM((tokens, D), BF),
+            pltpu.VMEM((tokens, D), BF),
+            dma((2,)),
+            dma((2,)),
+            dma((4,)),
+            dma((4, plane)),
+            dma((4, plane)),
+            dma((len(riders),)),
+            dma((len(riders),)),
+            dma((3,)),
+            dma((plane,)),
+            dma((plane,)),
+        ],
+        compiler_params=pltpu.CompilerParams(
+            vmem_limit_bytes=VMEM_BYTES, collective_id=2, has_side_effects=True
+        ),
+        cost_estimate=pl.CostEstimate(flops=3 * 10**10, bytes_accessed=4 * 10**8, transcendentals=0),
+        name="return_rows",
+    )(own_ranks, partner_ranks, dots, *early, *back, *results, *[array for array, _, _ in riders])
+    return outcome[0], outcome[1], outcome[2], outcome[3:5], outcome[5:]
+
+
+def normed_back(rows, gain, grads):
+    scale = lax.rsqrt(jnp.mean(rows * rows, axis=-1, keepdims=True) + epsilon)
+    weighted = grads * gain
+    mean = jnp.mean(rows * weighted, axis=-1, keepdims=True)
+    return scale * weighted - rows * (scale * scale * scale * mean), rows * scale * grads
+
+
+def context_peer(flip):
+    return {"context": lax.axis_index("context") ^ flip}
+
+
+def share_context(part_ref, all_ref, sems, sends, recvs):
+    here = lax.axis_index("context")
+    own = pltpu.make_async_copy(part_ref, all_ref.at[here], sems)
+    own.start()
+    across = remote(part_ref, all_ref.at[here], sends.at[0], recvs.at[here], context_peer(2))
+    across.start()
+    beside = remote(part_ref, all_ref.at[here], sends.at[1], recvs.at[here], context_peer(1))
+    beside.start()
+
+    def pass_on():
+        block = all_ref.at[here ^ 2]
+        remote(part_ref, block, sends.at[0], recvs.at[here ^ 2], context_peer(2)).wait_recv()
+        remote(block, block, sends.at[2], recvs.at[here ^ 2], context_peer(1)).start()
+
+    def finish():
+        block = all_ref.at[here ^ 2]
+        for flip in (1, 3):
+            remote(part_ref, all_ref.at[here ^ flip], sends.at[1], recvs.at[here ^ flip], context_peer(1)).wait_recv()
+        across.wait_send()
+        beside.wait_send()
+        remote(block, block, sends.at[2], recvs.at[here ^ 2], context_peer(1)).wait_send()
+        own.wait()
+
+    return pass_on, finish
+
+
+def backward_kernel(n_dp, prompt_len, riders, *refs):
+    (
+        dlog_ref,
+        router_ref,
+        cot_ref,
+        x_ref,
+        gain_one_ref,
+        gain_two_ref,
+        attended_ref,
+        qkv_ref,
+        kv_ref,
+        log_ref,
+        normed_ref,
+        cos_ref,
+        sin_ref,
+        mid_ref,
+        total_ref,
+        w_out_ref,
+        w_in_ref,
+        four_ref,
+    ) = refs[:18]
+    late = len(riders)
+    sources, refs = refs[18 : 18 + late], refs[18 + late :]
+    grad_x_ref, gains_ref, grad_out_ref, grad_in_ref, all_ref = refs[:5]
+    homes, refs = refs[5 : 5 + late], refs[5 + late :]
+    (
+        weights,
+        grad_mid,
+        grad_attn,
+        mid_block,
+        grad_qkv,
+        grad_kv,
+        kv_send,
+        kv_recv,
+        stage,
+        load_sems,
+        store_sems,
+        kv_send_sems,
+        kv_recv_sems,
+        home_send,
+        home_recv,
+        own_sem,
+        share_sends,
+        share_recvs,
+    ) = refs
+    block_index = lax.axis_index("context")
+    n_context = kv_send.shape[0]
+    tokens = x_ref.shape[0]
+    heads_width = HEADS * HD
+    kv_width = KVH * HD
+    greet([context_peer(flip) for flip in range(1, n_context)] + dp_peers(n_dp))
+    load_total = pltpu.make_async_copy(total_ref, grad_mid, load_sems.at[0])
+    load_out = pltpu.make_async_copy(w_out_ref, weights.at[:, pl.ds(0, D)], load_sems.at[1])
+    load_in = pltpu.make_async_copy(w_in_ref.at[:, pl.ds(0, weights.shape[1])], weights, load_sems.at[2])
+    load_total.start()
+    load_out.start()
+    homing = dp_moves(sources, homes, riders, home_send, home_recv)
+    for move in homing:
+        move.start()
+    pass_on, finish = share_context(four_ref, all_ref, own_sem.at[0], share_sends, share_recvs)
+    load_total.wait()
+    load_out.wait()
+    gains_ref[...] = jnp.zeros_like(gains_ref)
+
+    def block_rows(n):
+        return pl.ds(pl.multiple_of(n * PBLK, PBLK), PBLK)
+
+    def through_norm(n, carry):
+        rows = block_rows(n)
+        load_mid = pltpu.make_async_copy(mid_ref.at[rows], mid_block, load_sems.at[3])
+        load_mid.start()
+        load_mid.wait()
+        grads = grad_mid[rows, :] + mxu(dlog_ref[rows, :], router_ref[...], ((1,), (1,)))
+        by_rows, by_gain = normed_back(mid_block[...], gain_two_ref[...], grads)
+        gains_ref[1:2, :] += jnp.sum(by_gain, axis=0, keepdims=True)
+        by_mid = cot_ref[rows, :].astype(F32) + by_rows
+        grad_mid[rows, :] = by_mid
+        low = by_mid.astype(BF)
+        grad_attn[rows, :] = low
+        grad_qkv[rows, :D] = mxu(low, weights[:, :D], ((1,), (1,))).astype(BF)
+        return carry
+
+    lax.fori_loop(0, tokens // PBLK, through_norm, 0)
+    load_in.start()
+    grad_kv[...] = jnp.zeros_like(grad_kv)
+
+    def through_head(head, carry):
+        columns = pl.ds(pl.multiple_of(head * HD, HD), HD)
+        group = head // (HEADS // KVH)
+        key_columns = pl.ds(pl.multiple_of(group * HD, HD), HD)
+        value_columns = pl.ds(pl.multiple_of(kv_width + group * HD, HD), HD)
+        for first_row, keys in row_blocks(prompt_len):
+            rows = slice(first_row, first_row + PBLK)
+            queries, grads = qkv_ref[rows, columns], grad_qkv[rows, columns]
+            scores = mxu(queries, kv_ref[:keys, key_columns], ((1,), (1,)))
+            scores = masked_scores(scores, first_row, prompt_len, block_index)
+            lane = lax.broadcasted_iota(jnp.int32, (PBLK, log_ref.shape[1]), 1)
+            logs = jnp.sum(jnp.where(lane == head, log_ref[rows, :], 0.0), axis=-1, keepdims=True)
+            probs = jnp.exp(scores - logs)
+            grad_probs = mxu(grads, kv_ref[:keys, value_columns], ((1,), (1,)))
+            dots = jnp.sum(probs * grad_probs, axis=-1, keepdims=True)
+            grad_scores = (probs * (grad_probs - dots)).astype(BF)
+            grad_query = mxu(grad_scores, kv_ref[:keys, key_columns])
+            grad_query = turn(grad_query, cos_ref[rows, :], -sin_ref[rows, :]) * (1.0 / math.sqrt(HD))
+            grad_qkv[rows, columns] = grad_query.astype(BF)
+            grad_kv[:keys, key_columns] += mxu(grad_scores, queries, ((0,), (0,)))
+            grad_kv[:keys, value_columns] += mxu(probs.astype(BF), grads, ((0,), (0,)))
+        return carry
+
+    lax.fori_loop(0, HEADS, through_head, 0)
+
+    for place in range(n_context):
+        kv_send[place] = grad_kv[place * PBLK : (place + 1) * PBLK, :].astype(BF)
+    kv_moves = [
+        remote(
+            kv_send.at[block_index ^ flip],
+            kv_recv.at[flip],
+            kv_send_sems.at[flip],
+            kv_recv_sems.at[flip],
+            context_peer(flip),
+        )
+        for flip in range(1, n_context)
+    ]
+    for move in kv_moves:
+        move.start()
+    pass_on()
+
+    quarter = D // n_dp
+
+    def quarter_rows(q):
+        return pl.ds(pl.multiple_of(q * quarter, 128), quarter)
+
+    def share_of_out(q, carry):
+        made = mxu(attended_ref[:, quarter_rows(q)], grad_attn[...], ((0,), (0,)))
+        stage[:, :D] = made.astype(BF)
+        store = pltpu.make_async_copy(
+            stage.at[:, pl.ds(0, D)], grad_out_ref.at[quarter_rows(q)], store_sems.at[0]
+        )
+        store.start()
+        store.wait()
+        return carry
+
+    lax.fori_loop(0, n_dp, share_of_out, 0)
+
+    for move in kv_moves:
+        move.wait()
+    own_rows = pl.ds(pl.multiple_of(block_index * PBLK, PBLK), PBLK)
+    summed = grad_kv[own_rows, :]
+    for flip in range(1, n_context):
+        summed = summed + kv_recv[flip].astype(F32)
+    pieces = [(0, PBLK, summed), (PBLK, tokens, grad_kv[prompt_len:, :])]
+    for first, last, made in pieces:
+        for group in range(KVH):
+            turned = turn(
+                made[:, group * HD : (group + 1) * HD], cos_ref[first:last, :], -sin_ref[first:last, :]
+            )
+            start = heads_width + group * HD
+            grad_qkv[first:last, start : start + HD] = turned.astype(BF)
+        grad_qkv[first:last, heads_width + kv_width :] = made[:, kv_width:].astype(BF)
+
+    load_in.wait()
+
+    def share_of_in(q, carry):
+        stage[...] = mxu(normed_ref[:, quarter_rows(q)], grad_qkv[...], ((0,), (0,))).astype(BF)
+        store = pltpu.make_async_copy(stage, grad_in_ref.at[quarter_rows(q)], store_sems.at[0])
+        store.start()
+        store.wait()
+        return carry
+
+    lax.fori_loop(0, n_dp, share_of_in, 0)
+
+    def through_first(n, carry):
+        rows = block_rows(n)
+        grads = mxu(grad_qkv[rows, :], weights[...], ((1,), (1,)))
+        by_rows, by_gain = normed_back(x_ref[rows, :].astype(F32), gain_one_ref[...], grads)
+        gains_ref[0:1, :] += jnp.sum(by_gain, axis=0, keepdims=True)
+        grad_x_ref[rows, :] = (grad_mid[rows, :] + by_rows).astype(BF)
+        return carry
+
+    lax.fori_loop(0, tokens // PBLK, through_first, 0)
+    finish()
+    for move in homing:
+        move.wait()
+
+
+def backward(prompt_len, n_dp, in_vmem, in_hbm, riders):
+    tokens = in_vmem[0].shape[0]
+    width = D + 2 * KVH * HD
+    n_context = prompt_len // PBLK
+    key_rows = prompt_len + CONT
+    quarter = D // n_dp
+    vmem = pl.BlockSpec(memory_space=pltpu.VMEM)
+    anywhere = pl.BlockSpec(memory_space=pl.ANY)
+    four = in_hbm[-1]
+    shape = jax.ShapeDtypeStruct
+    return pl.pallas_call(
+        functools.partial(backward_kernel, n_dp, prompt_len, [(index, flip) for _, index, flip in riders]),
+        in_specs=[vmem] * len(in_vmem) + [anywhere] * (len(in_hbm) + len(riders)),
+        out_specs=[vmem] * 2 + [anywhere] * (3 + len(riders)),
+        out_shape=[
+            shape((tokens, D), BF),
+            shape((8, D), F32),
+            shape((D, D), BF),
+            shape((D, width), BF),
+            shape((n_context,) + four.shape, BF),
         ]
-
-    wide = pl.BlockSpec((step_rows, D), all_map)
-    narrow = pl.BlockSpec((step_rows, full_hidden), all_map)
-    half_shape = jax.ShapeDtypeStruct((half_rows, D), BF)
-    dot_shape = jax.ShapeDtypeStruct((half_rows, 1), F32)
-    wide_shape = jax.ShapeDtypeStruct((2 * half_rows, D), BF)
-    narrow_shape = jax.ShapeDtypeStruct((2 * half_rows, full_hidden), BF)
+        + [shape(picked_shape(array, index), BF) for array, index, _ in riders],
+        scratch_shapes=[
+            pltpu.VMEM((D, width), BF),
+            pltpu.VMEM((tokens, D), F32),
+            pltpu.VMEM((tokens, D), BF),
+            pltpu.VMEM((PBLK, D), F32),
+            pltpu.VMEM((tokens, width), BF),
+            pltpu.VMEM((key_rows, 2 * KVH * HD), F32),
+            pltpu.VMEM((n_context, PBLK, 2 * KVH * HD), BF),
+            pltpu.VMEM((n_context, PBLK, 2 * KVH * HD), BF),
+            pltpu.VMEM((quarter, width), BF),
+            pltpu.SemaphoreType.DMA((4,)),
+            pltpu.SemaphoreType.DMA((1,)),
+            pltpu.SemaphoreType.DMA((n_context,)),
+            pltpu.SemaphoreType.DMA((n_context,)),
+            pltpu.SemaphoreType.DMA((len(riders),)),
+            pltpu.SemaphoreType.DMA((len(riders),)),
+            pltpu.SemaphoreType.DMA((1,)),
+            pltpu.SemaphoreType.DMA((3,)),
+            pltpu.SemaphoreType.DMA((n_context,)),
+        ],
+        compiler_params=pltpu.CompilerParams(
+            vmem_limit_bytes=56 * 1024 * 1024, collective_id=4, has_side_effects=True
+        ),
+        name="backward",
+    )(*in_vmem, *in_hbm, *[array for array, _, _ in riders])
+
+
+def reduce_kernel(n_dp, widths, *refs):
+    count = len(widths)
+    shares, refs = refs[:count], refs[count:]
+    part_ref, for_partner_ref = refs[:2]
+    refs = refs[2:]
+    totals, refs = refs[:count], refs[count:]
+    all_ref, of_partner_ref = refs[:2]
+    refs = refs[2:]
+    sums, core_in, first_in, second_in, z_in = (refs[n * count : (n + 1) * count] for n in range(5))
+    (
+        load_sems,
+        core_send,
+        core_recv,
+        first_send,
+        first_recv,
+        second_send,
+        second_recv,
+        z_send,
+        z_recv,
+        out_send,
+        out_recv,
+        own_sems,
+        share_sends,
+        share_recvs,
+        pair_sems,
+    ) = refs[5 * count :]
+    here = plane_here()
+    z_index = lax.axis_index("dp")
+    greet(
+        [plane_peer(here ^ flip) for flip in (1, 2, 4)] + [{"dp": z_index ^ flip} for flip in range(1, n_dp)]
+    )
+    chips = (0, 2, 4, 6)
+    order = [1, 2, 3, 0] if n_dp == 4 else list(range(1, n_dp)) + [0]
+    loads, core_moves = {}, {}
+    for n in order:
+        z_to = z_index ^ n
+        for a in range(count):
+            for m, chip in enumerate(chips):
+                loads[n, a, m] = pltpu.make_async_copy(
+                    shares[a].at[z_to, here ^ chip], sums[a].at[n, m], load_sems.at[a, n, m]
+                )
+                loads[n, a, m].start()
+                core_moves[n, a, m] = remote(
+                    shares[a].at[z_to, here ^ 1 ^ chip],
+                    core_in[a].at[n, m],
+                    core_send.at[a, n, m],
+                    core_recv.at[a, n, m],
+                    plane_peer(here ^ 1),
+                )
+                core_moves[n, a, m].start()
+    pair = remote(for_partner_ref, of_partner_ref, pair_sems.at[0], pair_sems.at[1], {"dp": z_index ^ 1})
+    pair.start()
+    all_on, all_done = share_context(part_ref, all_ref, own_sems.at[0], share_sends, share_recvs)
+
+    def add(target, *others):
+        total = target[...].astype(F32)
+        for other in others:
+            total = total + other[...].astype(F32)
+        target[...] = total.astype(BF)
+
+    first_moves, second_moves, z_moves = {}, {}, {}
+    for n in order:
+        toward = 2 if n % 2 == 0 else 4
+        kept = 6 - toward
+        for a in range(count):
+            for m in range(4):
+                loads[n, a, m].wait()
+                core_moves[n, a, m].wait_recv()
+                add(sums[a].at[n, m], core_in[a].at[n, m])
+            for slot, chip in enumerate((toward, 6)):
+                first_moves[n, a, slot] = remote(
+                    sums[a].at[n, chip // 2],
+                    first_in[a].at[n, slot],
+                    first_send.at[a, n, slot],
+                    first_recv.at[a, n, slot],
+                    plane_peer(here ^ toward),
+                )
+                first_moves[n, a, slot].start()
+    for n in order:
+        toward = 2 if n % 2 == 0 else 4
+        kept = 6 - toward
+        for a in range(count):
+            for slot, chip in enumerate((0, kept)):
+                first_moves[n, a, slot].wait_recv()
+                add(sums[a].at[n, chip // 2], first_in[a].at[n, slot])
+            second_moves[n, a] = remote(
+                sums[a].at[n, kept // 2],
+                second_in[a].at[n],
+                second_send.at[a, n],
+                second_recv.at[a, n],
+                plane_peer(here ^ kept),
+            )
+            second_moves[n, a].start()
+    all_on()
+    for n in order:
+        for a in range(count):
+            second_moves[n, a].wait_recv()
+            add(sums[a].at[n, 0], second_in[a].at[n])
+            if n > 0:
+                z_moves[n, a] = remote(
+                    sums[a].at[n, 0], z_in[a].at[n], z_send.at[a, n], z_recv.at[a, n], {"dp": z_index ^ n}
+                )
+                z_moves[n, a].start()
+    started = list(core_moves.values()) + list(first_moves.values())
+    started += list(second_moves.values()) + list(z_moves.values())
+
+    def pass_on(a, lane, flip, place):
+        block = totals[a].at[place]
+        move = remote(
+            block, block, out_send.at[a, lane, place], out_recv.at[a, place], plane_peer(here ^ flip)
+        )
+        move.start()
+        started.append(move)
+
+    def landed(a, place):
+        block = totals[a].at[place]
+        remote(block, block, out_send.at[a, 0, place], out_recv.at[a, place], plane_peer(here ^ 1)).wait_recv()
+
+    for a in range(count):
+        for n in range(1, n_dp):
+            z_moves[n, a].wait_recv()
+        add(sums[a].at[0, 0], *[z_in[a].at[n] for n in range(1, n_dp)])
+        totals[a][here] = sums[a][0, 0]
+        for lane, flip in enumerate((2, 4, 1)):
+            pass_on(a, lane, flip, here)
+    for a in range(count):
+        landed(a, here ^ 2)
+        if a % 2 == 1:
+            pass_on(a, 1, 4, here ^ 2)
+        pass_on(a, 2, 1, here ^ 2)
+        landed(a, here ^ 4)
+        if a % 2 == 0:
+            pass_on(a, 0, 2, here ^ 4)
+        pass_on(a, 2, 1, here ^ 4)
+    for a in range(count):
+        landed(a, here ^ 6)
+        pass_on(a, 2, 1, here ^ 6)
+    for a in range(count):
+        for flip in (1, 3, 5, 7):
+            landed(a, here ^ flip)
+    for move in started:
+        move.wait_send()
+    all_done()
+    pair.wait()
+
+
+def reduce_shares(shares, part, for_partner, n_dp, n_context):
+    plane, rows = shares[0].shape[1:3]
+    widths = tuple(share.shape[3] for share in shares)
+    count = len(widths)
+    vmem = pl.BlockSpec(memory_space=pltpu.VMEM)
+    anywhere = pl.BlockSpec(memory_space=pl.ANY)
+    shape = jax.ShapeDtypeStruct
+    dma = pltpu.SemaphoreType.DMA
+
+    def buffers(*lead):
+        return [pltpu.VMEM(lead + (rows, width), BF) for width in widths]
+
     return pl.pallas_call(
-        functools.partial(expert_kernel, n_dp, half_steps),
-        grid=(2 * half_steps,),
-        in_specs=[pl.BlockSpec(memory_space=pltpu.SMEM)]
-        + pair(D)
-        + pair(D)
-        + pair(1)
-        + piece_specs(gate_pieces)
-        + piece_specs(up_pieces)
-        + piece_specs(down_pieces),
-        out_specs=pair(D) + pair(D) + pair(1) + [wide, narrow, narrow, narrow, wide],
-        out_shape=[half_shape] * 4
-        + [dot_shape] * 2
-        + [wide_shape, narrow_shape, narrow_shape, narrow_shape, wide_shape],
-        scratch_shapes=[
-            pltpu.VMEM((D, full_hidden), BF),
-            pltpu.VMEM((D, full_hidden), BF),
-            pltpu.VMEM((full_hidden, D), BF),
+        functools.partial(reduce_kernel, n_dp, widths),
+        in_specs=[anywhere] * (count + 2),
+        out_specs=[vmem] * count + [anywhere] * 2,
+        out_shape=[shape((plane, rows, width), BF) for width in widths]
+        + [
+            shape((n_context,) + part.shape, BF),
+            shape(for_partner.shape, BF),
         ],
-        compiler_params=grant(62 * 1024 * 1024),
-        name="experts",
-    )(z_index, x_own, x_par, g_own, g_par, s_own, s_par, *gate_pieces, *up_pieces, *down_pieces)
+        scratch_shapes=buffers(n_dp, 4)
+        + buffers(n_dp, 4)
+        + buffers(n_dp, 2)
+        + buffers(n_dp)
+        + buffers(n_dp)
+        + [
+            dma((count, n_dp, 4)),
+            dma((count, n_dp, 4)),
+            dma((count, n_dp, 4)),
+            dma((count, n_dp, 2)),
+            dma((count, n_dp, 2)),
+            dma((count, n_dp)),
+            dma((count, n_dp)),
+            dma((count, n_dp)),
+            dma((count, n_dp)),
+            dma((count, 3, plane)),
+            dma((count, plane)),
+            dma((1,)),
+            dma((3,)),
+            dma((n_context,)),
+            dma((2,)),
+        ],
+        compiler_params=pltpu.CompilerParams(
+            vmem_limit_bytes=VMEM_BYTES, collective_id=5, has_side_effects=True
+        ),
+        name="reduce_shares",
+    )(*shares, part, for_partner)
+
+
+def finish_kernel(down, first_ref, second_ref, out_ref):
+    experts = out_ref.shape[1]
+    both = [ref[:, :, 0].astype(F32) for ref in (first_ref, second_ref)]
+    both = jnp.stack(both, axis=2).reshape((experts,) + both[0].shape[2:])
+    if not down:
+        out_ref[...] = jnp.swapaxes(both, 0, 1)
+        return
+    half = out_ref.shape[2] // 2
+    for side in range(2):
+        out_ref[:, :, side * half : (side + 1) * half] = jnp.swapaxes(both[:, side], 0, 1)
+
+
+def finish_weight(which, first, second):
+    n_context, pair, _, rows, width = first.shape
+    experts = n_context * pair * 2
+    step = 32
+    down = which == 2
+    if down:
+        rows = rows // 2
+        first, second = (part.reshape(part.shape[:3] + (2, rows, width)) for part in (first, second))
+        spec = pl.BlockSpec((n_context, pair, 1, 2, step, width), lambda j: (0, 0, which, 0, j, 0))
+        width = 2 * width
+    else:
+        spec = pl.BlockSpec((n_context, pair, 1, step, width), lambda j: (0, 0, which, j, 0))
+    return pl.pallas_call(
+        functools.partial(finish_kernel, down),
+        grid=(rows // step,),
+        in_specs=[spec, spec],
+        out_specs=pl.BlockSpec((step, experts, width), lambda j: (j, 0, 0)),
+        out_shape=jax.ShapeDtypeStruct((rows, experts, width), F32),
+        compiler_params=grant(),
+        name="finish_weight",
+    )(first, second)
+
+
+def tie(*values):
+    return lax.optimization_barrier(values)
 
 
 def flip_permute(value, axis, size, flip):
     return lax.ppermute(value, axis, [(i, i ^ flip) for i in range(size)])
-
-
-def plane_exchange(rows):
-    plane = lax.axis_size("expert") * lax.axis_size("context")
-    parted = rows.reshape(plane, rows.shape[0] // plane, *rows.shape[1:])
-    moved = lax.all_to_all(parted, PLANE, split_axis=0, concat_axis=0, tiled=True)
-    return moved.reshape(rows.shape)
-
-
-def gather_dense(shard):
-    n_context, n_expert = lax.axis_size("context"), lax.axis_size("expert")
-    plane = n_context * n_expert
-    here = lax.axis_index("expert") * n_context + lax.axis_index("context")
-    rows = shard.shape[0] // plane
-    part = lax.dynamic_slice_in_dim(shard, here * rows, rows, 0)
-    part = lax.all_gather(part, "dp", axis=0, tiled=False)
-    whole = lax.all_gather(part, PLANE, axis=1, tiled=False)
-    return whole.reshape(-1, shard.shape[1])
-
-
-def scatter_dense(share):
-    n_context, n_expert, n_dp = lax.axis_size("context"), lax.axis_size("expert"), lax.axis_size("dp")
-    plane = n_context * n_expert
-    width = share.shape[1]
-    rows = share.shape[0] // (plane * n_dp)
-    parts = share.astype(BF).reshape(n_dp, plane, rows, width)
-    parts = lax.psum_scatter(parts, PLANE, scatter_dimension=1, tiled=True)
-    parts = lax.psum_scatter(parts.reshape(n_dp, rows, width), "dp", scatter_dimension=0, tiled=True)
-    whole = lax.all_gather(parts.reshape(rows, width), PLANE, axis=0, tiled=True)
-    return whole.astype(F32)
 
 
 def local_paired(
@@ -807,10 +1694,15 @@
     ).astype(BF)
     small = jnp.pad(small, ((0, 0), (0, 128 - small.shape[1])))
     shard_in = jnp.concatenate([attn_q.astype(BF), attn_k.astype(BF), attn_v.astype(BF), small], axis=1)
-    whole_in = gather_dense(shard_in)
-    w_out = gather_dense(attn_o.astype(BF))
+    here = lax.axis_index("expert") * n_context + block_index
+    part_rows = attn_q.shape[0] // plane
+    part_of = lambda shard: lax.dynamic_slice_in_dim(shard, here * part_rows, part_rows, 0)
+    whole_in, out_parts, partner_routes = gather_parts(
+        part_of(shard_in), part_of(attn_o).astype(BF), route_rows, n_dp, plane
+    )
+    whole_in = whole_in.reshape(-1, shard_in.shape[1])
+    w_out = lax.all_gather(out_parts, PLANE, axis=1, tiled=False).reshape(-1, D)
     qkv_width = D + 2 * KVH * HD
-    w_qkv = whole_in[:, :qkv_width]
     w_router = whole_in[:, qkv_width : qkv_width + EXPERTS]
     gain_one = whole_in[:, qkv_width + EXPERTS].astype(F32)
     gain_two = whole_in[:, qkv_width + EXPERTS + 1].astype(F32)
@@ -823,17 +1715,18 @@
         mine = mine.reshape(2, per_device // 2, mine.shape[1], mine.shape[2])
         same = lax.dynamic_index_in_dim(mine, parity, 0, keepdims=False)
         other = lax.dynamic_index_in_dim(mine, 1 - parity, 0, keepdims=False)
-        return [same] + [
-            flip_permute(other if flip % 2 else same, "dp", n_dp, flip) for flip in range(1, n_dp)
-        ]
-
-    gate_pieces, up_pieces, down_pieces = (
-        weight_pieces(expert_gate),
-        weight_pieces(expert_up),
-        weight_pieces(expert_down),
-    )
-
-    partner_routes = flip_permute(route_rows, "dp", n_dp, 1)
+        return same, other
+
+    weight_halves = [weight_pieces(weight) for weight in (expert_gate, expert_up, expert_down)]
+    pieces = {(which, 0, i): (weight_halves[which][0], i) for which in range(3) for i in range(2)}
+    moved_early = {flip: flip_permute(weight_halves[0][flip % 2], "dp", n_dp, flip) for flip in (2, 1)}
+
+    def riding(names):
+        return [(weight_halves[which][flip % 2], i, flip) for which, flip, i in names]
+
+    def pieces_of(expert):
+        return [pieces[which, flip, expert] for which in range(3) for flip in range(n_dp)]
+
 
     def ranks_of(rows):
         named = jnp.sum(
@@ -856,13 +1749,9 @@
     own_pair = [own_sel[:, :, i].astype(BF) for i in range(2)]
     partner_pair = [partner_sel[:, :, i].astype(BF) for i in range(2)]
 
-    def dispatch(rows, ranks):
-        slots = spread_rows(ranks[0].T, ranks[1].T, rows)
-        return [plane_exchange(s) for s in slots]
-
+    own_ranks_t = jnp.stack(own_pair, axis=0).transpose(0, 2, 1)
+    partner_ranks_t = jnp.stack(partner_pair, axis=0).transpose(0, 2, 1)
     partner_cot = flip_permute(cot_low, "dp", n_dp, 1)
-    cot_own = dispatch(cot_low, own_pair)
-    cot_partner = dispatch(partner_cot, partner_pair)
 
     positions = jnp.concatenate(
         [
@@ -876,7 +1765,7 @@
     sine = jnp.concatenate([-sin_half, sin_half], axis=1)
     block_word = block_index.astype(jnp.int32).reshape(1)
     z_word = z_index.astype(jnp.int32).reshape(1)
-    qkv, normed_one = project(x_low, gain_one[None, :], w_qkv, cosine, sine)
+    qkv, normed_one = project(x_low, gain_one[None, :], whole_in, qkv_width, cosine, sine)
     keys_own = qkv[:, D:]
     prompt_kv = lax.all_gather(keys_own[:PBLK], "context", axis=0, tiled=True)
     keys_values = jnp.concatenate([prompt_kv, keys_own[PBLK:]], axis=0)
@@ -885,9 +1774,16 @@
     mid_rows = x_rows + mxu(attended, w_out)
     normed_two = rms_scale(mid_rows, gain_two).astype(BF)
 
-    partner_normed = flip_permute(normed_two, "dp", n_dp, 1)
-    rows_own = dispatch(normed_two, own_pair)
-    rows_partner = dispatch(partner_normed, partner_pair)
+    normed_two, partner_cot, moved_early[1], moved_early[2] = tie(
+        normed_two, partner_cot, moved_early[1], moved_early[2]
+    )
+    for flip, moved in moved_early.items():
+        for i in range(2):
+            pieces[0, flip, i] = (moved, i)
+    landed, staged, arrived = dispatch_rows(
+        normed_two, cot_low, partner_cot, own_ranks_t, partner_ranks_t, riding(RIDE_DISPATCH), n_dp
+    )
+    pieces.update({name: (piece, None) for name, piece in zip(RIDE_DISPATCH, arrived)})
     logits = mxu(normed_two, w_router)
     top_logit = jnp.max(jnp.where(named, logits, masked_score), axis=1, keepdims=True)
     raised = jnp.where(named, jnp.exp(jnp.where(named, logits - top_logit, 0.0)), 0.0)
@@ -903,126 +1799,132 @@
     both_gates = jnp.stack([own_gates, partner_gates], axis=1)
     both_gates = lax.all_to_all(both_gates, PLANE, split_axis=0, concat_axis=0, tiled=True)
 
-    shares = []
-    returned = []
-    for i in range(2):
-        column = lambda side: both_gates[:, side, i].reshape(plane * SLOTS, 1)
-        returned.append(
-            run_expert(
-                i,
-                z_word,
-                rows_own[i],
-                rows_partner[i],
-                cot_own[i],
-                cot_partner[i],
-                column(0),
-                column(1),
-                gate_pieces,
-                up_pieces,
-                down_pieces,
-            )
-        )
-
-    back_partner = [plane_exchange(r[3]) for r in returned]
-    back_own = [plane_exchange(r[2]) for r in returned]
+    def gates_of(expert):
+        return [both_gates[:, side, expert].reshape(plane * SLOTS, 1) for side in range(2)]
+
+    def slots_of(arrays):
+        flat = [array.reshape(plane * SLOTS, D) for array in arrays]
+        return (flat[0], flat[3]), (flat[1], flat[2])
+
+    parted = lambda arrays: [array.reshape(plane, SLOTS, D) for array in arrays]
+    rows, cots = slots_of(landed)
+    first, first_dots, first_shares, landed, arrived = run_expert(
+        "first_expert", 6, rows, cots, gates_of(0), pieces_of(0), staged, riding(RIDE_FIRST)
+    )
+    pieces.update({name: (piece, None) for name, piece in zip(RIDE_FIRST, arrived)})
+    rows, cots = slots_of(landed)
+    home_of = {}
+
+    def homing(names, *shares):
+        return [(shares[i][which], flip, flip) for which, flip, i in names]
+
+    second, second_dots, second_shares, early, homes = run_expert(
+        "second_expert",
+        7,
+        rows,
+        cots,
+        gates_of(1),
+        pieces_of(1),
+        parted(first),
+        homing(HOME_SECOND, first_shares),
+    )
+    home_of.update(zip(HOME_SECOND, homes))
+
     dots = jnp.stack(
-        [
-            jnp.stack([r[4].reshape(plane, SLOTS), r[5].reshape(plane, SLOTS)], axis=1) for r in returned
-        ],
-        axis=2,
-    )
-    dots = lax.all_to_all(dots, PLANE, split_axis=0, concat_axis=0, tiled=True)
-    other_dots = flip_permute(dots[:, 1], "dp", n_dp, 1)
+        [d[side].reshape(plane, SLOTS) for side in range(2) for d in (first_dots, second_dots)], axis=1
+    )
+    dots = jnp.pad(dots, ((0, 0), (0, 0), (0, 128 - SLOTS)))
+    second = parted(second)
+    grad_rows, dots_here, dots_other, late, homes = return_rows(
+        jnp.stack(own_pair, axis=0),
+        jnp.stack(partner_pair, axis=0),
+        dots,
+        early[2:4],
+        second[2:4],
+        second[0:2],
+        homing(HOME_RETURN, first_shares, second_shares),
+        n_dp,
+    )
+    home_of.update(zip(HOME_RETURN, homes))
+    flat = lambda array: array.reshape(plane * SLOTS, D)
+    out_own, out_partner = ([flat(early[side]), flat(late[side])] for side in range(2))
+    own_dots = dots_here[:, 0:2, :SLOTS]
+    other_dots = dots_other[:, 2:4, :SLOTS]
     all_dots = jnp.where(
         parity == 0,
-        jnp.stack([dots[:, 0], other_dots], axis=1),
-        jnp.stack([other_dots, dots[:, 0]], axis=1),
+        jnp.stack([own_dots, other_dots], axis=1),
+        jnp.stack([other_dots, own_dots], axis=1),
     ).reshape(EXPERTS, SLOTS)
     grad_gates = jnp.sum(
         jnp.where(own_ranks[:, :, None] == slot_ids[None, None, :], all_dots[None], 0.0), axis=-1
     )
-    for_partner = collect_rows(partner_pair[0], partner_pair[1], back_partner[0], back_partner[1], BF)
-    from_partner = flip_permute(for_partner, "dp", n_dp, 1)
-    grad_normed_two = collect_rows(own_pair[0], own_pair[1], back_own[0], back_own[1], F32)
-    grad_normed_two = grad_normed_two + from_partner.astype(F32)
     grad_logits = gates * (grad_gates - jnp.sum(gates * grad_gates, axis=1, keepdims=True))
     grad_logits = grad_logits.astype(BF)
     grad_wrouter = mxu(normed_two, grad_logits, ((0,), (0,)))
-    grad_normed_two = grad_normed_two + mxu(grad_logits, w_router, ((1,), (1,)))
-    grad_out = cot_low.astype(F32)
-    norm_back_two = jax.vjp(rms_scale, mid_rows, gain_two)[1]
-    grad_mid_norm, grad_gain_two = norm_back_two(grad_normed_two)
-    grad_mid = grad_out + grad_mid_norm
-    grad_attn = grad_mid.astype(BF)
-    grad_attended = mxu(grad_attn, w_out, ((1,), (1,))).astype(BF)
-    grad_wout = mxu(attended, grad_attn, ((0,), (0,)))
-
-    def weight_shares(index_lhs, index_rhs):
-        made = [mxu(r[index_lhs], r[index_rhs], ((0,), (0,))).astype(BF) for r in returned]
-        made = jnp.stack(made, axis=0)
-        made = made.reshape(2, n_dp, made.shape[1] // n_dp, made.shape[2])
-
-        def quarter(flip):
-            return lax.dynamic_index_in_dim(made, z_index ^ flip, 1, keepdims=False)
-
-        got = [quarter(0)] + [
-            flip_permute(quarter(flip), "dp", n_dp, flip) for flip in range(1, n_dp)
-        ]
-        same = sum(got[flip].astype(F32) for flip in range(0, n_dp, 2)).astype(BF)
-        other = sum(got[flip].astype(F32) for flip in range(1, n_dp, 2)).astype(BF)
-        four = jnp.where(
-            parity == 0, jnp.concatenate([same, other], axis=0), jnp.concatenate([other, same], axis=0)
-        )
-        everything = lax.all_gather(four, "context", axis=0, tiled=True)
-        return everything.transpose(1, 0, 2).astype(F32)
-
-    grad_wdown = weight_shares(7, 10)
-    grad_wgate = weight_shares(6, 8)
-    grad_wup = weight_shares(6, 9)
-
-    grad_qproj, grad_keys, grad_values = attend_back(
-        block_word, qkv, keys_values, grad_attended, logs, cosine, sine, prompt_len
-    )
-    grad_kv = jnp.concatenate([grad_keys, grad_values], axis=1)
-    prompt_share = lax.psum_scatter(
-        grad_kv[:prompt_len].astype(BF), "context", scatter_dimension=0, tiled=True
-    ).astype(F32)
-    grad_kv = jnp.concatenate([prompt_share, grad_kv[prompt_len:]], axis=0)
-    grad_kproj = rotary(grad_kv[:, : KVH * HD].reshape(tokens, KVH, HD), angles, -1.0)
-    grad_kv = jnp.concatenate([grad_kproj.reshape(tokens, KVH * HD), grad_kv[:, KVH * HD :]], axis=1)
-    grad_qkv = jnp.concatenate([grad_qproj, grad_kv.astype(BF)], axis=1)
-    grad_wqkv = mxu(normed_one, grad_qkv, ((0,), (0,)))
-    grad_normed_one = mxu(grad_qkv, w_qkv, ((1,), (1,)))
-    norm_back_one = jax.vjp(rms_scale, x_rows, gain_one)[1]
-    grad_x_norm, grad_gain_one = norm_back_one(grad_normed_one)
-    grad_inputs = (grad_mid + grad_x_norm).astype(BF)
-
-    out_partner = [plane_exchange(r[1]) for r in returned]
-    out_own = [plane_exchange(r[0]) for r in returned]
-    out_for_partner = collect_rows(partner_pair[0], partner_pair[1], out_partner[0], out_partner[1], BF)
-    out_from_partner = flip_permute(out_for_partner, "dp", n_dp, 1)
-    moe_out = collect_rows(own_pair[0], own_pair[1], out_own[0], out_own[1], F32)
+
+    def part_of_expert(expert, shares):
+        parts = []
+        for which in range(3):
+            got = [shares[which][0]] + [home_of[which, flip, expert] for flip in range(1, n_dp)]
+            same = sum(got[flip].astype(F32) for flip in range(0, n_dp, 2)).astype(BF)
+            other = sum(got[flip].astype(F32) for flip in range(1, n_dp, 2)).astype(BF)
+            parts.append(
+                jnp.stack([jnp.where(parity == 0, same, other), jnp.where(parity == 0, other, same)])
+            )
+        return jnp.stack(parts, axis=1)
+
+    grad_inputs, grad_gains, grad_wout, grad_wqkv, all_first, *homes = backward(
+        prompt_len,
+        n_dp,
+        (
+            grad_logits,
+            w_router,
+            cot_low,
+            x_low,
+            gain_one[None, :],
+            gain_two[None, :],
+            attended,
+            qkv,
+            keys_values,
+            logs,
+            normed_one,
+            cosine,
+            sine,
+        ),
+        (mid_rows, grad_rows, w_out, whole_in, part_of_expert(0, first_shares)),
+        homing(HOME_BACKWARD, first_shares, second_shares),
+    )
+    home_of.update(zip(HOME_BACKWARD, homes))
+
+    out_for_partner = collect_rows(partner_pair[0], partner_pair[1], *out_partner, BF)
+    grad_small = jnp.concatenate([grad_wrouter, grad_gains[0][:, None], grad_gains[1][:, None]], axis=1)
+    grad_small = jnp.pad(grad_small, ((0, 0), (0, 128 - grad_small.shape[1]))).astype(BF)
+    parts = lambda share: share.reshape(n_dp, plane, -1, share.shape[1])
+    total_qkv, total_out, total_small, all_second, out_from_partner = reduce_shares(
+        [parts(grad_wqkv), parts(grad_wout), parts(grad_small)],
+        part_of_expert(1, second_shares),
+        out_for_partner,
+        n_dp,
+        n_context,
+    )
+    moe_out = collect_rows(own_pair[0], own_pair[1], *out_own, F32)
     result = (mid_rows + moe_out + out_from_partner.astype(F32)).astype(BF)
-
-    grad_small = jnp.concatenate(
-        [grad_wrouter, grad_gain_one[:, None], grad_gain_two[:, None]], axis=1
-    )
-    grad_small = jnp.pad(grad_small, ((0, 0), (0, 128 - grad_small.shape[1])))
-    total_out = scatter_dense(grad_wout)
-    total_in = scatter_dense(jnp.concatenate([grad_wqkv, grad_small], axis=1))
+    total_qkv = total_qkv.reshape(-1, qkv_width).astype(F32)
+    total_out = total_out.reshape(-1, D).astype(F32)
+    total_small = total_small.reshape(-1, 128).astype(F32)
     return (
         result[None],
         grad_inputs[None],
-        total_in[:, :D],
-        total_in[:, D : D + KVH * HD],
-        total_in[:, D + KVH * HD : qkv_width],
+        total_qkv[:, :D],
+        total_qkv[:, D : D + KVH * HD],
+        total_qkv[:, D + KVH * HD :],
         total_out,
-        total_in[:, qkv_width + EXPERTS],
-        total_in[:, qkv_width + EXPERTS + 1],
-        total_in[:, qkv_width : qkv_width + EXPERTS],
-        grad_wgate,
-        grad_wup,
-        grad_wdown,
+        total_small[:, EXPERTS],
+        total_small[:, EXPERTS + 1],
+        total_small[:, :EXPERTS],
+        finish_weight(0, all_first, all_second),
+        finish_weight(1, all_first, all_second),
+        finish_weight(2, all_first, all_second),
     )
 
 

time: 1880 us -> 1190 us (0.63)
  waiting for transfers between devices: 788 us -> 14.1 us
  Pallas kernels: 236 us -> 1000 us
  blocking collectives: 294 us -> 0 us
  starting transfers between devices: 185 us -> 6.49 us
  matrix products: 96.7 us -> 12.6 us
  local copies, waits for them, and re-layouts: 140 us -> 71.6 us
  other arithmetic: 101 us -> 56.9 us
    pallas_call x7 -> x10, Pallas kernels: 159 us -> 946 us  [the longest x2 271 us: run_expert(): pl.pallas_call(functools.partial(expert_kernel, plane, n_dp, half_steps,...]
    ppermute x25 -> x4, waiting for transfers between devices: 530 us -> 13.6 us  [flip_permute(): return lax.ppermute(value, axis, [(i, i ^ flip) for i in range(size)])]
    all_to_all x8 -> x0, blocking collectives: 255 us -> none  [the longest x7 247 us: plane_exchange(): lax.all_to_all(parted, PLANE, split_axis=0, concat_axis=0, tiled=True)]
    ppermute x25 -> x4, starting transfers between devices: 141 us -> 2.4 us  [flip_permute(): return lax.ppermute(value, axis, [(i, i ^ flip) for i in range(size)])]
    all_to_all x9 -> x0, waiting for transfers between devices: 109 us -> none  [plane_exchange(): lax.all_to_all(parted, PLANE, split_axis=0, concat_axis=0, tiled=True)]
    reduce_scatter x5 -> x0, waiting for transfers between devices: 103 us -> none  [the longest x2 83.9 us: scatter_dense(): parts = lax.psum_scatter(parts, PLANE, scatter_dimension=1, tiled=True)]
    dot_general x16 -> x5, matrix products: 96.7 us -> 12.6 us  [mxu(): lax.dot_general(lhs, rhs, (contract, ((), ())), preferred_element_type=F32)]
    unnamed x94 -> x62, local copies, waits for them, and re-layouts: 84.1 us -> 8.51 us
  transfers between devices with their start and end apart: 48 -> 7, of which waited for: 26 -> 2; matrix products, arithmetic and copies ran while one was open for 16% -> 5% of each run, Pallas kernels for 7% -> 15%
where the time goes in v3:
time: 1190 us; the launch traced here: 1180 us
  Pallas kernels  1000 us (84%)
  local copies, waits for them, and re-layouts  71.6 us (6%)
  other arithmetic  56.9 us (5%)
  between operations  15.2 us (1%)
  waiting for transfers between devices  14.1 us (1%)
  matrix products  12.6 us (1%)
    pallas_call x2, Pallas kernels, run_expert(): pl.pallas_call(functools.partial(expert_kernel, plane, n_dp, half_steps,...  271 us
    pallas_call x1, Pallas kernels, reduce_shares(): pl.pallas_call(functools.partial(reduce_kernel, n_dp, widths), in_specs=[...  158 us
    pallas_call x1, Pallas kernels, return_rows(): pl.pallas_call(functools.partial(return_kernel, plane, n_dp, [(index, fli...  151 us
    pallas_call x1, Pallas kernels, dispatch_rows(): pl.pallas_call(functools.partial(dispatch_kernel, plane, n_dp, [(index, f...  148 us
    pallas_call x1, Pallas kernels, backward(): pl.pallas_call(functools.partial(backward_kernel, n_dp, prompt_len, [(ind...  118 us
    pallas_call x1, Pallas kernels, gather_parts(): pl.pallas_call(functools.partial(gather_kernel, n_dp), in_specs=[anywhere...  59.4 us
    pallas_call x3, Pallas kernels, finish_weight(): pl.pallas_call(functools.partial(finish_kernel, down), grid=(rows // step...  40.3 us
    pallas_call x1, Pallas kernels, attend(): pl.pallas_call(functools.partial(attend_kernel, prompt_len), grid=(HEADS,...  26.3 us
  transfers between devices with their start and end apart: 7, of which 2 were waited for; matrix products, arithmetic and copies ran while one was open for 5% of the time, Pallas kernels for 15%

profile of v3, /device:TPU:0, one launch (start us, length us, event | category | flops | bytes accessed | tf_op | source)
XLA Modules:
  0.0 1181.1 jit_solution(7301488583884402275)
XLA Ops:
  10.9 1.7 convert_element_type.271
  12.5 1.7 convert_element_type.272
  15.9 1.8 convert_element_type.270
  19.8 59.4 %gather_parts.1 = (bf16[4,8,48,2176]{3,2,1,0:T(8,128)(2,1)}, bf16[4,48,1536]{2,1,0:T(8,128)(2,1)}, s32[768,4]{1,0:T(8,128)}) custom-call(bf16[48,2176]{1,0:T(8,128)(2,1)} %fusion.21.in_ref, bf16[48,1536]{1,0:T(8,128)(2,1)} %dynamic-slice_convert_fusion.3.out_part_ref, s32[768,4]{1,0:T(8,128)} %bitcast.223), custom_call_target="tpu_custom_call" | custom-call | tf_op jit(solution)/shard_map/gather_parts/pallas_call | solution.py:930
  79.2 1.7 convert_reduce_fusion
  81.5 2.1 fusion.22
  84.8 12.1 %project.1 = (bf16[768,2048]{1,0:T(8,128)(2,1)}, bf16[768,1536]{1,0:T(8,128)(2,1)}) custom-call(bf16[768,1536]{1,0:T(8,128)(2,1)} %bitcast.214, f32[1,1536]{1,0:T(1,128)} %reshape.301.gain_ref.refs_4_, bf16[1536,2176]{1,0:T(8,128)(2,1)} %bitcast.210, f32[768,128]{1,0:T(8,128)} %get-tuple-element.252.cos_ref.refs_11_, ...), custom_call_target="tpu_custom_call" | custom-call | tf_op jit(solution)/shard_map/project/pallas_call | solution.py:438
  96.9 1.7 slice.93
  99.4 10.7 fusion
  110.2 2.0 copy.221
  113.3 2.0 collective-permute-start.1
  116.5 1.8 slice.127.refs_1_
  118.3 1.9 slice.94
  122.3 5.0 fusion.2
  127.4 1.8 copy.223
  130.0 1.7 copy.182
  133.8 1.8 copy.183
  135.6 2.2 fusion.6
  143.9 1.9 fusion.29
  146.7 1.7 copy.192.refs_4_
  148.5 3.2 dynamic-slice_bitcast_fusion
  153.3 2.6 pad_maximum_fusion.2.k_ref.v_ref.refs_8_
  156.0 26.3 %attend.1 = (bf16[768,1536]{1,0:T(8,128)(2,1)}, f32[768,128]{1,0:T(8,128)}) custom-call(s32[1]{0:T(128)} %bitcast.1.block_ref, bf16[768,2048]{1,0:T(8,128)(2,1)} %get-tuple-element.105.q_ref.refs_7_, bf16[1536,512]{1,0:T(8,128)(2,1)} %pad_maximum_fusion.2.k_ref.v_ref.refs_8_, bf16[1536,512]{1,0:T(8,128)(2,1)} %pad_maximum_fusion.2.k_ref.v_ref.refs_8_), custom_call_target="tpu_custom_call" | custom-call | tf_op jit(solution)/shard_map/attend/pallas_call | solution.py:496
  182.3 6.7 multiply_reduce_fusion
  189.6 1.7 copy-done.2
  191.2 12.6 %collective-permute-done.1.refs_7_ = bf16[2,384,768]{2,1,0:T(8,128)(2,1)} collective-permute-done((bf16[2,384,768]{2,1,0:T(8,128)(2,1)}, bf16[2,384,768]{2,1,0:T(8,128)(2,1)}, u32[]{:S(2)}, u32[]{:S(2)}) %collective-permute-start.1) | collective-permute-done | bytes 1179680 | tf_op jit(solution)/shard_map/ppermute | solution.py:1663
  203.9 1.9 select_reduce_fusion.2
  212.7 3.8 all-to-all-start
  216.5 147.8 %dispatch_rows.1 = (bf16[8,112,1536]{2,1,0:T(8,128)(2,1)}, bf16[8,112,1536]{2,1,0:T(8,128)(2,1)}, bf16[8,112,1536]{2,1,0:T(8,128)(2,1)}, bf16[8,112,1536]{2,1,0:...) custom-call(bf16[768,1536]{1,0:T(8,128)(2,1)} %copy-done.3, ...), custom_call_target="tpu_custom_call" | custom-call | flops 20000000000 | bytes 400000000 | tf_op jit(solution)/shard_map/dispatch_rows/pallas_call | solution.py:1002
  368.2 125.8 %first_expert.1 = (bf16[896,1536]{1,0:T(8,128)(2,1)}, bf16[896,1536]{1,0:T(8,128)(2,1)}, bf16[896,1536]{1,0:T(8,128)(2,1)}, bf16[896,1536]{1,0:T(8,128)(2,1)}, f...) custom-call(bf16[896,1536]{1,0:T(8,128)(2,1)} %bitcast.237, ...), custom_call_target="tpu_custom_call" | custom-call | tf_op jit(solution)/shard_map/first_expert/pallas_call | solution.py:764
  496.7 145.5 %second_expert.1 = (bf16[896,1536]{1,0:T(8,128)(2,1)}, bf16[896,1536]{1,0:T(8,128)(2,1)}, bf16[896,1536]{1,0:T(8,128)(2,1)}, bf16[896,1536]{1,0:T(8,128)(2,1)}, ...) custom-call(bf16[896,1536]{1,0:T(8,128)(2,1)} %bitcast.233, ...), custom_call_target="tpu_custom_call" | custom-call | tf_op jit(solution)/shard_map/second_expert/pallas_call | solution.py:764
  644.8 2.1 select_bitcast_fusion.9
  649.2 150.7 %return_rows.1 = (f32[768,1536]{1,0:T(8,128)}, f32[8,4,128]{2,1,0:T(4,128)}, f32[8,4,128]{2,1,0:T(4,128)}, bf16[8,112,1536]{2,1,0:T(8,128)(2,1)}, bf16[8,112,153...) custom-call(bf16[2,768,8]{2,1,0:T(8,128)(2,1)} %get-tuple-element.23, ...), custom_call_target="tpu_custom_call" | custom-call | flops 30000001024 | bytes 400000000 | tf_op jit(solution)/shard_map/return_rows/pallas_call | solution.py:1124
  799.9 1.9 select_bitcast_fusion.7
  802.4 2.0 copy.211.refs_17_
  804.5 2.5 select_reduce_fusion
  808.7 118.3 %backward.1 = (bf16[768,1536]{1,0:T(8,128)(2,1)}, f32[8,1536]{1,0:T(8,128)}, bf16[1536,1536]{1,0:T(8,128)(2,1)}, bf16[1536,2048]{1,0:T(8,128)(2,1)}, bf16[4,2,3,...) custom-call(bf16[768,32]{1,0:T(8,128)(2,1)} %copy-done.9, ...), custom_call_target="tpu_custom_call" | custom-call | tf_op jit(solution)/shard_map/backward/pallas_call | solution.py:1388
  934.1 2.0 pad_maximum_fusion.1.refs_3_
  936.1 9.9 collect_rows.3.refs_4_
  945.9 158.1 %reduce_shares.1 = (bf16[8,48,2048]{2,1,0:T(8,128)(2,1)}, bf16[8,48,1536]{2,1,0:T(8,128)(2,1)}, bf16[8,48,128]{2,1,0:T(8,128)(2,1)}, bf16[4,2,3,384,768]{4,3,2,1,0:T(8,128)(2,1)}, bf16[768,1536]{1,0:T(8,128)(2,1)}) custom-call(bf16[4,8,48,2048]{3,2,1,0:T(8,128)(2,1)} %bitcast.219, bf16[4,8,48,1536]{3,2,1,0:T(8,128)(2,1)} %bitcast.222, ...), custom_call_target="tpu_custom_call" | custom-call | tf_op jit(solution)/shard_map/reduce_shares/pallas_call | solution.py:1585
  1105.8 1.8 bitcast_convert_fusion
  1110.1 14.1 %finish_weight.4 = f32[384,16,768]{2,1,0:T(8,128)} custom-call(bf16[4,2,3,384,768]{4,3,2,1,0:T(8,128)(2,1)} %get-tuple-element.194.first_ref, bf16[4,2,3,384,768]{4,3,2,1,0:T(8,128)(2,1)} %get-tuple-element.195.second_ref), custom_call_target="tpu_custom_call" | custom-call | tf_op jit(solution)/shard_map/finish_weight/pallas_call | solution.py:1647
  1124.2 14.2 %finish_weight.3 = f32[384,16,768]{2,1,0:T(8,128)} custom-call(bf16[4,2,3,384,768]{4,3,2,1,0:T(8,128)(2,1)} %get-tuple-element.194.first_ref, bf16[4,2,3,384,768]{4,3,2,1,0:T(8,128)(2,1)} %get-tuple-element.195.second_ref), custom_call_target="tpu_custom_call" | custom-call | tf_op jit(solution)/shard_map/finish_weight/pallas_call | solution.py:1647
  1140.0 1.8 bitcast_convert_fusion.1
  1141.8 10.0 collect_rows.2
  1151.8 6.5 fusion.3
  1158.3 12.1 %finish_weight.5 = f32[192,16,1536]{2,1,0:T(8,128)} custom-call(bf16[4,2,3,2,192,768]{5,4,3,2,1,0:T(8,128)(2,1)} %bitcast.207, bf16[4,2,3,2,192,768]{5,4,3,2,1,0:T(8,128)(2,1)} %bitcast.208), custom_call_target="tpu_custom_call" | custom-call | tf_op jit(solution)/shard_map/finish_weight/pallas_call | solution.py:1647
  1170.4 3.4 copy.237
  (160 shorter events, 59.8 us)
Async XLA Ops:
  7.2 10.5 copy-start
  7.2 146.1 %all-gather.4.cloned.1.call-start = ((), (), s32[]{:S(2)}) async-start(), calls=%async_computation.1 | async-start | bytes 1310720 | tf_op jit(solution)/shard_map/all_gather | solution.py:1770
  98.6 83.7 %all-gather.6.cloned.1.call-start = ((), (), s32[]{:S(2)}) async-start(), calls=%async_computation.2 | async-start | bytes 5308416 | tf_op jit(solution)/shard_map/all_gather | solution.py:1704
  99.3 104.5 %collective-permute-start = (bf16[768,1536]{1,0:T(8,128)(2,1)}, bf16[768,1536]{1,0:T(8,128)(2,1)}, u32[]{:S(2)}, u32[]{:S(2)}) collective-permute-start(bf16[768,1536]{1,0:T(8,128)(2,1)} %bitcast.8.refs_1_.refs_2_), channel_id=1, source_target_pairs={{0,1},{1,0},{2,3},{3,2},{4,5},{5,4},{6,7},{7,6},{8,9},{9,8},{10,11... | collective-permute-start | bytes 7077896 | tf_op jit(solution)/shard_map/ppermute | solution.py:1663
  113.3 8.2 copy-start.5
  113.3 77.9 %collective-permute-start.2 = (bf16[2,384,768]{2,1,0:T(8,128)(2,1)S(1)}, bf16[2,384,768]{2,1,0:T(8,128)(2,1)}, u32[]{:S(2)}, u32[]{:S(2)}) collective-permute-start(bf16[2,384,768]{2,1,0:T(8,128)(2,1)S(1)} %get-tuple-element.224.refs_6_), channel_id=1, source_target_pairs={{0,2},{1,3},{2,0},{3,1},{4,6},{5,7},{6,4},{7,5},{8,10},{9,11},{10,... | collective-permute-start | bytes 3538952 | tf_op jit(solution)/shard_map/ppermute | solution.py:1663
  113.3 90.5 %collective-permute-start.1 = (bf16[2,384,768]{2,1,0:T(8,128)(2,1)}, bf16[2,384,768]{2,1,0:T(8,128)(2,1)}, u32[]{:S(2)}, u32[]{:S(2)}) collective-permute-start(bf16[2,384,768]{2,1,0:T(8,128)(2,1)} %get-tuple-element.225.refs_5_.refs_22_), channel_id=1, source_target_pairs={{0,1},{1,0},{2,3},{3,2},{4,5},{5,4},{6,7},{7,6},{8,9},{9,8},{10,11... | collective-permute-start | bytes 3538952 | tf_op jit(solution)/shard_map/ppermute | solution.py:1663
  127.4 2.4 copy-start.7
  156.0 26.3 %copy-start.6 = (bf16[1,768,1536]{2,1,0:T(8,128)(2,1)S(1)}, bf16[1,768,1536]{2,1,0:T(8,128)(2,1)}, u32[]{:S(2)}) copy-start(bf16[1,768,1536]{2,1,0:T(8,128)(2,1)} %param.13) | copy-start | bytes 7077892
  189.0 2.2 copy-start.2
  189.1 14.8 %copy-start.10 = (pred[768,32]{1,0:T(32,128)(4,1)S(1)}, pred[768,32]{1,0:T(32,128)(4,1)}, u32[]{:S(2)}) copy-start(pred[768,32]{1,0:T(32,128)(4,1)} %get-tuple-element.205) | copy-start | bytes 73732
  191.2 14.6 %copy-start.3 = (bf16[768,1536]{1,0:T(8,128)(2,1)}, bf16[768,1536]{1,0:T(8,128)(2,1)S(1)}, u32[]{:S(2)}) copy-start(bf16[768,1536]{1,0:T(8,128)(2,1)S(1)} %multiply_convert_fusion.refs_0_) | copy-start | bytes 7077892
  203.9 1.9 copy-start.25
  205.8 0.9 copy-start.11
  205.8 1.3 copy-start.26
  208.3 3.7 collective-permute-start.3
  212.7 151.6 %all-to-all-start = ((f32[8,2,2,112]{3,2,1,0:T(2,128)}), f32[8,2,2,112]{3,2,1,0:T(2,128)S(1)}, u32[]{:S(2)}, u32[]{:S(2)}) async-start(f32[8,2,2,112]{3,2,1,0:T(2,128)} %pad_maximum_fusion.9), calls=%async_computation | async-start | bytes 32768 | tf_op jit(solution)/shard_map/all_to_all | solution.py:1800
  644.8 2.2 copy-start.19
  644.8 2.2 copy-start.20
  644.8 2.2 copy-start.21
  802.4 2.1 copy-start.28
  802.4 2.1 copy-start.27
  804.5 3.6 copy-start.4
  808.0 0.7 copy-start.9
  808.7 119.5 %copy-start.14 = (bf16[384,768]{1,0:T(8,128)(2,1)S(1)}, bf16[384,768]{1,0:T(8,128)(2,1)}, u32[]{:S(2)}) copy-start(bf16[384,768]{1,0:T(8,128)(2,1)} %get-tuple-element.178) | copy-start | bytes 1769476
  808.7 119.5 %copy-start.15 = (bf16[384,768]{1,0:T(8,128)(2,1)S(1)}, bf16[384,768]{1,0:T(8,128)(2,1)}, u32[]{:S(2)}) copy-start(bf16[384,768]{1,0:T(8,128)(2,1)} %get-tuple-element.180) | copy-start | bytes 1769476
  808.7 119.5 %copy-start.16 = (bf16[384,768]{1,0:T(8,128)(2,1)S(1)}, bf16[384,768]{1,0:T(8,128)(2,1)}, u32[]{:S(2)}) copy-start(bf16[384,768]{1,0:T(8,128)(2,1)} %get-tuple-element.179) | copy-start | bytes 1769476
  928.2 1.7 copy-start.22
  928.2 1.7 copy-start.23
  928.2 1.7 copy-start.24
  929.9 1.7 copy-start.13
  929.9 1.7 copy-start.17
  930.0 1.7 copy-start.18
  1124.2 15.8 %copy-start.12 = (bf16[8,48,1536]{2,1,0:T(8,128)(2,1)S(1)}, bf16[8,48,1536]{2,1,0:T(8,128)(2,1)}, u32[]{:S(2)}) copy-start(bf16[8,48,1536]{2,1,0:T(8,128)(2,1)} %get-tuple-element.192) | copy-start | bytes 3538948
  1141.8 10.0 copy-start.8
  1170.4 3.4 copy-start.1
Sparse Core Ops, SparseCore 0:
  98.7 14.0 all-gather.3
  114.7 39.1 all-gather.5

commit v4 on v3

--- a/solution.py
+++ b/solution.py
@@ -412,52 +412,6 @@
     return values * cosine + pltpu.roll(values, HD // 2, 1) * sine
 
 
-def project_kernel(x_ref, gain_ref, w_ref, cos_ref, sin_ref, out_ref, normed_ref):
-    step = pl.program_id(0)
-
-    @pl.when(step == 0)
-    def _():
-        rows = x_ref[...].astype(F32)
-        scale = lax.rsqrt(jnp.mean(rows * rows, axis=-1, keepdims=True) + epsilon)
-        normed_ref[...] = (rows * scale * gain_ref[...]).astype(BF)
-
-    product = mxu(normed_ref[...], w_ref[...])
-    is_query = step < HEADS // 2
-    is_value = step == HEADS // 2 + KVH // 2
-    cosine = jnp.where(is_value, 1.0, cos_ref[...])
-    sine = jnp.where(is_value, 0.0, sin_ref[...])
-    factor = jnp.where(is_query, 1.0 / math.sqrt(HD), 1.0)
-    for half in range(2):
-        part = product[:, half * HD : (half + 1) * HD]
-        out_ref[:, half * HD : (half + 1) * HD] = (turn(part, cosine, sine) * factor).astype(BF)
-
-
-def project(x_low, gain, w_in, width, cosine, sine):
-    tokens = x_low.shape[0]
-    whole = lambda j: (0, 0)
-    return pl.pallas_call(
-        project_kernel,
-        grid=(width // (2 * HD),),
-        in_specs=[
-            pl.BlockSpec((tokens, D), whole),
-            pl.BlockSpec((1, D), whole),
-            pl.BlockSpec((D, 2 * HD), lambda j: (0, j)),
-            pl.BlockSpec((tokens, HD), whole),
-            pl.BlockSpec((tokens, HD), whole),
-        ],
-        out_specs=[
-            pl.BlockSpec((tokens, 2 * HD), lambda j: (0, j)),
-            pl.BlockSpec((tokens, D), whole),
-        ],
-        out_shape=[
-            jax.ShapeDtypeStruct((tokens, width), BF),
-            jax.ShapeDtypeStruct((tokens, D), BF),
-        ],
-        compiler_params=grant(),
-        name="project",
-    )(x_low, gain, w_in, cosine, sine)
-
-
 def row_blocks(prompt_len):
     blocks = [(0, prompt_len)]
     for start in range(0, CONT, PBLK):
@@ -473,46 +427,6 @@
     else:
         limit = row + (prompt_len + first_row - PBLK)
     return jnp.where(column <= limit, scores, masked_score)
-
-
-def attend_kernel(prompt_len, block_ref, q_ref, k_ref, v_ref, out_ref, log_ref):
-    for first_row, keys in row_blocks(prompt_len):
-        rows = slice(first_row, first_row + PBLK)
-        scores = mxu(q_ref[rows, :], k_ref[:keys, :], ((1,), (1,)))
-        scores = masked_scores(scores, first_row, prompt_len, block_ref[0])
-        top = jnp.max(scores, axis=-1, keepdims=True)
-        unnormed = jnp.exp(scores - top)
-        total = jnp.sum(unnormed, axis=-1, keepdims=True)
-        mixed = mxu(unnormed.astype(BF), v_ref[:keys, :]) / total
-        out_ref[rows, :] = mixed.astype(BF)
-        lane = lax.broadcasted_iota(jnp.int32, (PBLK, log_ref.shape[1]), 1)
-        kept = jnp.where(pl.program_id(0) == 0, 0.0, log_ref[rows, :])
-        log_ref[rows, :] = jnp.where(lane == pl.program_id(0), top + jnp.log(total), kept)
-
-
-def attend(block_index, qkv, keys_values, prompt_len):
-    tokens, key_rows = qkv.shape[0], keys_values.shape[0]
-    width = HEADS // KVH
-    return pl.pallas_call(
-        functools.partial(attend_kernel, prompt_len),
-        grid=(HEADS,),
-        in_specs=[
-            pl.BlockSpec(memory_space=pltpu.SMEM),
-            pl.BlockSpec((tokens, HD), lambda h: (0, h)),
-            pl.BlockSpec((key_rows, HD), lambda h: (0, h // width)),
-            pl.BlockSpec((key_rows, HD), lambda h: (0, KVH + h // width)),
-        ],
-        out_specs=[
-            pl.BlockSpec((tokens, HD), lambda h: (0, h)),
-            pl.BlockSpec((tokens, 128), lambda h: (0, 0)),
-        ],
-        out_shape=[
-            jax.ShapeDtypeStruct((tokens, D), BF),
-            jax.ShapeDtypeStruct((tokens, 128), F32),
-        ],
-        compiler_params=grant(),
-        name="attend",
-    )(block_index, qkv, keys_values, keys_values)
 
 
 def segment_matrix(parts, transposed):
@@ -535,34 +449,26 @@
     return jnp.where(spread == slot.astype(F32), 1.0, 0.0).astype(BF)
 
 
-def collect_kernel(parts, rank0_ref, rank1_ref, rows0_ref, rows1_ref, out_ref):
-    total = mxu(slot_matrix(rank0_ref[...], parts, False), rows0_ref[...])
-    total = total + mxu(slot_matrix(rank1_ref[...], parts, False), rows1_ref[...])
-    out_ref[...] = total.astype(out_ref.dtype)
-
-
-def collect_rows(rank0, rank1, rows0, rows1, kind):
-    tokens, dests = rank0.shape
-    step = PBLK
-    ranks = pl.BlockSpec((step, dests), lambda j: (j, 0))
-    slots = pl.BlockSpec((dests * SLOTS, D), lambda j: (0, 0))
-    return pl.pallas_call(
-        functools.partial(collect_kernel, dests),
-        grid=(tokens // step,),
-        in_specs=[ranks, ranks, slots, slots],
-        out_specs=pl.BlockSpec((step, D), lambda j: (j, 0)),
-        out_shape=jax.ShapeDtypeStruct((tokens, D), kind),
-        compiler_params=grant(),
-        name="collect_rows",
-    )(rank0, rank1, rows0, rows1)
-
-
-def plane_exchange(slot, source, target, local_sems, send_sems, recv_sems):
+def collect_into(plane, rank_ref, held, base, target, finish):
+    def block(n, carry):
+        rows = pl.ds(pl.multiple_of(n * PBLK, PBLK), PBLK)
+        made = jnp.zeros((PBLK, D), F32)
+        for expert in range(2):
+            chooser = slot_matrix(rank_ref[expert, rows, :], plane, False)
+            made = made + mxu(chooser, held[base + expert].reshape(plane * SLOTS, D))
+        target[rows, :] = finish(rows, made)
+        return carry
+
+    lax.fori_loop(0, target.shape[0] // PBLK, block, 0)
+
+
+def plane_exchange(slot, source, target, local_sems, send_sems, recv_sems, bounce=None):
     here = plane_here()
     plane = source.shape[0]
+    own_first = target.at[here] if bounce is None else bounce.at[slot]
 
     def begin():
-        pltpu.make_async_copy(source.at[here], target.at[here], local_sems.at[slot]).start()
+        pltpu.make_async_copy(source.at[here], own_first, local_sems.at[slot]).start()
 
         def one(flip, carry):
             peer = here ^ flip
@@ -578,7 +484,11 @@
         lax.fori_loop(1, plane, one, 0)
 
     def finish():
-        pltpu.make_async_copy(source.at[here], target.at[here], local_sems.at[slot]).wait()
+        pltpu.make_async_copy(source.at[here], own_first, local_sems.at[slot]).wait()
+        if bounce is not None:
+            onward = pltpu.make_async_copy(own_first, target.at[here], local_sems.at[slot])
+            onward.start()
+            onward.wait()
 
         def one(flip, carry):
             peer = here ^ flip
@@ -599,11 +509,13 @@
 
 
 ALL_FLIPS = (2, 3, 1)
-RIDE_DISPATCH = ((0, 3, 0),) + tuple((m, f, 0) for m in (1, 2) for f in ALL_FLIPS)
-RIDE_FIRST = ((0, 3, 1),) + tuple((m, f, 1) for m in (1, 2) for f in ALL_FLIPS)
-HOME_SECOND = tuple((m, f, 0) for m in (0, 1) for f in ALL_FLIPS) + ((2, 2, 0),)
-HOME_RETURN = ((2, 3, 0), (0, 2, 1), (0, 3, 1), (1, 2, 1), (2, 1, 0), (0, 1, 1))
-HOME_BACKWARD = ((1, 3, 1), (2, 2, 1), (2, 3, 1), (1, 1, 1), (2, 1, 1))
+RIDE_FRONT = ((0, 2, None),)
+RIDE_DISPATCH = ((0, 3, 0), (0, 1, 0)) + tuple((m, f, 0) for m in (1, 2) for f in ALL_FLIPS)
+RIDE_FIRST = ((0, 3, 1), (0, 1, 1)) + tuple((m, f, 1) for m in (1, 2) for f in ALL_FLIPS)
+HOME_SECOND = ((0, 2, 0), (0, 3, 0), (1, 2, 0), (1, 3, 0), (0, 1, 0))
+HOME_RETURN = ((2, 2, 0), (1, 1, 0), (2, 1, 0), (2, 3, 0))
+RETURN_FIRST = 3
+HOME_BACKWARD = tuple((m, f, 1) for f in ALL_FLIPS for m in range(3))
 
 
 def pick(array, index):
@@ -611,7 +523,9 @@
 
 
 def picked_shape(array, index):
-    return array.shape if index is None else array.shape[1:]
+    if index is None:
+        return array.shape
+    return array.shape[len(index) if isinstance(index, tuple) else 1 :]
 
 
 def dp_moves(sources, targets, riders, sends, recvs):
@@ -626,15 +540,15 @@
     return [{"dp": lax.axis_index("dp") ^ flip} for flip in range(1, n_dp)]
 
 
-def expert_kernel(plane, n_dp, half_steps, picks, riders, *refs):
+def expert_kernel(plane, n_dp, half_steps, n_carried, picks, riders, *refs):
     (xo_ref, xp_ref, go_ref, gp_ref, so_ref, sp_ref), refs = refs[:6], refs[6:]
     pieces, refs = refs[: 3 * n_dp], refs[3 * n_dp :]
-    carried, refs = refs[:4], refs[4:]
+    carried, refs = refs[:n_carried], refs[n_carried:]
     sources, refs = refs[: len(riders)], refs[len(riders) :]
     (yo_ref, yp_ref, bo_ref, bp_ref, do_ref, dp_ref, gate_ref, up_ref, down_ref), refs = refs[:9], refs[9:]
-    landed, refs = refs[:4], refs[4:]
+    landed, refs = refs[:n_carried], refs[n_carried:]
     targets, refs = refs[: len(riders)], refs[len(riders) :]
-    (wg_ref, wu_ref, wd_ref, x_all, de_all, a_all, dg_all, du_all, stage), sems = refs[:9], refs[9:]
+    (wg_ref, wu_ref, wd_ref, x_all, de_all, a_all, dg_all, du_all, stage, bounce), sems = refs[:10], refs[10:]
     weight_sems, store_sems, local_sems, send_sems, recv_sems, ride_send, ride_recv = sems
     weights = (wg_ref, wu_ref, wd_ref)
     z_index = lax.axis_index("dp")
@@ -642,7 +556,7 @@
     own = step < half_steps
     rows_of_step = xo_ref.shape[0]
     exchanges = [
-        plane_exchange(n, source, target, local_sems, send_sems, recv_sems)
+        plane_exchange(n, source, target, local_sems, send_sems, recv_sems, bounce)
         for n, (source, target) in enumerate(zip(carried, landed))
     ]
     moves = dp_moves(sources, targets, riders, ride_send, ride_recv)
@@ -767,12 +681,13 @@
             plane,
             n_dp,
             half_steps,
+            len(carried),
             [index for _, index in pieces],
             [(index, flip) for _, index, flip in riders],
         ),
         grid=(2 * half_steps,),
-        in_specs=pair(D) + pair(D) + pair(1) + [anywhere] * (len(pieces) + 4 + len(riders)),
-        out_specs=pair(D) + pair(D) + pair(1) + [anywhere] * (7 + len(riders)),
+        in_specs=pair(D) + pair(D) + pair(1) + [anywhere] * (len(pieces) + len(carried) + len(riders)),
+        out_specs=pair(D) + pair(D) + pair(1) + [anywhere] * (3 + len(carried) + len(riders)),
         out_shape=[shape((half_rows, D), BF)] * 4
         + [shape((half_rows, 1), F32)] * 2
         + [share] * 3
@@ -788,11 +703,12 @@
             pltpu.VMEM((all_rows, hidden), BF),
             pltpu.VMEM((all_rows, hidden), BF),
             pltpu.VMEM((2, D // n_dp, hidden), BF),
+            pltpu.VMEM((len(carried), SLOTS, D), BF),
             dma((len(pieces),)),
             dma((2,)),
-            dma((4,)),
-            dma((4, plane)),
-            dma((4, plane)),
+            dma((len(carried),)),
+            dma((len(carried), plane)),
+            dma((len(carried), plane)),
             dma((len(riders),)),
             dma((len(riders),)),
         ],
@@ -801,7 +717,8 @@
         ),
         name=name,
     )(*rows, *cots, *gates, *[a for a, _ in pieces], *carried, *[a for a, _, _ in riders])
-    return results[:4], results[4:6], results[6:9], results[9:13], results[13:]
+    last = 9 + len(carried)
+    return results[:4], results[4:6], results[6:9], results[9:last], results[last:]
 
 
 def plane_peer(index):
@@ -818,11 +735,6 @@
     for peer in peers:
         pl.semaphore_signal(barrier, inc=1, device_id=peer, device_id_type=MESH_ID)
     pl.semaphore_wait(barrier, len(peers))
-
-
-def plane_and_partner(plane):
-    here = plane_here()
-    return [plane_peer(here ^ flip) for flip in range(1, plane)] + [{"dp": lax.axis_index("dp") ^ 1}]
 
 
 def remote(source, target, send, receive, peer):
@@ -836,139 +748,494 @@
     )
 
 
+def cast_halves(source_ref, halves_ref, loaded, made, load_sems, store_sems):
+    rows, experts, width = source_ref.shape
+    mine = experts // lax.axis_size("context")
+    group = 8
+    first = lax.axis_index("context") * mine
+    start = pl.multiple_of(first // group * group, group)
+    step = loaded.shape[1] * loaded.shape[3] // width
+    lower = lax.rem(first, group) == 0
+    even = lax.rem(lax.axis_index("dp"), 2) == 0
+    steps = rows // step
+
+    def load(n):
+        slot = lax.rem(n, 2)
+        block = source_ref.at[pl.ds(pl.multiple_of(n * step, step), step), pl.ds(start, group), :]
+        return pltpu.make_async_copy(block, loaded.at[slot], load_sems.at[slot])
+
+    def store(n, half):
+        slot = lax.rem(n, 2)
+        block = halves_ref.at[half, :, pl.ds(pl.multiple_of(n * step, step), step), :]
+        return pltpu.make_async_copy(made.at[slot, half], block, store_sems.at[slot, half])
+
+    load(0).start()
+
+    def body(n, carry):
+        @pl.when(n + 1 < steps)
+        def _():
+            load(n + 1).start()
+
+        load(n).wait()
+
+        @pl.when(n >= 2)
+        def _():
+            for half in range(2):
+                store(n - 2, half).wait()
+
+        slot = lax.rem(n, 2)
+        block = loaded[slot]
+        kept = jnp.where(lower, block[:, :mine, :], block[:, group - mine :, :])
+        by_expert = jnp.swapaxes(kept, 0, 1).astype(BF)
+        low, high = by_expert[: mine // 2], by_expert[mine // 2 :]
+        made[slot, 0] = jnp.where(even, low, high)
+        made[slot, 1] = jnp.where(even, high, low)
+        for half in range(2):
+            store(n, half).start()
+        return carry
+
+    lax.fori_loop(0, steps, body, 0)
+    for n in (steps - 2, steps - 1):
+        for half in range(2):
+            store(n, half).wait()
+
+
+def rank_tables(routes, plane, row_ref, column_ref):
+    tokens = routes.shape[1]
+    expert = lax.broadcasted_iota(jnp.int32, (EXPERTS, tokens), 0)
+    named = jnp.zeros((EXPERTS, tokens), F32)
+    for k in range(TOP):
+        named = named + jnp.where(routes[k : k + 1, :] == expert, 1.0, 0.0)
+    before = lax.broadcasted_iota(jnp.int32, (tokens, tokens), 0) < lax.broadcasted_iota(
+        jnp.int32, (tokens, tokens), 1
+    )
+    count = mxu(named.astype(BF), jnp.where(before, 1.0, 0.0).astype(BF))
+    ranks = jnp.where(named > 0, count, -1.0)
+    low = ranks.astype(BF)
+    owned = EXPERTS // plane
+    parity = lax.rem(lax.axis_index("dp"), 2)
+    for i in range(2):
+        place = lax.broadcasted_iota(jnp.int32, (plane, EXPERTS), 0) * owned + parity * 2 + i
+        column = lax.broadcasted_iota(jnp.int32, (plane, EXPERTS), 1)
+        chosen = jnp.where(place == column, 1.0, 0.0).astype(BF)
+        row_ref[i] = mxu(chosen, low).astype(BF)
+        column_ref[i] = mxu(low, chosen, ((0,), (1,))).astype(BF)
+    return ranks
+
+
 def gather_kernel(
     n_dp,
+    plane,
+    routes_ref,
     in_ref,
-    out_part_ref,
-    routes_ref,
-    whole_ref,
     out_ref,
-    partner_routes_ref,
+    gate_ref,
+    up_ref,
+    down_ref,
+    cot_ref,
+    ranks_ref,
+    own_row_ref,
+    own_column_ref,
+    partner_row_ref,
+    partner_column_ref,
+    whole_in_ref,
+    whole_out_ref,
+    gate_halves_ref,
+    up_halves_ref,
+    down_halves_ref,
+    cot_partner_ref,
+    partner_routes,
+    loaded,
+    made,
+    loaded_wide,
+    made_wide,
+    load_sems,
+    store_sems,
     local_sems,
     z_send,
-    o_send,
-    o_recv,
     sends,
     recvs,
     route_sems,
 ):
     here = plane_here()
     z_index = lax.axis_index("dp")
+    parts, wholes = (in_ref, out_ref), (whole_in_ref, whole_out_ref)
     z_peer = lambda flip: {"dp": z_index ^ flip}
     greet([z_peer(flip) for flip in range(1, n_dp)] + [plane_peer(here ^ flip) for flip in (1, 2, 4)])
+    routing = remote(routes_ref, partner_routes, route_sems.at[0], route_sems.at[1], z_peer(1))
+    routing.start()
     keep = [
-        pltpu.make_async_copy(in_ref, whole_ref.at[z_index, here], local_sems.at[0]),
-        pltpu.make_async_copy(out_part_ref, out_ref.at[z_index], local_sems.at[1]),
+        pltpu.make_async_copy(part, whole.at[z_index, here], local_sems.at[a])
+        for a, (part, whole) in enumerate(zip(parts, wholes))
     ]
     for copy in keep:
         copy.start()
-    routing = remote(routes_ref, partner_routes_ref, route_sems.at[0], route_sems.at[1], z_peer(1))
-    routing.start()
     started = []
-    for flip in range(1, n_dp):
-        started.append(
-            remote(in_ref, whole_ref.at[z_index, here], z_send.at[flip], recvs.at[z_index, here], z_peer(flip))
-        )
-        started[-1].start()
-    for flip in range(1, n_dp):
-        started.append(
-            remote(out_part_ref, out_ref.at[z_index], o_send.at[flip], o_recv.at[z_index], z_peer(flip))
-        )
-        started[-1].start()
-
-    def pass_on(lane, flip, z_from, place, source=None):
-        block = whole_ref.at[z_from, place]
+    for a in range(2):
+        for flip in range(1, n_dp):
+            started.append(
+                remote(
+                    parts[a],
+                    wholes[a].at[z_index, here],
+                    z_send.at[a, flip],
+                    recvs.at[a, z_index, here],
+                    z_peer(flip),
+                )
+            )
+            started[-1].start()
+
+    half = cot_partner_ref.shape[0]
+    cot_pair = remote(
+        cot_ref.at[pl.ds(0, half)], cot_partner_ref, route_sems.at[2], route_sems.at[3], z_peer(1)
+    )
+    cot_pair.start()
+
+    def pass_on(a, lane, flip, z_from, place, source=None):
+        block = wholes[a].at[z_from, place]
         move = remote(
             block if source is None else source,
             block,
-            sends.at[lane, z_from, place],
-            recvs.at[z_from, place],
+            sends.at[a, lane, z_from, place],
+            recvs.at[a, z_from, place],
             plane_peer(here ^ flip),
         )
         move.start()
         started.append(move)
 
-    def landed(z_from, place):
-        block = whole_ref.at[z_from, place]
-        remote(block, block, z_send.at[0], recvs.at[z_from, place], z_peer(1)).wait_recv()
+    def landed(a, z_from, place):
+        block = wholes[a].at[z_from, place]
+        remote(block, block, z_send.at[a, 0], recvs.at[a, z_from, place], z_peer(1)).wait_recv()
 
     froms = [z_index ^ flip for flip in range(n_dp)]
-    for n, z_from in enumerate(froms):
-        if n > 0:
-            landed(z_from, here)
-        source = in_ref if n == 0 else None
-        pass_on(0, 2, z_from, here, source)
-        pass_on(1, 4, z_from, here, source)
-        pass_on(2, 1, z_from, here, source)
-    for n, z_from in enumerate(froms):
-        landed(z_from, here ^ 2)
-        if n % 2 == 1:
-            pass_on(1, 4, z_from, here ^ 2)
-        pass_on(2, 1, z_from, here ^ 2)
-        landed(z_from, here ^ 4)
-        if n % 2 == 0:
-            pass_on(0, 2, z_from, here ^ 4)
-        pass_on(2, 1, z_from, here ^ 4)
-    for z_from in froms:
-        landed(z_from, here ^ 6)
-        pass_on(2, 1, z_from, here ^ 6)
-    for place in (1, 3, 5, 7):
+    for a in range(2):
+        for lane, flip in enumerate((2, 4, 1)):
+            pass_on(a, lane, flip, z_index, here, parts[a])
+    ranks_ref[...] = rank_tables(routes_ref[...], plane, own_row_ref, own_column_ref)
+    cast_halves(gate_ref, gate_halves_ref, loaded, made, load_sems, store_sems)
+    for a in range(2):
+        for z_from in froms[1:]:
+            landed(a, z_from, here)
+            for lane, flip in enumerate((2, 4, 1)):
+                pass_on(a, lane, flip, z_from, here)
+    cast_halves(up_ref, up_halves_ref, loaded, made, load_sems, store_sems)
+    for a in range(2):
+        for n, z_from in enumerate(froms):
+            landed(a, z_from, here ^ 2)
+            if n % 2 == 1:
+                pass_on(a, 1, 4, z_from, here ^ 2)
+            pass_on(a, 2, 1, z_from, here ^ 2)
+            landed(a, z_from, here ^ 4)
+            if n % 2 == 0:
+                pass_on(a, 0, 2, z_from, here ^ 4)
+            pass_on(a, 2, 1, z_from, here ^ 4)
+    routing.wait()
+    rank_tables(partner_routes[...], plane, partner_row_ref, partner_column_ref)
+    cast_halves(down_ref, down_halves_ref, loaded_wide, made_wide, load_sems, store_sems)
+    for a in range(2):
         for z_from in froms:
-            landed(z_from, here ^ place)
-    for flip in range(1, n_dp):
-        z_from = z_index ^ flip
-        remote(out_part_ref, out_ref.at[z_from], o_send.at[0], o_recv.at[z_from], z_peer(1)).wait_recv()
+            landed(a, z_from, here ^ 6)
+            pass_on(a, 2, 1, z_from, here ^ 6)
+    for a in range(2):
+        for place in (1, 3, 5, 7):
+            for z_from in froms:
+                landed(a, z_from, here ^ place)
     for move in started:
         move.wait_send()
     for copy in keep:
         copy.wait()
-    routing.wait()
-
-
-def gather_parts(part_in, part_out, routes, n_dp, plane):
+    cot_pair.wait()
+
+
+def gather_parts(routes, part_in, part_out, weights, cot, n_dp, n_context, plane):
+    tokens = routes.shape[1]
+    vmem = pl.BlockSpec(memory_space=pltpu.VMEM)
     anywhere = pl.BlockSpec(memory_space=pl.ANY)
+    shape = jax.ShapeDtypeStruct
+    dma = pltpu.SemaphoreType.DMA
+    row, column = shape((2, plane, tokens), BF), shape((2, tokens, plane), BF)
+    mine = weights[0].shape[1] // n_context
+    rows, width = 64, weights[0].shape[2]
     return pl.pallas_call(
-        functools.partial(gather_kernel, n_dp),
-        in_specs=[anywhere] * 3,
-        out_specs=[anywhere] * 3,
-        out_shape=[
-            jax.ShapeDtypeStruct((n_dp, plane) + part_in.shape, BF),
-            jax.ShapeDtypeStruct((n_dp,) + part_out.shape, BF),
-            jax.ShapeDtypeStruct(routes.shape, routes.dtype),
+        functools.partial(gather_kernel, n_dp, plane),
+        in_specs=[vmem] + [anywhere] * 6,
+        out_specs=[vmem] * 5 + [anywhere] * 6,
+        out_shape=[shape((EXPERTS, tokens), F32), row, column, row, column]
+        + [shape((n_dp, plane) + part.shape, BF) for part in (part_in, part_out)]
+        + [shape((2, mine // 2, w.shape[0], w.shape[2]), BF) for w in weights]
+        + [shape((tokens // 2, D), BF)],
+        scratch_shapes=[
+            pltpu.VMEM(routes.shape, routes.dtype),
+            pltpu.VMEM((2, rows, 8, width), F32),
+            pltpu.VMEM((2, 2, mine // 2, rows, width), BF),
+            pltpu.VMEM((2, rows // 2, 8, 2 * width), F32),
+            pltpu.VMEM((2, 2, mine // 2, rows // 2, 2 * width), BF),
+            dma((2,)),
+            dma((2, 2)),
+            dma((2,)),
+            dma((2, n_dp)),
+            dma((2, 3, n_dp, plane)),
+            dma((2, n_dp, plane)),
+            dma((4,)),
         ],
-        scratch_shapes=[
-            pltpu.SemaphoreType.DMA((2,)),
-            pltpu.SemaphoreType.DMA((n_dp,)),
-            pltpu.SemaphoreType.DMA((n_dp,)),
-            pltpu.SemaphoreType.DMA((n_dp,)),
-            pltpu.SemaphoreType.DMA((3, n_dp, plane)),
-            pltpu.SemaphoreType.DMA((n_dp, plane)),
-            pltpu.SemaphoreType.DMA((2,)),
-        ],
-        compiler_params=pltpu.CompilerParams(collective_id=3, has_side_effects=True),
+        compiler_params=pltpu.CompilerParams(
+            vmem_limit_bytes=60 * 1024 * 1024, collective_id=3, has_side_effects=True
+        ),
         name="gather_parts",
-    )(part_in, part_out, routes)
-
-
-def dispatch_kernel(plane, n_dp, riders, *refs):
-    (normed_ref, cot_ref, cot_partner_ref, own_rank_ref, partner_rank_ref), refs = refs[:5], refs[5:]
+    )(routes, part_in, part_out, *weights, cot)
+
+
+def front_kernel(n_dp, prompt_len, riders, *refs):
+    (x_ref, cos_ref, sin_ref, w_in_ref, w_out_ref, cot_ref), refs = refs[:6], refs[6:]
     sources, refs = refs[: len(riders)], refs[len(riders) :]
-    landed, staged, targets = refs[:4], refs[4:8], refs[8 : 8 + len(riders)]
-    refs = refs[8 + len(riders) :]
-    stage, normed_partner, pair_sems, stage_sems, local_sems, send_sems, recv_sems, ride_send, ride_recv = refs
-    here = plane_here()
-    greet([plane_peer(here ^ flip) for flip in range(1, plane)] + dp_peers(n_dp))
+    (
+        gains_ref,
+        normed_one_ref,
+        qkv_ref,
+        kv_ref,
+        attended_ref,
+        log_ref,
+        normed_two_ref,
+        logits_ref,
+        mid_ref,
+        cot_partner_ref,
+    ), refs = refs[:10], refs[10:]
+    targets, refs = refs[: len(riders)], refs[len(riders) :]
+    (
+        columns_buf,
+        small,
+        w_out,
+        mid_block,
+        load_sems,
+        column_sems,
+        pair_sems,
+        kv_send,
+        kv_recv,
+        ride_send,
+        ride_recv,
+    ) = refs
+    block_index = lax.axis_index("context")
+    n_context = prompt_len // PBLK
+    tokens = x_ref.shape[0]
+    width = qkv_ref.shape[1]
+    greet([context_peer(flip) for flip in range(1, n_context)] + dp_peers(n_dp))
+    load_small = pltpu.make_async_copy(w_in_ref.at[:, pl.ds(width, 128)], small, load_sems.at[0])
+    load_out = pltpu.make_async_copy(w_out_ref, w_out, load_sems.at[1])
+    step_width = columns_buf.shape[2]
+    steps = width // step_width
+    kv_steps = (width - D) // step_width
+
+    def place_of(n):
+        return lax.rem(n + steps - kv_steps, steps)
+
+    def load_columns(n):
+        slot = lax.rem(n, 2)
+        start = pl.multiple_of(place_of(n) * step_width, step_width)
+        return pltpu.make_async_copy(
+            w_in_ref.at[:, pl.ds(start, step_width)], columns_buf.at[slot], column_sems.at[slot]
+        )
+
+    load_small.start()
+    load_columns(0).start()
+    load_out.start()
+    half = cot_partner_ref.shape[0]
     pair = remote(
-        normed_ref, normed_partner, pair_sems.at[0], pair_sems.at[1], {"dp": lax.axis_index("dp") ^ 1}
+        cot_ref.at[pl.ds(half, half)],
+        cot_partner_ref,
+        pair_sems.at[0],
+        pair_sems.at[1],
+        {"dp": lax.axis_index("dp") ^ 1},
     )
     pair.start()
     moves = dp_moves(sources, targets, riders, ride_send, ride_recv)
     for move in moves:
         move.start()
+    load_small.wait()
+    picked = lax.broadcasted_iota(jnp.int32, (8, 128), 1) - lax.broadcasted_iota(jnp.int32, (8, 128), 0)
+    gains_ref[...] = mxu(jnp.where(picked == EXPERTS, 1.0, 0.0).astype(BF), small[...], ((1,), (1,)))
+
+    def normed(rows, gain):
+        scale = lax.rsqrt(jnp.mean(rows * rows, axis=-1, keepdims=True) + epsilon)
+        return (rows * scale * gain).astype(BF)
+
+    def block_rows(n):
+        return pl.ds(pl.multiple_of(n * PBLK, PBLK), PBLK)
+
+    def first_norm(n, carry):
+        rows = block_rows(n)
+        normed_one_ref[rows, :] = normed(x_ref[rows, :].astype(F32), gains_ref[0:1, :])
+        return carry
+
+    lax.fori_loop(0, tokens // PBLK, first_norm, 0)
+
+    def project(n, carry):
+        @pl.when(n + 1 < steps)
+        def _():
+            load_columns(n + 1).start()
+
+        load_columns(n).wait()
+        place = place_of(n)
+        product = mxu(normed_one_ref[...], columns_buf[lax.rem(n, 2)])
+        is_value = place == steps - kv_steps // 2
+        cosine = jnp.where(is_value, 1.0, cos_ref[...])
+        sine = jnp.where(is_value, 0.0, sin_ref[...])
+        factor = jnp.where(place < steps - kv_steps, 1.0 / math.sqrt(HD), 1.0)
+        for half in range(step_width // HD):
+            part = product[:, half * HD : (half + 1) * HD]
+            start = pl.multiple_of(place * step_width + half * HD, HD)
+            qkv_ref[:, pl.ds(start, HD)] = (turn(part, cosine, sine) * factor).astype(BF)
+        return carry
+
+    lax.fori_loop(0, kv_steps, project, 0)
+    own_keys = pl.ds(pl.multiple_of(block_index * PBLK, PBLK), PBLK)
+    kv_ref[own_keys, :] = qkv_ref[:PBLK, D:]
+    kv_ref[prompt_len:, :] = qkv_ref[PBLK:, D:]
+    kv_moves = [
+        remote(
+            kv_ref.at[own_keys],
+            kv_ref.at[own_keys],
+            kv_send.at[flip],
+            kv_recv.at[flip],
+            context_peer(flip),
+        )
+        for flip in range(1, n_context)
+    ]
+    for move in kv_moves:
+        move.start()
+    lax.fori_loop(kv_steps, steps, project, 0)
+    for move in kv_moves:
+        move.wait()
+    log_ref[...] = jnp.zeros_like(log_ref)
+
+    def through_head(head, carry):
+        columns = pl.ds(pl.multiple_of(head * HD, HD), HD)
+        group = head // (HEADS // KVH)
+        key_columns = pl.ds(pl.multiple_of(group * HD, HD), HD)
+        value_columns = pl.ds(pl.multiple_of(KVH * HD + group * HD, HD), HD)
+        for first_row, keys in row_blocks(prompt_len):
+            rows = slice(first_row, first_row + PBLK)
+            scores = mxu(qkv_ref[rows, columns], kv_ref[:keys, key_columns], ((1,), (1,)))
+            scores = masked_scores(scores, first_row, prompt_len, block_index)
+            top = jnp.max(scores, axis=-1, keepdims=True)
+            unnormed = jnp.exp(scores - top)
+            total = jnp.sum(unnormed, axis=-1, keepdims=True)
+            mixed = mxu(unnormed.astype(BF), kv_ref[:keys, value_columns]) / total
+            attended_ref[rows, columns] = mixed.astype(BF)
+            lane = lax.broadcasted_iota(jnp.int32, (PBLK, log_ref.shape[1]), 1)
+            log_ref[rows, :] = jnp.where(lane == head, top + jnp.log(total), log_ref[rows, :])
+        return carry
+
+    lax.fori_loop(0, HEADS, through_head, 0)
+    load_out.wait()
+
+    def second_norm(n, carry):
+        rows = block_rows(n)
+        mid = x_ref[rows, :].astype(F32) + mxu(attended_ref[rows, :], w_out[...])
+        mid_block[...] = mid
+        store = pltpu.make_async_copy(mid_block, mid_ref.at[rows], load_sems.at[2])
+        store.start()
+        low = normed(mid, gains_ref[1:2, :])
+        normed_two_ref[rows, :] = low
+        logits_ref[rows, :] = mxu(low, small[...])
+        store.wait()
+        return carry
+
+    lax.fori_loop(0, tokens // PBLK, second_norm, 0)
+    pair.wait()
+    for move in moves:
+        move.wait()
+
+
+def front(prompt_len, n_dp, x_low, cosine, sine, w_in, w_out, cot, riders):
+    tokens = x_low.shape[0]
+    width = D + 2 * KVH * HD
+    key_rows = prompt_len + CONT
+    n_context = prompt_len // PBLK
+    vmem = pl.BlockSpec(memory_space=pltpu.VMEM)
+    anywhere = pl.BlockSpec(memory_space=pl.ANY)
+    shape = jax.ShapeDtypeStruct
+    dma = pltpu.SemaphoreType.DMA
+    return pl.pallas_call(
+        functools.partial(front_kernel, n_dp, prompt_len, [(index, flip) for _, index, flip in riders]),
+        in_specs=[vmem] * 3 + [anywhere] * (3 + len(riders)),
+        out_specs=[vmem] * 8 + [anywhere] * (2 + len(riders)),
+        out_shape=[
+            shape((8, D), F32),
+            shape((tokens, D), BF),
+            shape((tokens, width), BF),
+            shape((key_rows, 2 * KVH * HD), BF),
+            shape((tokens, D), BF),
+            shape((tokens, 128), F32),
+            shape((tokens, D), BF),
+            shape((tokens, 128), F32),
+            shape((tokens, D), F32),
+            shape((tokens // 2, D), BF),
+        ]
+        + [shape(picked_shape(array, index), BF) for array, index, _ in riders],
+        scratch_shapes=[
+            pltpu.VMEM((2, D, 2 * HD), BF),
+            pltpu.VMEM((D, 128), BF),
+            pltpu.VMEM((D, D), BF),
+            pltpu.VMEM((PBLK, D), F32),
+            dma((3,)),
+            dma((2,)),
+            dma((2,)),
+            dma((n_context,)),
+            dma((n_context,)),
+            dma((len(riders),)),
+            dma((len(riders),)),
+        ],
+        compiler_params=pltpu.CompilerParams(
+            vmem_limit_bytes=56 * 1024 * 1024, collective_id=8, has_side_effects=True
+        ),
+        name="front",
+    )(x_low, cosine, sine, w_in, w_out, cot, *[array for array, _, _ in riders])
+
+
+def dispatch_kernel(plane, n_dp, riders, *refs):
+    normed_ref, cot_ref, own_rank_ref, partner_rank_ref, gates_ref, other_gates_ref = refs[:6]
+    cot_halves, refs = refs[6:8], refs[8:]
+    sources, refs = refs[: len(riders)], refs[len(riders) :]
+    gates_here_ref, refs = refs[0], refs[1:]
+    landed, staged, targets = refs[:4], refs[4:8], refs[8 : 8 + len(riders)]
+    (
+        stage,
+        normed_partner,
+        pair_sems,
+        stage_sems,
+        local_sems,
+        send_sems,
+        recv_sems,
+        ride_send,
+        ride_recv,
+        all_gates,
+        partner_gates,
+        gate_sems,
+        gate_send,
+        gate_recv,
+        cot_partner,
+        cot_sems,
+    ) = refs[8 + len(riders) :]
+    here = plane_here()
+    greet([plane_peer(here ^ flip) for flip in range(1, plane)] + dp_peers(n_dp))
+    partner = {"dp": lax.axis_index("dp") ^ 1}
+    gate_pair = remote(other_gates_ref, partner_gates, gate_sems.at[0], gate_sems.at[1], partner)
+    gate_pair.start()
+    pair = remote(normed_ref, normed_partner, pair_sems.at[0], pair_sems.at[1], partner)
+    pair.start()
+    moves = dp_moves(sources, targets, riders, ride_send, ride_recv)
+    for move in moves:
+        move.start()
+    half = cot_halves[0].shape[0]
+    cot_loads = [
+        pltpu.make_async_copy(part, cot_partner.at[pl.ds(n * half, half)], cot_sems.at[n])
+        for n, part in enumerate(cot_halves)
+    ]
+    for load in cot_loads:
+        load.start()
     plans = (
         (0, normed_ref, own_rank_ref),
         (1, cot_ref, own_rank_ref),
-        (2, cot_partner_ref, partner_rank_ref),
+        (2, cot_partner, partner_rank_ref),
         (3, normed_partner, partner_rank_ref),
     )
     exchanges = [
@@ -977,6 +1244,9 @@
     copies = [pltpu.make_async_copy(stage.at[4 + n], staged[n], stage_sems.at[n]) for n in range(4)]
     for expert in range(2):
         for n, rows_ref, rank_ref in plans:
+            if expert == 0 and n == 2:
+                for load in cot_loads:
+                    load.wait()
             if expert == 0 and n == 3:
                 pair.wait()
             chooser = slot_matrix(rank_ref[expert], plane, True)
@@ -985,15 +1255,31 @@
                 exchanges[n][0]()
             else:
                 copies[n].start()
+    gate_pair.wait()
+    all_gates[:, 0:2, :] = gates_ref[...]
+    all_gates[:, 2:4, :] = partner_gates[...]
+    gates_here_ref[here] = all_gates[here]
+    gate_moves = [
+        remote(
+            all_gates.at[here ^ flip],
+            gates_here_ref.at[here],
+            gate_send.at[flip],
+            gate_recv.at[flip],
+            plane_peer(here ^ flip),
+        )
+        for flip in range(1, plane)
+    ]
+    for move in gate_moves:
+        move.start()
     for copy in copies:
         copy.wait()
     for _, finish in exchanges:
         finish()
-    for move in moves:
+    for move in gate_moves + moves:
         move.wait()
 
 
-def dispatch_rows(normed, cot, cot_partner, own_ranks, partner_ranks, riders, n_dp):
+def dispatch_rows(normed, cot, cot_halves, own_ranks, partner_ranks, gates, other_gates, riders, n_dp):
     plane, tokens = own_ranks.shape[1:]
     vmem = pl.BlockSpec(memory_space=pltpu.VMEM)
     anywhere = pl.BlockSpec(memory_space=pl.ANY)
@@ -1001,9 +1287,10 @@
     dma = pltpu.SemaphoreType.DMA
     results = pl.pallas_call(
         functools.partial(dispatch_kernel, plane, n_dp, [(index, flip) for _, index, flip in riders]),
-        in_specs=[vmem] * 5 + [anywhere] * len(riders),
-        out_specs=[anywhere] * (8 + len(riders)),
-        out_shape=[shape((plane, SLOTS, D), BF)] * 8
+        in_specs=[vmem] * 6 + [anywhere] * (2 + len(riders)),
+        out_specs=[vmem] + [anywhere] * (8 + len(riders)),
+        out_shape=[shape((plane, 4, gates.shape[2]), F32)]
+        + [shape((plane, SLOTS, D), BF)] * 8
         + [shape(picked_shape(array, index), BF) for array, index, _ in riders],
         scratch_shapes=[
             pltpu.VMEM((8, plane, SLOTS, D), BF),
@@ -1015,21 +1302,38 @@
             dma((4, plane)),
             dma((len(riders),)),
             dma((len(riders),)),
+            pltpu.VMEM((plane, 4, gates.shape[2]), F32),
+            pltpu.VMEM(gates.shape, F32),
+            dma((2,)),
+            dma((plane,)),
+            dma((plane,)),
+            pltpu.VMEM((tokens, D), BF),
+            dma((2,)),
         ],
         compiler_params=pltpu.CompilerParams(
-            vmem_limit_bytes=VMEM_BYTES, collective_id=1, has_side_effects=True
+            vmem_limit_bytes=56 * 1024 * 1024, collective_id=1, has_side_effects=True
         ),
         cost_estimate=pl.CostEstimate(flops=2 * 10**10, bytes_accessed=4 * 10**8, transcendentals=0),
         name="dispatch_rows",
-    )(normed, cot, cot_partner, own_ranks, partner_ranks, *[array for array, _, _ in riders])
-    return results[:4], results[4:8], results[8:]
-
-
-def return_kernel(plane, n_dp, riders, own_rank_ref, partner_rank_ref, dots_ref, *refs):
-    early, back, results = refs[0:2], refs[2:4], refs[4:6]
-    sources, refs = refs[6 : 6 + len(riders)], refs[6 + len(riders) :]
-    total_ref, dots_here_ref, dots_other_ref = refs[:3]
-    results_back, targets = refs[3:5], refs[5 : 5 + len(riders)]
+    )(
+        normed, cot, own_ranks, partner_ranks, gates, other_gates, *cot_halves, *[a for a, _, _ in riders]
+    )
+    return results[0], results[1:5], results[5:9], results[9:]
+
+
+def return_kernel(
+    plane, n_dp, n_results, riders, names, own_rank_ref, partner_rank_ref, dots_ref, ranks_ref, gates_ref, *refs
+):
+    early, back = refs[0:2], refs[2:4]
+    results, refs = refs[4 : 4 + n_results], refs[4 + n_results :]
+    sources, refs = refs[: len(riders)], refs[len(riders) :]
+    mine, refs = refs[:3], refs[3:]
+    arrived, refs = refs[: len(HOME_SECOND)], refs[len(HOME_SECOND) :]
+    total_ref, dlog_ref, part_ref = refs[:3]
+    results_back, refs = refs[3 : 3 + n_results], refs[3 + n_results :]
+    targets = refs[: len(riders)]
+    homes = dict(zip(HOME_SECOND, arrived))
+    homes.update(zip(names, targets))
     (
         held,
         to_partner,
@@ -1044,7 +1348,14 @@
         dot_sems,
         dot_send,
         dot_recv,
-    ) = refs[5 + len(riders) :]
+        dots_here_ref,
+        dots_other_ref,
+        bounce,
+        summed,
+        sums,
+        piece_sems,
+        sum_sems,
+    ) = refs[len(riders) :]
     here = plane_here()
     partner = {"dp": lax.axis_index("dp") ^ 1}
     greet([plane_peer(here ^ flip) for flip in range(1, plane)] + dp_peers(n_dp))
@@ -1069,13 +1380,11 @@
         exchanges[side] = plane_exchange(
             side, back[side], held.at[2 * side + 1], local_sems, send_sems, recv_sems
         )
-        exchanges[side][0]()
+    exchanges[1][0]()
     later = [
-        plane_exchange(2 + side, results[side], results_back[side], local_sems, send_sems, recv_sems)
-        for side in range(2)
+        plane_exchange(2 + n, results[n], results_back[n], local_sems, send_sems, recv_sems, bounce)
+        for n in range(n_results)
     ]
-    for begin, _ in later:
-        begin()
     moves = dp_moves(sources, targets, riders, ride_send, ride_recv)
     own_dots.wait()
     for move in dot_moves:
@@ -1083,50 +1392,93 @@
     dots_pair = remote(dots_here_ref, dots_other_ref, dot_sems.at[1], dot_sems.at[2], partner)
     dots_pair.start()
 
-    def collect(rank_ref, side, target, kind):
-        loads[side].wait()
-        exchanges[side][1]()
-
-        def block(n, carry):
-            rows = pl.ds(pl.multiple_of(n * PBLK, PBLK), PBLK)
-            made = jnp.zeros((PBLK, D), F32)
-            for expert in range(2):
-                chooser = slot_matrix(rank_ref[expert, rows, :], plane, False)
-                made = made + mxu(chooser, held[2 * side + expert].reshape(plane * SLOTS, D))
-            target[rows, :] = made.astype(kind)
-            return carry
-
-        lax.fori_loop(0, total_ref.shape[0] // PBLK, block, 0)
-
-    for move in moves[: len(moves) // 2]:
+    def sum_matrix(which):
+        sources = [mine[which].at[0]] + [homes[which, flip, 0] for flip in range(1, n_dp)]
+        copies = [
+            pltpu.make_async_copy(source, summed.at[n], piece_sems.at[n]) for n, source in enumerate(sources)
+        ]
+        for copy in copies:
+            copy.start()
+        for copy in copies:
+            copy.wait()
+        parity = lax.rem(lax.axis_index("dp"), 2)
+        stores = []
+        for side in range(2):
+            total = summed[side].astype(F32)
+            for n in range(side + 2, n_dp, 2):
+                total = total + summed[n].astype(F32)
+            sums[side] = total.astype(BF)
+            place = parity if side == 0 else 1 - parity
+            stores.append(pltpu.make_async_copy(sums.at[side], part_ref.at[place, which], sum_sems.at[side]))
+            stores[-1].start()
+        for store in stores:
+            store.wait()
+
+    def of_gates():
+        tokens = ranks_ref.shape[0]
+        parity = lax.rem(lax.axis_index("dp"), 2)
+        owned = EXPERTS // plane
+        slot = lax.broadcasted_iota(jnp.int32, (tokens, 128), 1).astype(F32)
+        lane = lax.broadcasted_iota(jnp.int32, (tokens, EXPERTS), 1)
+        made = jnp.zeros((tokens, EXPERTS), F32)
+        for expert in range(EXPERTS):
+            place, side, i = expert // owned, expert % owned // 2, expert % 2
+            row = jnp.where(
+                parity == side,
+                dots_here_ref[place, i : i + 1, :],
+                dots_other_ref[place, 2 + i : 3 + i, :],
+            )
+            hit = ranks_ref[:, expert : expert + 1] == slot
+            value = jnp.sum(jnp.where(hit, row, 0.0), axis=-1, keepdims=True)
+            made = jnp.where(lane == expert, value, made)
+        gates = gates_ref[...]
+        mean = jnp.sum(gates * made, axis=-1, keepdims=True)
+        dlog_ref[...] = jnp.zeros_like(dlog_ref)
+        dlog_ref[:, :EXPERTS] = (gates * (made - mean)).astype(BF)
+
+    for move in moves[:RETURN_FIRST]:
         move.start()
-    collect(partner_rank_ref, 1, to_partner, BF)
+    sum_matrix(0)
+    loads[1].wait()
+    exchanges[1][1]()
+    exchanges[0][0]()
+    collect_into(plane, partner_rank_ref, held, 2, to_partner, lambda rows, made: made.astype(BF))
     pair = remote(to_partner, of_partner, pair_sems.at[0], pair_sems.at[1], partner)
     pair.start()
-    for move in moves[len(moves) // 2 :]:
+    for move in moves[RETURN_FIRST:]:
         move.start()
-    collect(own_rank_ref, 0, total_ref, F32)
+    for begin, _ in later:
+        begin()
+    loads[0].wait()
+    exchanges[0][1]()
+    collect_into(plane, own_rank_ref, held, 0, total_ref, lambda rows, made: made)
+    dots_pair.wait()
+    of_gates()
     pair.wait()
     total_ref[...] += of_partner[...].astype(F32)
-    dots_pair.wait()
     for _, finish in later:
         finish()
     for move in moves:
         move.wait()
-
-
-def return_rows(own_ranks, partner_ranks, dots, early, back, results, riders, n_dp):
+    sum_matrix(1)
+    sum_matrix(2)
+
+
+def return_rows(
+    own_ranks, partner_ranks, dots, ranks, gates, early, back, results, riders, names, shares, arrived, n_dp
+):
     tokens, plane = own_ranks.shape[1:]
     vmem = pl.BlockSpec(memory_space=pltpu.VMEM)
     anywhere = pl.BlockSpec(memory_space=pl.ANY)
     shape = jax.ShapeDtypeStruct
     dma = pltpu.SemaphoreType.DMA
     outcome = pl.pallas_call(
-        functools.partial(return_kernel, plane, n_dp, [(index, flip) for _, index, flip in riders]),
-        in_specs=[vmem, vmem, vmem] + [anywhere] * (6 + len(riders)),
-        out_specs=[vmem, vmem, vmem] + [anywhere] * (2 + len(riders)),
-        out_shape=[shape((tokens, D), F32)]
-        + [shape(dots.shape, F32)] * 2
+        functools.partial(
+            return_kernel, plane, n_dp, len(results), [(index, flip) for _, index, flip in riders], names
+        ),
+        in_specs=[vmem] * 5 + [anywhere] * (7 + len(results) + len(riders) + len(arrived)),
+        out_specs=[vmem] * 2 + [anywhere] * (1 + len(results) + len(riders)),
+        out_shape=[shape((tokens, D), F32), shape((tokens, 128), BF), shape((2, 3) + shares[0].shape[1:], BF)]
         + [shape(rows.shape, BF) for rows in results]
         + [shape(picked_shape(array, index), BF) for array, index, _ in riders],
         scratch_shapes=[
@@ -1143,14 +1495,34 @@
             dma((3,)),
             dma((plane,)),
             dma((plane,)),
+            pltpu.VMEM(dots.shape, F32),
+            pltpu.VMEM(dots.shape, F32),
+            pltpu.VMEM((2 + len(results), SLOTS, D), BF),
+            pltpu.VMEM(shares[0].shape, BF),
+            pltpu.VMEM((2,) + shares[0].shape[1:], BF),
+            dma((n_dp,)),
+            dma((2,)),
         ],
         compiler_params=pltpu.CompilerParams(
-            vmem_limit_bytes=VMEM_BYTES, collective_id=2, has_side_effects=True
+            vmem_limit_bytes=56 * 1024 * 1024, collective_id=2, has_side_effects=True
         ),
         cost_estimate=pl.CostEstimate(flops=3 * 10**10, bytes_accessed=4 * 10**8, transcendentals=0),
         name="return_rows",
-    )(own_ranks, partner_ranks, dots, *early, *back, *results, *[array for array, _, _ in riders])
-    return outcome[0], outcome[1], outcome[2], outcome[3:5], outcome[5:]
+    )(
+        own_ranks,
+        partner_ranks,
+        dots,
+        ranks,
+        gates,
+        *early,
+        *back,
+        *results,
+        *[array for array, _, _ in riders],
+        *shares,
+        *arrived,
+    )
+    last = 3 + len(results)
+    return outcome[0], outcome[1], outcome[2], outcome[3:last], outcome[last:]
 
 
 def normed_back(rows, gain, grads):
@@ -1164,40 +1536,37 @@
     return {"context": lax.axis_index("context") ^ flip}
 
 
-def share_context(part_ref, all_ref, sems, sends, recvs):
+def share_context(part, place_of, sends, recvs):
     here = lax.axis_index("context")
-    own = pltpu.make_async_copy(part_ref, all_ref.at[here], sems)
-    own.start()
-    across = remote(part_ref, all_ref.at[here], sends.at[0], recvs.at[here], context_peer(2))
-    across.start()
-    beside = remote(part_ref, all_ref.at[here], sends.at[1], recvs.at[here], context_peer(1))
-    beside.start()
+    across = remote(part, place_of(here), sends.at[0], recvs.at[here], context_peer(2))
+    beside = remote(part, place_of(here), sends.at[1], recvs.at[here], context_peer(1))
+    block = place_of(here ^ 2)
+    onward = remote(block, block, sends.at[2], recvs.at[here ^ 2], context_peer(1))
+
+    def begin():
+        across.start()
+        beside.start()
 
     def pass_on():
-        block = all_ref.at[here ^ 2]
-        remote(part_ref, block, sends.at[0], recvs.at[here ^ 2], context_peer(2)).wait_recv()
-        remote(block, block, sends.at[2], recvs.at[here ^ 2], context_peer(1)).start()
+        remote(part, block, sends.at[0], recvs.at[here ^ 2], context_peer(2)).wait_recv()
+        onward.start()
 
     def finish():
-        block = all_ref.at[here ^ 2]
         for flip in (1, 3):
-            remote(part_ref, all_ref.at[here ^ flip], sends.at[1], recvs.at[here ^ flip], context_peer(1)).wait_recv()
+            remote(part, place_of(here ^ flip), sends.at[1], recvs.at[here ^ flip], context_peer(1)).wait_recv()
         across.wait_send()
         beside.wait_send()
-        remote(block, block, sends.at[2], recvs.at[here ^ 2], context_peer(1)).wait_send()
-        own.wait()
-
-    return pass_on, finish
+        onward.wait_send()
+
+    return begin, pass_on, finish
 
 
 def backward_kernel(n_dp, prompt_len, riders, *refs):
     (
         dlog_ref,
-        router_ref,
         cot_ref,
         x_ref,
-        gain_one_ref,
-        gain_two_ref,
+        gains_in_ref,
         attended_ref,
         qkv_ref,
         kv_ref,
@@ -1209,12 +1578,14 @@
         total_ref,
         w_out_ref,
         w_in_ref,
-        four_ref,
-    ) = refs[:18]
+        part_ref,
+    ) = refs[:16]
+    results, refs = refs[16:18], refs[18:]
     late = len(riders)
-    sources, refs = refs[18 : 18 + late], refs[18 + late :]
+    sources, refs = refs[:late], refs[late:]
     grad_x_ref, gains_ref, grad_out_ref, grad_in_ref, all_ref = refs[:5]
-    homes, refs = refs[5 : 5 + late], refs[5 + late :]
+    results_back, refs = refs[5:7], refs[7:]
+    homes, refs = refs[:late], refs[late:]
     (
         weights,
         grad_mid,
@@ -1231,16 +1602,26 @@
         kv_recv_sems,
         home_send,
         home_recv,
-        own_sem,
         share_sends,
         share_recvs,
+        small,
+        bounce,
+        local_sems,
+        send_sems,
+        recv_sems,
     ) = refs
     block_index = lax.axis_index("context")
     n_context = kv_send.shape[0]
     tokens = x_ref.shape[0]
     heads_width = HEADS * HD
     kv_width = KVH * HD
-    greet([context_peer(flip) for flip in range(1, n_context)] + dp_peers(n_dp))
+    here = plane_here()
+    plane = results[0].shape[0]
+    greet([plane_peer(here ^ flip) for flip in range(1, plane)] + dp_peers(n_dp))
+    load_small = pltpu.make_async_copy(
+        w_in_ref.at[:, pl.ds(weights.shape[1], 128)], small, load_sems.at[4]
+    )
+    load_small.start()
     load_total = pltpu.make_async_copy(total_ref, grad_mid, load_sems.at[0])
     load_out = pltpu.make_async_copy(w_out_ref, weights.at[:, pl.ds(0, D)], load_sems.at[1])
     load_in = pltpu.make_async_copy(w_in_ref.at[:, pl.ds(0, weights.shape[1])], weights, load_sems.at[2])
@@ -1249,7 +1630,15 @@
     homing = dp_moves(sources, homes, riders, home_send, home_recv)
     for move in homing:
         move.start()
-    pass_on, finish = share_context(four_ref, all_ref, own_sem.at[0], share_sends, share_recvs)
+    begin_all, pass_on, finish = share_context(
+        part_ref, lambda place: all_ref.at[place], share_sends, share_recvs
+    )
+    begin_all()
+    exchanges = [
+        plane_exchange(side, results[side], results_back[side], local_sems, send_sems, recv_sems, bounce)
+        for side in range(2)
+    ]
+    load_small.wait()
     load_total.wait()
     load_out.wait()
     gains_ref[...] = jnp.zeros_like(gains_ref)
@@ -1262,8 +1651,8 @@
         load_mid = pltpu.make_async_copy(mid_ref.at[rows], mid_block, load_sems.at[3])
         load_mid.start()
         load_mid.wait()
-        grads = grad_mid[rows, :] + mxu(dlog_ref[rows, :], router_ref[...], ((1,), (1,)))
-        by_rows, by_gain = normed_back(mid_block[...], gain_two_ref[...], grads)
+        grads = grad_mid[rows, :] + mxu(dlog_ref[rows, :], small[...], ((1,), (1,)))
+        by_rows, by_gain = normed_back(mid_block[...], gains_in_ref[1:2, :], grads)
         gains_ref[1:2, :] += jnp.sum(by_gain, axis=0, keepdims=True)
         by_mid = cot_ref[rows, :].astype(F32) + by_rows
         grad_mid[rows, :] = by_mid
@@ -1315,7 +1704,8 @@
     ]
     for move in kv_moves:
         move.start()
-    pass_on()
+    for begin, _ in exchanges:
+        begin()
 
     quarter = D // n_dp
 
@@ -1364,18 +1754,21 @@
     def through_first(n, carry):
         rows = block_rows(n)
         grads = mxu(grad_qkv[rows, :], weights[...], ((1,), (1,)))
-        by_rows, by_gain = normed_back(x_ref[rows, :].astype(F32), gain_one_ref[...], grads)
+        by_rows, by_gain = normed_back(x_ref[rows, :].astype(F32), gains_in_ref[0:1, :], grads)
         gains_ref[0:1, :] += jnp.sum(by_gain, axis=0, keepdims=True)
         grad_x_ref[rows, :] = (grad_mid[rows, :] + by_rows).astype(BF)
         return carry
 
     lax.fori_loop(0, tokens // PBLK, through_first, 0)
+    pass_on()
     finish()
+    for _, end in exchanges:
+        end()
     for move in homing:
         move.wait()
 
 
-def backward(prompt_len, n_dp, in_vmem, in_hbm, riders):
+def backward(prompt_len, n_dp, in_vmem, in_hbm, results, riders):
     tokens = in_vmem[0].shape[0]
     width = D + 2 * KVH * HD
     n_context = prompt_len // PBLK
@@ -1383,19 +1776,21 @@
     quarter = D // n_dp
     vmem = pl.BlockSpec(memory_space=pltpu.VMEM)
     anywhere = pl.BlockSpec(memory_space=pl.ANY)
-    four = in_hbm[-1]
+    part = in_hbm[-1]
+    plane = results[0].shape[0]
     shape = jax.ShapeDtypeStruct
     return pl.pallas_call(
         functools.partial(backward_kernel, n_dp, prompt_len, [(index, flip) for _, index, flip in riders]),
-        in_specs=[vmem] * len(in_vmem) + [anywhere] * (len(in_hbm) + len(riders)),
-        out_specs=[vmem] * 2 + [anywhere] * (3 + len(riders)),
+        in_specs=[vmem] * len(in_vmem) + [anywhere] * (len(in_hbm) + 2 + len(riders)),
+        out_specs=[vmem] * 2 + [anywhere] * (5 + len(riders)),
         out_shape=[
             shape((tokens, D), BF),
             shape((8, D), F32),
             shape((D, D), BF),
             shape((D, width), BF),
-            shape((n_context,) + four.shape, BF),
+            shape((n_context,) + part.shape, BF),
         ]
+        + [shape(rows.shape, BF) for rows in results]
         + [shape(picked_shape(array, index), BF) for array, index, _ in riders],
         scratch_shapes=[
             pltpu.VMEM((D, width), BF),
@@ -1407,30 +1802,34 @@
             pltpu.VMEM((n_context, PBLK, 2 * KVH * HD), BF),
             pltpu.VMEM((n_context, PBLK, 2 * KVH * HD), BF),
             pltpu.VMEM((quarter, width), BF),
-            pltpu.SemaphoreType.DMA((4,)),
+            pltpu.SemaphoreType.DMA((5,)),
             pltpu.SemaphoreType.DMA((1,)),
             pltpu.SemaphoreType.DMA((n_context,)),
             pltpu.SemaphoreType.DMA((n_context,)),
             pltpu.SemaphoreType.DMA((len(riders),)),
             pltpu.SemaphoreType.DMA((len(riders),)),
-            pltpu.SemaphoreType.DMA((1,)),
             pltpu.SemaphoreType.DMA((3,)),
             pltpu.SemaphoreType.DMA((n_context,)),
+            pltpu.VMEM((D, 128), BF),
+            pltpu.VMEM((2, SLOTS, D), BF),
+            pltpu.SemaphoreType.DMA((2,)),
+            pltpu.SemaphoreType.DMA((2, plane)),
+            pltpu.SemaphoreType.DMA((2, plane)),
         ],
         compiler_params=pltpu.CompilerParams(
             vmem_limit_bytes=56 * 1024 * 1024, collective_id=4, has_side_effects=True
         ),
         name="backward",
-    )(*in_vmem, *in_hbm, *[array for array, _, _ in riders])
+    )(*in_vmem, *in_hbm, *results, *[array for array, _, _ in riders])
 
 
 def reduce_kernel(n_dp, widths, *refs):
     count = len(widths)
     shares, refs = refs[:count], refs[count:]
-    part_ref, for_partner_ref = refs[:2]
-    refs = refs[2:]
+    part_ref, own_rank_ref, partner_rank_ref, mid_ref = refs[:4]
+    rows_of, refs = (refs[4:6], refs[6:8]), refs[8:]
     totals, refs = refs[:count], refs[count:]
-    all_ref, of_partner_ref = refs[:2]
+    result_ref, all_ref = refs[:2]
     refs = refs[2:]
     sums, core_in, first_in, second_in, z_in = (refs[n * count : (n + 1) * count] for n in range(5))
     (
@@ -1445,12 +1844,18 @@
         z_recv,
         out_send,
         out_recv,
-        own_sems,
         share_sends,
         share_recvs,
         pair_sems,
+        held,
+        to_partner,
+        of_partner,
+        mixed,
+        mid_block,
+        held_sems,
     ) = refs[5 * count :]
     here = plane_here()
+    plane = held.shape[1]
     z_index = lax.axis_index("dp")
     greet(
         [plane_peer(here ^ flip) for flip in (1, 2, 4)] + [{"dp": z_index ^ flip} for flip in range(1, n_dp)]
@@ -1474,9 +1879,34 @@
                     plane_peer(here ^ 1),
                 )
                 core_moves[n, a, m].start()
-    pair = remote(for_partner_ref, of_partner_ref, pair_sems.at[0], pair_sems.at[1], {"dp": z_index ^ 1})
+
+    def load_rows(side):
+        copies = [
+            pltpu.make_async_copy(rows_of[side][expert], held.at[expert], held_sems.at[expert])
+            for expert in range(2)
+        ]
+        for copy in copies:
+            copy.start()
+        return copies
+
+    rows_here = load_rows(1)
+    gathers = [
+        share_context(
+            part_ref.at[:, m],
+            lambda place, m=m: all_ref.at[place, :, m],
+            share_sends.at[m],
+            share_recvs.at[m],
+        )
+        for m in range(3)
+    ]
+    gathers[0][0]()
+
+    for copy in rows_here:
+        copy.wait()
+    collect_into(plane, partner_rank_ref, held, 0, to_partner, lambda rows, made: made.astype(BF))
+    pair = remote(to_partner, of_partner, pair_sems.at[0], pair_sems.at[1], {"dp": z_index ^ 1})
     pair.start()
-    all_on, all_done = share_context(part_ref, all_ref, own_sems.at[0], share_sends, share_recvs)
+    rows_here = load_rows(0)
 
     def add(target, *others):
         total = target[...].astype(F32)
@@ -1502,6 +1932,16 @@
                     plane_peer(here ^ toward),
                 )
                 first_moves[n, a, slot].start()
+    for copy in rows_here:
+        copy.wait()
+
+    def with_mid(rows, made):
+        load = pltpu.make_async_copy(mid_ref.at[rows], mid_block, held_sems.at[2])
+        load.start()
+        load.wait()
+        return mid_block[...] + made
+
+    collect_into(plane, own_rank_ref, held, 0, mixed, with_mid)
     for n in order:
         toward = 2 if n % 2 == 0 else 4
         kept = 6 - toward
@@ -1517,7 +1957,9 @@
                 plane_peer(here ^ kept),
             )
             second_moves[n, a].start()
-    all_on()
+    gathers[1][0]()
+    gathers[2][0]()
+    gathers[0][1]()
     for n in order:
         for a in range(count):
             second_moves[n, a].wait_recv()
@@ -1561,16 +2003,20 @@
     for a in range(count):
         landed(a, here ^ 6)
         pass_on(a, 2, 1, here ^ 6)
+    gathers[1][1]()
+    gathers[2][1]()
+    pair.wait()
+    result_ref[...] = (mixed[...] + of_partner[...].astype(F32)).astype(BF)
     for a in range(count):
         for flip in (1, 3, 5, 7):
             landed(a, here ^ flip)
     for move in started:
         move.wait_send()
-    all_done()
-    pair.wait()
-
-
-def reduce_shares(shares, part, for_partner, n_dp, n_context):
+    for _, _, finish in gathers:
+        finish()
+
+
+def reduce_shares(shares, part, ranks, mid, slot_rows, n_dp, n_context):
     plane, rows = shares[0].shape[1:3]
     widths = tuple(share.shape[3] for share in shares)
     count = len(widths)
@@ -1584,12 +2030,12 @@
 
     return pl.pallas_call(
         functools.partial(reduce_kernel, n_dp, widths),
-        in_specs=[anywhere] * (count + 2),
-        out_specs=[vmem] * count + [anywhere] * 2,
+        in_specs=[anywhere] * (count + 1) + [vmem] * 2 + [anywhere] * 5,
+        out_specs=[vmem] * (count + 1) + [anywhere],
         out_shape=[shape((plane, rows, width), BF) for width in widths]
         + [
+            shape(mid.shape, BF),
             shape((n_context,) + part.shape, BF),
-            shape(for_partner.shape, BF),
         ],
         scratch_shapes=buffers(n_dp, 4)
         + buffers(n_dp, 4)
@@ -1608,21 +2054,35 @@
             dma((count, n_dp)),
             dma((count, 3, plane)),
             dma((count, plane)),
-            dma((1,)),
+            dma((3, 3)),
+            dma((3, n_context)),
+            dma((2,)),
+            pltpu.VMEM((2, plane, SLOTS, D), BF),
+            pltpu.VMEM(mid.shape, BF),
+            pltpu.VMEM(mid.shape, BF),
+            pltpu.VMEM(mid.shape, F32),
+            pltpu.VMEM((PBLK, D), F32),
             dma((3,)),
-            dma((n_context,)),
-            dma((2,)),
         ],
         compiler_params=pltpu.CompilerParams(
-            vmem_limit_bytes=VMEM_BYTES, collective_id=5, has_side_effects=True
+            vmem_limit_bytes=56 * 1024 * 1024, collective_id=5, has_side_effects=True
         ),
         name="reduce_shares",
-    )(*shares, part, for_partner)
-
-
-def finish_kernel(down, first_ref, second_ref, out_ref):
+    )(*shares, part, *ranks, mid, *slot_rows[0], *slot_rows[1])
+
+
+def finish_kernel(down, first_ref, second_ref, own_first_ref, own_second_ref, out_ref):
+    n_context = first_ref.shape[0]
     experts = out_ref.shape[1]
-    both = [ref[:, :, 0].astype(F32) for ref in (first_ref, second_ref)]
+    here = lax.axis_index("context")
+
+    def of_expert(all_ref, own_ref):
+        own = own_ref[:, 0].astype(F32)
+        return jnp.stack(
+            [jnp.where(here == place, own, all_ref[place, :, 0].astype(F32)) for place in range(n_context)]
+        )
+
+    both = [of_expert(first_ref, own_first_ref), of_expert(second_ref, own_second_ref)]
     both = jnp.stack(both, axis=2).reshape((experts,) + both[0].shape[2:])
     if not down:
         out_ref[...] = jnp.swapaxes(both, 0, 1)
@@ -1632,35 +2092,30 @@
         out_ref[:, :, side * half : (side + 1) * half] = jnp.swapaxes(both[:, side], 0, 1)
 
 
-def finish_weight(which, first, second):
+def finish_weight(which, first, second, own_first, own_second):
     n_context, pair, _, rows, width = first.shape
     experts = n_context * pair * 2
     step = 32
     down = which == 2
+    parts = (first, second, own_first, own_second)
     if down:
         rows = rows // 2
-        first, second = (part.reshape(part.shape[:3] + (2, rows, width)) for part in (first, second))
+        parts = [part.reshape(part.shape[:-2] + (2, rows, width)) for part in parts]
         spec = pl.BlockSpec((n_context, pair, 1, 2, step, width), lambda j: (0, 0, which, 0, j, 0))
+        own = pl.BlockSpec((pair, 1, 2, step, width), lambda j: (0, which, 0, j, 0))
         width = 2 * width
     else:
         spec = pl.BlockSpec((n_context, pair, 1, step, width), lambda j: (0, 0, which, j, 0))
+        own = pl.BlockSpec((pair, 1, step, width), lambda j: (0, which, j, 0))
     return pl.pallas_call(
         functools.partial(finish_kernel, down),
         grid=(rows // step,),
-        in_specs=[spec, spec],
+        in_specs=[spec, spec, own, own],
         out_specs=pl.BlockSpec((step, experts, width), lambda j: (j, 0, 0)),
         out_shape=jax.ShapeDtypeStruct((rows, experts, width), F32),
         compiler_params=grant(),
         name="finish_weight",
-    )(first, second)
-
-
-def tie(*values):
-    return lax.optimization_barrier(values)
-
-
-def flip_permute(value, axis, size, flip):
-    return lax.ppermute(value, axis, [(i, i ^ flip) for i in range(size)])
+    )(*parts)
 
 
 def local_paired(
@@ -1689,69 +2144,37 @@
     cot_low = cotangent[0]
     route_rows = routes[0]
 
-    small = jnp.concatenate(
-        [router, norm_attn[:, None], norm_moe[:, None]], axis=1
-    ).astype(BF)
-    small = jnp.pad(small, ((0, 0), (0, 128 - small.shape[1])))
-    shard_in = jnp.concatenate([attn_q.astype(BF), attn_k.astype(BF), attn_v.astype(BF), small], axis=1)
     here = lax.axis_index("expert") * n_context + block_index
     part_rows = attn_q.shape[0] // plane
-    part_of = lambda shard: lax.dynamic_slice_in_dim(shard, here * part_rows, part_rows, 0)
-    whole_in, out_parts, partner_routes = gather_parts(
-        part_of(shard_in), part_of(attn_o).astype(BF), route_rows, n_dp, plane
-    )
-    whole_in = whole_in.reshape(-1, shard_in.shape[1])
-    w_out = lax.all_gather(out_parts, PLANE, axis=1, tiled=False).reshape(-1, D)
+
+    def part_of(shard):
+        return lax.dynamic_slice_in_dim(shard, here * part_rows, part_rows, 0).astype(BF)
+
+    part_in = jnp.concatenate(
+        [part_of(attn_q), part_of(attn_k), part_of(attn_v), part_of(router)]
+        + [part_of(norm_attn)[:, None], part_of(norm_moe)[:, None]]
+        + [jnp.zeros((part_rows, 128 - EXPERTS - 2), BF)],
+        axis=1,
+    )
     qkv_width = D + 2 * KVH * HD
-    w_router = whole_in[:, qkv_width : qkv_width + EXPERTS]
-    gain_one = whole_in[:, qkv_width + EXPERTS].astype(F32)
-    gain_two = whole_in[:, qkv_width + EXPERTS + 1].astype(F32)
-
-    per_device = expert_gate.shape[1] // n_context
-
-    def weight_pieces(weight):
-        mine = lax.dynamic_slice_in_dim(weight, block_index * per_device, per_device, 1)
-        mine = mine.astype(BF).transpose(1, 0, 2)
-        mine = mine.reshape(2, per_device // 2, mine.shape[1], mine.shape[2])
-        same = lax.dynamic_index_in_dim(mine, parity, 0, keepdims=False)
-        other = lax.dynamic_index_in_dim(mine, 1 - parity, 0, keepdims=False)
-        return same, other
-
-    weight_halves = [weight_pieces(weight) for weight in (expert_gate, expert_up, expert_down)]
-    pieces = {(which, 0, i): (weight_halves[which][0], i) for which in range(3) for i in range(2)}
-    moved_early = {flip: flip_permute(weight_halves[0][flip % 2], "dp", n_dp, flip) for flip in (2, 1)}
+    weights = (expert_gate, expert_up, expert_down)
+    own_ranks_t, own_rows, own_columns, partner_rows, partner_columns, whole_in, w_out, *weight_halves = (
+        gather_parts(route_rows.T, part_in, part_of(attn_o), weights, cot_low, n_dp, n_context, plane)
+    )
+    partner_cot = [weight_halves.pop()]
+    whole_in = whole_in.reshape(-1, part_in.shape[1])
+    w_out = w_out.reshape(-1, D)
+    own_ranks = own_ranks_t.T
+    named = own_ranks >= 0
+    pieces = {(which, 0, i): (weight_halves[which], (0, i)) for which in range(3) for i in range(2)}
 
     def riding(names):
-        return [(weight_halves[which][flip % 2], i, flip) for which, flip, i in names]
+        return [
+            (weight_halves[which], flip % 2 if i is None else (flip % 2, i), flip) for which, flip, i in names
+        ]
 
     def pieces_of(expert):
         return [pieces[which, flip, expert] for which in range(3) for flip in range(n_dp)]
-
-
-    def ranks_of(rows):
-        named = jnp.sum(
-            (rows[:, :, None] == jnp.arange(EXPERTS, dtype=jnp.int32)[None, None, :]).astype(F32), axis=1
-        )
-        order = jnp.arange(tokens, dtype=jnp.int32)
-        before = (order[None, :] < order[:, None]).astype(BF)
-        count = mxu(before, named.astype(BF))
-        return named > 0, jnp.where(named > 0, count, -1.0)
-
-    named, own_ranks = ranks_of(route_rows)
-    partner_ranks = ranks_of(partner_routes)[1]
-
-    def mine_of(table):
-        parted = table.reshape(tokens, plane, 2, 2)
-        return lax.dynamic_index_in_dim(parted, parity, 2, keepdims=False)
-
-    own_sel = mine_of(own_ranks)
-    partner_sel = mine_of(partner_ranks)
-    own_pair = [own_sel[:, :, i].astype(BF) for i in range(2)]
-    partner_pair = [partner_sel[:, :, i].astype(BF) for i in range(2)]
-
-    own_ranks_t = jnp.stack(own_pair, axis=0).transpose(0, 2, 1)
-    partner_ranks_t = jnp.stack(partner_pair, axis=0).transpose(0, 2, 1)
-    partner_cot = flip_permute(cot_low, "dp", n_dp, 1)
 
     positions = jnp.concatenate(
         [
@@ -1763,44 +2186,31 @@
     cos_half, sin_half = jnp.cos(angles), jnp.sin(angles)
     cosine = jnp.concatenate([cos_half, cos_half], axis=1)
     sine = jnp.concatenate([-sin_half, sin_half], axis=1)
-    block_word = block_index.astype(jnp.int32).reshape(1)
-    z_word = z_index.astype(jnp.int32).reshape(1)
-    qkv, normed_one = project(x_low, gain_one[None, :], whole_in, qkv_width, cosine, sine)
-    keys_own = qkv[:, D:]
-    prompt_kv = lax.all_gather(keys_own[:PBLK], "context", axis=0, tiled=True)
-    keys_values = jnp.concatenate([prompt_kv, keys_own[PBLK:]], axis=0)
-    attended, logs = attend(block_word, qkv, keys_values, prompt_len)
-    x_rows = x_low.astype(F32)
-    mid_rows = x_rows + mxu(attended, w_out)
-    normed_two = rms_scale(mid_rows, gain_two).astype(BF)
-
-    normed_two, partner_cot, moved_early[1], moved_early[2] = tie(
-        normed_two, partner_cot, moved_early[1], moved_early[2]
-    )
-    for flip, moved in moved_early.items():
+    gains, normed_one, qkv, keys_values, attended, logs, normed_two, logits, mid_rows, cot_half, *moved = (
+        front(prompt_len, n_dp, x_low, cosine, sine, whole_in, w_out, cot_low, riding(RIDE_FRONT))
+    )
+    partner_cot.append(cot_half)
+    for (which, flip, _), piece in zip(RIDE_FRONT, moved):
         for i in range(2):
-            pieces[0, flip, i] = (moved, i)
-    landed, staged, arrived = dispatch_rows(
-        normed_two, cot_low, partner_cot, own_ranks_t, partner_ranks_t, riding(RIDE_DISPATCH), n_dp
-    )
-    pieces.update({name: (piece, None) for name, piece in zip(RIDE_DISPATCH, arrived)})
-    logits = mxu(normed_two, w_router)
+            pieces[which, flip, i] = (piece, i)
+
+    logits = logits[:, :EXPERTS]
     top_logit = jnp.max(jnp.where(named, logits, masked_score), axis=1, keepdims=True)
     raised = jnp.where(named, jnp.exp(jnp.where(named, logits - top_logit, 0.0)), 0.0)
     gates = raised / jnp.sum(raised, axis=1, keepdims=True)
 
     slot_ids = jnp.arange(SLOTS, dtype=F32)
-    hits = own_ranks.T[:, None, :] == slot_ids[None, :, None]
+    hits = own_ranks_t[:, None, :] == slot_ids[None, :, None]
     slot_gates = jnp.sum(jnp.where(hits, gates.T[:, None, :], 0.0), axis=-1)
-    slot_gates = slot_gates.reshape(plane, 2, 2, SLOTS)
+    slot_gates = jnp.pad(slot_gates, ((0, 0), (0, 128 - SLOTS))).reshape(plane, 2, 2, 128)
     own_gates = lax.dynamic_index_in_dim(slot_gates, parity, 1, keepdims=False)
     other_gates = lax.dynamic_index_in_dim(slot_gates, 1 - parity, 1, keepdims=False)
-    partner_gates = flip_permute(other_gates, "dp", n_dp, 1)
-    both_gates = jnp.stack([own_gates, partner_gates], axis=1)
-    both_gates = lax.all_to_all(both_gates, PLANE, split_axis=0, concat_axis=0, tiled=True)
-
+    gates_here, landed, staged, arrived = dispatch_rows(
+        normed_two, cot_low, partner_cot, own_rows, partner_rows, own_gates, other_gates, riding(RIDE_DISPATCH), n_dp
+    )
+    pieces.update({name: (piece, None) for name, piece in zip(RIDE_DISPATCH, arrived)})
     def gates_of(expert):
-        return [both_gates[:, side, expert].reshape(plane * SLOTS, 1) for side in range(2)]
+        return [gates_here[:, 2 * side + expert, :SLOTS].reshape(plane * SLOTS, 1) for side in range(2)]
 
     def slots_of(arrays):
         flat = [array.reshape(plane * SLOTS, D) for array in arrays]
@@ -1825,42 +2235,31 @@
         cots,
         gates_of(1),
         pieces_of(1),
-        parted(first),
+        parted(first)[1:4],
         homing(HOME_SECOND, first_shares),
     )
-    home_of.update(zip(HOME_SECOND, homes))
 
     dots = jnp.stack(
         [d[side].reshape(plane, SLOTS) for side in range(2) for d in (first_dots, second_dots)], axis=1
     )
     dots = jnp.pad(dots, ((0, 0), (0, 0), (0, 128 - SLOTS)))
     second = parted(second)
-    grad_rows, dots_here, dots_other, late, homes = return_rows(
-        jnp.stack(own_pair, axis=0),
-        jnp.stack(partner_pair, axis=0),
+    grad_rows, grad_logits, part_first, late, _ = return_rows(
+        own_columns,
+        partner_columns,
         dots,
-        early[2:4],
+        own_ranks,
+        gates,
+        early[1:3],
         second[2:4],
-        second[0:2],
+        parted(first)[0:1],
         homing(HOME_RETURN, first_shares, second_shares),
+        HOME_RETURN,
+        first_shares,
+        homes,
         n_dp,
     )
-    home_of.update(zip(HOME_RETURN, homes))
-    flat = lambda array: array.reshape(plane * SLOTS, D)
-    out_own, out_partner = ([flat(early[side]), flat(late[side])] for side in range(2))
-    own_dots = dots_here[:, 0:2, :SLOTS]
-    other_dots = dots_other[:, 2:4, :SLOTS]
-    all_dots = jnp.where(
-        parity == 0,
-        jnp.stack([own_dots, other_dots], axis=1),
-        jnp.stack([other_dots, own_dots], axis=1),
-    ).reshape(EXPERTS, SLOTS)
-    grad_gates = jnp.sum(
-        jnp.where(own_ranks[:, :, None] == slot_ids[None, None, :], all_dots[None], 0.0), axis=-1
-    )
-    grad_logits = gates * (grad_gates - jnp.sum(gates * grad_gates, axis=1, keepdims=True))
-    grad_logits = grad_logits.astype(BF)
-    grad_wrouter = mxu(normed_two, grad_logits, ((0,), (0,)))
+    grad_wrouter = mxu(normed_two, grad_logits, ((0,), (0,)))[:, :EXPERTS]
 
     def part_of_expert(expert, shares):
         parts = []
@@ -1878,11 +2277,9 @@
         n_dp,
         (
             grad_logits,
-            w_router,
             cot_low,
             x_low,
-            gain_one[None, :],
-            gain_two[None, :],
+            gains,
             attended,
             qkv,
             keys_values,
@@ -1891,24 +2288,27 @@
             cosine,
             sine,
         ),
-        (mid_rows, grad_rows, w_out, whole_in, part_of_expert(0, first_shares)),
+        (mid_rows, grad_rows, w_out, whole_in, part_first),
+        second[0:2],
         homing(HOME_BACKWARD, first_shares, second_shares),
     )
+    last, homes = homes[:2], homes[2:]
+    out_own, out_partner = [late[0], last[0]], [early[0], last[1]]
     home_of.update(zip(HOME_BACKWARD, homes))
 
-    out_for_partner = collect_rows(partner_pair[0], partner_pair[1], *out_partner, BF)
     grad_small = jnp.concatenate([grad_wrouter, grad_gains[0][:, None], grad_gains[1][:, None]], axis=1)
     grad_small = jnp.pad(grad_small, ((0, 0), (0, 128 - grad_small.shape[1]))).astype(BF)
     parts = lambda share: share.reshape(n_dp, plane, -1, share.shape[1])
-    total_qkv, total_out, total_small, all_second, out_from_partner = reduce_shares(
+    part_second = part_of_expert(1, second_shares)
+    total_qkv, total_out, total_small, result, all_second = reduce_shares(
         [parts(grad_wqkv), parts(grad_wout), parts(grad_small)],
-        part_of_expert(1, second_shares),
-        out_for_partner,
+        part_second,
+        (own_columns, partner_columns),
+        mid_rows,
+        (out_own, out_partner),
         n_dp,
         n_context,
     )
-    moe_out = collect_rows(own_pair[0], own_pair[1], *out_own, F32)
-    result = (mid_rows + moe_out + out_from_partner.astype(F32)).astype(BF)
     total_qkv = total_qkv.reshape(-1, qkv_width).astype(F32)
     total_out = total_out.reshape(-1, D).astype(F32)
     total_small = total_small.reshape(-1, 128).astype(F32)
@@ -1922,9 +2322,9 @@
         total_small[:, EXPERTS],
         total_small[:, EXPERTS + 1],
         total_small[:, :EXPERTS],
-        finish_weight(0, all_first, all_second),
-        finish_weight(1, all_first, all_second),
-        finish_weight(2, all_first, all_second),
+        finish_weight(0, all_first, all_second, part_first, part_second),
+        finish_weight(1, all_first, all_second, part_first, part_second),
+        finish_weight(2, all_first, all_second, part_first, part_second),
     )
 
 

time: 1190 us -> 1070 us (0.90)
  local copies, waits for them, and re-layouts: 71.6 us -> 25.7 us
  other arithmetic: 56.9 us -> 26.7 us
  waiting for transfers between devices: 14.1 us -> 0 us
  between operations: 15.2 us -> 1.56 us
    pallas_call x1, Pallas kernels: 118 us -> 157 us  [backward(): pl.pallas_call(functools.partial(backward_kernel, n_dp, prompt_len, [(ind...]
    pallas_call x2, Pallas kernels: 271 us -> 233 us  [run_expert(): pl.pallas_call(functools.partial(expert_kernel, plane, n_dp, half_steps,...]
    transpose x4 -> x1, local copies, waits for them, and re-layouts: 18.3 us -> 0.13 us  [local_paired(): slot_gates = jnp.sum(jnp.where(hits, gates.T[:, None, :], 0.0), axis=-1)]
    another operation x11 -> x1, other arithmetic: 13.7 us -> 0.01 us  [the longest x6 10 us: part_of_expert(): jnp.stack([jnp.where(parity == 0, same, other), jnp.where(parity == 0, ot...]
    ppermute x4 -> x0, waiting for transfers between devices: 13.6 us -> none  [flip_permute(): return lax.ppermute(value, axis, [(i, i ^ flip) for i in range(size)])]
    pallas_call x1, Pallas kernels: 148 us -> 160 us  [dispatch_rows(): pl.pallas_call(functools.partial(dispatch_kernel, plane, n_dp, [(index, f...]
    pallas_call x6 -> x3, Pallas kernels: 268 us -> 259 us  [the longest x1 132 us: return_rows(): pl.pallas_call(functools.partial(return_kernel, plane, n_dp, len(results)...]
  transfers between devices with their start and end apart: 7 -> 0, of which waited for: 2 -> 0; matrix products, arithmetic and copies ran while one was open for 5% -> 0% of each run, Pallas kernels for 15% -> 0%
where the time goes in v4:
time: 1070 us; the launch traced here: 1060 us
  Pallas kernels  1010 us (94%)
  other arithmetic  26.7 us (2%)
  local copies, waits for them, and re-layouts  25.7 us (2%)
    pallas_call x2, Pallas kernels, run_expert(): pl.pallas_call(functools.partial(expert_kernel, plane, n_dp, half_steps,...  233 us
    pallas_call x1, Pallas kernels, dispatch_rows(): pl.pallas_call(functools.partial(dispatch_kernel, plane, n_dp, [(index, f...  160 us
    pallas_call x1, Pallas kernels, backward(): pl.pallas_call(functools.partial(backward_kernel, n_dp, prompt_len, [(ind...  157 us
    pallas_call x1, Pallas kernels, reduce_shares(): pl.pallas_call(functools.partial(reduce_kernel, n_dp, widths), in_specs=[...  154 us
    pallas_call x1, Pallas kernels, return_rows(): pl.pallas_call(functools.partial(return_kernel, plane, n_dp, len(results)...  132 us
    pallas_call x1, Pallas kernels, front(): pl.pallas_call(functools.partial(front_kernel, n_dp, prompt_len, [(index,...  63.9 us
    pallas_call x1, Pallas kernels, gather_parts(): pl.pallas_call(functools.partial(gather_kernel, n_dp, plane), in_specs=[v...  63.4 us
    pallas_call x3, Pallas kernels, finish_weight(): pl.pallas_call(functools.partial(finish_kernel, down), grid=(rows // step...  43.3 us

profile of v4, /device:TPU:0, one launch (start us, length us, event | category | flops | bytes accessed | tf_op | source)
XLA Modules:
  0.0 1061.7 jit_solution(2106089756976246125)
XLA Ops:
  0.7 0.8 convert_bitcast_fusion
  1.9 0.8 dynamic-slice_convert_fusion.2
  2.7 1.7 dynamic-slice_convert_fusion
  4.5 0.8 concatenate.24.in_ref
  5.3 1.4 fusion.5
  6.7 1.2 pad_maximum_fusion.1
  7.9 63.4 %gather_parts.1 = (f32[32,768]{1,0:T(8,128)}, bf16[2,8,768]{2,1,0:T(8,128)(2,1)}, bf16[2,768,8]{2,1,0:T(8,128)(2,1)}, bf16[2,8,768]{2,1,0:T(8,128)(2,1)}, bf16[2...) custom-call(s32[4,768]{1,0:T(4,128)} %bitcast.157, ...), custom_call_target="tpu_custom_call" | custom-call | tf_op jit(solution)/shard_map/gather_parts/pallas_call | solution.py:958
  71.3 1.1 copy.56
  72.4 63.9 %front.1 = (f32[8,1536]{1,0:T(8,128)}, bf16[768,1536]{1,0:T(8,128)(2,1)}, bf16[768,2048]{1,0:T(8,128)(2,1)}, bf16[1536,512]{1,0:T(8,128)(2,1)}, bf16[768,1536]{1...) custom-call(bf16[768,1536]{1,0:T(8,128)(2,1)} %bitcast.116, ...), custom_call_target="tpu_custom_call" | custom-call | tf_op jit(solution)/shard_map/front/pallas_call | solution.py:1157
  136.3 1.2 select_reduce_fusion.1
  137.5 1.3 fusion.4
  138.8 1.3 fusion.3.gates_ref
  140.2 1.2 select_reduce_fusion
  142.1 160.0 %dispatch_rows.1 = (f32[8,4,128]{2,1,0:T(4,128)}, bf16[8,112,1536]{2,1,0:T(8,128)(2,1)}, bf16[8,112,1536]{2,1,0:T(8,128)(2,1)}, bf16[8,112,1536]{2,1,0:T(8,128)(...) custom-call(bf16[768,1536]{1,0:T(8,128)(2,1)} %get-tuple-element.119, ...), custom_call_target="tpu_custom_call" | custom-call | flops 20000000000 | bytes 400000000 | tf_op jit(solution)/shard_map/dispatch_rows/pallas_call | solution.py:1288
  302.1 0.9 slice_reduce_fusion.2
  303.0 1.0 reshape_squeeze.19.refs_5_
  303.9 1.0 reshape_squeeze.18.refs_4_
  304.9 1.0 reshape_squeeze.17.refs_5_
  305.9 1.0 reshape_squeeze.16.refs_4_
  306.8 125.6 %first_expert.1 = (bf16[896,1536]{1,0:T(8,128)(2,1)}, bf16[896,1536]{1,0:T(8,128)(2,1)}, bf16[896,1536]{1,0:T(8,128)(2,1)}, bf16[896,1536]{1,0:T(8,128)(2,1)}, f...) custom-call(bf16[896,1536]{1,0:T(8,128)(2,1)} %bitcast.141, ...), custom_call_target="tpu_custom_call" | custom-call | tf_op jit(solution)/shard_map/first_expert/pallas_call | solution.py:678
  432.4 1.2 reduce.2
  433.7 106.9 %second_expert.1 = (bf16[896,1536]{1,0:T(8,128)(2,1)}, bf16[896,1536]{1,0:T(8,128)(2,1)}, bf16[896,1536]{1,0:T(8,128)(2,1)}, bf16[896,1536]{1,0:T(8,128)(2,1)}, ...) custom-call(bf16[896,1536]{1,0:T(8,128)(2,1)} %bitcast.137, ...), custom_call_target="tpu_custom_call" | custom-call | tf_op jit(solution)/shard_map/second_expert/pallas_call | solution.py:678
  540.6 1.2 reduce.5
  541.9 1.2 reduce.7
  544.2 131.7 %return_rows.1 = (f32[768,1536]{1,0:T(8,128)}, bf16[768,128]{1,0:T(8,128)(2,1)}, bf16[2,3,384,768]{3,2,1,0:T(8,128)(2,1)}, bf16[8,112,1536]{2,1,0:T(8,128)(2,1)}...) custom-call(bf16[2,768,8]{2,1,0:T(8,128)(2,1)} %get-tuple-element.11, ...), custom_call_target="tpu_custom_call" | custom-call | flops 30000001024 | bytes 400000000 | tf_op jit(solution)/shard_map/return_rows/pallas_call | solution.py:1475
  675.9 1.5 fusion.7
  677.4 157.3 %backward.1 = (bf16[768,1536]{1,0:T(8,128)(2,1)}, f32[8,1536]{1,0:T(8,128)}, bf16[1536,1536]{1,0:T(8,128)(2,1)}, bf16[1536,2048]{1,0:T(8,128)(2,1)}, bf16[4,2,3,...) custom-call(bf16[768,128]{1,0:T(8,128)(2,1)} %get-tuple-element.178., ...), custom_call_target="tpu_custom_call" | custom-call | tf_op jit(solution)/shard_map/backward/pallas_call | solution.py:1782
  834.7 2.1 broadcast_select_fusion.1
  836.8 1.5 broadcast_select_fusion.3
  838.4 1.5 broadcast_select_fusion.5
  840.6 1.9 copy.76
  842.4 1.8 pad.15.clone
  844.6 2.1 pad_maximum_fusion.refs_3_.own_second_ref
  846.7 154.2 %reduce_shares.1 = (bf16[8,48,2048]{2,1,0:T(8,128)(2,1)}, bf16[8,48,1536]{2,1,0:T(8,128)(2,1)}, bf16[8,48,128]{2,1,0:T(8,128)(2,1)}, bf16[768,1536]{1,0:T(8,128)(2,1)}, bf16[4,2,3,384,768]{4,3,2,1,0:T(8,128)(2,1)}) custom-call(bf16[4,8,48,2048]{3,2,1,0:T(8,128)(2,1)} %bitcast.118, bf16[4,8,48,1536]{3,2,1,0:T(8,128)(2,1)} %bitcast.131, ...), custom_call_target="tpu_custom_call" | custom-call | tf_op jit(solution)/shard_map/reduce_shares/pallas_call | solution.py:2031
  1000.9 1.6 slice.79
  1002.4 1.7 copy.75
  1004.1 1.0 convert.23
  1005.1 0.9 slice_reduce_fusion
  1006.0 3.0 bitcast_convert_fusion.1
  1009.4 0.9 fusion.6
  1010.4 1.6 slice.74
  1012.0 2.0 maximum_maximum_fusion.own_second_ref
  1014.0 12.8 %finish_weight.5 = f32[192,16,1536]{2,1,0:T(8,128)} custom-call(bf16[4,2,3,2,192,768]{5,4,3,2,1,0:T(8,128)(2,1)} %bitcast.105, bf16[4,2,3,2,192,768]{5,4,3,2,1,0:T(8,128)(2,1)} %bitcast.106, bf16[2,3,2,192,768]{4,3,2,1,0:T(8,128)(2,1)} %bitcast.107, bf16[2,3,2,192,768]{4,3,2,1,0:T(8,128)(2,1)} %maximum_maximum_fusion.own_second_ref), custom_call_target="tpu_custom_call" | custom-call | tf_op jit(solution)/shard_map/finish_weight/pallas_call | solution.py:2110
  1026.8 15.2 %finish_weight.4 = f32[384,16,768]{2,1,0:T(8,128)} custom-call(bf16[4,2,3,384,768]{4,3,2,1,0:T(8,128)(2,1)} %get-tuple-element.214.first_ref, bf16[4,2,3,384,768]{4,3,2,1,0:T(8,128)(2,1)} %get-tuple-element.215.second_ref, bf16[2,3,384,768]{3,2,1,0:T(8,128)(2,1)} %get-tuple-element.187.refs_15_.own_first_ref, ...), custom_call_target="tpu_custom_call" | custom-call | tf_op jit(solution)/shard_map/finish_weight/pallas_call | solution.py:2110
  1042.0 15.3 %finish_weight.3 = f32[384,16,768]{2,1,0:T(8,128)} custom-call(bf16[4,2,3,384,768]{4,3,2,1,0:T(8,128)(2,1)} %get-tuple-element.214.first_ref, bf16[4,2,3,384,768]{4,3,2,1,0:T(8,128)(2,1)} %get-tuple-element.215.second_ref, bf16[2,3,384,768]{3,2,1,0:T(8,128)(2,1)} %get-tuple-element.187.refs_15_.own_first_ref, ...), custom_call_target="tpu_custom_call" | custom-call | tf_op jit(solution)/shard_map/finish_weight/pallas_call | solution.py:2110
  1057.3 1.4 copy.81
  1058.7 1.1 copy-done.3
  1059.8 1.4 copy.82
  (62 shorter events, 3.9 us)
Async XLA Ops:
  0.6 0.9 copy-start
  72.4 63.9 %copy-start.5 = (f32[32,768]{0,1:T(8,128)}, f32[32,768]{0,1:T(8,128)S(1)}, u32[]{:S(2)}) copy-start(f32[32,768]{0,1:T(8,128)S(1)} %copy.56) | copy-start | bytes 294916
  136.3 4.0 copy-start.16
  140.1 162.0 %copy-start.6 = (f32[768,32]{1,0:T(8,128)}, f32[768,32]{1,0:T(8,128)S(1)}, u32[]{:S(2)}) copy-start(f32[768,32]{1,0:T(8,128)S(1)} %fusion.3.gates_ref) | copy-start | bytes 294916
  433.7 109.5 %copy-start.15 = (f32[896,1]{1,0:T(8,128)S(1)}, f32[896,1]{1,0:T(8,128)}, u32[]{:S(2)}) copy-start(f32[896,1]{1,0:T(8,128)} %get-tuple-element.165) | copy-start | bytes 10756
  544.2 131.7 %copy-start.2 = (bf16[768,1536]{1,0:T(8,128)(2,1)S(1)}, bf16[768,1536]{1,0:T(8,128)(2,1)}, u32[]{:S(2)}) copy-start(bf16[768,1536]{1,0:T(8,128)(2,1)} %get-tuple-element.119.refs_0_) | copy-start | bytes 7077892
  677.3 157.3 %copy-start.8 = (bf16[1536,128]{0,1:T(8,128)(2,1)}, bf16[1536,128]{0,1:T(8,128)(2,1)S(1)}, u32[]{:S(2)}) copy-start(bf16[1536,128]{0,1:T(8,128)(2,1)S(1)} %fusion.7) | copy-start | bytes 1179652
  834.6 2.1 copy-start.12
  834.6 2.1 copy-start.13
  834.7 2.1 copy-start.14
  836.7 1.6 copy-start.9
  836.7 1.6 copy-start.10
  836.8 1.6 copy-start.11
  838.3 1.5 copy-start.17
  838.3 1.6 slice-start
  1004.1 4.9 copy-start.7
  1042.0 15.3 %copy-start.4 = (bf16[768,1536]{1,0:T(8,128)(2,1)S(1)}, bf16[768,1536]{1,0:T(8,128)(2,1)}, u32[]{:S(2)}) copy-start(bf16[768,1536]{1,0:T(8,128)(2,1)} %get-tuple-element.209) | copy-start | bytes 7077892
  1057.3 2.5 copy-start.3
  1057.3 3.9 copy-start.1

commit v5 on v4

--- a/solution.py
+++ b/solution.py
@@ -419,14 +419,13 @@
     return blocks
 
 
-def masked_scores(scores, first_row, prompt_len, block_index):
-    row = lax.broadcasted_iota(jnp.int32, scores.shape, 0)
-    column = lax.broadcasted_iota(jnp.int32, scores.shape, 1)
-    if first_row == 0:
-        limit = row + block_index * PBLK
-    else:
-        limit = row + (prompt_len + first_row - PBLK)
-    return jnp.where(column <= limit, scores, masked_score)
+def masked_scores(scores, first_row, block_index):
+    tail = scores if first_row == 0 else scores[:, -PBLK:]
+    row = lax.broadcasted_iota(jnp.int32, tail.shape, 0)
+    column = lax.broadcasted_iota(jnp.int32, tail.shape, 1)
+    limit = row + block_index * PBLK if first_row == 0 else row
+    tail = jnp.where(column <= limit, tail, masked_score)
+    return tail if first_row == 0 else jnp.concatenate([scores[:, :-PBLK], tail], axis=1)
 
 
 def segment_matrix(parts, transposed):
@@ -509,13 +508,13 @@
 
 
 ALL_FLIPS = (2, 3, 1)
-RIDE_FRONT = ((0, 2, None),)
-RIDE_DISPATCH = ((0, 3, 0), (0, 1, 0)) + tuple((m, f, 0) for m in (1, 2) for f in ALL_FLIPS)
+RIDE_FRONT = ((0, 2, None), (0, 1, 0), (1, 1, 0))
+RIDE_DISPATCH = ((0, 3, 0), (1, 2, 0), (1, 3, 0), (2, 2, 0), (2, 3, 0), (2, 1, 0))
 RIDE_FIRST = ((0, 3, 1), (0, 1, 1)) + tuple((m, f, 1) for m in (1, 2) for f in ALL_FLIPS)
-HOME_SECOND = ((0, 2, 0), (0, 3, 0), (1, 2, 0), (1, 3, 0), (0, 1, 0))
-HOME_RETURN = ((2, 2, 0), (1, 1, 0), (2, 1, 0), (2, 3, 0))
-RETURN_FIRST = 3
-HOME_BACKWARD = tuple((m, f, 1) for f in ALL_FLIPS for m in range(3))
+HOME_SECOND = tuple((m, f, 0) for m in (0, 1) for f in (2, 3)) + tuple((m, 1, 0) for m in range(3))
+HOME_RETURN = ((2, 2, 0), (2, 3, 0), (0, 2, 1), (0, 3, 1))
+RETURN_FIRST = 2
+HOME_BACKWARD = tuple((m, f, 1) for m in (1, 2) for f in (2, 3)) + tuple((m, 1, 1) for m in range(3))
 
 
 def pick(array, index):
@@ -540,12 +539,12 @@
     return [{"dp": lax.axis_index("dp") ^ flip} for flip in range(1, n_dp)]
 
 
-def expert_kernel(plane, n_dp, half_steps, n_carried, picks, riders, *refs):
-    (xo_ref, xp_ref, go_ref, gp_ref, so_ref, sp_ref), refs = refs[:6], refs[6:]
+def expert_kernel(plane, n_dp, half_steps, number, n_carried, picks, riders, *refs):
+    (xo_ref, xp_ref, go_ref, gp_ref, gates_ref), refs = refs[:5], refs[5:]
     pieces, refs = refs[: 3 * n_dp], refs[3 * n_dp :]
     carried, refs = refs[:n_carried], refs[n_carried:]
     sources, refs = refs[: len(riders)], refs[len(riders) :]
-    (yo_ref, yp_ref, bo_ref, bp_ref, do_ref, dp_ref, gate_ref, up_ref, down_ref), refs = refs[:9], refs[9:]
+    (yo_ref, yp_ref, bo_ref, bp_ref, dots_ref, gate_ref, up_ref, down_ref), refs = refs[:8], refs[8:]
     landed, refs = refs[:n_carried], refs[n_carried:]
     targets, refs = refs[: len(riders)], refs[len(riders) :]
     (wg_ref, wu_ref, wd_ref, x_all, de_all, a_all, dg_all, du_all, stage, bounce), sems = refs[:10], refs[10:]
@@ -583,7 +582,16 @@
 
     rows = jnp.where(own, xo_ref[...], xp_ref[...])
     cot = jnp.where(own, go_ref[...], gp_ref[...])
-    share = jnp.where(own, so_ref[...], sp_ref[...])
+    places = rows_of_step // SLOTS
+    first_place = lax.rem(step, half_steps) * places
+    at = (SLOTS, 128)
+    diagonal = lax.broadcasted_iota(jnp.int32, at, 0) == lax.broadcasted_iota(jnp.int32, at, 1)
+    columns = []
+    for n in range(places):
+        own_row = gates_ref[first_place + n, number : number + 1, :]
+        row = jnp.where(own, own_row, gates_ref[first_place + n, 2 + number : 3 + number, :])
+        columns.append(jnp.sum(jnp.where(diagonal, row, 0.0), axis=-1, keepdims=True))
+    share = jnp.concatenate(columns, axis=0)
     place = pl.ds(pl.multiple_of(step * rows_of_step, 32), rows_of_step)
     x_all[place, :] = rows
     gate_pre = mxu(rows, wg_ref[...])
@@ -610,13 +618,17 @@
     def _():
         yo_ref[...] = scaled
         bo_ref[...] = back
-        do_ref[...] = dots
 
     @pl.when(jnp.logical_not(own))
     def _():
         yp_ref[...] = scaled
         bp_ref[...] = back
-        dp_ref[...] = dots
+
+    for n in range(places):
+        column = dots[n * SLOTS : (n + 1) * SLOTS]
+        dots_ref[step // half_steps, first_place + n] = jnp.sum(
+            jnp.where(diagonal, column, 0.0), axis=0, keepdims=True
+        )
 
     @pl.when(step == 2 * half_steps - 1)
     def _():
@@ -657,7 +669,7 @@
             move.wait()
 
 
-def run_expert(name, number, rows, cots, gates, pieces, carried, riders):
+def run_expert(name, which, number, rows, cots, gates, pieces, carried, riders):
     half_rows = rows[0].shape[0]
     half_steps = 4
     step_rows = half_rows // half_steps
@@ -681,15 +693,22 @@
             plane,
             n_dp,
             half_steps,
+            which,
             len(carried),
             [index for _, index in pieces],
             [(index, flip) for _, index, flip in riders],
         ),
         grid=(2 * half_steps,),
-        in_specs=pair(D) + pair(D) + pair(1) + [anywhere] * (len(pieces) + len(carried) + len(riders)),
-        out_specs=pair(D) + pair(D) + pair(1) + [anywhere] * (3 + len(carried) + len(riders)),
+        in_specs=pair(D)
+        + pair(D)
+        + [pl.BlockSpec(gates.shape, lambda j: (0, 0, 0))]
+        + [anywhere] * (len(pieces) + len(carried) + len(riders)),
+        out_specs=pair(D)
+        + pair(D)
+        + [pl.BlockSpec((2, plane, 1, 128), lambda j: (0, 0, 0, 0))]
+        + [anywhere] * (3 + len(carried) + len(riders)),
         out_shape=[shape((half_rows, D), BF)] * 4
-        + [shape((half_rows, 1), F32)] * 2
+        + [shape((2, plane, 1, 128), F32)]
         + [share] * 3
         + [shape(array.shape, BF) for array in carried]
         + [shape(picked_shape(array, index), BF) for array, index, _ in riders],
@@ -716,9 +735,9 @@
             vmem_limit_bytes=56 * 1024 * 1024, collective_id=number, has_side_effects=True
         ),
         name=name,
-    )(*rows, *cots, *gates, *[a for a, _ in pieces], *carried, *[a for a, _, _ in riders])
-    last = 9 + len(carried)
-    return results[:4], results[4:6], results[6:9], results[9:last], results[last:]
+    )(*rows, *cots, gates, *[a for a, _ in pieces], *carried, *[a for a, _, _ in riders])
+    last = 8 + len(carried)
+    return results[:4], results[4], results[5:8], results[8:last], results[last:]
 
 
 def plane_peer(index):
@@ -820,7 +839,10 @@
         chosen = jnp.where(place == column, 1.0, 0.0).astype(BF)
         row_ref[i] = mxu(chosen, low).astype(BF)
         column_ref[i] = mxu(low, chosen, ((0,), (1,))).astype(BF)
-    return ranks
+    one = lax.broadcasted_iota(jnp.int32, (EXPERTS, EXPERTS), 0) == lax.broadcasted_iota(
+        jnp.int32, (EXPERTS, EXPERTS), 1
+    )
+    return mxu(low, jnp.where(one, 1.0, 0.0).astype(BF), ((0,), (0,)))
 
 
 def gather_kernel(
@@ -959,10 +981,10 @@
         functools.partial(gather_kernel, n_dp, plane),
         in_specs=[vmem] + [anywhere] * 6,
         out_specs=[vmem] * 5 + [anywhere] * 6,
-        out_shape=[shape((EXPERTS, tokens), F32), row, column, row, column]
+        out_shape=[shape((tokens, EXPERTS), F32), row, column, row, column]
         + [shape((n_dp, plane) + part.shape, BF) for part in (part_in, part_out)]
         + [shape((2, mine // 2, w.shape[0], w.shape[2]), BF) for w in weights]
-        + [shape((tokens // 2, D), BF)],
+        + [shape((tokens * 3 // 4, D), BF)],
         scratch_shapes=[
             pltpu.VMEM(routes.shape, routes.dtype),
             pltpu.VMEM((2, rows, 8, width), F32),
@@ -1037,9 +1059,9 @@
     load_small.start()
     load_columns(0).start()
     load_out.start()
-    half = cot_partner_ref.shape[0]
+    rest = cot_partner_ref.shape[0]
     pair = remote(
-        cot_ref.at[pl.ds(half, half)],
+        cot_ref.at[pl.ds(tokens - rest, rest)],
         cot_partner_ref,
         pair_sems.at[0],
         pair_sems.at[1],
@@ -1114,7 +1136,7 @@
         for first_row, keys in row_blocks(prompt_len):
             rows = slice(first_row, first_row + PBLK)
             scores = mxu(qkv_ref[rows, columns], kv_ref[:keys, key_columns], ((1,), (1,)))
-            scores = masked_scores(scores, first_row, prompt_len, block_index)
+            scores = masked_scores(scores, first_row, block_index)
             top = jnp.max(scores, axis=-1, keepdims=True)
             unnormed = jnp.exp(scores - top)
             total = jnp.sum(unnormed, axis=-1, keepdims=True)
@@ -1168,7 +1190,7 @@
             shape((tokens, D), BF),
             shape((tokens, 128), F32),
             shape((tokens, D), F32),
-            shape((tokens // 2, D), BF),
+            shape((tokens // 4, D), BF),
         ]
         + [shape(picked_shape(array, index), BF) for array, index, _ in riders],
         scratch_shapes=[
@@ -1192,10 +1214,10 @@
 
 
 def dispatch_kernel(plane, n_dp, riders, *refs):
-    normed_ref, cot_ref, own_rank_ref, partner_rank_ref, gates_ref, other_gates_ref = refs[:6]
+    normed_ref, cot_ref, own_rank_ref, partner_rank_ref, logits_ref, ranks_ref = refs[:6]
     cot_halves, refs = refs[6:8], refs[8:]
     sources, refs = refs[: len(riders)], refs[len(riders) :]
-    gates_here_ref, refs = refs[0], refs[1:]
+    gates_ref, gates_here_ref, refs = refs[0], refs[1], refs[2:]
     landed, staged, targets = refs[:4], refs[4:8], refs[8 : 8 + len(riders)]
     (
         stage,
@@ -1208,6 +1230,7 @@
         ride_send,
         ride_recv,
         all_gates,
+        other_gates,
         partner_gates,
         gate_sems,
         gate_send,
@@ -1218,17 +1241,17 @@
     here = plane_here()
     greet([plane_peer(here ^ flip) for flip in range(1, plane)] + dp_peers(n_dp))
     partner = {"dp": lax.axis_index("dp") ^ 1}
-    gate_pair = remote(other_gates_ref, partner_gates, gate_sems.at[0], gate_sems.at[1], partner)
-    gate_pair.start()
+    gate_pair = remote(other_gates, partner_gates, gate_sems.at[0], gate_sems.at[1], partner)
     pair = remote(normed_ref, normed_partner, pair_sems.at[0], pair_sems.at[1], partner)
     pair.start()
     moves = dp_moves(sources, targets, riders, ride_send, ride_recv)
     for move in moves:
         move.start()
-    half = cot_halves[0].shape[0]
+    first = cot_halves[0].shape[0]
+    places = (pl.ds(0, first), pl.ds(first, cot_halves[1].shape[0]))
     cot_loads = [
-        pltpu.make_async_copy(part, cot_partner.at[pl.ds(n * half, half)], cot_sems.at[n])
-        for n, part in enumerate(cot_halves)
+        pltpu.make_async_copy(part, cot_partner.at[place], cot_sems.at[n])
+        for n, (part, place) in enumerate(zip(cot_halves, places))
     ]
     for load in cot_loads:
         load.start()
@@ -1242,12 +1265,37 @@
         plane_exchange(n, stage.at[n], landed[n], local_sems, send_sems, recv_sems) for n in range(4)
     ]
     copies = [pltpu.make_async_copy(stage.at[4 + n], staged[n], stage_sems.at[n]) for n in range(4)]
+
+    def slot_gates():
+        ranks = ranks_ref[...]
+        parity = lax.rem(lax.axis_index("dp"), 2)
+        named = ranks >= 0
+        logits = jnp.where(named, logits_ref[:, :EXPERTS], masked_score)
+        top = jnp.max(logits, axis=-1, keepdims=True)
+        raised = jnp.where(named, jnp.exp(logits - top), 0.0)
+        gates = raised / jnp.sum(raised, axis=-1, keepdims=True)
+        gates_ref[...] = gates
+        slot = lax.broadcasted_iota(jnp.int32, (ranks.shape[0], 128), 1).astype(F32)
+        owned = EXPERTS // plane
+        for place in range(plane):
+            for i in range(2):
+                rows = []
+                for expert in (place * owned + i, place * owned + 2 + i):
+                    hit = ranks[:, expert : expert + 1] == slot
+                    rows.append(
+                        jnp.sum(jnp.where(hit, gates[:, expert : expert + 1], 0.0), axis=0, keepdims=True)
+                    )
+                all_gates[place, i : i + 1, :] = jnp.where(parity == 0, rows[0], rows[1])
+                other_gates[place, i : i + 1, :] = jnp.where(parity == 0, rows[1], rows[0])
+
     for expert in range(2):
         for n, rows_ref, rank_ref in plans:
             if expert == 0 and n == 2:
                 for load in cot_loads:
                     load.wait()
             if expert == 0 and n == 3:
+                slot_gates()
+                gate_pair.start()
                 pair.wait()
             chooser = slot_matrix(rank_ref[expert], plane, True)
             stage[4 * expert + n] = mxu(chooser, rows_ref[...]).astype(BF).reshape(plane, SLOTS, D)
@@ -1256,7 +1304,6 @@
             else:
                 copies[n].start()
     gate_pair.wait()
-    all_gates[:, 0:2, :] = gates_ref[...]
     all_gates[:, 2:4, :] = partner_gates[...]
     gates_here_ref[here] = all_gates[here]
     gate_moves = [
@@ -1279,7 +1326,7 @@
         move.wait()
 
 
-def dispatch_rows(normed, cot, cot_halves, own_ranks, partner_ranks, gates, other_gates, riders, n_dp):
+def dispatch_rows(normed, cot, cot_halves, own_ranks, partner_ranks, logits, ranks, riders, n_dp):
     plane, tokens = own_ranks.shape[1:]
     vmem = pl.BlockSpec(memory_space=pltpu.VMEM)
     anywhere = pl.BlockSpec(memory_space=pl.ANY)
@@ -1288,8 +1335,8 @@
     results = pl.pallas_call(
         functools.partial(dispatch_kernel, plane, n_dp, [(index, flip) for _, index, flip in riders]),
         in_specs=[vmem] * 6 + [anywhere] * (2 + len(riders)),
-        out_specs=[vmem] + [anywhere] * (8 + len(riders)),
-        out_shape=[shape((plane, 4, gates.shape[2]), F32)]
+        out_specs=[vmem] * 2 + [anywhere] * (8 + len(riders)),
+        out_shape=[shape(ranks.shape, F32), shape((plane, 4, 128), F32)]
         + [shape((plane, SLOTS, D), BF)] * 8
         + [shape(picked_shape(array, index), BF) for array, index, _ in riders],
         scratch_shapes=[
@@ -1302,8 +1349,9 @@
             dma((4, plane)),
             dma((len(riders),)),
             dma((len(riders),)),
-            pltpu.VMEM((plane, 4, gates.shape[2]), F32),
-            pltpu.VMEM(gates.shape, F32),
+            pltpu.VMEM((plane, 4, 128), F32),
+            pltpu.VMEM((plane, 2, 128), F32),
+            pltpu.VMEM((plane, 2, 128), F32),
             dma((2,)),
             dma((plane,)),
             dma((plane,)),
@@ -1316,13 +1364,44 @@
         cost_estimate=pl.CostEstimate(flops=2 * 10**10, bytes_accessed=4 * 10**8, transcendentals=0),
         name="dispatch_rows",
     )(
-        normed, cot, own_ranks, partner_ranks, gates, other_gates, *cot_halves, *[a for a, _, _ in riders]
-    )
-    return results[0], results[1:5], results[5:9], results[9:]
+        normed, cot, own_ranks, partner_ranks, logits, ranks, *cot_halves, *[a for a, _, _ in riders]
+    )
+    return results[0], results[1], results[2:6], results[6:10], results[10:]
+
+
+def sum_matrix(which, sources, summed, sums, part_ref, piece_sems, sum_sems):
+    copies = [pltpu.make_async_copy(source, summed.at[n], piece_sems.at[n]) for n, source in enumerate(sources)]
+    for copy in copies:
+        copy.start()
+    for copy in copies:
+        copy.wait()
+    parity = lax.rem(lax.axis_index("dp"), 2)
+    stores = []
+    for side in range(2):
+        total = summed[side].astype(F32)
+        for n in range(side + 2, len(sources), 2):
+            total = total + summed[n].astype(F32)
+        sums[side] = total.astype(BF)
+        place = parity if side == 0 else 1 - parity
+        stores.append(pltpu.make_async_copy(sums.at[side], part_ref.at[place, which], sum_sems.at[side]))
+        stores[-1].start()
+    for store in stores:
+        store.wait()
 
 
 def return_kernel(
-    plane, n_dp, n_results, riders, names, own_rank_ref, partner_rank_ref, dots_ref, ranks_ref, gates_ref, *refs
+    plane,
+    n_dp,
+    n_results,
+    riders,
+    names,
+    own_rank_ref,
+    partner_rank_ref,
+    first_dots_ref,
+    second_dots_ref,
+    ranks_ref,
+    gates_ref,
+    *refs,
 ):
     early, back = refs[0:2], refs[2:4]
     results, refs = refs[4 : 4 + n_results], refs[4 + n_results :]
@@ -1348,17 +1427,22 @@
         dot_sems,
         dot_send,
         dot_recv,
+        dots_ref,
         dots_here_ref,
         dots_other_ref,
         bounce,
         summed,
         sums,
+        partial,
         piece_sems,
         sum_sems,
     ) = refs[len(riders) :]
     here = plane_here()
     partner = {"dp": lax.axis_index("dp") ^ 1}
     greet([plane_peer(here ^ flip) for flip in range(1, plane)] + dp_peers(n_dp))
+    for n, by_side in enumerate((first_dots_ref, second_dots_ref)):
+        for side in range(2):
+            dots_ref[:, 2 * side + n : 2 * side + n + 1, :] = by_side[side]
     own_dots = pltpu.make_async_copy(dots_ref.at[here], dots_here_ref.at[here], dot_sems.at[0])
     own_dots.start()
     dot_moves = [
@@ -1392,28 +1476,6 @@
     dots_pair = remote(dots_here_ref, dots_other_ref, dot_sems.at[1], dot_sems.at[2], partner)
     dots_pair.start()
 
-    def sum_matrix(which):
-        sources = [mine[which].at[0]] + [homes[which, flip, 0] for flip in range(1, n_dp)]
-        copies = [
-            pltpu.make_async_copy(source, summed.at[n], piece_sems.at[n]) for n, source in enumerate(sources)
-        ]
-        for copy in copies:
-            copy.start()
-        for copy in copies:
-            copy.wait()
-        parity = lax.rem(lax.axis_index("dp"), 2)
-        stores = []
-        for side in range(2):
-            total = summed[side].astype(F32)
-            for n in range(side + 2, n_dp, 2):
-                total = total + summed[n].astype(F32)
-            sums[side] = total.astype(BF)
-            place = parity if side == 0 else 1 - parity
-            stores.append(pltpu.make_async_copy(sums.at[side], part_ref.at[place, which], sum_sems.at[side]))
-            stores[-1].start()
-        for store in stores:
-            store.wait()
-
     def of_gates():
         tokens = ranks_ref.shape[0]
         parity = lax.rem(lax.axis_index("dp"), 2)
@@ -1436,36 +1498,59 @@
         dlog_ref[...] = jnp.zeros_like(dlog_ref)
         dlog_ref[:, :EXPERTS] = (gates * (made - mean)).astype(BF)
 
+    def sum_of(which):
+        sources = [mine[which].at[0]] + [homes[which, flip, 0] for flip in range(1, n_dp)]
+        sum_matrix(which, sources, summed, sums, part_ref, piece_sems, sum_sems)
+
+    blocks = [slice(start, start + PBLK) for start in range(0, total_ref.shape[0], PBLK)]
+
+    def collected(rank_ref, rows, side, expert):
+        chooser = slot_matrix(rank_ref[expert, rows, :], plane, False)
+        return mxu(chooser, held[2 * side + expert].reshape(plane * SLOTS, D))
+
     for move in moves[:RETURN_FIRST]:
         move.start()
-    sum_matrix(0)
     loads[1].wait()
+    for rows in blocks:
+        partial[rows, :] = collected(partner_rank_ref, rows, 1, 0)
+    loads[0].wait()
+    for rows in blocks:
+        total_ref[rows, :] = collected(own_rank_ref, rows, 0, 0)
+    sum_of(0)
+    sum_of(1)
     exchanges[1][1]()
     exchanges[0][0]()
-    collect_into(plane, partner_rank_ref, held, 2, to_partner, lambda rows, made: made.astype(BF))
-    pair = remote(to_partner, of_partner, pair_sems.at[0], pair_sems.at[1], partner)
-    pair.start()
+    pairs = []
+    for n, rows in enumerate(blocks):
+        to_partner[rows, :] = (partial[rows, :] + collected(partner_rank_ref, rows, 1, 1)).astype(BF)
+        block = pl.ds(n * PBLK, PBLK)
+        pairs.append(
+            remote(to_partner.at[block], of_partner.at[block], pair_sems.at[0, n], pair_sems.at[1, n], partner)
+        )
+        pairs[-1].start()
     for move in moves[RETURN_FIRST:]:
         move.start()
     for begin, _ in later:
         begin()
-    loads[0].wait()
-    exchanges[0][1]()
-    collect_into(plane, own_rank_ref, held, 0, total_ref, lambda rows, made: made)
     dots_pair.wait()
     of_gates()
-    pair.wait()
-    total_ref[...] += of_partner[...].astype(F32)
+    for move in moves[:RETURN_FIRST]:
+        move.wait()
+    sum_of(2)
+    exchanges[0][1]()
+    for rows in blocks:
+        total_ref[rows, :] += collected(own_rank_ref, rows, 0, 1)
+    for pair, rows in zip(pairs, blocks):
+        pair.wait()
+        total_ref[rows, :] += of_partner[rows, :].astype(F32)
+    for move in moves[RETURN_FIRST:]:
+        move.wait()
     for _, finish in later:
         finish()
-    for move in moves:
-        move.wait()
-    sum_matrix(1)
-    sum_matrix(2)
 
 
 def return_rows(
-    own_ranks, partner_ranks, dots, ranks, gates, early, back, results, riders, names, shares, arrived, n_dp
+    own_ranks, partner_ranks, first_dots, second_dots, ranks, gates, early, back, results, riders, names, shares, arrived, n_dp
 ):
     tokens, plane = own_ranks.shape[1:]
     vmem = pl.BlockSpec(memory_space=pltpu.VMEM)
@@ -1476,7 +1561,7 @@
         functools.partial(
             return_kernel, plane, n_dp, len(results), [(index, flip) for _, index, flip in riders], names
         ),
-        in_specs=[vmem] * 5 + [anywhere] * (7 + len(results) + len(riders) + len(arrived)),
+        in_specs=[vmem] * 6 + [anywhere] * (7 + len(results) + len(riders) + len(arrived)),
         out_specs=[vmem] * 2 + [anywhere] * (1 + len(results) + len(riders)),
         out_shape=[shape((tokens, D), F32), shape((tokens, 128), BF), shape((2, 3) + shares[0].shape[1:], BF)]
         + [shape(rows.shape, BF) for rows in results]
@@ -1486,7 +1571,7 @@
             pltpu.VMEM((tokens, D), BF),
             pltpu.VMEM((tokens, D), BF),
             dma((2,)),
-            dma((2,)),
+            dma((2, tokens // PBLK)),
             dma((4,)),
             dma((4, plane)),
             dma((4, plane)),
@@ -1495,11 +1580,13 @@
             dma((3,)),
             dma((plane,)),
             dma((plane,)),
-            pltpu.VMEM(dots.shape, F32),
-            pltpu.VMEM(dots.shape, F32),
+            pltpu.VMEM((plane, 4, 128), F32),
+            pltpu.VMEM((plane, 4, 128), F32),
+            pltpu.VMEM((plane, 4, 128), F32),
             pltpu.VMEM((2 + len(results), SLOTS, D), BF),
             pltpu.VMEM(shares[0].shape, BF),
             pltpu.VMEM((2,) + shares[0].shape[1:], BF),
+            pltpu.VMEM((tokens, D), F32),
             dma((n_dp,)),
             dma((2,)),
         ],
@@ -1511,7 +1598,8 @@
     )(
         own_ranks,
         partner_ranks,
-        dots,
+        first_dots,
+        second_dots,
         ranks,
         gates,
         *early,
@@ -1561,7 +1649,7 @@
     return begin, pass_on, finish
 
 
-def backward_kernel(n_dp, prompt_len, riders, *refs):
+def backward_kernel(n_dp, prompt_len, n_results, riders, *refs):
     (
         dlog_ref,
         cot_ref,
@@ -1578,13 +1666,14 @@
         total_ref,
         w_out_ref,
         w_in_ref,
+        normed_two_ref,
         part_ref,
-    ) = refs[:16]
-    results, refs = refs[16:18], refs[18:]
+    ) = refs[:17]
+    results, refs = refs[17 : 17 + n_results], refs[17 + n_results :]
     late = len(riders)
     sources, refs = refs[:late], refs[late:]
-    grad_x_ref, gains_ref, grad_out_ref, grad_in_ref, all_ref = refs[:5]
-    results_back, refs = refs[5:7], refs[7:]
+    grad_x_ref, grad_out_ref, grad_in_ref, grad_small_ref, all_ref = refs[:5]
+    results_back, refs = refs[5 : 5 + n_results], refs[5 + n_results :]
     homes, refs = refs[:late], refs[late:]
     (
         weights,
@@ -1605,6 +1694,7 @@
         share_sends,
         share_recvs,
         small,
+        gains_ref,
         bounce,
         local_sems,
         send_sems,
@@ -1636,7 +1726,7 @@
     begin_all()
     exchanges = [
         plane_exchange(side, results[side], results_back[side], local_sems, send_sems, recv_sems, bounce)
-        for side in range(2)
+        for side in range(n_results)
     ]
     load_small.wait()
     load_total.wait()
@@ -1674,7 +1764,7 @@
             rows = slice(first_row, first_row + PBLK)
             queries, grads = qkv_ref[rows, columns], grad_qkv[rows, columns]
             scores = mxu(queries, kv_ref[:keys, key_columns], ((1,), (1,)))
-            scores = masked_scores(scores, first_row, prompt_len, block_index)
+            scores = masked_scores(scores, first_row, block_index)
             lane = lax.broadcasted_iota(jnp.int32, (PBLK, log_ref.shape[1]), 1)
             logs = jnp.sum(jnp.where(lane == head, log_ref[rows, :], 0.0), axis=-1, keepdims=True)
             probs = jnp.exp(scores - logs)
@@ -1723,6 +1813,8 @@
         return carry
 
     lax.fori_loop(0, n_dp, share_of_out, 0)
+    load_normed = pltpu.make_async_copy(normed_two_ref, grad_attn, load_sems.at[0])
+    load_normed.start()
 
     for move in kv_moves:
         move.wait()
@@ -1759,9 +1851,18 @@
         grad_x_ref[rows, :] = (grad_mid[rows, :] + by_rows).astype(BF)
         return carry
 
+    pass_on()
     lax.fori_loop(0, tokens // PBLK, through_first, 0)
-    pass_on()
+    load_normed.wait()
+    lane = lax.broadcasted_iota(jnp.int32, (8, 128), 1)
+    column = lax.broadcasted_iota(jnp.int32, (8, 128), 0) + EXPERTS
+    place = jnp.where((lane == column) & (column < EXPERTS + 2), 1.0, 0.0).astype(BF)
+    of_router = mxu(grad_attn[...], dlog_ref[...], ((0,), (0,)))
+    small[...] = (of_router + mxu(gains_ref[...].astype(BF), place, ((0,), (0,)))).astype(BF)
+    store_small = pltpu.make_async_copy(small, grad_small_ref, store_sems.at[0])
+    store_small.start()
     finish()
+    store_small.wait()
     for _, end in exchanges:
         end()
     for move in homing:
@@ -1780,14 +1881,16 @@
     plane = results[0].shape[0]
     shape = jax.ShapeDtypeStruct
     return pl.pallas_call(
-        functools.partial(backward_kernel, n_dp, prompt_len, [(index, flip) for _, index, flip in riders]),
-        in_specs=[vmem] * len(in_vmem) + [anywhere] * (len(in_hbm) + 2 + len(riders)),
-        out_specs=[vmem] * 2 + [anywhere] * (5 + len(riders)),
+        functools.partial(
+            backward_kernel, n_dp, prompt_len, len(results), [(index, flip) for _, index, flip in riders]
+        ),
+        in_specs=[vmem] * len(in_vmem) + [anywhere] * (len(in_hbm) + len(results) + len(riders)),
+        out_specs=[vmem] + [anywhere] * (4 + len(results) + len(riders)),
         out_shape=[
             shape((tokens, D), BF),
-            shape((8, D), F32),
             shape((D, D), BF),
             shape((D, width), BF),
+            shape((D, 128), BF),
             shape((n_context,) + part.shape, BF),
         ]
         + [shape(rows.shape, BF) for rows in results]
@@ -1811,10 +1914,11 @@
             pltpu.SemaphoreType.DMA((3,)),
             pltpu.SemaphoreType.DMA((n_context,)),
             pltpu.VMEM((D, 128), BF),
-            pltpu.VMEM((2, SLOTS, D), BF),
-            pltpu.SemaphoreType.DMA((2,)),
-            pltpu.SemaphoreType.DMA((2, plane)),
-            pltpu.SemaphoreType.DMA((2, plane)),
+            pltpu.VMEM((8, D), F32),
+            pltpu.VMEM((len(results), SLOTS, D), BF),
+            pltpu.SemaphoreType.DMA((len(results),)),
+            pltpu.SemaphoreType.DMA((len(results), plane)),
+            pltpu.SemaphoreType.DMA((len(results), plane)),
         ],
         compiler_params=pltpu.CompilerParams(
             vmem_limit_bytes=56 * 1024 * 1024, collective_id=4, has_side_effects=True
@@ -1826,11 +1930,13 @@
 def reduce_kernel(n_dp, widths, *refs):
     count = len(widths)
     shares, refs = refs[:count], refs[count:]
-    part_ref, own_rank_ref, partner_rank_ref, mid_ref = refs[:4]
-    rows_of, refs = (refs[4:6], refs[6:8]), refs[8:]
+    own_rank_ref, partner_rank_ref, mid_ref = refs[:3]
+    rows_of, mine, refs = (refs[3:5], refs[5:7]), refs[7:10], refs[10:]
+    names = HOME_RETURN[RETURN_FIRST:] + HOME_BACKWARD
+    homes, refs = dict(zip(names, refs)), refs[len(names) :]
     totals, refs = refs[:count], refs[count:]
-    result_ref, all_ref = refs[:2]
-    refs = refs[2:]
+    result_ref, all_ref, part_ref = refs[:3]
+    refs = refs[3:]
     sums, core_in, first_in, second_in, z_in = (refs[n * count : (n + 1) * count] for n in range(5))
     (
         load_sems,
@@ -1853,6 +1959,10 @@
         mixed,
         mid_block,
         held_sems,
+        summed,
+        matrix_sums,
+        piece_sems,
+        sum_sems,
     ) = refs[5 * count :]
     here = plane_here()
     plane = held.shape[1]
@@ -1897,10 +2007,15 @@
             share_sends.at[m],
             share_recvs.at[m],
         )
-        for m in range(3)
+        for m in range(2)
     ]
+
+    def sum_of(which):
+        sources = [mine[which].at[0]] + [homes[which, flip, 1] for flip in range(1, n_dp)]
+        sum_matrix(which, sources, summed, matrix_sums, part_ref, piece_sems, sum_sems)
+
+    sum_of(0)
     gathers[0][0]()
-
     for copy in rows_here:
         copy.wait()
     collect_into(plane, partner_rank_ref, held, 0, to_partner, lambda rows, made: made.astype(BF))
@@ -1932,6 +2047,8 @@
                     plane_peer(here ^ toward),
                 )
                 first_moves[n, a, slot].start()
+    sum_of(1)
+    sum_of(2)
     for copy in rows_here:
         copy.wait()
 
@@ -1958,7 +2075,6 @@
             )
             second_moves[n, a].start()
     gathers[1][0]()
-    gathers[2][0]()
     gathers[0][1]()
     for n in order:
         for a in range(count):
@@ -2004,7 +2120,6 @@
         landed(a, here ^ 6)
         pass_on(a, 2, 1, here ^ 6)
     gathers[1][1]()
-    gathers[2][1]()
     pair.wait()
     result_ref[...] = (mixed[...] + of_partner[...].astype(F32)).astype(BF)
     for a in range(count):
@@ -2016,7 +2131,7 @@
         finish()
 
 
-def reduce_shares(shares, part, ranks, mid, slot_rows, n_dp, n_context):
+def reduce_shares(shares, ranks, mid, slot_rows, mine, homes, n_dp, n_context):
     plane, rows = shares[0].shape[1:3]
     widths = tuple(share.shape[3] for share in shares)
     count = len(widths)
@@ -2030,12 +2145,13 @@
 
     return pl.pallas_call(
         functools.partial(reduce_kernel, n_dp, widths),
-        in_specs=[anywhere] * (count + 1) + [vmem] * 2 + [anywhere] * 5,
-        out_specs=[vmem] * (count + 1) + [anywhere],
+        in_specs=[anywhere] * count + [vmem] * 2 + [anywhere] * (8 + len(homes)),
+        out_specs=[vmem] * (count + 1) + [anywhere] * 2,
         out_shape=[shape((plane, rows, width), BF) for width in widths]
         + [
             shape(mid.shape, BF),
-            shape((n_context,) + part.shape, BF),
+            shape((n_context, 2, 2) + homes[0].shape, BF),
+            shape((2, 3) + homes[0].shape, BF),
         ],
         scratch_shapes=buffers(n_dp, 4)
         + buffers(n_dp, 4)
@@ -2054,8 +2170,8 @@
             dma((count, n_dp)),
             dma((count, 3, plane)),
             dma((count, plane)),
-            dma((3, 3)),
-            dma((3, n_context)),
+            dma((2, 3)),
+            dma((2, n_context)),
             dma((2,)),
             pltpu.VMEM((2, plane, SLOTS, D), BF),
             pltpu.VMEM(mid.shape, BF),
@@ -2063,59 +2179,93 @@
             pltpu.VMEM(mid.shape, F32),
             pltpu.VMEM((PBLK, D), F32),
             dma((3,)),
+            pltpu.VMEM((n_dp,) + homes[0].shape, BF),
+            pltpu.VMEM((2,) + homes[0].shape, BF),
+            dma((n_dp,)),
+            dma((2,)),
         ],
         compiler_params=pltpu.CompilerParams(
             vmem_limit_bytes=56 * 1024 * 1024, collective_id=5, has_side_effects=True
         ),
         name="reduce_shares",
-    )(*shares, part, *ranks, mid, *slot_rows[0], *slot_rows[1])
-
-
-def finish_kernel(down, first_ref, second_ref, own_first_ref, own_second_ref, out_ref):
-    n_context = first_ref.shape[0]
-    experts = out_ref.shape[1]
+    )(*shares, *ranks, mid, *slot_rows[0], *slot_rows[1], *mine, *homes)
+
+
+def finish_kernel(n_context, apart, halves, *refs):
+    (first_ref, own_first_ref), out_ref = refs[:2], refs[-1]
+    seconds = refs[2:-1]
+    step, experts, _ = out_ref.shape
     here = lax.axis_index("context")
-
-    def of_expert(all_ref, own_ref):
-        own = own_ref[:, 0].astype(F32)
-        return jnp.stack(
-            [jnp.where(here == place, own, all_ref[place, :, 0].astype(F32)) for place in range(n_context)]
-        )
-
-    both = [of_expert(first_ref, own_first_ref), of_expert(second_ref, own_second_ref)]
-    both = jnp.stack(both, axis=2).reshape((experts,) + both[0].shape[2:])
-    if not down:
-        out_ref[...] = jnp.swapaxes(both, 0, 1)
-        return
-    half = out_ref.shape[2] // 2
-    for side in range(2):
-        out_ref[:, :, side * half : (side + 1) * half] = jnp.swapaxes(both[:, side], 0, 1)
-
-
-def finish_weight(which, first, second, own_first, own_second):
-    n_context, pair, _, rows, width = first.shape
-    experts = n_context * pair * 2
+    group = 16
+    size = group * experts
+    log_group, log_experts = group.bit_length() - 1, experts.bit_length() - 1
+    to = lax.broadcasted_iota(jnp.int32, (size, size), 0)
+    of = lax.broadcasted_iota(jnp.int32, (size, size), 1)
+    same_row = (to >> log_experts) == (of & (group - 1))
+    same_expert = (to & (experts - 1)) == (of >> log_group)
+    turned = jnp.where(same_row & same_expert, 1.0, 0.0).astype(BF)
+
+    def gathered(all_ref, own_ref, place, side, at):
+        return jnp.where(here == place, own_ref[(side, 0) + at], all_ref[(place, side, 0) + at])
+
+    def by_distance(place, side, at):
+        value = seconds[0][(side, 0) + at]
+        for flip in range(1, n_context):
+            value = jnp.where((here ^ place) == flip, seconds[flip][(side, 0) + at], value)
+        return value
+
+    width = out_ref.shape[2] // halves
+    for half in range(halves):
+        at_half = (half,) if halves > 1 else ()
+        for start in range(0, step, group):
+            at = at_half + (slice(start, start + group),)
+            rows = []
+            for place in range(n_context):
+                for side in range(2):
+                    rows.append(gathered(first_ref, own_first_ref, place, side, at))
+                    if apart:
+                        rows.append(by_distance(place, side, at))
+                    else:
+                        rows.append(gathered(seconds[0], seconds[1], place, side, at))
+            made = mxu(turned, jnp.concatenate(rows, axis=0))
+            out_ref[start : start + group, :, half * width : (half + 1) * width] = made.reshape(
+                group, experts, width
+            )
+
+
+def finish_weight(which, first, own_first, seconds):
+    n_context, _, _, rows, width = first.shape
+    experts = n_context * 4
     step = 32
-    down = which == 2
-    parts = (first, second, own_first, own_second)
-    if down:
-        rows = rows // 2
-        parts = [part.reshape(part.shape[:-2] + (2, rows, width)) for part in parts]
-        spec = pl.BlockSpec((n_context, pair, 1, 2, step, width), lambda j: (0, 0, which, 0, j, 0))
-        own = pl.BlockSpec((pair, 1, 2, step, width), lambda j: (0, which, 0, j, 0))
-        width = 2 * width
-    else:
-        spec = pl.BlockSpec((n_context, pair, 1, step, width), lambda j: (0, 0, which, j, 0))
-        own = pl.BlockSpec((pair, 1, step, width), lambda j: (0, which, j, 0))
+    apart = len(seconds) == n_context
+    halves = 2 if which == 2 else 1
+    rows, wide = rows // halves, width * halves
+    parts = [first, own_first, *seconds]
+    specs = []
+    for n, part in enumerate(parts):
+        lead = part.shape[:-3]
+        matrix = 0 if part.shape[-3] == 1 else which
+        if halves > 1:
+            parts[n] = part.reshape(part.shape[:-2] + (halves, rows, width))
+            block = lead + (1, halves, step, width)
+            specs.append(pl.BlockSpec(block, lambda j, k=len(lead), m=matrix: (0,) * k + (m, 0, j, 0)))
+        else:
+            block = lead + (1, step, width)
+            specs.append(pl.BlockSpec(block, lambda j, k=len(lead), m=matrix: (0,) * k + (m, j, 0)))
     return pl.pallas_call(
-        functools.partial(finish_kernel, down),
+        functools.partial(finish_kernel, n_context, apart, halves),
         grid=(rows // step,),
-        in_specs=[spec, spec, own, own],
-        out_specs=pl.BlockSpec((step, experts, width), lambda j: (j, 0, 0)),
-        out_shape=jax.ShapeDtypeStruct((rows, experts, width), F32),
+        in_specs=specs,
+        out_specs=pl.BlockSpec((step, experts, wide), lambda j: (j, 0, 0)),
+        out_shape=jax.ShapeDtypeStruct((rows, experts, wide), F32),
         compiler_params=grant(),
+        cost_estimate=pl.CostEstimate(flops=2 * 10**9, bytes_accessed=30 * 10**6, transcendentals=0),
         name="finish_weight",
     )(*parts)
+
+
+def flip_permute(value, axis, size, flip):
+    return lax.ppermute(value, axis, [(i, i ^ flip) for i in range(size)])
 
 
 def local_paired(
@@ -2158,14 +2308,12 @@
     )
     qkv_width = D + 2 * KVH * HD
     weights = (expert_gate, expert_up, expert_down)
-    own_ranks_t, own_rows, own_columns, partner_rows, partner_columns, whole_in, w_out, *weight_halves = (
+    own_ranks, own_rows, own_columns, partner_rows, partner_columns, whole_in, w_out, *weight_halves = (
         gather_parts(route_rows.T, part_in, part_of(attn_o), weights, cot_low, n_dp, n_context, plane)
     )
     partner_cot = [weight_halves.pop()]
     whole_in = whole_in.reshape(-1, part_in.shape[1])
     w_out = w_out.reshape(-1, D)
-    own_ranks = own_ranks_t.T
-    named = own_ranks >= 0
     pieces = {(which, 0, i): (weight_halves[which], (0, i)) for which in range(3) for i in range(2)}
 
     def riding(names):
@@ -2190,27 +2338,16 @@
         front(prompt_len, n_dp, x_low, cosine, sine, whole_in, w_out, cot_low, riding(RIDE_FRONT))
     )
     partner_cot.append(cot_half)
-    for (which, flip, _), piece in zip(RIDE_FRONT, moved):
-        for i in range(2):
-            pieces[which, flip, i] = (piece, i)
-
-    logits = logits[:, :EXPERTS]
-    top_logit = jnp.max(jnp.where(named, logits, masked_score), axis=1, keepdims=True)
-    raised = jnp.where(named, jnp.exp(jnp.where(named, logits - top_logit, 0.0)), 0.0)
-    gates = raised / jnp.sum(raised, axis=1, keepdims=True)
-
-    slot_ids = jnp.arange(SLOTS, dtype=F32)
-    hits = own_ranks_t[:, None, :] == slot_ids[None, :, None]
-    slot_gates = jnp.sum(jnp.where(hits, gates.T[:, None, :], 0.0), axis=-1)
-    slot_gates = jnp.pad(slot_gates, ((0, 0), (0, 128 - SLOTS))).reshape(plane, 2, 2, 128)
-    own_gates = lax.dynamic_index_in_dim(slot_gates, parity, 1, keepdims=False)
-    other_gates = lax.dynamic_index_in_dim(slot_gates, 1 - parity, 1, keepdims=False)
-    gates_here, landed, staged, arrived = dispatch_rows(
-        normed_two, cot_low, partner_cot, own_rows, partner_rows, own_gates, other_gates, riding(RIDE_DISPATCH), n_dp
+    for (which, flip, expert), piece in zip(RIDE_FRONT, moved):
+        if expert is None:
+            pieces.update({(which, flip, i): (piece, i) for i in range(2)})
+        else:
+            pieces[which, flip, expert] = (piece, None)
+
+    gates, gates_here, landed, staged, arrived = dispatch_rows(
+        normed_two, cot_low, partner_cot, own_rows, partner_rows, logits, own_ranks, riding(RIDE_DISPATCH), n_dp
     )
     pieces.update({name: (piece, None) for name, piece in zip(RIDE_DISPATCH, arrived)})
-    def gates_of(expert):
-        return [gates_here[:, 2 * side + expert, :SLOTS].reshape(plane * SLOTS, 1) for side in range(2)]
 
     def slots_of(arrays):
         flat = [array.reshape(plane * SLOTS, D) for array in arrays]
@@ -2219,60 +2356,44 @@
     parted = lambda arrays: [array.reshape(plane, SLOTS, D) for array in arrays]
     rows, cots = slots_of(landed)
     first, first_dots, first_shares, landed, arrived = run_expert(
-        "first_expert", 6, rows, cots, gates_of(0), pieces_of(0), staged, riding(RIDE_FIRST)
+        "first_expert", 0, 6, rows, cots, gates_here, pieces_of(0), staged, riding(RIDE_FIRST)
     )
     pieces.update({name: (piece, None) for name, piece in zip(RIDE_FIRST, arrived)})
     rows, cots = slots_of(landed)
-    home_of = {}
 
     def homing(names, *shares):
         return [(shares[i][which], flip, flip) for which, flip, i in names]
 
     second, second_dots, second_shares, early, homes = run_expert(
         "second_expert",
+        1,
         7,
         rows,
         cots,
-        gates_of(1),
+        gates_here,
         pieces_of(1),
         parted(first)[1:4],
         homing(HOME_SECOND, first_shares),
     )
 
-    dots = jnp.stack(
-        [d[side].reshape(plane, SLOTS) for side in range(2) for d in (first_dots, second_dots)], axis=1
-    )
-    dots = jnp.pad(dots, ((0, 0), (0, 0), (0, 128 - SLOTS)))
     second = parted(second)
-    grad_rows, grad_logits, part_first, late, _ = return_rows(
+    grad_rows, grad_logits, part_first, late, homes_second = return_rows(
         own_columns,
         partner_columns,
-        dots,
+        first_dots,
+        second_dots,
         own_ranks,
         gates,
         early[1:3],
         second[2:4],
-        parted(first)[0:1],
+        [parted(first)[0], second[1]],
         homing(HOME_RETURN, first_shares, second_shares),
         HOME_RETURN,
         first_shares,
         homes,
         n_dp,
     )
-    grad_wrouter = mxu(normed_two, grad_logits, ((0,), (0,)))[:, :EXPERTS]
-
-    def part_of_expert(expert, shares):
-        parts = []
-        for which in range(3):
-            got = [shares[which][0]] + [home_of[which, flip, expert] for flip in range(1, n_dp)]
-            same = sum(got[flip].astype(F32) for flip in range(0, n_dp, 2)).astype(BF)
-            other = sum(got[flip].astype(F32) for flip in range(1, n_dp, 2)).astype(BF)
-            parts.append(
-                jnp.stack([jnp.where(parity == 0, same, other), jnp.where(parity == 0, other, same)])
-            )
-        return jnp.stack(parts, axis=1)
-
-    grad_inputs, grad_gains, grad_wout, grad_wqkv, all_first, *homes = backward(
+    grad_inputs, grad_wout, grad_wqkv, grad_small, all_first, *homes = backward(
         prompt_len,
         n_dp,
         (
@@ -2288,27 +2409,32 @@
             cosine,
             sine,
         ),
-        (mid_rows, grad_rows, w_out, whole_in, part_first),
-        second[0:2],
+        (mid_rows, grad_rows, w_out, whole_in, normed_two, part_first),
+        second[0:1],
         homing(HOME_BACKWARD, first_shares, second_shares),
     )
-    last, homes = homes[:2], homes[2:]
-    out_own, out_partner = [late[0], last[0]], [early[0], last[1]]
-    home_of.update(zip(HOME_BACKWARD, homes))
-
-    grad_small = jnp.concatenate([grad_wrouter, grad_gains[0][:, None], grad_gains[1][:, None]], axis=1)
-    grad_small = jnp.pad(grad_small, ((0, 0), (0, 128 - grad_small.shape[1]))).astype(BF)
+    last, homes = homes[0], list(homes_second[RETURN_FIRST:]) + list(homes[1:])
+    out_own, out_partner = [late[0], last], [early[0], late[1]]
+
     parts = lambda share: share.reshape(n_dp, plane, -1, share.shape[1])
-    part_second = part_of_expert(1, second_shares)
-    total_qkv, total_out, total_small, result, all_second = reduce_shares(
+    total_qkv, total_out, total_small, result, all_second, part_second = reduce_shares(
         [parts(grad_wqkv), parts(grad_wout), parts(grad_small)],
-        part_second,
         (own_columns, partner_columns),
         mid_rows,
         (out_own, out_partner),
+        second_shares,
+        homes,
         n_dp,
         n_context,
     )
+    own = part_second[:, 2:]
+    across = flip_permute(own, "context", n_context, 2)
+    beside = flip_permute(own, "context", n_context, 1)
+    grad_gate, grad_up = (
+        finish_weight(which, all_first, part_first, (all_second, part_second)) for which in range(2)
+    )
+    across, beside, grad_gate, grad_up = lax.optimization_barrier((across, beside, grad_gate, grad_up))
+    apart = (own, beside, across, flip_permute(across, "context", n_context, 1))
     total_qkv = total_qkv.reshape(-1, qkv_width).astype(F32)
     total_out = total_out.reshape(-1, D).astype(F32)
     total_small = total_small.reshape(-1, 128).astype(F32)
@@ -2322,9 +2448,9 @@
         total_small[:, EXPERTS],
         total_small[:, EXPERTS + 1],
         total_small[:, :EXPERTS],
-        finish_weight(0, all_first, all_second, part_first, part_second),
-        finish_weight(1, all_first, all_second, part_first, part_second),
-        finish_weight(2, all_first, all_second, part_first, part_second),
+        grad_gate,
+        grad_up,
+        finish_weight(2, all_first, part_first, apart),
     )
 
 

time: 1070 us -> 992 us (0.927)
  Pallas kernels: 1010 us -> 961 us
  other arithmetic: 26.7 us -> 6.17 us
    pallas_call x4, Pallas kernels: 201 us -> 170 us  [the longest x1 127 us: backward(): pl.pallas_call(functools.partial(backward_kernel, n_dp, prompt_len, len(r...]
    pallas_call x1, Pallas kernels: 154 us -> 129 us  [reduce_shares(): pl.pallas_call(functools.partial(reduce_kernel, n_dp, widths), in_specs=[...]
    pallas_call x1, Pallas kernels: 160 us -> 143 us  [dispatch_rows(): pl.pallas_call(functools.partial(dispatch_kernel, plane, n_dp, [(index, f...]
  transfers between devices with their start and end apart: 0 -> 3, of which waited for: 0 -> 0; matrix products, arithmetic and copies ran while one was open for 0% -> 1% of each run, Pallas kernels for 0% -> 3%
where the time goes in v5:
time: 992 us; the launch traced here: 987 us
  Pallas kernels  961 us (97%)
  local copies, waits for them, and re-layouts  17.3 us (2%)
    pallas_call x2, Pallas kernels, run_expert(): pl.pallas_call(functools.partial(expert_kernel, plane, n_dp, half_steps,...  232 us
    pallas_call x1, Pallas kernels, dispatch_rows(): pl.pallas_call(functools.partial(dispatch_kernel, plane, n_dp, [(index, f...  143 us
    pallas_call x1, Pallas kernels, return_rows(): pl.pallas_call(functools.partial(return_kernel, plane, n_dp, len(results)...  141 us
    pallas_call x1, Pallas kernels, reduce_shares(): pl.pallas_call(functools.partial(reduce_kernel, n_dp, widths), in_specs=[...  129 us
    pallas_call x1, Pallas kernels, backward(): pl.pallas_call(functools.partial(backward_kernel, n_dp, prompt_len, len(r...  127 us
    pallas_call x1, Pallas kernels, front(): pl.pallas_call(functools.partial(front_kernel, n_dp, prompt_len, [(index,...  74.2 us
    pallas_call x1, Pallas kernels, gather_parts(): pl.pallas_call(functools.partial(gather_kernel, n_dp, plane), in_specs=[v...  71.5 us
    pallas_call x3, Pallas kernels, finish_weight(): pl.pallas_call(functools.partial(finish_kernel, n_context, apart, halves)...  42.6 us
  transfers between devices with their start and end apart: 3, of which 0 were waited for; matrix products, arithmetic and copies ran while one was open for 1% of the time, Pallas kernels for 3%

profile of v5, /device:TPU:0, one launch (start us, length us, event | category | flops | bytes accessed | tf_op | source)
XLA Modules:
  0.0 987.2 jit_solution(6006945637003216608)
XLA Ops:
  0.6 0.0 copy-start
  0.7 0.7 copy-done
  1.4 0.1 constant_dynamic-slice_fusion
  1.5 0.1 copy.35
  1.6 0.8 convert_bitcast_fusion
  2.4 0.1 copy.31
  2.5 0.1 copy.30
  2.6 0.8 dynamic-slice_convert_fusion.2
  3.5 1.7 dynamic-slice_convert_fusion
  5.2 1.4 fusion
  6.7 1.2 pad_maximum_fusion
  7.8 0.8 concatenate.16.in_ref
  8.6 71.5 %gather_parts.1 = (f32[768,32]{1,0:T(8,128)}, bf16[2,8,768]{2,1,0:T(8,128)(2,1)}, bf16[2,768,8]{2,1,0:T(8,128)(2,1)}, bf16[2,8,768]{2,1,0:T(8,128)(2,1)}, bf16[2...) custom-call(s32[4,768]{1,0:T(4,128)} %bitcast.79, ...), custom_call_target="tpu_custom_call" | custom-call | tf_op jit(solution)/shard_map/gather_parts/pallas_call | solution.py:980
  80.1 74.2 %front.1 = (f32[8,1536]{1,0:T(8,128)}, bf16[768,1536]{1,0:T(8,128)(2,1)}, bf16[768,2048]{1,0:T(8,128)(2,1)}, bf16[1536,512]{1,0:T(8,128)(2,1)}, bf16[768,1536]{1...) custom-call(bf16[768,1536]{1,0:T(8,128)(2,1)} %bitcast.56, ...), custom_call_target="tpu_custom_call" | custom-call | tf_op jit(solution)/shard_map/front/pallas_call | solution.py:1179
  154.4 142.7 %dispatch_rows.1 = (f32[768,32]{1,0:T(8,128)}, f32[8,4,128]{2,1,0:T(4,128)}, bf16[8,112,1536]{2,1,0:T(8,128)(2,1)}, bf16[8,112,1536]{2,1,0:T(8,128)(2,1)}, bf16[...) custom-call(bf16[768,1536]{1,0:T(8,128)(2,1)} %get-tuple-element.126, ...), custom_call_target="tpu_custom_call" | custom-call | flops 20000000000 | bytes 400000000 | tf_op jit(solution)/shard_map/dispatch_rows/pallas_call | solution.py:1335
  297.1 127.0 %first_expert.1 = (bf16[896,1536]{1,0:T(8,128)(2,1)}, bf16[896,1536]{1,0:T(8,128)(2,1)}, bf16[896,1536]{1,0:T(8,128)(2,1)}, bf16[896,1536]{1,0:T(8,128)(2,1)}, f...) custom-call(bf16[896,1536]{1,0:T(8,128)(2,1)} %bitcast.69, ...), custom_call_target="tpu_custom_call" | custom-call | tf_op jit(solution)/shard_map/first_expert/pallas_call | solution.py:690
  424.2 105.3 %second_expert.1 = (bf16[896,1536]{1,0:T(8,128)(2,1)}, bf16[896,1536]{1,0:T(8,128)(2,1)}, bf16[896,1536]{1,0:T(8,128)(2,1)}, bf16[896,1536]{1,0:T(8,128)(2,1)}, ...) custom-call(bf16[896,1536]{1,0:T(8,128)(2,1)} %bitcast.65, ...), custom_call_target="tpu_custom_call" | custom-call | tf_op jit(solution)/shard_map/second_expert/pallas_call | solution.py:690
  529.5 140.8 %return_rows.1 = (f32[768,1536]{1,0:T(8,128)}, bf16[768,128]{1,0:T(8,128)(2,1)}, bf16[2,3,384,768]{3,2,1,0:T(8,128)(2,1)}, bf16[8,112,1536]{2,1,0:T(8,128)(2,1)}...) custom-call(bf16[2,768,8]{2,1,0:T(8,128)(2,1)} %get-tuple-element.12, ...), custom_call_target="tpu_custom_call" | custom-call | flops 30000001024 | bytes 400000000 | tf_op jit(solution)/shard_map/return_rows/pallas_call | solution.py:1560
  670.3 127.4 %backward.1 = (bf16[768,1536]{1,0:T(8,128)(2,1)}, bf16[1536,1536]{1,0:T(8,128)(2,1)}, bf16[1536,2048]{1,0:T(8,128)(2,1)}, bf16[1536,128]{1,0:T(8,128)(2,1)}, bf1...) custom-call(bf16[768,128]{1,0:T(8,128)(2,1)} %get-tuple-element.187., ...), custom_call_target="tpu_custom_call" | custom-call | tf_op jit(solution)/shard_map/backward/pallas_call | solution.py:1883
  797.7 129.3 %reduce_shares.1 = (bf16[8,48,2048]{2,1,0:T(8,128)(2,1)}, bf16[8,48,1536]{2,1,0:T(8,128)(2,1)}, bf16[8,48,128]{2,1,0:T(8,128)(2,1)}, bf16[768,1536]{1,0:T(8,128)...) custom-call(bf16[4,8,48,2048]{3,2,1,0:T(8,128)(2,1)} %bitcast.58, ...), custom_call_target="tpu_custom_call" | custom-call | tf_op jit(solution)/shard_map/reduce_shares/pallas_call | solution.py:2146
  927.0 1.4 slice.27
  928.4 0.0 copy-start.2
  928.4 0.4 collective-permute-start.1
  928.8 1.0 collective-permute-start
  929.8 15.2 %finish_weight.4 = f32[384,16,768]{2,1,0:T(8,128)} custom-call(bf16[4,2,3,384,768]{4,3,2,1,0:T(8,128)(2,1)} %get-tuple-element.222.refs_0_, bf16[2,3,384,768]{3,2,1,0:T(8,128)(2,1)} %get-tuple-element.196.refs_16_.refs_1_, bf16[4,2,2,384,768]{4,3,2,1,0:T(8,128)(2,1)} %get-tuple-element.223.refs_2_, bf16[2,3,384,768]{3,2,1,0:T(8,128)(2,1)} %get-tuple-element.221.refs_3_), custom_call_target="tpu_custom_call" | custom-call | flops 2000000000 | bytes 30000000 | tf_op jit(solution)/shard_map/finish_weight/pallas_call | solution.py:2255
  945.0 0.0 copy-done.2
  945.0 15.2 %finish_weight.3 = f32[384,16,768]{2,1,0:T(8,128)} custom-call(bf16[4,2,3,384,768]{4,3,2,1,0:T(8,128)(2,1)} %get-tuple-element.222.refs_0_, bf16[2,3,384,768]{3,2,1,0:T(8,128)(2,1)} %get-tuple-element.196.refs_16_.refs_1_, bf16[4,2,2,384,768]{4,3,2,1,0:T(8,128)(2,1)} %get-tuple-element.223.refs_2_, bf16[2,3,384,768]{3,2,1,0:T(8,128)(2,1)} %get-tuple-element.221.refs_3_), custom_call_target="tpu_custom_call" | custom-call | flops 2000000000 | bytes 30000000 | tf_op jit(solution)/shard_map/finish_weight/pallas_call | solution.py:2255
  960.3 0.0 collective-permute-done.1
  960.3 0.0 copy-start.5
  960.3 0.0 collective-permute-done
  960.3 0.1 collective-permute-start.2
  960.4 0.9 copy-done.5
  961.3 1.8 bitcast_convert_fusion
  963.1 0.0 copy-done.7
  963.1 0.7 slice.33
  963.8 1.7 copy.38
  965.5 1.6 slice.28
  967.1 0.9 slice_reduce_fusion
  968.0 0.9 fusion.1
  968.9 0.0 copy-done.6
  968.9 1.8 bitcast_convert_fusion.1
  970.7 0.0 collective-permute-done.2
  970.7 12.2 %finish_weight.5 = f32[192,16,1536]{2,1,0:T(8,128)} custom-call(bf16[4,2,3,2,192,768]{5,4,3,2,1,0:T(8,128)(2,1)} %bitcast.46, bf16[2,3,2,192,768]{4,3,2,1,0:T(8,128)(2,1)} %bitcast.47, bf16[2,1,2,192,768]{4,3,2,1,0:T(8,128)(2,1)} %bitcast.60, bf16[2,1,2,192,768]{4,3,2,1,0:T(8,128)(2,1)} %bitcast.75, bf16[2,1,2,192,768]{4,3,2,1,0:T(8,128)(2,1)} %bitcast.37.refs_4_, ...), custom_call_target="tpu_custom_call" | custom-call | flops 2000000000 | bytes 30000000 | tf_op jit(solution)/shard_map/finish_weight/pallas_call | solution.py:2255
  982.8 0.0 copy-done.4
  982.8 0.0 copy-start.1
  982.9 1.4 copy.43
  984.3 1.1 copy-done.3
  985.4 1.4 copy.44
  (11 shorter events, 0.1 us)
Async XLA Ops:
  0.6 0.8 copy-start
  928.4 16.7 %copy-start.2 = (bf16[2,1,384,768]{3,2,1,0:T(8,128)(2,1)}, bf16[2,1,384,768]{3,2,1,0:T(8,128)(2,1)S(1)}, u32[]{:S(2)}) copy-start(bf16[2,1,384,768]{3,2,1,0:T(8,128)(2,1)S(1)} %slice.27) | copy-start | bytes 3538948
  928.4 31.9 %collective-permute-start.1 = (bf16[2,1,384,768]{3,2,1,0:T(8,128)(2,1)S(1)}, bf16[2,1,384,768]{3,2,1,0:T(8,128)(2,1)S(1)}, u32[]{:S(2)}, u32[]{:S(2)}) collective-permute-start(bf16[2,1,384,768]{3,2,1,0:T(8,128)(2,1)S(1)} %slice.27), channel_id=1, source_target_pairs={{0,4},{4,0},{8,12},{12,8},{1,5},{5,1},{9,13},{13,9},{2,6},{6,2},{1... | collective-permute-start | bytes 3538952 | tf_op jit(solution)/shard_map/ppermute | solution.py:2268
  928.8 31.4 %collective-permute-start = (bf16[2,1,384,768]{3,2,1,0:T(8,128)(2,1)S(1)}, bf16[2,1,384,768]{3,2,1,0:T(8,128)(2,1)}, u32[]{:S(2)}, u32[]{:S(2)}) collective-permute-start(bf16[2,1,384,768]{3,2,1,0:T(8,128)(2,1)S(1)} %slice.27), channel_id=1, source_target_pairs={{0,8},{4,12},{8,0},{12,4},{1,9},{5,13},{9,1},{13,5},{2,10},{6,14},... | collective-permute-start | bytes 3538952 | tf_op jit(solution)/shard_map/ppermute | solution.py:2268
  960.3 2.8 copy-start.7
  960.3 1.0 copy-start.5
  960.3 10.4 %collective-permute-start.2 = (bf16[2,1,384,768]{3,2,1,0:T(8,128)(2,1)}, bf16[2,1,384,768]{3,2,1,0:T(8,128)(2,1)}, u32[]{:S(2)}, u32[]{:S(2)}) collective-permute-start(bf16[2,1,384,768]{3,2,1,0:T(8,128)(2,1)} %collective-permute-done), channel_id=1, source_target_pairs={{0,4},{4,0},{8,12},{12,8},{1,5},{5,1},{9,13},{13,9},{2,6},{6,2},{1... | collective-permute-start | bytes 3538952 | tf_op jit(solution)/shard_map/ppermute | solution.py:2268
  965.5 3.5 copy-start.6
  970.7 12.2 %copy-start.4 = (bf16[768,1536]{1,0:T(8,128)(2,1)S(1)}, bf16[768,1536]{1,0:T(8,128)(2,1)}, u32[]{:S(2)}) copy-start(bf16[768,1536]{1,0:T(8,128)(2,1)} %get-tuple-element.216) | copy-start | bytes 7077892
  982.8 2.5 copy-start.3
  982.8 3.9 copy-start.1

commit v6 on v5

--- a/solution.py
+++ b/solution.py
@@ -508,8 +508,9 @@
 
 
 ALL_FLIPS = (2, 3, 1)
-RIDE_FRONT = ((0, 2, None), (0, 1, 0), (1, 1, 0))
-RIDE_DISPATCH = ((0, 3, 0), (1, 2, 0), (1, 3, 0), (2, 2, 0), (2, 3, 0), (2, 1, 0))
+RIDE_FRONT = ((0, 2, 1), (0, 3, 0), (0, 1, 0))
+RIDE_DISPATCH = ((1, 2, 0), (1, 3, 0), (2, 2, 0), (2, 3, 0), (1, 1, 0), (2, 1, 0))
+DISPATCH_FIRST = 4
 RIDE_FIRST = ((0, 3, 1), (0, 1, 1)) + tuple((m, f, 1) for m in (1, 2) for f in ALL_FLIPS)
 HOME_SECOND = tuple((m, f, 0) for m in (0, 1) for f in (2, 3)) + tuple((m, 1, 0) for m in range(3))
 HOME_RETURN = ((2, 2, 0), (2, 3, 0), (0, 2, 1), (0, 3, 1))
@@ -866,6 +867,7 @@
     up_halves_ref,
     down_halves_ref,
     cot_partner_ref,
+    gate_piece_ref,
     partner_routes,
     loaded,
     made,
@@ -934,6 +936,10 @@
             pass_on(a, lane, flip, z_index, here, parts[a])
     ranks_ref[...] = rank_tables(routes_ref[...], plane, own_row_ref, own_column_ref)
     cast_halves(gate_ref, gate_halves_ref, loaded, made, load_sems, store_sems)
+    gate_move = remote(
+        gate_halves_ref.at[0, 0], gate_piece_ref, route_sems.at[4], route_sems.at[5], z_peer(2)
+    )
+    gate_move.start()
     for a in range(2):
         for z_from in froms[1:]:
             landed(a, z_from, here)
@@ -966,6 +972,7 @@
     for copy in keep:
         copy.wait()
     cot_pair.wait()
+    gate_move.wait()
 
 
 def gather_parts(routes, part_in, part_out, weights, cot, n_dp, n_context, plane):
@@ -980,11 +987,11 @@
     return pl.pallas_call(
         functools.partial(gather_kernel, n_dp, plane),
         in_specs=[vmem] + [anywhere] * 6,
-        out_specs=[vmem] * 5 + [anywhere] * 6,
+        out_specs=[vmem] * 5 + [anywhere] * 7,
         out_shape=[shape((tokens, EXPERTS), F32), row, column, row, column]
         + [shape((n_dp, plane) + part.shape, BF) for part in (part_in, part_out)]
         + [shape((2, mine // 2, w.shape[0], w.shape[2]), BF) for w in weights]
-        + [shape((tokens * 3 // 4, D), BF)],
+        + [shape((tokens // 2, D), BF), shape(weights[0].shape[::2], BF)],
         scratch_shapes=[
             pltpu.VMEM(routes.shape, routes.dtype),
             pltpu.VMEM((2, rows, 8, width), F32),
@@ -997,7 +1004,7 @@
             dma((2, n_dp)),
             dma((2, 3, n_dp, plane)),
             dma((2, n_dp, plane)),
-            dma((4,)),
+            dma((6,)),
         ],
         compiler_params=pltpu.CompilerParams(
             vmem_limit_bytes=60 * 1024 * 1024, collective_id=3, has_side_effects=True
@@ -1009,20 +1016,16 @@
 def front_kernel(n_dp, prompt_len, riders, *refs):
     (x_ref, cos_ref, sin_ref, w_in_ref, w_out_ref, cot_ref), refs = refs[:6], refs[6:]
     sources, refs = refs[: len(riders)], refs[len(riders) :]
+    (gains_ref, log_ref, logits_ref), refs = refs[:3], refs[3:]
+    saved, (mid_ref, cot_partner_ref), refs = refs[:5], refs[5:7], refs[7:]
+    targets, refs = refs[: len(riders)], refs[len(riders) :]
     (
-        gains_ref,
         normed_one_ref,
         qkv_ref,
         kv_ref,
         attended_ref,
-        log_ref,
         normed_two_ref,
-        logits_ref,
-        mid_ref,
-        cot_partner_ref,
-    ), refs = refs[:10], refs[10:]
-    targets, refs = refs[: len(riders)], refs[len(riders) :]
-    (
+        save_sems,
         columns_buf,
         small,
         w_out,
@@ -1040,6 +1043,8 @@
     tokens = x_ref.shape[0]
     width = qkv_ref.shape[1]
     greet([context_peer(flip) for flip in range(1, n_context)] + dp_peers(n_dp))
+    held = (normed_one_ref, qkv_ref, kv_ref, attended_ref, normed_two_ref)
+    saves = [pltpu.make_async_copy(buf, out, save_sems.at[n]) for n, (buf, out) in enumerate(zip(held, saved))]
     load_small = pltpu.make_async_copy(w_in_ref.at[:, pl.ds(width, 128)], small, load_sems.at[0])
     load_out = pltpu.make_async_copy(w_out_ref, w_out, load_sems.at[1])
     step_width = columns_buf.shape[2]
@@ -1126,6 +1131,8 @@
     lax.fori_loop(kv_steps, steps, project, 0)
     for move in kv_moves:
         move.wait()
+    for save in saves[:3]:
+        save.start()
     log_ref[...] = jnp.zeros_like(log_ref)
 
     def through_head(head, carry):
@@ -1147,6 +1154,7 @@
         return carry
 
     lax.fori_loop(0, HEADS, through_head, 0)
+    saves[3].start()
     load_out.wait()
 
     def second_norm(n, carry):
@@ -1162,9 +1170,12 @@
         return carry
 
     lax.fori_loop(0, tokens // PBLK, second_norm, 0)
+    saves[4].start()
     pair.wait()
     for move in moves:
         move.wait()
+    for save in saves:
+        save.wait()
 
 
 def front(prompt_len, n_dp, x_low, cosine, sine, w_in, w_out, cot, riders):
@@ -1179,21 +1190,27 @@
     return pl.pallas_call(
         functools.partial(front_kernel, n_dp, prompt_len, [(index, flip) for _, index, flip in riders]),
         in_specs=[vmem] * 3 + [anywhere] * (3 + len(riders)),
-        out_specs=[vmem] * 8 + [anywhere] * (2 + len(riders)),
+        out_specs=[vmem] * 3 + [anywhere] * (7 + len(riders)),
         out_shape=[
             shape((8, D), F32),
+            shape((tokens, 128), F32),
+            shape((tokens, 128), F32),
             shape((tokens, D), BF),
             shape((tokens, width), BF),
             shape((key_rows, 2 * KVH * HD), BF),
             shape((tokens, D), BF),
-            shape((tokens, 128), F32),
             shape((tokens, D), BF),
-            shape((tokens, 128), F32),
             shape((tokens, D), F32),
-            shape((tokens // 4, D), BF),
+            shape((tokens // 2, D), BF),
         ]
         + [shape(picked_shape(array, index), BF) for array, index, _ in riders],
         scratch_shapes=[
+            pltpu.VMEM((tokens, D), BF),
+            pltpu.VMEM((tokens, width), BF),
+            pltpu.VMEM((key_rows, 2 * KVH * HD), BF),
+            pltpu.VMEM((tokens, D), BF),
+            pltpu.VMEM((tokens, D), BF),
+            dma((5,)),
             pltpu.VMEM((2, D, 2 * HD), BF),
             pltpu.VMEM((D, 128), BF),
             pltpu.VMEM((D, D), BF),
@@ -1245,8 +1262,6 @@
     pair = remote(normed_ref, normed_partner, pair_sems.at[0], pair_sems.at[1], partner)
     pair.start()
     moves = dp_moves(sources, targets, riders, ride_send, ride_recv)
-    for move in moves:
-        move.start()
     first = cot_halves[0].shape[0]
     places = (pl.ds(0, first), pl.ds(first, cot_halves[1].shape[0]))
     cot_loads = [
@@ -1294,9 +1309,13 @@
                 for load in cot_loads:
                     load.wait()
             if expert == 0 and n == 3:
+                for move in moves[:DISPATCH_FIRST]:
+                    move.start()
                 slot_gates()
                 gate_pair.start()
                 pair.wait()
+                for move in moves[DISPATCH_FIRST:]:
+                    move.start()
             chooser = slot_matrix(rank_ref[expert], plane, True)
             stage[4 * expert + n] = mxu(chooser, rows_ref[...]).astype(BF).reshape(plane, SLOTS, D)
             if expert == 0:
@@ -1650,26 +1669,9 @@
 
 
 def backward_kernel(n_dp, prompt_len, n_results, riders, *refs):
-    (
-        dlog_ref,
-        cot_ref,
-        x_ref,
-        gains_in_ref,
-        attended_ref,
-        qkv_ref,
-        kv_ref,
-        log_ref,
-        normed_ref,
-        cos_ref,
-        sin_ref,
-        mid_ref,
-        total_ref,
-        w_out_ref,
-        w_in_ref,
-        normed_two_ref,
-        part_ref,
-    ) = refs[:17]
-    results, refs = refs[17 : 17 + n_results], refs[17 + n_results :]
+    (dlog_ref, gains_in_ref, log_ref, cos_ref, sin_ref), kept, refs = refs[:5], refs[5:11], refs[11:]
+    (mid_ref, total_ref, w_out_ref, w_in_ref, normed_two_ref, part_ref), refs = refs[:6], refs[6:]
+    results, refs = refs[:n_results], refs[n_results:]
     late = len(riders)
     sources, refs = refs[:late], refs[late:]
     grad_x_ref, grad_out_ref, grad_in_ref, grad_small_ref, all_ref = refs[:5]
@@ -1699,6 +1701,14 @@
         local_sems,
         send_sems,
         recv_sems,
+        cot_ref,
+        qkv_ref,
+        kv_ref,
+        attended_ref,
+        normed_ref,
+        x_ref,
+        kept_sems,
+        mid_sems,
     ) = refs
     block_index = lax.axis_index("context")
     n_context = kv_send.shape[0]
@@ -1712,11 +1722,17 @@
         w_in_ref.at[:, pl.ds(weights.shape[1], 128)], small, load_sems.at[4]
     )
     load_small.start()
+    buffers = (cot_ref, qkv_ref, kv_ref, attended_ref, normed_ref, x_ref)
+    kept_loads = [
+        pltpu.make_async_copy(source, buf, kept_sems.at[n]) for n, (source, buf) in enumerate(zip(kept, buffers))
+    ]
     load_total = pltpu.make_async_copy(total_ref, grad_mid, load_sems.at[0])
     load_out = pltpu.make_async_copy(w_out_ref, weights.at[:, pl.ds(0, D)], load_sems.at[1])
     load_in = pltpu.make_async_copy(w_in_ref.at[:, pl.ds(0, weights.shape[1])], weights, load_sems.at[2])
     load_total.start()
     load_out.start()
+    for load in kept_loads:
+        load.start()
     homing = dp_moves(sources, homes, riders, home_send, home_recv)
     for move in homing:
         move.start()
@@ -1732,17 +1748,28 @@
     load_total.wait()
     load_out.wait()
     gains_ref[...] = jnp.zeros_like(gains_ref)
+    kept_loads[0].wait()
+
+    def load_mid(n):
+        slot = lax.rem(n, 2)
+        block = mid_ref.at[pl.ds(pl.multiple_of(n * PBLK, PBLK), PBLK)]
+        return pltpu.make_async_copy(block, mid_block.at[slot], mid_sems.at[slot])
+
+    load_mid(0).start()
 
     def block_rows(n):
         return pl.ds(pl.multiple_of(n * PBLK, PBLK), PBLK)
 
     def through_norm(n, carry):
         rows = block_rows(n)
-        load_mid = pltpu.make_async_copy(mid_ref.at[rows], mid_block, load_sems.at[3])
-        load_mid.start()
-        load_mid.wait()
+
+        @pl.when(n + 1 < tokens // PBLK)
+        def _():
+            load_mid(n + 1).start()
+
+        load_mid(n).wait()
         grads = grad_mid[rows, :] + mxu(dlog_ref[rows, :], small[...], ((1,), (1,)))
-        by_rows, by_gain = normed_back(mid_block[...], gains_in_ref[1:2, :], grads)
+        by_rows, by_gain = normed_back(mid_block[lax.rem(n, 2)], gains_in_ref[1:2, :], grads)
         gains_ref[1:2, :] += jnp.sum(by_gain, axis=0, keepdims=True)
         by_mid = cot_ref[rows, :].astype(F32) + by_rows
         grad_mid[rows, :] = by_mid
@@ -1753,6 +1780,8 @@
 
     lax.fori_loop(0, tokens // PBLK, through_norm, 0)
     load_in.start()
+    for load in kept_loads[1:3]:
+        load.wait()
     grad_kv[...] = jnp.zeros_like(grad_kv)
 
     def through_head(head, carry):
@@ -1802,17 +1831,27 @@
     def quarter_rows(q):
         return pl.ds(pl.multiple_of(q * quarter, 128), quarter)
 
+    def store_of(q, out_ref, width):
+        slot = lax.rem(q, 2)
+        return pltpu.make_async_copy(
+            stage.at[slot, :, pl.ds(0, width)], out_ref.at[quarter_rows(q)], store_sems.at[slot]
+        )
+
     def share_of_out(q, carry):
         made = mxu(attended_ref[:, quarter_rows(q)], grad_attn[...], ((0,), (0,)))
-        stage[:, :D] = made.astype(BF)
-        store = pltpu.make_async_copy(
-            stage.at[:, pl.ds(0, D)], grad_out_ref.at[quarter_rows(q)], store_sems.at[0]
-        )
-        store.start()
-        store.wait()
+
+        @pl.when(q >= 2)
+        def _():
+            store_of(q - 2, grad_out_ref, D).wait()
+
+        stage[lax.rem(q, 2), :, :D] = made.astype(BF)
+        store_of(q, grad_out_ref, D).start()
         return carry
 
+    kept_loads[3].wait()
     lax.fori_loop(0, n_dp, share_of_out, 0)
+    for q in (n_dp - 2, n_dp - 1):
+        store_of(q, grad_out_ref, D).wait()
     load_normed = pltpu.make_async_copy(normed_two_ref, grad_attn, load_sems.at[0])
     load_normed.start()
 
@@ -1834,14 +1873,22 @@
 
     load_in.wait()
 
+    width = weights.shape[1]
+
     def share_of_in(q, carry):
-        stage[...] = mxu(normed_ref[:, quarter_rows(q)], grad_qkv[...], ((0,), (0,))).astype(BF)
-        store = pltpu.make_async_copy(stage, grad_in_ref.at[quarter_rows(q)], store_sems.at[0])
-        store.start()
-        store.wait()
+        made = mxu(normed_ref[:, quarter_rows(q)], grad_qkv[...], ((0,), (0,)))
+
+        @pl.when(q >= 2)
+        def _():
+            store_of(q - 2, grad_in_ref, width).wait()
+
+        stage[lax.rem(q, 2)] = made.astype(BF)
+        store_of(q, grad_in_ref, width).start()
         return carry
 
+    kept_loads[4].wait()
     lax.fori_loop(0, n_dp, share_of_in, 0)
+    kept_loads[5].wait()
 
     def through_first(n, carry):
         rows = block_rows(n)
@@ -1853,6 +1900,8 @@
 
     pass_on()
     lax.fori_loop(0, tokens // PBLK, through_first, 0)
+    for q in (n_dp - 2, n_dp - 1):
+        store_of(q, grad_in_ref, width).wait()
     load_normed.wait()
     lane = lax.broadcasted_iota(jnp.int32, (8, 128), 1)
     column = lax.broadcasted_iota(jnp.int32, (8, 128), 0) + EXPERTS
@@ -1899,14 +1948,14 @@
             pltpu.VMEM((D, width), BF),
             pltpu.VMEM((tokens, D), F32),
             pltpu.VMEM((tokens, D), BF),
-            pltpu.VMEM((PBLK, D), F32),
+            pltpu.VMEM((2, PBLK, D), F32),
             pltpu.VMEM((tokens, width), BF),
             pltpu.VMEM((key_rows, 2 * KVH * HD), F32),
             pltpu.VMEM((n_context, PBLK, 2 * KVH * HD), BF),
             pltpu.VMEM((n_context, PBLK, 2 * KVH * HD), BF),
-            pltpu.VMEM((quarter, width), BF),
+            pltpu.VMEM((2, quarter, width), BF),
             pltpu.SemaphoreType.DMA((5,)),
-            pltpu.SemaphoreType.DMA((1,)),
+            pltpu.SemaphoreType.DMA((2,)),
             pltpu.SemaphoreType.DMA((n_context,)),
             pltpu.SemaphoreType.DMA((n_context,)),
             pltpu.SemaphoreType.DMA((len(riders),)),
@@ -1919,6 +1968,9 @@
             pltpu.SemaphoreType.DMA((len(results),)),
             pltpu.SemaphoreType.DMA((len(results), plane)),
             pltpu.SemaphoreType.DMA((len(results), plane)),
+            *[pltpu.VMEM(array.shape, BF) for array in in_hbm[:6]],
+            pltpu.SemaphoreType.DMA((6,)),
+            pltpu.SemaphoreType.DMA((2,)),
         ],
         compiler_params=pltpu.CompilerParams(
             vmem_limit_bytes=56 * 1024 * 1024, collective_id=4, has_side_effects=True
@@ -1971,7 +2023,7 @@
         [plane_peer(here ^ flip) for flip in (1, 2, 4)] + [{"dp": z_index ^ flip} for flip in range(1, n_dp)]
     )
     chips = (0, 2, 4, 6)
-    order = [1, 2, 3, 0] if n_dp == 4 else list(range(1, n_dp)) + [0]
+    order = list(range(1, n_dp)) + [0]
     loads, core_moves = {}, {}
     for n in order:
         z_to = z_index ^ n
@@ -2016,12 +2068,6 @@
 
     sum_of(0)
     gathers[0][0]()
-    for copy in rows_here:
-        copy.wait()
-    collect_into(plane, partner_rank_ref, held, 0, to_partner, lambda rows, made: made.astype(BF))
-    pair = remote(to_partner, of_partner, pair_sems.at[0], pair_sems.at[1], {"dp": z_index ^ 1})
-    pair.start()
-    rows_here = load_rows(0)
 
     def add(target, *others):
         total = target[...].astype(F32)
@@ -2047,18 +2093,13 @@
                     plane_peer(here ^ toward),
                 )
                 first_moves[n, a, slot].start()
-    sum_of(1)
-    sum_of(2)
     for copy in rows_here:
         copy.wait()
-
-    def with_mid(rows, made):
-        load = pltpu.make_async_copy(mid_ref.at[rows], mid_block, held_sems.at[2])
-        load.start()
-        load.wait()
-        return mid_block[...] + made
-
-    collect_into(plane, own_rank_ref, held, 0, mixed, with_mid)
+    collect_into(plane, partner_rank_ref, held, 0, to_partner, lambda rows, made: made.astype(BF))
+    pair = remote(to_partner, of_partner, pair_sems.at[0], pair_sems.at[1], {"dp": z_index ^ 1})
+    pair.start()
+    rows_here = load_rows(0)
+    sum_of(1)
     for n in order:
         toward = 2 if n % 2 == 0 else 4
         kept = 6 - toward
@@ -2075,6 +2116,17 @@
             )
             second_moves[n, a].start()
     gathers[1][0]()
+
+    def with_mid(rows, made):
+        load = pltpu.make_async_copy(mid_ref.at[rows], mid_block, held_sems.at[2])
+        load.start()
+        load.wait()
+        return mid_block[...] + made
+
+    for copy in rows_here:
+        copy.wait()
+    collect_into(plane, own_rank_ref, held, 0, mixed, with_mid)
+    sum_of(2)
     gathers[0][1]()
     for n in order:
         for a in range(count):
@@ -2236,7 +2288,7 @@
 def finish_weight(which, first, own_first, seconds):
     n_context, _, _, rows, width = first.shape
     experts = n_context * 4
-    step = 32
+    step = 32 if which == 2 else 64
     apart = len(seconds) == n_context
     halves = 2 if which == 2 else 1
     rows, wide = rows // halves, width * halves
@@ -2311,14 +2363,16 @@
     own_ranks, own_rows, own_columns, partner_rows, partner_columns, whole_in, w_out, *weight_halves = (
         gather_parts(route_rows.T, part_in, part_of(attn_o), weights, cot_low, n_dp, n_context, plane)
     )
+    gate_piece = weight_halves.pop()
     partner_cot = [weight_halves.pop()]
     whole_in = whole_in.reshape(-1, part_in.shape[1])
     w_out = w_out.reshape(-1, D)
     pieces = {(which, 0, i): (weight_halves[which], (0, i)) for which in range(3) for i in range(2)}
+    pieces[0, 2, 0] = (gate_piece, None)
 
     def riding(names):
         return [
-            (weight_halves[which], flip % 2 if i is None else (flip % 2, i), flip) for which, flip, i in names
+            (weight_halves[which], (flip % 2, i), flip) for which, flip, i in names
         ]
 
     def pieces_of(expert):
@@ -2334,15 +2388,11 @@
     cos_half, sin_half = jnp.cos(angles), jnp.sin(angles)
     cosine = jnp.concatenate([cos_half, cos_half], axis=1)
     sine = jnp.concatenate([-sin_half, sin_half], axis=1)
-    gains, normed_one, qkv, keys_values, attended, logs, normed_two, logits, mid_rows, cot_half, *moved = (
+    gains, logs, logits, normed_one, qkv, keys_values, attended, normed_two, mid_rows, cot_half, *moved = (
         front(prompt_len, n_dp, x_low, cosine, sine, whole_in, w_out, cot_low, riding(RIDE_FRONT))
     )
     partner_cot.append(cot_half)
-    for (which, flip, expert), piece in zip(RIDE_FRONT, moved):
-        if expert is None:
-            pieces.update({(which, flip, i): (piece, i) for i in range(2)})
-        else:
-            pieces[which, flip, expert] = (piece, None)
+    pieces.update({name: (piece, None) for name, piece in zip(RIDE_FRONT, moved)})
 
     gates, gates_here, landed, staged, arrived = dispatch_rows(
         normed_two, cot_low, partner_cot, own_rows, partner_rows, logits, own_ranks, riding(RIDE_DISPATCH), n_dp
@@ -2396,20 +2446,21 @@
     grad_inputs, grad_wout, grad_wqkv, grad_small, all_first, *homes = backward(
         prompt_len,
         n_dp,
+        (grad_logits, gains, logs, cosine, sine),
         (
-            grad_logits,
             cot_low,
-            x_low,
-            gains,
-            attended,
             qkv,
             keys_values,
-            logs,
+            attended,
             normed_one,
-            cosine,
-            sine,
+            x_low,
+            mid_rows,
+            grad_rows,
+            w_out,
+            whole_in,
+            normed_two,
+            part_first,
         ),
-        (mid_rows, grad_rows, w_out, whole_in, normed_two, part_first),
         second[0:1],
         homing(HOME_BACKWARD, first_shares, second_shares),
     )

time: 992 us -> 972 us (0.980)
  Pallas kernels: 961 us -> 940 us
  transfers between devices with their start and end apart: 3 -> 3, of which waited for: 0 -> 1; matrix products, arithmetic and copies ran while one was open for 1% -> 1% of each run, Pallas kernels for 3% -> 3%
where the time goes in v6:
time: 972 us; the launch traced here: 968 us
  Pallas kernels  940 us (97%)
  local copies, waits for them, and re-layouts  16.4 us (2%)
    pallas_call x2, Pallas kernels, run_expert(): pl.pallas_call(functools.partial(expert_kernel, plane, n_dp, half_steps,...  233 us
    pallas_call x1, Pallas kernels, return_rows(): pl.pallas_call(functools.partial(return_kernel, plane, n_dp, len(results)...  142 us
    pallas_call x1, Pallas kernels, dispatch_rows(): pl.pallas_call(functools.partial(dispatch_kernel, plane, n_dp, [(index, f...  135 us
    pallas_call x1, Pallas kernels, reduce_shares(): pl.pallas_call(functools.partial(reduce_kernel, n_dp, widths), in_specs=[...  129 us
    pallas_call x1, Pallas kernels, backward(): pl.pallas_call(functools.partial(backward_kernel, n_dp, prompt_len, len(r...  124 us
    pallas_call x1, Pallas kernels, gather_parts(): pl.pallas_call(functools.partial(gather_kernel, n_dp, plane), in_specs=[v...  71.6 us
    pallas_call x1, Pallas kernels, front(): pl.pallas_call(functools.partial(front_kernel, n_dp, prompt_len, [(index,...  70.7 us
    pallas_call x3, Pallas kernels, finish_weight(): pl.pallas_call(functools.partial(finish_kernel, n_context, apart, halves)...  36.6 us
  transfers between devices with their start and end apart: 3, of which 1 were waited for; matrix products, arithmetic and copies ran while one was open for 1% of the time, Pallas kernels for 3%

profile of v6, /device:TPU:0, one launch (start us, length us, event | category | flops | bytes accessed | tf_op | source)
XLA Modules:
  0.0 968.2 jit_solution(3336461863590088608)
XLA Ops:
  0.6 0.0 copy-start
  0.7 0.7 copy-done
  1.4 0.1 constant_dynamic-slice_fusion
  1.5 0.1 copy.35
  1.6 0.8 convert_bitcast_fusion
  2.4 0.1 copy.31
  2.5 0.1 copy.30
  2.6 0.8 dynamic-slice_convert_fusion.2
  3.5 1.7 dynamic-slice_convert_fusion
  5.2 1.4 fusion
  6.7 1.2 pad_maximum_fusion
  7.8 0.8 concatenate.16.in_ref
  8.6 71.6 %gather_parts.1 = (f32[768,32]{1,0:T(8,128)}, bf16[2,8,768]{2,1,0:T(8,128)(2,1)}, bf16[2,768,8]{2,1,0:T(8,128)(2,1)}, bf16[2,8,768]{2,1,0:T(8,128)(2,1)}, bf16[2...) custom-call(s32[4,768]{1,0:T(4,128)} %bitcast.79, ...), custom_call_target="tpu_custom_call" | custom-call | tf_op jit(solution)/shard_map/gather_parts/pallas_call | solution.py:987
  80.2 70.7 %front.1 = (f32[8,1536]{1,0:T(8,128)}, f32[768,128]{1,0:T(8,128)}, f32[768,128]{1,0:T(8,128)}, bf16[768,1536]{1,0:T(8,128)(2,1)}, bf16[768,2048]{1,0:T(8,128)(2,...) custom-call(bf16[768,1536]{1,0:T(8,128)(2,1)} %bitcast.56, ...), custom_call_target="tpu_custom_call" | custom-call | tf_op jit(solution)/shard_map/front/pallas_call | solution.py:1190
  150.9 134.5 %dispatch_rows.1 = (f32[768,32]{1,0:T(8,128)}, f32[8,4,128]{2,1,0:T(4,128)}, bf16[8,112,1536]{2,1,0:T(8,128)(2,1)}, bf16[8,112,1536]{2,1,0:T(8,128)(2,1)}, bf16[...) custom-call(bf16[768,1536]{1,0:T(8,128)(2,1)} %get-tuple-element.126, ...), custom_call_target="tpu_custom_call" | custom-call | flops 20000000000 | bytes 400000000 | tf_op jit(solution)/shard_map/dispatch_rows/pallas_call | solution.py:1354
  285.4 125.8 %first_expert.1 = (bf16[896,1536]{1,0:T(8,128)(2,1)}, bf16[896,1536]{1,0:T(8,128)(2,1)}, bf16[896,1536]{1,0:T(8,128)(2,1)}, bf16[896,1536]{1,0:T(8,128)(2,1)}, f...) custom-call(bf16[896,1536]{1,0:T(8,128)(2,1)} %bitcast.69, ...), custom_call_target="tpu_custom_call" | custom-call | tf_op jit(solution)/shard_map/first_expert/pallas_call | solution.py:691
  411.1 107.1 %second_expert.1 = (bf16[896,1536]{1,0:T(8,128)(2,1)}, bf16[896,1536]{1,0:T(8,128)(2,1)}, bf16[896,1536]{1,0:T(8,128)(2,1)}, bf16[896,1536]{1,0:T(8,128)(2,1)}, ...) custom-call(bf16[896,1536]{1,0:T(8,128)(2,1)} %bitcast.65, ...), custom_call_target="tpu_custom_call" | custom-call | tf_op jit(solution)/shard_map/second_expert/pallas_call | solution.py:691
  518.3 141.7 %return_rows.1 = (f32[768,1536]{1,0:T(8,128)}, bf16[768,128]{1,0:T(8,128)(2,1)}, bf16[2,3,384,768]{3,2,1,0:T(8,128)(2,1)}, bf16[8,112,1536]{2,1,0:T(8,128)(2,1)}...) custom-call(bf16[2,768,8]{2,1,0:T(8,128)(2,1)} %get-tuple-element.12, ...), custom_call_target="tpu_custom_call" | custom-call | flops 30000001024 | bytes 400000000 | tf_op jit(solution)/shard_map/return_rows/pallas_call | solution.py:1579
  660.0 123.7 %backward.1 = (bf16[768,1536]{1,0:T(8,128)(2,1)}, bf16[1536,1536]{1,0:T(8,128)(2,1)}, bf16[1536,2048]{1,0:T(8,128)(2,1)}, bf16[1536,128]{1,0:T(8,128)(2,1)}, bf1...) custom-call(bf16[768,128]{1,0:T(8,128)(2,1)} %get-tuple-element.189., ...), custom_call_target="tpu_custom_call" | custom-call | tf_op jit(solution)/shard_map/backward/pallas_call | solution.py:1932
  783.7 128.6 %reduce_shares.1 = (bf16[8,48,2048]{2,1,0:T(8,128)(2,1)}, bf16[8,48,1536]{2,1,0:T(8,128)(2,1)}, bf16[8,48,128]{2,1,0:T(8,128)(2,1)}, bf16[768,1536]{1,0:T(8,128)...) custom-call(bf16[4,8,48,2048]{3,2,1,0:T(8,128)(2,1)} %bitcast.58, ...), custom_call_target="tpu_custom_call" | custom-call | tf_op jit(solution)/shard_map/reduce_shares/pallas_call | solution.py:2198
  912.4 1.4 slice.27
  913.7 0.0 copy-start.2
  913.7 0.4 collective-permute-start.1
  914.2 0.8 collective-permute-start
  915.0 12.2 %finish_weight.4 = f32[384,16,768]{2,1,0:T(8,128)} custom-call(bf16[4,2,3,384,768]{4,3,2,1,0:T(8,128)(2,1)} %get-tuple-element.224.refs_0_, bf16[2,3,384,768]{3,2,1,0:T(8,128)(2,1)} %get-tuple-element.198.refs_16_.refs_1_, bf16[4,2,2,384,768]{4,3,2,1,0:T(8,128)(2,1)} %get-tuple-element.225.refs_2_, bf16[2,3,384,768]{3,2,1,0:T(8,128)(2,1)} %get-tuple-element.223.refs_3_), custom_call_target="tpu_custom_call" | custom-call | flops 2000000000 | bytes 30000000 | tf_op jit(solution)/shard_map/finish_weight/pallas_call | solution.py:2307
  927.2 0.0 copy-done.2
  927.2 12.2 %finish_weight.3 = f32[384,16,768]{2,1,0:T(8,128)} custom-call(bf16[4,2,3,384,768]{4,3,2,1,0:T(8,128)(2,1)} %get-tuple-element.224.refs_0_, bf16[2,3,384,768]{3,2,1,0:T(8,128)(2,1)} %get-tuple-element.198.refs_16_.refs_1_, bf16[4,2,2,384,768]{4,3,2,1,0:T(8,128)(2,1)} %get-tuple-element.225.refs_2_, bf16[2,3,384,768]{3,2,1,0:T(8,128)(2,1)} %get-tuple-element.223.refs_3_), custom_call_target="tpu_custom_call" | custom-call | flops 2000000000 | bytes 30000000 | tf_op jit(solution)/shard_map/finish_weight/pallas_call | solution.py:2307
  939.5 0.0 collective-permute-done.1
  939.5 0.0 copy-start.5
  939.5 2.8 collective-permute-done
  942.3 0.0 collective-permute-start.2
  942.3 0.0 copy-done.5
  942.3 1.8 bitcast_convert_fusion
  944.1 0.0 copy-done.7
  944.1 0.7 slice.33
  944.8 1.7 copy.38
  946.5 1.6 slice.28
  948.1 0.9 slice_reduce_fusion
  949.0 0.9 fusion.1
  949.9 0.0 copy-done.6
  949.9 1.8 bitcast_convert_fusion.1
  951.7 0.0 collective-permute-done.2
  951.7 12.1 %finish_weight.5 = f32[192,16,1536]{2,1,0:T(8,128)} custom-call(bf16[4,2,3,2,192,768]{5,4,3,2,1,0:T(8,128)(2,1)} %bitcast.46, bf16[2,3,2,192,768]{4,3,2,1,0:T(8,128)(2,1)} %bitcast.47, bf16[2,1,2,192,768]{4,3,2,1,0:T(8,128)(2,1)} %bitcast.60, bf16[2,1,2,192,768]{4,3,2,1,0:T(8,128)(2,1)} %bitcast.75, bf16[2,1,2,192,768]{4,3,2,1,0:T(8,128)(2,1)} %bitcast.37.refs_4_, ...), custom_call_target="tpu_custom_call" | custom-call | flops 2000000000 | bytes 30000000 | tf_op jit(solution)/shard_map/finish_weight/pallas_call | solution.py:2307
  963.8 0.0 copy-done.4
  963.8 0.0 copy-start.1
  963.9 1.4 copy.43
  965.3 1.1 copy-done.3
  966.4 1.4 copy.44
  (11 shorter events, 0.1 us)
Async XLA Ops:
  0.6 0.8 copy-start
  913.7 13.5 %copy-start.2 = (bf16[2,1,384,768]{3,2,1,0:T(8,128)(2,1)}, bf16[2,1,384,768]{3,2,1,0:T(8,128)(2,1)S(1)}, u32[]{:S(2)}) copy-start(bf16[2,1,384,768]{3,2,1,0:T(8,128)(2,1)S(1)} %slice.27) | copy-start | bytes 3538948
  913.7 25.7 %collective-permute-start.1 = (bf16[2,1,384,768]{3,2,1,0:T(8,128)(2,1)S(1)}, bf16[2,1,384,768]{3,2,1,0:T(8,128)(2,1)S(1)}, u32[]{:S(2)}, u32[]{:S(2)}) collective-permute-start(bf16[2,1,384,768]{3,2,1,0:T(8,128)(2,1)S(1)} %slice.27), channel_id=1, source_target_pairs={{0,4},{4,0},{8,12},{12,8},{1,5},{5,1},{9,13},{13,9},{2,6},{6,2},{1... | collective-permute-start | bytes 3538952 | tf_op jit(solution)/shard_map/ppermute | solution.py:2320
  914.2 28.1 %collective-permute-start = (bf16[2,1,384,768]{3,2,1,0:T(8,128)(2,1)S(1)}, bf16[2,1,384,768]{3,2,1,0:T(8,128)(2,1)}, u32[]{:S(2)}, u32[]{:S(2)}) collective-permute-start(bf16[2,1,384,768]{3,2,1,0:T(8,128)(2,1)S(1)} %slice.27), channel_id=1, source_target_pairs={{0,8},{4,12},{8,0},{12,4},{1,9},{5,13},{9,1},{13,5},{2,10},{6,14},... | collective-permute-start | bytes 3538952 | tf_op jit(solution)/shard_map/ppermute | solution.py:2320
  939.5 4.6 copy-start.7
  939.5 2.8 copy-start.5
  942.3 9.4 collective-permute-start.2
  946.5 3.5 copy-start.6
  951.7 12.2 %copy-start.4 = (bf16[768,1536]{1,0:T(8,128)(2,1)S(1)}, bf16[768,1536]{1,0:T(8,128)(2,1)}, u32[]{:S(2)}) copy-start(bf16[768,1536]{1,0:T(8,128)(2,1)} %get-tuple-element.218) | copy-start | bytes 7077892
  963.8 2.5 copy-start.3
  963.8 3.9 copy-start.1

commit v7 on v6

--- a/solution.py
+++ b/solution.py
@@ -1427,7 +1427,7 @@
     sources, refs = refs[: len(riders)], refs[len(riders) :]
     mine, refs = refs[:3], refs[3:]
     arrived, refs = refs[: len(HOME_SECOND)], refs[len(HOME_SECOND) :]
-    total_ref, dlog_ref, part_ref = refs[:3]
+    saved_ref, dlog_ref, part_ref = refs[:3]
     results_back, refs = refs[3 : 3 + n_results], refs[3 + n_results :]
     targets = refs[: len(riders)]
     homes = dict(zip(HOME_SECOND, arrived))
@@ -1453,6 +1453,8 @@
         summed,
         sums,
         partial,
+        total_ref,
+        save_sems,
         piece_sems,
         sum_sems,
     ) = refs[len(riders) :]
@@ -1559,13 +1561,19 @@
     exchanges[0][1]()
     for rows in blocks:
         total_ref[rows, :] += collected(own_rank_ref, rows, 0, 1)
-    for pair, rows in zip(pairs, blocks):
+    saves = []
+    for n, (pair, rows) in enumerate(zip(pairs, blocks)):
         pair.wait()
         total_ref[rows, :] += of_partner[rows, :].astype(F32)
+        block = pl.ds(n * PBLK, PBLK)
+        saves.append(pltpu.make_async_copy(total_ref.at[block], saved_ref.at[block], save_sems.at[n]))
+        saves[-1].start()
     for move in moves[RETURN_FIRST:]:
         move.wait()
     for _, finish in later:
         finish()
+    for save in saves:
+        save.wait()
 
 
 def return_rows(
@@ -1581,7 +1589,7 @@
             return_kernel, plane, n_dp, len(results), [(index, flip) for _, index, flip in riders], names
         ),
         in_specs=[vmem] * 6 + [anywhere] * (7 + len(results) + len(riders) + len(arrived)),
-        out_specs=[vmem] * 2 + [anywhere] * (1 + len(results) + len(riders)),
+        out_specs=[anywhere, vmem] + [anywhere] * (1 + len(results) + len(riders)),
         out_shape=[shape((tokens, D), F32), shape((tokens, 128), BF), shape((2, 3) + shares[0].shape[1:], BF)]
         + [shape(rows.shape, BF) for rows in results]
         + [shape(picked_shape(array, index), BF) for array, index, _ in riders],
@@ -1606,6 +1614,8 @@
             pltpu.VMEM(shares[0].shape, BF),
             pltpu.VMEM((2,) + shares[0].shape[1:], BF),
             pltpu.VMEM((tokens, D), F32),
+            pltpu.VMEM((tokens, D), F32),
+            dma((tokens // PBLK,)),
             dma((n_dp,)),
             dma((2,)),
         ],
@@ -1709,6 +1719,8 @@
         x_ref,
         kept_sems,
         mid_sems,
+        grad_x,
+        grad_x_sems,
     ) = refs
     block_index = lax.axis_index("context")
     n_context = kv_send.shape[0]
@@ -1895,7 +1907,8 @@
         grads = mxu(grad_qkv[rows, :], weights[...], ((1,), (1,)))
         by_rows, by_gain = normed_back(x_ref[rows, :].astype(F32), gains_in_ref[0:1, :], grads)
         gains_ref[0:1, :] += jnp.sum(by_gain, axis=0, keepdims=True)
-        grad_x_ref[rows, :] = (grad_mid[rows, :] + by_rows).astype(BF)
+        grad_x[rows, :] = (grad_mid[rows, :] + by_rows).astype(BF)
+        pltpu.make_async_copy(grad_x.at[rows], grad_x_ref.at[rows], grad_x_sems.at[n]).start()
         return carry
 
     pass_on()
@@ -1912,6 +1925,8 @@
     store_small.start()
     finish()
     store_small.wait()
+    for n in range(tokens // PBLK):
+        pltpu.make_async_copy(grad_x.at[block_rows(n)], grad_x_ref.at[block_rows(n)], grad_x_sems.at[n]).wait()
     for _, end in exchanges:
         end()
     for move in homing:
@@ -1934,7 +1949,7 @@
             backward_kernel, n_dp, prompt_len, len(results), [(index, flip) for _, index, flip in riders]
         ),
         in_specs=[vmem] * len(in_vmem) + [anywhere] * (len(in_hbm) + len(results) + len(riders)),
-        out_specs=[vmem] + [anywhere] * (4 + len(results) + len(riders)),
+        out_specs=[anywhere] * (5 + len(results) + len(riders)),
         out_shape=[
             shape((tokens, D), BF),
             shape((D, D), BF),
@@ -1971,6 +1986,8 @@
             *[pltpu.VMEM(array.shape, BF) for array in in_hbm[:6]],
             pltpu.SemaphoreType.DMA((6,)),
             pltpu.SemaphoreType.DMA((2,)),
+            pltpu.VMEM((tokens, D), BF),
+            pltpu.SemaphoreType.DMA((tokens // PBLK,)),
         ],
         compiler_params=pltpu.CompilerParams(
             vmem_limit_bytes=56 * 1024 * 1024, collective_id=4, has_side_effects=True
@@ -1987,8 +2004,8 @@
     names = HOME_RETURN[RETURN_FIRST:] + HOME_BACKWARD
     homes, refs = dict(zip(names, refs)), refs[len(names) :]
     totals, refs = refs[:count], refs[count:]
-    result_ref, all_ref, part_ref = refs[:3]
-    refs = refs[3:]
+    result_ref, all_ref, part_ref, last_ref = refs[:4]
+    refs = refs[4:]
     sums, core_in, first_in, second_in, z_in = (refs[n * count : (n + 1) * count] for n in range(5))
     (
         load_sems,
@@ -2064,7 +2081,8 @@
 
     def sum_of(which):
         sources = [mine[which].at[0]] + [homes[which, flip, 1] for flip in range(1, n_dp)]
-        sum_matrix(which, sources, summed, matrix_sums, part_ref, piece_sems, sum_sems)
+        target, place = (last_ref, 0) if which == 2 else (part_ref, which)
+        sum_matrix(place, sources, summed, matrix_sums, target, piece_sems, sum_sems)
 
     sum_of(0)
     gathers[0][0]()
@@ -2173,7 +2191,9 @@
         pass_on(a, 2, 1, here ^ 6)
     gathers[1][1]()
     pair.wait()
-    result_ref[...] = (mixed[...] + of_partner[...].astype(F32)).astype(BF)
+    to_partner[...] = (mixed[...] + of_partner[...].astype(F32)).astype(BF)
+    store_result = pltpu.make_async_copy(to_partner, result_ref, held_sems.at[2])
+    store_result.start()
     for a in range(count):
         for flip in (1, 3, 5, 7):
             landed(a, here ^ flip)
@@ -2181,6 +2201,7 @@
         move.wait_send()
     for _, _, finish in gathers:
         finish()
+    store_result.wait()
 
 
 def reduce_shares(shares, ranks, mid, slot_rows, mine, homes, n_dp, n_context):
@@ -2198,12 +2219,13 @@
     return pl.pallas_call(
         functools.partial(reduce_kernel, n_dp, widths),
         in_specs=[anywhere] * count + [vmem] * 2 + [anywhere] * (8 + len(homes)),
-        out_specs=[vmem] * (count + 1) + [anywhere] * 2,
+        out_specs=[vmem] * count + [anywhere] * 4,
         out_shape=[shape((plane, rows, width), BF) for width in widths]
         + [
             shape(mid.shape, BF),
             shape((n_context, 2, 2) + homes[0].shape, BF),
-            shape((2, 3) + homes[0].shape, BF),
+            shape((2, 2) + homes[0].shape, BF),
+            shape((2, 1) + homes[0].shape, BF),
         ],
         scratch_shapes=buffers(n_dp, 4)
         + buffers(n_dp, 4)
@@ -2468,7 +2490,7 @@
     out_own, out_partner = [late[0], last], [early[0], late[1]]
 
     parts = lambda share: share.reshape(n_dp, plane, -1, share.shape[1])
-    total_qkv, total_out, total_small, result, all_second, part_second = reduce_shares(
+    total_qkv, total_out, total_small, result, all_second, part_second, own = reduce_shares(
         [parts(grad_wqkv), parts(grad_wout), parts(grad_small)],
         (own_columns, partner_columns),
         mid_rows,
@@ -2478,7 +2500,6 @@
         n_dp,
         n_context,
     )
-    own = part_second[:, 2:]
     across = flip_permute(own, "context", n_context, 2)
     beside = flip_permute(own, "context", n_context, 1)
     grad_gate, grad_up = (

time: 972 us -> 968 us (level)
  no operation moved by 1% of the time
where the time goes in v7:
time: 968 us; the launch traced here: 964 us
  Pallas kernels  937 us (97%)
  local copies, waits for them, and re-layouts  15 us (2%)
    pallas_call x2, Pallas kernels, run_expert(): pl.pallas_call(functools.partial(expert_kernel, plane, n_dp, half_steps,...  233 us
    pallas_call x1, Pallas kernels, return_rows(): pl.pallas_call(functools.partial(return_kernel, plane, n_dp, len(results)...  140 us
    pallas_call x1, Pallas kernels, dispatch_rows(): pl.pallas_call(functools.partial(dispatch_kernel, plane, n_dp, [(index, f...  135 us
    pallas_call x1, Pallas kernels, reduce_shares(): pl.pallas_call(functools.partial(reduce_kernel, n_dp, widths), in_specs=[...  128 us
    pallas_call x1, Pallas kernels, backward(): pl.pallas_call(functools.partial(backward_kernel, n_dp, prompt_len, len(r...  122 us
    pallas_call x1, Pallas kernels, gather_parts(): pl.pallas_call(functools.partial(gather_kernel, n_dp, plane), in_specs=[v...  71.6 us
    pallas_call x1, Pallas kernels, front(): pl.pallas_call(functools.partial(front_kernel, n_dp, prompt_len, [(index,...  70.7 us
    pallas_call x3, Pallas kernels, finish_weight(): pl.pallas_call(functools.partial(finish_kernel, n_context, apart, halves)...  36.6 us
  transfers between devices with their start and end apart: 3, of which 1 were waited for; matrix products, arithmetic and copies ran while one was open for 1% of the time, Pallas kernels for 3%

profile of v7, /device:TPU:0, one launch (start us, length us, event | category | flops | bytes accessed | tf_op | source)
XLA Modules:
  0.0 963.6 jit_solution(12629890421036115299)
XLA Ops:
  0.6 0.0 copy-start
  0.7 0.7 copy-done
  1.4 0.1 constant_dynamic-slice_fusion
  1.5 0.1 copy.35
  1.6 0.8 convert_bitcast_fusion
  2.4 0.1 copy.31
  2.5 0.1 copy.30
  2.6 0.8 dynamic-slice_convert_fusion.2
  3.5 1.7 dynamic-slice_convert_fusion
  5.2 1.4 fusion
  6.7 1.2 pad_maximum_fusion
  7.8 0.8 concatenate.16.in_ref
  8.6 71.6 %gather_parts.1 = (f32[768,32]{1,0:T(8,128)}, bf16[2,8,768]{2,1,0:T(8,128)(2,1)}, bf16[2,768,8]{2,1,0:T(8,128)(2,1)}, bf16[2,8,768]{2,1,0:T(8,128)(2,1)}, bf16[2...) custom-call(s32[4,768]{1,0:T(4,128)} %bitcast.79, ...), custom_call_target="tpu_custom_call" | custom-call | tf_op jit(solution)/shard_map/gather_parts/pallas_call | solution.py:987
  80.2 70.7 %front.1 = (f32[8,1536]{1,0:T(8,128)}, f32[768,128]{1,0:T(8,128)}, f32[768,128]{1,0:T(8,128)}, bf16[768,1536]{1,0:T(8,128)(2,1)}, bf16[768,2048]{1,0:T(8,128)(2,...) custom-call(bf16[768,1536]{1,0:T(8,128)(2,1)} %bitcast.56, ...), custom_call_target="tpu_custom_call" | custom-call | tf_op jit(solution)/shard_map/front/pallas_call | solution.py:1190
  150.9 134.5 %dispatch_rows.1 = (f32[768,32]{1,0:T(8,128)}, f32[8,4,128]{2,1,0:T(4,128)}, bf16[8,112,1536]{2,1,0:T(8,128)(2,1)}, bf16[8,112,1536]{2,1,0:T(8,128)(2,1)}, bf16[...) custom-call(bf16[768,1536]{1,0:T(8,128)(2,1)} %get-tuple-element.127, ...), custom_call_target="tpu_custom_call" | custom-call | flops 20000000000 | bytes 400000000 | tf_op jit(solution)/shard_map/dispatch_rows/pallas_call | solution.py:1354
  285.4 125.8 %first_expert.1 = (bf16[896,1536]{1,0:T(8,128)(2,1)}, bf16[896,1536]{1,0:T(8,128)(2,1)}, bf16[896,1536]{1,0:T(8,128)(2,1)}, bf16[896,1536]{1,0:T(8,128)(2,1)}, f...) custom-call(bf16[896,1536]{1,0:T(8,128)(2,1)} %bitcast.68, ...), custom_call_target="tpu_custom_call" | custom-call | tf_op jit(solution)/shard_map/first_expert/pallas_call | solution.py:691
  411.2 107.2 %second_expert.1 = (bf16[896,1536]{1,0:T(8,128)(2,1)}, bf16[896,1536]{1,0:T(8,128)(2,1)}, bf16[896,1536]{1,0:T(8,128)(2,1)}, bf16[896,1536]{1,0:T(8,128)(2,1)}, ...) custom-call(bf16[896,1536]{1,0:T(8,128)(2,1)} %bitcast.64, ...), custom_call_target="tpu_custom_call" | custom-call | tf_op jit(solution)/shard_map/second_expert/pallas_call | solution.py:691
  518.4 140.3 %return_rows.1 = (f32[768,1536]{1,0:T(8,128)}, bf16[768,128]{1,0:T(8,128)(2,1)}, bf16[2,3,384,768]{3,2,1,0:T(8,128)(2,1)}, bf16[8,112,1536]{2,1,0:T(8,128)(2,1)}...) custom-call(bf16[2,768,8]{2,1,0:T(8,128)(2,1)} %get-tuple-element.12, ...), custom_call_target="tpu_custom_call" | custom-call | flops 30000001024 | bytes 400000000 | tf_op jit(solution)/shard_map/return_rows/pallas_call | solution.py:1587
  658.6 122.4 %backward.1 = (bf16[768,1536]{1,0:T(8,128)(2,1)}, bf16[1536,1536]{1,0:T(8,128)(2,1)}, bf16[1536,2048]{1,0:T(8,128)(2,1)}, bf16[1536,128]{1,0:T(8,128)(2,1)}, bf1...) custom-call(bf16[768,128]{1,0:T(8,128)(2,1)} %get-tuple-element.190., ...), custom_call_target="tpu_custom_call" | custom-call | tf_op jit(solution)/shard_map/backward/pallas_call | solution.py:1947
  781.0 127.9 %reduce_shares.1 = (bf16[8,48,2048]{2,1,0:T(8,128)(2,1)}, bf16[8,48,1536]{2,1,0:T(8,128)(2,1)}, bf16[8,48,128]{2,1,0:T(8,128)(2,1)}, bf16[768,1536]{1,0:T(8,128)...) custom-call(bf16[4,8,48,2048]{3,2,1,0:T(8,128)(2,1)} %bitcast.58, ...), custom_call_target="tpu_custom_call" | custom-call | tf_op jit(solution)/shard_map/reduce_shares/pallas_call | solution.py:2219
  908.9 0.4 collective-permute-start.1
  909.4 0.8 collective-permute-start
  910.2 12.2 %finish_weight.4 = f32[384,16,768]{2,1,0:T(8,128)} custom-call(bf16[4,2,3,384,768]{4,3,2,1,0:T(8,128)(2,1)} %get-tuple-element.225.refs_0_, bf16[2,3,384,768]{3,2,1,0:T(8,128)(2,1)} %get-tuple-element.199.refs_16_.refs_1_, bf16[4,2,2,384,768]{4,3,2,1,0:T(8,128)(2,1)} %get-tuple-element.226.refs_2_, bf16[2,2,384,768]{3,2,1,0:T(8,128)(2,1)} %get-tuple-element.227.refs_3_), custom_call_target="tpu_custom_call" | custom-call | flops 2000000000 | bytes 30000000 | tf_op jit(solution)/shard_map/finish_weight/pallas_call | solution.py:2329
  922.4 12.2 %finish_weight.3 = f32[384,16,768]{2,1,0:T(8,128)} custom-call(bf16[4,2,3,384,768]{4,3,2,1,0:T(8,128)(2,1)} %get-tuple-element.225.refs_0_, bf16[2,3,384,768]{3,2,1,0:T(8,128)(2,1)} %get-tuple-element.199.refs_16_.refs_1_, bf16[4,2,2,384,768]{4,3,2,1,0:T(8,128)(2,1)} %get-tuple-element.226.refs_2_, bf16[2,2,384,768]{3,2,1,0:T(8,128)(2,1)} %get-tuple-element.227.refs_3_), custom_call_target="tpu_custom_call" | custom-call | flops 2000000000 | bytes 30000000 | tf_op jit(solution)/shard_map/finish_weight/pallas_call | solution.py:2329
  934.7 0.0 copy-start.6
  934.7 0.0 collective-permute-done.1
  934.7 0.0 copy-start.4
  934.7 3.0 collective-permute-done
  937.7 0.0 collective-permute-start.2
  937.7 0.0 copy-done.4
  937.7 1.8 bitcast_convert_fusion
  939.5 0.0 copy-done.6
  939.5 0.7 slice.29
  940.2 1.7 copy.38
  941.8 0.0 copy-start.5
  941.8 1.6 slice.24
  943.5 0.9 slice_reduce_fusion
  944.3 0.9 fusion.1
  945.3 0.0 copy-done.5
  945.3 1.8 bitcast_convert_fusion.1
  947.1 0.0 collective-permute-done.2
  947.1 12.2 %finish_weight.5 = f32[192,16,1536]{2,1,0:T(8,128)} custom-call(bf16[4,2,3,2,192,768]{5,4,3,2,1,0:T(8,128)(2,1)} %bitcast.46, bf16[2,3,2,192,768]{4,3,2,1,0:T(8,128)(2,1)} %bitcast.47, bf16[2,1,2,192,768]{4,3,2,1,0:T(8,128)(2,1)} %bitcast.74, bf16[2,1,2,192,768]{4,3,2,1,0:T(8,128)(2,1)} %bitcast.75, bf16[2,1,2,192,768]{4,3,2,1,0:T(8,128)(2,1)} %bitcast.37.refs_4_, ...), custom_call_target="tpu_custom_call" | custom-call | flops 2000000000 | bytes 30000000 | tf_op jit(solution)/shard_map/finish_weight/pallas_call | solution.py:2329
  959.2 0.0 copy-done.3
  959.2 0.0 copy-start.1
  959.3 1.4 copy.43
  960.7 1.1 copy-done.2
  961.8 1.4 copy.44
  963.2 0.0 copy-done.1
  (8 shorter events, 0.0 us)
Async XLA Ops:
  0.6 0.8 copy-start
  908.9 25.7 %collective-permute-start.1 = (bf16[2,1,384,768]{3,2,1,0:T(8,128)(2,1)}, bf16[2,1,384,768]{3,2,1,0:T(8,128)(2,1)S(1)}, u32[]{:S(2)}, u32[]{:S(2)}) collective-permute-start(bf16[2,1,384,768]{3,2,1,0:T(8,128)(2,1)} %get-tuple-element.224), channel_id=1, source_target_pairs={{0,4},{4,0},{8,12},{12,8},{1,5},{5,1},{9,13},{13,9},{2,6},{6,2},{1... | collective-permute-start | bytes 3538952 | tf_op jit(solution)/shard_map/ppermute | solution.py:2342
  909.4 28.3 %collective-permute-start = (bf16[2,1,384,768]{3,2,1,0:T(8,128)(2,1)}, bf16[2,1,384,768]{3,2,1,0:T(8,128)(2,1)}, u32[]{:S(2)}, u32[]{:S(2)}) collective-permute-start(bf16[2,1,384,768]{3,2,1,0:T(8,128)(2,1)} %get-tuple-element.224), channel_id=1, source_target_pairs={{0,8},{4,12},{8,0},{12,4},{1,9},{5,13},{9,1},{13,5},{2,10},{6,14},... | collective-permute-start | bytes 3538952 | tf_op jit(solution)/shard_map/ppermute | solution.py:2342
  934.7 4.8 copy-start.6
  934.7 3.0 copy-start.4
  937.7 9.4 collective-permute-start.2
  941.8 3.5 copy-start.5
  947.1 12.2 %copy-start.3 = (bf16[768,1536]{1,0:T(8,128)(2,1)S(1)}, bf16[768,1536]{1,0:T(8,128)(2,1)}, u32[]{:S(2)}) copy-start(bf16[768,1536]{1,0:T(8,128)(2,1)} %get-tuple-element.219) | copy-start | bytes 7077892
  959.2 2.5 copy-start.2
  959.2 3.9 copy-start.1
